TPU v7x, 32 devices: a whole 2x2x4 slice. The times are simulated.
32 devices in a mesh: chan: 4 (over x, core), tm: 8 (over z, y).
Axes of the slice: x: 2, y: 2, z: 4, core: 2. Of those that a mesh axis runs over, the one named last changes fastest.
Arguments:
- ref_signal: float32 [2, 16384], P(None, 'tm'), may hold values from -40 to 40
- surveillance: float32 [2, 256, 16384], P(None, 'chan', 'tm'), may hold values from -2000 to 2000
- steering: float32 [2, 64, 256], P(None, None, 'chan'), may hold values from -0.5 to 0.5
Outputs:
- range_doppler: float32 [64, 2, 256, 256], P('chan', None, 'tm')
All inputs are finite; a program needn't handle non-finite values.
Results may differ from a plain program's by a relative error of at most 0.0003.
Values sent between devices are 32-bit elements; how exact they have to be, the bound alone decides.
No kernel may reach another device: no remote copies, remote signals or barrier semaphores. Data moves between devices by JAX's collectives and lax.ppermute only.
A program may use at most 64 MiB of HBM per device.

v0:
```python
import math

import jax
import jax.numpy as jnp
from jax import lax
from jax.sharding import PartitionSpec as P

BEAMS = 64
LAGS = 256
DOPPLER = 256
TAPS = 64
BLOCK_LEN = 256


def from_behind(x, axis, by):
    length = lax.axis_size(axis)
    pairs = [(i, i + by) for i in range(length) if 0 <= i + by < length]
    return lax.ppermute(x, axis, pairs)


def lag_table(ref_ext, offset):
    span_len = BLOCK_LEN + LAGS + 1
    window = lax.dynamic_slice_in_dim(ref_ext, offset, span_len, 1)
    tiled_ref = jnp.tile(window, (1, LAGS))[:, : LAGS * (span_len - 1)]
    return tiled_ref.reshape(2, LAGS, span_len - 1)[:, :, LAGS : LAGS + BLOCK_LEN]


def doppler_table(block_count):
    block_ids = jnp.arange(block_count, dtype=jnp.int32)
    doppler_bins = jnp.arange(DOPPLER, dtype=jnp.int32)
    phase_arg = (block_ids[:, None] * doppler_bins[None, :] % DOPPLER).astype(jnp.float32) * (
        2.0 * math.pi / DOPPLER
    )
    cosine = jnp.cos(phase_arg)
    sine_neg = -jnp.sin(phase_arg)
    upper_rows = jnp.concatenate([cosine, sine_neg], 1)
    lower_rows = jnp.concatenate([-sine_neg, cosine], 1)
    return jnp.concatenate([upper_rows, lower_rows], 0)


def on_device(ref_signal, surveillance, steering):
    highest = lax.Precision.HIGHEST
    length = ref_signal.shape[1]
    blocks_dev = length // BLOCK_LEN
    chan_local = surveillance.shape[1]
    edge_cells = from_behind(ref_signal[:, length - LAGS :], "tm", 1)
    ref_ext = jnp.concatenate([edge_cells, ref_signal, jnp.zeros((2, 1), jnp.float32)], axis=1)
    survey = surveillance.reshape(2 * chan_local, length)
    block_ids = jnp.arange(blocks_dev, dtype=jnp.int32)

    def statistics(carry, block_idx):
        gram_sum, cross_sum = carry
        offset = block_idx * BLOCK_LEN
        basis = lag_table(ref_ext, offset)[:, :TAPS, :].reshape(2 * TAPS, BLOCK_LEN)
        portion = lax.dynamic_slice_in_dim(survey, offset, BLOCK_LEN, 1)
        gram_sum = gram_sum + jnp.dot(basis, basis.T, precision=highest)
        cross_sum = cross_sum + jnp.dot(basis, portion.T, precision=highest)
        return ((gram_sum, cross_sum), None)

    start_carry = (
        jnp.zeros((2 * TAPS, 2 * TAPS), jnp.float32),
        jnp.zeros((2 * TAPS, 2 * chan_local), jnp.float32),
    )
    (gram_sum, cross_sum), _ = lax.scan(statistics, start_carry, block_ids)
    gram_sum, cross_sum = lax.psum((gram_sum, cross_sum), "tm")
    g_real = gram_sum[:TAPS, :TAPS] + gram_sum[TAPS:, TAPS:]
    g_imag = gram_sum[:TAPS, TAPS:] - gram_sum[TAPS:, :TAPS]
    system = jnp.concatenate(
        [jnp.concatenate([g_real, -g_imag], 1), jnp.concatenate([g_imag, g_real], 1)], 0
    )
    b_real = cross_sum[:TAPS, :chan_local] + cross_sum[TAPS:, chan_local:]
    b_imag = cross_sum[:TAPS, chan_local:] - cross_sum[TAPS:, :chan_local]
    factor = jnp.linalg.cholesky(system)
    solved = jax.scipy.linalg.cho_solve((factor, True), jnp.concatenate([b_real, b_imag], 0))
    a_real = solved[:TAPS].T
    a_imag = solved[TAPS:].T
    mixing = jnp.concatenate(
        [jnp.concatenate([a_real, -a_imag], 1), jnp.concatenate([a_imag, a_real], 1)], 0
    )

    def cleanse(carry, block_idx):
        offset = block_idx * BLOCK_LEN
        basis = lag_table(ref_ext, offset)[:, :TAPS, :].reshape(2 * TAPS, BLOCK_LEN)
        portion = lax.dynamic_slice_in_dim(survey, offset, BLOCK_LEN, 1)
        return (carry, portion - jnp.dot(mixing, basis, precision=highest))

    _, cleaned_blocks = lax.scan(cleanse, None, block_ids)
    cleaned = cleaned_blocks.transpose(1, 0, 2).reshape(2 * chan_local, length)
    beams_local = BEAMS // lax.axis_size("chan")
    w_real = steering[0]
    w_imag = steering[1]
    w_rows = jnp.stack(
        [jnp.concatenate([w_real, -w_imag], 1), jnp.concatenate([w_imag, w_real], 1)], 1
    )
    w_rows = w_rows.reshape(2 * (beams_local * lax.axis_size("chan")), 2 * chan_local)
    beam_signal = lax.psum_scatter(
        jnp.dot(w_rows, cleaned, precision=highest).reshape(
            beams_local * lax.axis_size("chan"), 2, length
        ),
        "chan",
        scatter_dimension=0,
        tiled=True,
    )

    def correlate(carry, block_idx):
        offset = block_idx * BLOCK_LEN
        lag_rows = lag_table(ref_ext, offset).reshape(2 * LAGS, BLOCK_LEN)
        segment = lax.dynamic_slice_in_dim(beam_signal, offset, BLOCK_LEN, 2).reshape(
            2 * beams_local, BLOCK_LEN
        )
        product = jnp.dot(segment, lag_rows.T, precision=highest).reshape(beams_local, 2, 2, LAGS)
        real_part = product[:, 0, 0] + product[:, 1, 1]
        imag_part = product[:, 1, 0] - product[:, 0, 1]
        return (carry, jnp.stack([real_part, imag_part], 1))

    _, lagged = lax.scan(correlate, None, block_ids)
    decimated = lagged.transpose(3, 1, 2, 0)
    tm_count = lax.axis_size("tm")
    scale = 0.125 / math.sqrt(length * tm_count)
    portion = lax.all_to_all(decimated, "tm", split_axis=0, concat_axis=3, tiled=True)
    total_blocks = portion.shape[3]
    flat_rows = portion.reshape(portion.shape[0], portion.shape[1], 2 * total_blocks)
    spectrum = jnp.matmul(flat_rows, doppler_table(total_blocks), precision=highest)
    lag_local = spectrum.shape[0]
    result = spectrum.reshape(lag_local, beams_local, 2, DOPPLER).transpose(1, 2, 0, 3) * scale
    return result


def solution(mesh):
    placed = (P(None, "tm"), P(None, "chan", "tm"), P(None, None, "chan"))
    return jax.shard_map(
        on_device,
        mesh=mesh,
        in_specs=placed,
        out_specs=P("chan", None, "tm", None),
        check_vma=False,
    )
```

profile of v0, /device:TPU:0, one launch (start us, length us, event | category | flops | bytes accessed | tf_op | source)
XLA Modules:
  0.0 294.6 jit_solution(2311119023637422505)
XLA Ops:
  7.2 4.9 %collective-permute-start = (f32[2,256]{1,0:T(2,128)S(1)}, f32[2,256]{1,0:T(2,128)S(1)}, u32[]{:S(2)}, u32[]{:S(2)}) collective-permute-start(f32[2,256]{1,0:T(2,128)S(1)} %slice.93), channel_id=1, source_target_pairs={{0,1},{1,2},{2,3},{3,4},{4,5},{5,6},{6,7},{8,9},{9,10},{10,11},{11... | collective-permute-start | bytes 6152 | tf_op jit(solution)/shard_map/ppermute | solution.py:18
  14.1 39.8 %while.35 = (s32[]{:T(128)}, f32[128,128]{1,0:T(8,128)S(1)}, f32[128,128]{1,0:T(8,128)S(1)}, s32[8]{0:T(128)S(1)}, f32[2,2305]{1,0:T(2,128)S(1)}, /*index=5*/f32...) while((s32[]{:T(128)}, f32[128,128]{1,0:T(8,128)S(1)}, ...), condition=%wide.region_1.2_spmd.clone, body=%wide.region_0.1_spmd.clone.sunk | while | flops 100728840 | bytes 8276203 | solution.py:64
  15.7 1.6 tile.40
  20.6 1.6 tile.40
  40.6 1.6 tile.40
  45.5 1.6 tile.40
  50.5 1.6 tile.40
  55.5 71.3 %all-reduce.3.cloned.1.call-done = (f32[128,128]{1,0:T(8,128)}, f32[128,128]{0,1:T(8,128)}) async-done(((f32[128,128]{1,0:T(8,128)}, f32[128,128]{0,1:T(8,128)}), (f32[128,128]{1,0:T(8,128)}, f32[128,128]{0,1:T(8,128)})) %all-reduce.3.cloned.1.call-update) | async-done | bytes 131088 | tf_op jit(solution)/shard_map/psum | solution.py:65
  128.0 11.7 %cholesky.15 = f32[128,128]{1,0:T(8,128)S(1)} custom-call(f32[128,128]{1,0:T(8,128)S(1)} %fusion.31), custom_call_target="Cholesky" | custom-call | tf_op jit(solution)/shard_map/jit(cholesky)/cholesky | solution.py:73
  141.0 9.8 %custom-call.10 = f32[1,128,128]{1,2,0:T(8,128)S(1)} custom-call(f32[1,128,128]{2,1,0:T(8,128)S(1)} %fusion.19), custom_call_target="InvertDiagBlocksLowerTriangular" | custom-call | tf_op jit(solution)/shard_map/jit(_cho_solve)/triangular_solve | solution.py:74
  152.5 38.4 %while.33 = (s32[]{:T(128)}, f32[8,128,256]{1,2,0:T(8,128)S(1)}, s32[8]{0:T(128)S(1)}, f32[128,2048]{1,0:T(8,128)}, f32[2,2305]{1,0:T(2,128)S(1)}, /*index=5*/f3...) while((s32[]{:T(128)}, f32[8,128,256]{1,2,0:T(8,128)S(1)}, ...), condition=%wide.region_7.8_spmd, body=%wide.region_6.7_spmd.sunk | while | flops 50364424 | bytes 8603876 | solution.py:87
  191.0 2.8 fusion.20
  193.8 24.3 %reduce-scatter.2.cloned.1.call-done = f32[16,2,2048]{2,0,1:T(8,128)} async-done(((f32[64,2,2048]{2,0,1:T(8,128)}), f32[16,2,2048]{2,0,1:T(8,128)}) %reduce-scatter.2.cloned.1.call-update) | async-done | bytes 262160 | tf_op jit(solution)/shard_map/reduce_scatter | solution.py:96
  218.0 37.6 %while.34 = (s32[]{:T(128)}, f32[8,16,2,256]{3,1,2,0:T(8,128)S(1)}, s32[8]{0:T(128)S(1)}, f32[16,2,2048]{2,0,1:T(8,128)}, f32[2,2305]{1,0:T(2,128)S(1)}, /*index...) while((s32[]{:T(128)}, f32[8,16,2,256]{3,1,2,0:T(8,128)S(1)}, s32[8]{0:T(128)S(1)}, ...), condition=%wide.region_10.11_spmd, body=%wide.region_9.10_spmd.sunk | while | flops 50348040 | bytes 8145116 | solution.py:116
  224.2 1.6 tile.38
  228.9 1.6 tile.38
  233.6 1.6 tile.38
  238.3 1.6 tile.38
  243.0 1.6 tile.38
  257.2 2.1 bitcast_bitcast_fusion
  259.3 5.0 %reshape.116 = f32[8,1,8192]{2,1,0:T(1,128)} reshape(f32[256,8,2,16]{3,2,1,0:T(2,128)} %bitcast_bitcast_fusion) | data formatting | bytes 524288
  264.3 5.5 %all-to-all-start = ((f32[8,1,8192]{2,1,0:T(1,128)}), f32[8,1,8192]{2,1,0:T(1,128)S(1)}, u32[]{:S(2)}, u32[]{:S(2)}) async-start(f32[8,1,8192]{2,1,0:T(1,128)} %reshape.116), calls=%async_computation.1 | async-start | bytes 524288 | tf_op jit(solution)/shard_map/all_to_all | solution.py:120
  270.9 7.7 %all-to-all-done = f32[8,1,8192]{2,1,0:T(1,128)S(1)} async-done(((f32[8,1,8192]{2,1,0:T(1,128)}), f32[8,1,8192]{2,1,0:T(1,128)S(1)}, u32[]{:S(2)}, u32[]{:S(2)}) %all-to-all-start) | async-done | bytes 262176 | tf_op jit(solution)/shard_map/all_to_all | solution.py:120
  280.5 2.8 reshape.117
  (260 shorter events, 99.0 us)
Async XLA Ops:
  6.5 120.2 %all-reduce.3.cloned.1.call-start = ((), (), s32[]{:S(2)}) async-start(), calls=%async_computation.3 | async-start | bytes 262144 | tf_op jit(solution)/shard_map/psum | solution.py:65
  7.2 6.2 %collective-permute-start = (f32[2,256]{1,0:T(2,128)S(1)}, f32[2,256]{1,0:T(2,128)S(1)}, u32[]{:S(2)}, u32[]{:S(2)}) collective-permute-start(f32[2,256]{1,0:T(2,128)S(1)} %slice.93), channel_id=1, source_target_pairs={{0,1},{1,2},{2,3},{3,4},{4,5},{5,6},{6,7},{8,9},{9,10},{10,11},{11... | collective-permute-start | bytes 6152 | tf_op jit(solution)/shard_map/ppermute | solution.py:18
  14.1 40.6 %copy-start.1 = (f32[2,64,64]{2,1,0:T(8,128)S(1)}, f32[2,64,64]{2,1,0:T(8,128)}, u32[]{:S(2)}) copy-start(f32[2,64,64]{2,1,0:T(8,128)} %param.11) | copy-start | bytes 98308
  54.0 0.7 copy-start
  54.7 163.3 %reduce-scatter.2.cloned.1.call-start = ((), (), s32[]{:S(2)}) async-start(), calls=%async_computation.2 | async-start | bytes 1310720 | tf_op jit(solution)/shard_map/reduce_scatter | solution.py:96
  264.3 14.4 %all-to-all-start = ((f32[8,1,8192]{2,1,0:T(1,128)}), f32[8,1,8192]{2,1,0:T(1,128)S(1)}, u32[]{:S(2)}, u32[]{:S(2)}) async-start(f32[8,1,8192]{2,1,0:T(1,128)} %reshape.116), calls=%async_computation.1 | async-start | bytes 524288 | tf_op jit(solution)/shard_map/all_to_all | solution.py:120
Sparse Core Ops, SparseCore 0:
  54.8 71.8 all-reduce.2
  193.9 24.1 reduce-scatter.1
where the time goes:
time: 296 us; the launch traced here: 295 us
  waiting for transfers between devices  104 us (35%)
  local copies, waits for them, and re-layouts  89.7 us (30%)
  matrix products  29.9 us (10%)
  other arithmetic  29 us (10%)
  loops' own time  18.1 us (6%)
  between operations  13.6 us (5%)
  starting transfers between devices  10.4 us (4%)
    psum x1, waiting for transfers between devices, on_device(): gram_sum, cross_sum = lax.psum((gram_sum, cross_sum), 'tm')  71.3 us
    another operation x48, local copies, waits for them, and re-layouts, lag_table(): tiled_ref = jnp.tile(window, (1, LAGS))[:, :LAGS * (span_len - 1)]  40.6 us
    reduce_scatter x1, waiting for transfers between devices, on_device(): lax.psum_scatter(jnp.dot(w_rows, cleaned, precision=highest).reshape(beam...  24.3 us
    dynamic_slice x24, local copies, waits for them, and re-layouts, on_device(): (gram_sum, cross_sum), _ = lax.scan(statistics, start_carry, block_ids)  14.6 us
    another operation x3, other arithmetic, on_device(): factor = jnp.linalg.cholesky(system)  12.4 us
    dot_general x8, matrix products, correlate(): jnp.dot(segment, lag_rows.T, precision=highest)  10.6 us
    another operation x2, other arithmetic, on_device(): jax.scipy.linalg.cho_solve((factor, True), jnp.concatenate([b_real, b_ima...  10.5 us
    unnamed x7, local copies, waits for them, and re-layouts  9.86 us
  transfers between devices with their start and end apart: 4, of which 4 were waited for; matrix products, arithmetic and copies ran while one was open for 1% of the time, Pallas kernels for 0%

commit v1 on v0

v1 whole, which is shorter than its diff:
```python
import functools
import math

import jax
import jax.numpy as jnp
import numpy as np
from jax import lax
from jax.experimental import pallas as pl
from jax.experimental.pallas import tpu as pltpu
from jax.sharding import PartitionSpec as P

LAGS = 256
DOPPLER = 256
TAPS = 64
BLOCK_LEN = 256
LANES = 128
SUBLANES = 8

HIGHEST = lax.Precision.HIGHEST
VMEM_BYTES = 48 * 1024 * 1024


def params():
    return pltpu.CompilerParams(vmem_limit_bytes=VMEM_BYTES)


def halves(x):
    high = x.astype(jnp.bfloat16)
    return high, (x - high.astype(jnp.float32)).astype(jnp.bfloat16)


def dot_nt(a, b, precision=None):
    return lax.dot_general(
        a, b, (((1,), (1,)), ((), ())), precision=precision, preferred_element_type=jnp.float32
    )


def row_sign(shape):
    rows = lax.broadcasted_iota(jnp.int32, shape, 0)
    return jnp.where(rows % SUBLANES < SUBLANES // 2, 1.0, -1.0).astype(jnp.float32)


def lane_sign(shape):
    lanes = lax.broadcasted_iota(jnp.int32, shape, 1)
    return jnp.where(lanes % LANES < LANES // 2, 1.0, -1.0).astype(jnp.float32)


def swap_groups(rows, groups):
    width = LANES // groups
    lane_group = lax.broadcasted_iota(jnp.int32, rows[0].shape, 1) // width
    outs = []
    for j in range(groups):
        out = rows[j]
        for i in range(groups):
            if i != j:
                moved = pltpu.roll(rows[i], (width * (i - j)) % LANES, 1)
                out = jnp.where(lane_group == i, moved, out)
        outs.append(out)
    return outs


def beam_kernel(chan_count, beams_local, w_ref, s_ref, even_ref, odd_ref):
    me = lax.axis_index("chan")
    half = SUBLANES // 2
    sub = lax.broadcasted_iota(jnp.int32, (SUBLANES, w_ref.shape[2]), 0)
    top = sub < half
    parts = []
    for parity in range(2):
        rows = []
        for e in range(parity, chan_count, 2):
            base = (me ^ e) * beams_local
            for tile in range(beams_local // SUBLANES):
                start = pl.multiple_of(base + tile * SUBLANES, SUBLANES)
                wr = w_ref[0, pl.ds(start, SUBLANES), :]
                wi = w_ref[1, pl.ds(start, SUBLANES), :]
                wr_s = pltpu.roll(wr, half, 0)
                wi_s = pltpu.roll(wi, half, 0)
                first = [jnp.where(top, wr, wi_s), jnp.where(top, -wi, wr_s)]
                second = [jnp.where(top, wr_s, wi), jnp.where(top, -wi_s, wr)]
                rows.append(jnp.concatenate(first, 1))
                rows.append(jnp.concatenate(second, 1))
        parts.append(jnp.concatenate(rows, 0))
    weights = jnp.concatenate(parts, 0)
    product = jnp.dot(
        weights, s_ref[...], precision=HIGHEST, preferred_element_type=jnp.float32
    )
    mid = product.shape[0] // 2
    even_ref[...] = product[:mid]
    odd_ref[...] = product[mid:]


def beam_call(steering, survey, chan_count, beams_local):
    depth, length = survey.shape
    rows = chan_count * beams_local
    steps = 4
    width = length // steps
    out = jax.ShapeDtypeStruct((rows, length), jnp.float32)
    return pl.pallas_call(
        functools.partial(beam_kernel, chan_count, beams_local),
        grid=(steps,),
        in_specs=[
            pl.BlockSpec(steering.shape, lambda i: (0, 0, 0)),
            pl.BlockSpec((depth, width), lambda i: (0, i)),
        ],
        out_specs=[pl.BlockSpec((rows, width), lambda i: (0, i))] * 2,
        out_shape=[out, out],
        compiler_params=params(),
        cost_estimate=pl.CostEstimate(
            flops=4 * rows * depth * length, bytes_accessed=4 * length * (depth + 2 * rows), transcendentals=0
        ),
        name="beams",
    )(steering, survey)


def table_kernel(ref_ref, out_ref):
    me = lax.axis_index("tm")
    length = ref_ref.shape[2]
    before = jnp.maximum(me - 1, 0)
    edge = ref_ref[before, :, length - 2 * LANES :]
    edge = jnp.where(me > 0, edge, jnp.zeros_like(edge))
    span = jnp.concatenate([edge, ref_ref[me]], 1)
    for c in range(2):
        tiled = jnp.broadcast_to(span[c : c + 1], (LANES, span.shape[1]))
        shifted = pltpu.roll(tiled, 0, 1, stride=1, stride_axis=0)[:, LANES:]
        high, low = halves(shifted)
        out_ref[0, c] = high
        out_ref[1, c] = low


def table_call(ref_all):
    length = ref_all.shape[2]
    shape = (2, 2, LANES, LANES + length)
    return pl.pallas_call(
        table_kernel,
        out_shape=jax.ShapeDtypeStruct(shape, jnp.bfloat16),
        compiler_params=params(),
        cost_estimate=pl.CostEstimate(
            flops=8 * math.prod(shape), bytes_accessed=2 * math.prod(shape), transcendentals=0
        ),
        name="shifted_reference",
    )(ref_all)


def lag_kernel(groups, owners, *refs):
    *y_refs, table_ref, out_ref = refs
    y = y_refs[0][...]
    for y_ref in y_refs[1:]:
        y = y + y_ref[...]
    rows, length = y.shape
    blocks = length // BLOCK_LEN
    turned = jnp.concatenate(
        [pltpu.roll(y[r : r + SUBLANES], SUBLANES // 2, 0) for r in range(0, rows, SUBLANES)], 0
    )
    turned = turned * row_sign(turned.shape)
    y_high, y_low = halves(y)
    t_high, t_low = halves(turned)
    both = jnp.concatenate([y_high, y_low], 0)
    turned_both = jnp.concatenate([t_high, t_low], 0)
    taps_sum = None
    for q in range(blocks):
        near = slice(q * BLOCK_LEN + LANES, q * BLOCK_LEN + LANES + BLOCK_LEN)
        far = slice(q * BLOCK_LEN, (q + 1) * BLOCK_LEN)
        cols = slice(q * BLOCK_LEN, (q + 1) * BLOCK_LEN)
        tables = []
        for h in range(2):
            tables.append(
                jnp.concatenate(
                    [
                        jnp.concatenate([table_ref[h, 0, :, near], table_ref[h, 1, :, near]], 1),
                        jnp.concatenate([table_ref[h, 0, :, far], table_ref[h, 1, :, far]], 1),
                    ],
                    0,
                )
            )
        lhs = jnp.concatenate([both[:, cols], turned_both[:, cols]], 1)
        by_high = dot_nt(lhs, tables[0])
        by_low = dot_nt(lhs[:rows], tables[1])
        product = by_high[:rows] + (by_high[rows:] + by_low)
        taps = product[:, :LANES]
        taps_sum = taps if taps_sum is None else taps_sum + taps
        for h in range(LAGS // LANES):
            lanes = slice(h * LANES, (h + 1) * LANES)
            tiles = [product[r : r + SUBLANES, lanes] for r in range(0, rows, SUBLANES)]
            for j, tile in enumerate(swap_groups(tiles, groups)):
                out_ref[h * groups + j, q] = tile
    left = lax.broadcasted_iota(jnp.int32, (SUBLANES, LANES), 1) < TAPS
    packed = []
    for i in range(groups // 2):
        a = taps_sum[i * SUBLANES : (i + 1) * SUBLANES]
        other = i + groups // 2
        b = taps_sum[other * SUBLANES : (other + 1) * SUBLANES]
        packed.append(jnp.where(left, a, pltpu.roll(b, LANES - TAPS, 1)))
    for owner in range(owners):
        for i, tile in enumerate(packed):
            out_ref[owner, blocks + i] = tile


def lag_call(ys, table, groups, owners):
    rows, length = ys[0].shape
    blocks = length // BLOCK_LEN
    shape = (owners, blocks + groups // 2, SUBLANES, LANES)
    return pl.pallas_call(
        functools.partial(lag_kernel, groups, owners),
        out_shape=jax.ShapeDtypeStruct(shape, jnp.float32),
        compiler_params=params(),
        cost_estimate=pl.CostEstimate(
            flops=12 * rows * LAGS * 2 * length,
            bytes_accessed=4 * math.prod(shape) + 2 * math.prod(table.shape),
            transcendentals=0,
        ),
        name="lag_products",
    )(*ys, table)


def complex_inverse(a):
    size = a.shape[0]
    lanes = lax.broadcasted_iota(jnp.int32, (1, 2 * size), 1)
    rows = lax.broadcasted_iota(jnp.int32, (size, 1), 0)
    all_lanes = lax.broadcasted_iota(jnp.int32, a.shape, 1)
    all_rows = lax.broadcasted_iota(jnp.int32, a.shape, 0)
    sign = -lane_sign((1, 2 * size))
    for j in range(size):
        col_r = a[:, j : j + 1]
        col_i = a[:, size + j : size + j + 1]
        row = a[j : j + 1]
        pivot = 1.0 / a[j : j + 1, j : j + 1]
        row = jnp.where(lanes == j, 1.0, jnp.where(lanes == size + j, 0.0, row))
        turned = pltpu.roll(row, size, 1) * sign
        row = row * pivot
        turned = turned * pivot
        col_r = jnp.where(rows == j, 0.0, col_r)
        col_i = jnp.where(rows == j, 0.0, col_i)
        kept = jnp.where((all_lanes == j) | (all_lanes == size + j), 0.0, a)
        kept = jnp.where(all_rows == j, row, kept)
        a = kept - (col_r * row + col_i * turned)
    return a


def own_kernel(lags_local, ref_ref, out_ref, span_ref, late_ref):
    owners, _, length = ref_ref.shape
    samples = owners * length
    blocks = samples // BLOCK_LEN
    first_lag = lax.axis_index("tm") * lags_local
    span_ref[:, :BLOCK_LEN] = jnp.zeros((2, BLOCK_LEN), jnp.float32)
    span_ref[:, BLOCK_LEN + samples :] = jnp.zeros((2, BLOCK_LEN), jnp.float32)
    for t in range(owners):
        span_ref[:, BLOCK_LEN + t * length : BLOCK_LEN + (t + 1) * length] = ref_ref[t]
    late_ref[...] = pltpu.roll(span_ref[...], first_lag, 1)

    def shifted(window, count):
        tiled = jnp.broadcast_to(window, (count, window.shape[1]))
        return pltpu.roll(tiled, 0, 1, stride=1, stride_axis=0)[:, LANES : LANES + BLOCK_LEN]

    def taps_of(window):
        return jnp.concatenate(
            [shifted(window[c : c + 1, BLOCK_LEN - LANES :], TAPS) for c in range(2)], 0
        )

    turn = lane_sign((lags_local, LANES))

    def step(q, total):
        lanes = pl.ds(pl.multiple_of(q * BLOCK_LEN, BLOCK_LEN), 2 * BLOCK_LEN)
        window, late = span_ref[:, lanes], late_ref[:, lanes]
        taps_high, taps_low = halves(taps_of(window))
        lag_rows = [shifted(late[c : c + 1, BLOCK_LEN - LANES :], lags_local) for c in range(2)]
        pad = jnp.zeros((2 * SUBLANES - 2, BLOCK_LEN), jnp.float32)
        lag_rows = jnp.concatenate(lag_rows + [window[:, BLOCK_LEN:], pad], 0)
        lags_high, lags_low = halves(lag_rows)
        product = dot_nt(
            jnp.concatenate([lags_high, lags_low], 0), jnp.concatenate([taps_high, taps_low], 0)
        )
        count = lag_rows.shape[0]
        product = product[:count, :LANES] + (product[:count, LANES:] + product[count:, :LANES])
        by_real = product[:lags_local]
        by_imag = product[lags_local : 2 * lags_local]
        rows = pl.ds(pl.multiple_of(q * lags_local, lags_local), lags_local)
        out_ref[rows, :] = by_real + turn * pltpu.roll(by_imag, TAPS, 1)
        return total + product[2 * lags_local : 2 * lags_local + SUBLANES]

    total = lax.fori_loop(0, blocks, step, jnp.zeros((SUBLANES, LANES), jnp.float32))

    line = total[0:1] + lane_sign((1, LANES)) * pltpu.roll(total[1:2], TAPS, 1)
    low = lax.broadcasted_iota(jnp.int32, (1, LANES), 1) < TAPS
    line_r = jnp.where(low, line, 0.0)
    line_i = jnp.where(low, pltpu.roll(line, TAPS, 1), 0.0)
    above = lax.broadcasted_iota(jnp.int32, (TAPS, TAPS), 1) > lax.broadcasted_iota(jnp.int32, (TAPS, TAPS), 0)
    equal = lax.broadcasted_iota(jnp.int32, (TAPS, TAPS), 1) == lax.broadcasted_iota(jnp.int32, (TAPS, TAPS), 0)

    def upper(x):
        spread = pltpu.roll(jnp.broadcast_to(x, (TAPS, LANES)), 0, 1, stride=1, stride_axis=0)
        return spread[:, :TAPS]

    up_r = upper(line_r)
    up_i = jnp.where(above, upper(line_i), 0.0)
    strict_r = jnp.where(above, up_r, 0.0)
    diag_r = jnp.where(equal, up_r, 0.0)
    gram_r = strict_r + strict_r.T + diag_r
    gram_i = up_i - up_i.T
    tail = taps_of(span_ref[:, samples:])
    tails = dot_nt(tail, tail, HIGHEST)
    gram_r = gram_r - (tails[:TAPS, :TAPS] + tails[TAPS:, TAPS:])
    gram_i = gram_i - (tails[:TAPS, TAPS:] - tails[TAPS:, :TAPS])

    inverse = complex_inverse(jnp.concatenate([gram_r, gram_i], 1))
    lower = -lane_sign(inverse.shape) * pltpu.roll(inverse, TAPS, 1)
    solver = jnp.concatenate([inverse, lower], 0)
    out_ref[...] = jnp.dot(
        out_ref[...], solver, precision=HIGHEST, preferred_element_type=jnp.float32
    )


def own_call(ref_all, lags_local):
    owners, _, length = ref_all.shape
    samples = owners * length
    blocks = samples // BLOCK_LEN
    shape = (blocks * lags_local, 2 * TAPS)
    return pl.pallas_call(
        functools.partial(own_kernel, lags_local),
        out_shape=jax.ShapeDtypeStruct(shape, jnp.float32),
        scratch_shapes=[pltpu.VMEM((2, samples + 2 * BLOCK_LEN), jnp.float32)] * 2,
        compiler_params=params(),
        cost_estimate=pl.CostEstimate(
            flops=12 * samples * 2 * TAPS * 4 * lags_local, bytes_accessed=4 * math.prod(shape), transcendentals=0
        ),
        name="reference_products",
    )(ref_all)


def doppler_table(block_count, scale):
    phase = (np.arange(block_count)[:, None] * np.arange(DOPPLER)[None, :] % DOPPLER) * (2.0 * math.pi / DOPPLER)
    cosine, sine = np.cos(phase), np.sin(phase)
    upper = np.concatenate([cosine, -sine], 1)
    lower = np.concatenate([sine, cosine], 1)
    return (np.concatenate([upper, lower], 0) * scale).astype(np.float32)


def map_kernel(groups, got_ref, own_ref, wave_ref, out_ref, held_ref):
    owners, pieces = got_ref.shape[:2]
    blocks = pieces - groups // 2
    lags_local = LANES // groups
    total = owners * blocks
    left = lax.broadcasted_iota(jnp.int32, (SUBLANES, LANES), 1) < TAPS
    sign = row_sign((SUBLANES, LANES))
    rows = [None] * groups
    for i in range(groups // 2):
        tile = got_ref[0, blocks + i]
        for owner in range(1, owners):
            tile = tile + got_ref[owner, blocks + i]
        swapped = pltpu.roll(tile, TAPS, 1)
        for part, here, there in ((i, tile, swapped), (i + groups // 2, swapped, tile)):
            other = -sign * pltpu.roll(there, SUBLANES // 2, 0)
            rows[part] = jnp.where(left, here, other)
    cross = jnp.concatenate(rows, 0)
    clutter = dot_nt(cross, own_ref[...], HIGHEST)
    for q in range(0, total, groups):
        lanes = slice(q * lags_local, q * lags_local + LANES)
        tiles = [clutter[r : r + SUBLANES, lanes] for r in range(0, groups * SUBLANES, SUBLANES)]
        for j, tile in enumerate(swap_groups(tiles, groups)):
            at = q + j
            held_ref[at * SUBLANES : (at + 1) * SUBLANES, :] = got_ref[at // blocks, at % blocks] - tile
    half = SUBLANES // 2
    wave = wave_ref[...]
    for g in range(half):
        parts = [held_ref[pl.ds(c * half + g, total, stride=SUBLANES), :] for c in range(2)]
        lagged = jnp.concatenate(parts, 0).T
        spectrum = jnp.dot(lagged, wave, precision=HIGHEST, preferred_element_type=jnp.float32)
        for i in range(groups):
            for c in range(2):
                out_ref[half * i + g, c] = spectrum[
                    i * lags_local : (i + 1) * lags_local, c * DOPPLER : (c + 1) * DOPPLER
                ]


def map_call(got, own, wave, groups, beams_local):
    owners, pieces = got.shape[:2]
    total = owners * (pieces - groups // 2)
    lags_local = LANES // groups
    shape = (beams_local, 2, lags_local, DOPPLER)
    return pl.pallas_call(
        functools.partial(map_kernel, groups),
        out_shape=jax.ShapeDtypeStruct(shape, jnp.float32),
        scratch_shapes=[pltpu.VMEM((total * SUBLANES, LANES), jnp.float32)],
        compiler_params=params(),
        cost_estimate=pl.CostEstimate(
            flops=12 * math.prod(shape) * total, bytes_accessed=4 * math.prod(shape), transcendentals=0
        ),
        name="range_doppler",
    )(got, own, wave)


def swap(x, axis, by):
    pairs = [(i, i ^ by) for i in range(lax.axis_size(axis))]
    return lax.ppermute(x, axis, pairs)


def tiled_device(ref_signal, surveillance, steering):
    chan_count, tm_count = lax.axis_size("chan"), lax.axis_size("tm")
    channels, length = surveillance.shape[1:]
    beams_local = steering.shape[1] // chan_count
    lags_local = LAGS // tm_count
    groups = LANES // lags_local
    samples = length * tm_count

    ref_all = lax.all_to_all(
        jnp.broadcast_to(ref_signal[None], (tm_count,) + ref_signal.shape), "tm", 0, 0, tiled=True
    )
    even, odd = beam_call(steering, surveillance.reshape(2 * channels, length), chan_count, beams_local)
    rows = 2 * beams_local
    parts = [even.reshape(chan_count // 2, rows, length), swap(odd, "chan", 1).reshape(chan_count // 2, rows, length)]
    by = 2
    while by < chan_count:
        sent = parts[0][1::2]
        for part in parts[1:]:
            sent = sent + part[1::2]
        parts = [part[::2] for part in parts] + [swap(sent, "chan", by)]
        by *= 2
    table = table_call(ref_all)
    pieces = lag_call([part[0] for part in parts], table, groups, tm_count)
    got = lax.all_to_all(pieces, "tm", 0, 0, tiled=True)
    own = own_call(ref_all, lags_local)
    wave = doppler_table(samples // BLOCK_LEN, 0.125 / math.sqrt(samples))
    return map_call(got, own, jnp.asarray(wave), groups, beams_local)


def lag_table(ref_ext, offset, lags):
    window = lax.dynamic_slice_in_dim(ref_ext, offset, BLOCK_LEN + LAGS, 1)
    span = BLOCK_LEN + LAGS
    tiled = jnp.tile(jnp.pad(window, ((0, 0), (0, 1))), (1, lags))[:, : lags * span]
    return tiled.reshape(2, lags, span)[:, :, LAGS:]


def times_conj(a, b):
    real = jnp.einsum("...t,lt->...l", a[..., 0, :], b[0], precision=HIGHEST) + jnp.einsum(
        "...t,lt->...l", a[..., 1, :], b[1], precision=HIGHEST
    )
    imag = jnp.einsum("...t,lt->...l", a[..., 1, :], b[0], precision=HIGHEST) - jnp.einsum(
        "...t,lt->...l", a[..., 0, :], b[1], precision=HIGHEST
    )
    return jnp.stack([real, imag], -2)


def plain_device(ref_signal, surveillance, steering):
    chan_count, tm_count = lax.axis_size("chan"), lax.axis_size("tm")
    length = surveillance.shape[2]
    beams = steering.shape[1]
    lags_local = LAGS // tm_count
    samples = length * tm_count
    local_blocks = length // BLOCK_LEN
    here = lax.axis_index("tm")

    w_real, w_imag = steering
    real = jnp.dot(w_real, surveillance[0], precision=HIGHEST) - jnp.dot(w_imag, surveillance[1], precision=HIGHEST)
    imag = jnp.dot(w_imag, surveillance[0], precision=HIGHEST) + jnp.dot(w_real, surveillance[1], precision=HIGHEST)
    beam = lax.psum_scatter(jnp.stack([real, imag], 1), "chan", scatter_dimension=0, tiled=True)
    ref_all = lax.all_gather(ref_signal, "tm", axis=1, tiled=True)
    ref_ext = jnp.pad(ref_all, ((0, 0), (LAGS, 0)))

    def beam_step(carry, q):
        offset = q * BLOCK_LEN
        table = lag_table(ref_ext, here * length + offset, LAGS)
        segment = lax.dynamic_slice_in_dim(beam, offset, BLOCK_LEN, 2)
        return carry, times_conj(segment, table)

    _, products = lax.scan(beam_step, None, jnp.arange(local_blocks, dtype=jnp.int32))
    cross = lax.psum(products[..., :TAPS].sum(0), "tm")
    got = lax.all_to_all(products, "tm", 3, 0, tiled=True)

    def own_step(gram, q):
        offset = q * BLOCK_LEN
        table = lag_table(ref_ext, offset, LAGS)
        taps = table[:, :TAPS].transpose(1, 0, 2)
        mine = lax.dynamic_slice_in_dim(table, here * lags_local, lags_local, 1)
        return gram + times_conj(taps, table[:, :TAPS]), times_conj(taps, mine)

    start = jnp.zeros((TAPS, 2, TAPS), jnp.float32)
    gram, own = lax.scan(own_step, start, jnp.arange(samples // BLOCK_LEN, dtype=jnp.int32))
    g_real, g_imag = gram[:, 0].T, gram[:, 1].T
    system = jnp.concatenate([jnp.concatenate([g_real, -g_imag], 1), jnp.concatenate([g_imag, g_real], 1)], 0)
    right = jnp.concatenate([cross[:, 0].T, cross[:, 1].T], 0)
    solved = jax.scipy.linalg.cho_solve((jnp.linalg.cholesky(system), True), right)
    b_real, b_imag = solved[:TAPS].T, solved[TAPS:].T
    mixing = jnp.concatenate([jnp.stack([b_real, b_imag], 1), jnp.stack([-b_imag, b_real], 1)], 2)
    stacked = jnp.concatenate([own[:, :, 0], own[:, :, 1]], 1)
    lagged = got - jnp.einsum("mck,qkl->qmcl", mixing, stacked, precision=HIGHEST)
    wave = jnp.asarray(doppler_table(samples // BLOCK_LEN, 0.125 / math.sqrt(samples)))
    wave = wave.reshape(2, samples // BLOCK_LEN, 2, DOPPLER)
    return jnp.einsum("qmcl,cqdk->mdlk", lagged, wave, precision=HIGHEST)


def on_device(ref_signal, surveillance, steering):
    chan_count, tm_count = lax.axis_size("chan"), lax.axis_size("tm")
    beams_local = steering.shape[1] // chan_count
    lags_local = LAGS // tm_count
    fills = (
        LANES % lags_local == 0
        and lags_local % (2 * SUBLANES) == 0
        and beams_local * lags_local == LANES * SUBLANES // 2
        and chan_count > 1
        and chan_count & (chan_count - 1) == 0
        and 2 * surveillance.shape[1] % LANES == 0
        and surveillance.shape[2] % (4 * BLOCK_LEN) == 0
    )
    device = tiled_device if fills else plain_device
    return device(ref_signal, surveillance, steering)


def solution(mesh):
    placed = (P(None, "tm"), P(None, "chan", "tm"), P(None, None, "chan"))
    return jax.shard_map(
        on_device,
        mesh=mesh,
        in_specs=placed,
        out_specs=P("chan", None, "tm", None),
        check_vma=False,
    )
```

time: 296 us -> 63.4 us (0.21)
  waiting for transfers between devices: 104 us -> 1.54 us
  local copies, waits for them, and re-layouts: 89.7 us -> 2.11 us
  Pallas kernels: 0 us -> 39.4 us
  matrix products: 29.9 us -> 0 us
  other arithmetic: 29 us -> 0.07 us
  loops' own time: 18.1 us -> 0 us
  between operations: 13.6 us -> 0.08 us
  blocking collectives: 0 us -> 13 us
  starting transfers between devices: 10.4 us -> 6.88 us
    psum x1 -> x0, waiting for transfers between devices: 71.3 us -> none  [on_device(): gram_sum, cross_sum = lax.psum((gram_sum, cross_sum), 'tm')]
    another operation x48 -> x0, local copies, waits for them, and re-layouts: 40.6 us -> none  [lag_table(): tiled_ref = jnp.tile(window, (1, LAGS))[:, :LAGS * (span_len - 1)]]
    pallas_call x0 -> x5, Pallas kernels: none -> 39.4 us  [the longest x1 31.3 us: own_call(): pl.pallas_call(functools.partial(own_kernel, lags_local), out_shape=jax.S...]
    dot_general x34 -> x0, matrix products: 29.4 us -> none  [the longest x8 10.6 us: correlate(): jnp.dot(segment, lag_rows.T, precision=highest)]
    dynamic_slice x64 -> x0, local copies, waits for them, and re-layouts: 24.6 us -> none  [the longest x24 14.6 us: on_device(): (gram_sum, cross_sum), _ = lax.scan(statistics, start_carry, block_ids)]
    reduce_scatter x1 -> x0, waiting for transfers between devices: 24.3 us -> none  [on_device(): lax.psum_scatter(jnp.dot(w_rows, cleaned, precision=highest).reshape(beam...]
    another operation x6 -> x0, other arithmetic: 23.5 us -> none  [the longest x3 12.4 us: on_device(): factor = jnp.linalg.cholesky(system)]
    another operation x3 -> x0, loops' own time: 18.1 us -> none  [the longest x1 6.18 us: on_device(): (gram_sum, cross_sum), _ = lax.scan(statistics, start_carry, block_ids)]
  transfers between devices with their start and end apart: 4 -> 3, of which waited for: 4 -> 1; matrix products, arithmetic and copies ran while one was open for 1% -> 0% of each run, Pallas kernels for 0% -> 51%
where the time goes in v1:
time: 63.4 us; the launch traced here: 63 us
  Pallas kernels  39.4 us (62%)
  blocking collectives  13 us (21%)
  starting transfers between devices  6.88 us (11%)
  local copies, waits for them, and re-layouts  2.11 us (3%)
  waiting for transfers between devices  1.54 us (2%)
    pallas_call x1, Pallas kernels, own_call(): pl.pallas_call(functools.partial(own_kernel, lags_local), out_shape=jax.S...  31.3 us
    all_to_all x1, blocking collectives, tiled_device(): lax.all_to_all(jnp.broadcast_to(ref_signal[None], (tm_count,) + ref_signa...  13 us
    ppermute x2, starting transfers between devices, swap(): return lax.ppermute(x, axis, pairs)  3.44 us
    all_to_all x1, starting transfers between devices, tiled_device(): got = lax.all_to_all(pieces, 'tm', 0, 0, tiled=True)  3.43 us
    pallas_call x1, Pallas kernels, map_call(): pl.pallas_call(functools.partial(map_kernel, groups), out_shape=jax.Shape...  3.33 us
    pallas_call x1, Pallas kernels, lag_call(): pl.pallas_call(functools.partial(lag_kernel, groups, owners), out_shape=j...  2.2 us
    unnamed x8, local copies, waits for them, and re-layouts  2.07 us
    pallas_call x1, Pallas kernels, beam_call(): pl.pallas_call(functools.partial(beam_kernel, chan_count, beams_local), g...  1.91 us
  transfers between devices with their start and end apart: 3, of which 1 were waited for; matrix products, arithmetic and copies ran while one was open for 0% of the time, Pallas kernels for 51%

profile of v1, /device:TPU:0, one launch (start us, length us, event | category | flops | bytes accessed | tf_op | source)
XLA Modules:
  0.0 63.0 jit_solution(14409420966638497835)
XLA Ops:
  0.0 0.0 copy-start
  0.0 1.2 %copy-done = f32[2,64,2048]{2,1,0:T(8,128)S(1)} copy-done((f32[2,64,2048]{2,1,0:T(8,128)S(1)}, f32[2,64,2048]{2,1,0:T(8,128)}, u32[]{:S(2)}) %copy-start) | copy-done | bytes 1048600
  1.2 0.0 copy-start.2
  1.2 0.8 %copy-done.2 = f32[2,64,64]{2,1,0:T(8,128)S(1)} copy-done((f32[2,64,64]{2,1,0:T(8,128)S(1)}, f32[2,64,64]{2,1,0:T(8,128)}, u32[]{:S(2)}) %copy-start.2) | copy-done | bytes 32792
  2.1 0.0 copy-start.3
  2.1 1.9 %beams.1 = (f32[64,2048]{1,0:T(8,128)S(1)}, f32[64,2048]{1,0:T(8,128)S(1)}) custom-call(f32[2,64,64]{2,1,0:T(8,128)S(1)} %copy-done.2, f32[128,2048]{1,0:T(8,128)S(1)} %bitcast.4), custom_call_target="tpu_custom_call" | custom-call | flops 67108864 | bytes 2097152 | tf_op jit(solution)/shard_map/beams/pallas_call | solution.py:98
  4.0 0.5 collective-permute-start
  4.5 1.5 %collective-permute-done = f32[64,2048]{1,0:T(8,128)S(1)} collective-permute-done((f32[64,2048]{1,0:T(8,128)S(1)}, f32[64,2048]{1,0:T(8,128)S(1)}, u32[]{:S(2)}, u32[]{:S(2)}) %collective-permute-start) | collective-permute-done | bytes 524320 | tf_op jit(solution)/shard_map/ppermute | solution.py:393
  6.0 0.1 fusion
  6.1 2.9 %collective-permute-start.1 = (f32[1,32,2048]{2,1,0:T(8,128)S(1)}, f32[1,32,2048]{2,1,0:T(8,128)S(1)}, u32[]{:S(2)}, u32[]{:S(2)}) collective-permute-start(f32[1,32,2048]{2,1,0:T(8,128)S(1)} %get-tuple-element.9), channel_id=1, source_target_pairs={{0,16},{8,24},{16,0},{24,8},{1,17},{9,25},{17,1},{25,9},{2,18},{10... | collective-permute-start | bytes 786440 | tf_op jit(solution)/shard_map/ppermute | solution.py:393
  9.0 0.0 copy-done.3
  9.1 13.0 %all_to_all.10.ref_ref = f32[8,2,2048]{2,1,0:T(2,128)S(1)} all-to-all(f32[8,2,2048]{2,1,0:T(2,128)S(1)} %broadcast_in_dim.2), channel_id=1, replica_groups=mesh['chan'=4,'tm'=8] {'tm'}, dimensions={0} | all-to-all | bytes 262144 | tf_op jit(solution)/shard_map/all_to_all | solution.py:404
  22.1 0.7 %shifted_reference.1.refs_3_ = bf16[2,2,128,2176]{3,2,1,0:T(8,128)(2,1)S(1)} custom-call(f32[8,2,2048]{2,1,0:T(2,128)S(1)} %all_to_all.10.ref_ref), custom_call_target="tpu_custom_call" | custom-call | flops 8912896 | bytes 2228224 | tf_op jit(solution)/shard_map/shifted_reference/pallas_call | solution.py:133
  22.7 0.0 collective-permute-done.1
  22.8 2.2 %lag_products.1 = f32[8,10,8,128]{3,2,1,0:T(8,128)} custom-call(f32[32,2048]{1,0:T(8,128)S(1)} %get-tuple-element.10.refs_0_, f32[32,2048]{1,0:T(8,128)S(1)} %get-tuple-element.11.refs_1_, f32[32,2048]{1,0:T(8,128)S(1)} %bitcast.5, bf16[2,2,128,2176]{3,2,1,0:T(8,128)(2,1)S(1)} %shifted_reference.1.refs_3_), custom_call_target="tpu_custom_call" | custom-call | flops 402653184 | bytes 2555904 | tf_op jit(solution)/shard_map/lag_products/pallas_call | solution.py:202
  24.9 3.4 %all-to-all-start.1 = ((f32[8,10,8,128]{3,2,1,0:T(8,128)}), f32[8,10,8,128]{3,2,1,0:T(8,128)S(1)}, u32[]{:S(2)}, u32[]{:S(2)}) async-start(f32[8,10,8,128]{3,2,1,0:T(8,128)} %lag_products.1), calls=%async_computation.1 | async-start | bytes 655360 | tf_op jit(solution)/shard_map/all_to_all | solution.py:419
  28.4 0.0 copy-start.1
  28.4 31.3 %reference_products.1.own_ref = f32[2048,128]{1,0:T(8,128)S(1)} custom-call(f32[8,2,2048]{2,1,0:T(2,128)S(1)} %all_to_all.10.ref_ref), custom_call_target="tpu_custom_call" | custom-call | flops 3221225472 | bytes 1048576 | tf_op jit(solution)/shard_map/reference_products/pallas_call | solution.py:317
  59.7 0.0 all-to-all-done.1.got_ref
  59.7 0.0 copy-done.1
  59.7 3.3 %range_doppler.1 = f32[16,2,32,256]{3,2,1,0:T(8,128)} custom-call(f32[8,10,8,128]{3,2,1,0:T(8,128)S(1)} %all-to-all-done.1.got_ref, f32[2048,128]{1,0:T(8,128)S(1)} %reference_products.1.own_ref, f32[128,512]{1,0:T(8,128)S(1)} %copy-done.1), custom_call_target="tpu_custom_call" | custom-call | flops 201326592 | bytes 1048576 | tf_op jit(solution)/shard_map/range_doppler/pallas_call | solution.py:379
  (1 shorter events, 0.0 us)
Async XLA Ops:
  0.0 1.2 %copy-start = (f32[2,64,2048]{2,1,0:T(8,128)S(1)}, f32[2,64,2048]{2,1,0:T(8,128)}, u32[]{:S(2)}) copy-start(f32[2,64,2048]{2,1,0:T(8,128)} %param.5) | copy-start | bytes 3145732
  1.2 0.8 %copy-start.2 = (f32[2,64,64]{2,1,0:T(8,128)S(1)}, f32[2,64,64]{2,1,0:T(8,128)}, u32[]{:S(2)}) copy-start(f32[2,64,64]{2,1,0:T(8,128)} %w_ref.1) | copy-start | bytes 98308
  2.1 7.0 %copy-start.3 = (f32[2,2048]{1,0:T(2,128)S(1)}, f32[2,2048]{1,0:T(2,128)}, u32[]{:S(2)}) copy-start(f32[2,2048]{1,0:T(2,128)} %param.4) | copy-start | bytes 49156
  4.0 2.1 %collective-permute-start = (f32[64,2048]{1,0:T(8,128)S(1)}, f32[64,2048]{1,0:T(8,128)S(1)}, u32[]{:S(2)}, u32[]{:S(2)}) collective-permute-start(f32[64,2048]{1,0:T(8,128)S(1)} %get-tuple-element.8), channel_id=1, source_target_pairs={{0,8},{8,0},{16,24},{24,16},{1,9},{9,1},{17,25},{25,17},{2,10},{10... | collective-permute-start | bytes 1572872 | tf_op jit(solution)/shard_map/ppermute | solution.py:393
  6.1 16.6 %collective-permute-start.1 = (f32[1,32,2048]{2,1,0:T(8,128)S(1)}, f32[1,32,2048]{2,1,0:T(8,128)S(1)}, u32[]{:S(2)}, u32[]{:S(2)}) collective-permute-start(f32[1,32,2048]{2,1,0:T(8,128)S(1)} %get-tuple-element.9), channel_id=1, source_target_pairs={{0,16},{8,24},{16,0},{24,8},{1,17},{9,25},{17,1},{25,9},{2,18},{10... | collective-permute-start | bytes 786440 | tf_op jit(solution)/shard_map/ppermute | solution.py:393
  24.9 34.7 %all-to-all-start.1 = ((f32[8,10,8,128]{3,2,1,0:T(8,128)}), f32[8,10,8,128]{3,2,1,0:T(8,128)S(1)}, u32[]{:S(2)}, u32[]{:S(2)}) async-start(f32[8,10,8,128]{3,2,1,0:T(8,128)} %lag_products.1), calls=%async_computation.1 | async-start | bytes 655360 | tf_op jit(solution)/shard_map/all_to_all | solution.py:419
  28.4 31.3 %copy-start.1 = (f32[128,512]{1,0:T(8,128)S(1)}, f32[128,512]{1,0:T(8,128)}, u32[]{:S(2)}) copy-start(f32[128,512]{1,0:T(8,128)} %constant.2.clone.wave_ref) | copy-start | bytes 786436

commit v2 on v1

--- a/solution.py
+++ b/solution.py
@@ -112,13 +112,8 @@
     )(steering, survey)
 
 
-def table_kernel(ref_ref, out_ref):
-    me = lax.axis_index("tm")
-    length = ref_ref.shape[2]
-    before = jnp.maximum(me - 1, 0)
-    edge = ref_ref[before, :, length - 2 * LANES :]
-    edge = jnp.where(me > 0, edge, jnp.zeros_like(edge))
-    span = jnp.concatenate([edge, ref_ref[me]], 1)
+def table_kernel(edge_ref, ref_ref, out_ref):
+    span = jnp.concatenate([edge_ref[...], ref_ref[...]], 1)
     for c in range(2):
         tiled = jnp.broadcast_to(span[c : c + 1], (LANES, span.shape[1]))
         shifted = pltpu.roll(tiled, 0, 1, stride=1, stride_axis=0)[:, LANES:]
@@ -127,9 +122,8 @@
         out_ref[1, c] = low
 
 
-def table_call(ref_all):
-    length = ref_all.shape[2]
-    shape = (2, 2, LANES, LANES + length)
+def table_call(edge, ref):
+    shape = (2, 2, LANES, LANES + ref.shape[1])
     return pl.pallas_call(
         table_kernel,
         out_shape=jax.ShapeDtypeStruct(shape, jnp.bfloat16),
@@ -138,11 +132,15 @@
             flops=8 * math.prod(shape), bytes_accessed=2 * math.prod(shape), transcendentals=0
         ),
         name="shifted_reference",
-    )(ref_all)
+    )(edge, ref)
 
 
 def lag_kernel(groups, owners, *refs):
-    *y_refs, table_ref, out_ref = refs
+    y_refs = refs[: -(owners + 2)]
+    table_ref = refs[-(owners + 2)]
+    out_refs = refs[-(owners + 1) : -1]
+    held_ref = refs[-1]
+    me = lax.axis_index("tm")
     y = y_refs[0][...]
     for y_ref in y_refs[1:]:
         y = y + y_ref[...]
@@ -182,109 +180,137 @@
             lanes = slice(h * LANES, (h + 1) * LANES)
             tiles = [product[r : r + SUBLANES, lanes] for r in range(0, rows, SUBLANES)]
             for j, tile in enumerate(swap_groups(tiles, groups)):
-                out_ref[h * groups + j, q] = tile
+                held_ref[h * groups + j, q] = tile
     left = lax.broadcasted_iota(jnp.int32, (SUBLANES, LANES), 1) < TAPS
-    packed = []
     for i in range(groups // 2):
         a = taps_sum[i * SUBLANES : (i + 1) * SUBLANES]
         other = i + groups // 2
         b = taps_sum[other * SUBLANES : (other + 1) * SUBLANES]
-        packed.append(jnp.where(left, a, pltpu.roll(b, LANES - TAPS, 1)))
-    for owner in range(owners):
-        for i, tile in enumerate(packed):
-            out_ref[owner, blocks + i] = tile
+        tile = jnp.where(left, a, pltpu.roll(b, LANES - TAPS, 1))
+        for out_ref in out_refs:
+            out_ref[blocks + i] = tile
+    for e, out_ref in enumerate(out_refs):
+        out_ref[:blocks] = held_ref[me ^ e]
 
 
 def lag_call(ys, table, groups, owners):
     rows, length = ys[0].shape
     blocks = length // BLOCK_LEN
-    shape = (owners, blocks + groups // 2, SUBLANES, LANES)
+    shape = (blocks + groups // 2, SUBLANES, LANES)
     return pl.pallas_call(
         functools.partial(lag_kernel, groups, owners),
-        out_shape=jax.ShapeDtypeStruct(shape, jnp.float32),
+        out_shape=[jax.ShapeDtypeStruct(shape, jnp.float32)] * owners,
+        scratch_shapes=[pltpu.VMEM((owners, blocks, SUBLANES, LANES), jnp.float32)],
         compiler_params=params(),
         cost_estimate=pl.CostEstimate(
             flops=12 * rows * LAGS * 2 * length,
-            bytes_accessed=4 * math.prod(shape) + 2 * math.prod(table.shape),
+            bytes_accessed=4 * owners * math.prod(shape) + 2 * math.prod(table.shape),
             transcendentals=0,
         ),
         name="lag_products",
     )(*ys, table)
 
 
-def complex_inverse(a):
-    size = a.shape[0]
-    lanes = lax.broadcasted_iota(jnp.int32, (1, 2 * size), 1)
-    rows = lax.broadcasted_iota(jnp.int32, (size, 1), 0)
-    all_lanes = lax.broadcasted_iota(jnp.int32, a.shape, 1)
-    all_rows = lax.broadcasted_iota(jnp.int32, a.shape, 0)
-    sign = -lane_sign((1, 2 * size))
-    for j in range(size):
-        col_r = a[:, j : j + 1]
-        col_i = a[:, size + j : size + j + 1]
-        row = a[j : j + 1]
-        pivot = 1.0 / a[j : j + 1, j : j + 1]
-        row = jnp.where(lanes == j, 1.0, jnp.where(lanes == size + j, 0.0, row))
-        turned = pltpu.roll(row, size, 1) * sign
-        row = row * pivot
-        turned = turned * pivot
-        col_r = jnp.where(rows == j, 0.0, col_r)
-        col_i = jnp.where(rows == j, 0.0, col_i)
-        kept = jnp.where((all_lanes == j) | (all_lanes == size + j), 0.0, a)
-        kept = jnp.where(all_rows == j, row, kept)
-        a = kept - (col_r * row + col_i * turned)
-    return a
-
-
-def own_kernel(lags_local, ref_ref, out_ref, span_ref, late_ref):
-    owners, _, length = ref_ref.shape
+SHARES = 2
+BATCH = 4
+
+
+def own_kernel(lags_local, *refs):
+    *part_refs, out_ref, tail_ref, span_ref, late_ref = refs
+    me = lax.axis_index("tm")
+    length = part_refs[0].shape[2]
+    owners = sum(part_ref.shape[0] for part_ref in part_refs)
     samples = owners * length
-    blocks = samples // BLOCK_LEN
-    first_lag = lax.axis_index("tm") * lags_local
+    blocks = samples // BLOCK_LEN // SHARES
+    first_block = lax.rem(lax.axis_index("chan"), SHARES) * blocks
     span_ref[:, :BLOCK_LEN] = jnp.zeros((2, BLOCK_LEN), jnp.float32)
     span_ref[:, BLOCK_LEN + samples :] = jnp.zeros((2, BLOCK_LEN), jnp.float32)
-    for t in range(owners):
-        span_ref[:, BLOCK_LEN + t * length : BLOCK_LEN + (t + 1) * length] = ref_ref[t]
-    late_ref[...] = pltpu.roll(span_ref[...], first_lag, 1)
+    e = 0
+    for part_ref in part_refs:
+        for i in range(part_ref.shape[0]):
+            start = pl.multiple_of((me ^ e) * length + BLOCK_LEN, BLOCK_LEN)
+            span_ref[:, pl.ds(start, length)] = part_ref[i]
+            e += 1
+    late_ref[...] = pltpu.roll(span_ref[...], me * lags_local, 1)
 
     def shifted(window, count):
         tiled = jnp.broadcast_to(window, (count, window.shape[1]))
-        return pltpu.roll(tiled, 0, 1, stride=1, stride_axis=0)[:, LANES : LANES + BLOCK_LEN]
-
-    def taps_of(window):
-        return jnp.concatenate(
-            [shifted(window[c : c + 1, BLOCK_LEN - LANES :], TAPS) for c in range(2)], 0
-        )
+        return pltpu.roll(tiled, 0, 1, stride=1, stride_axis=0)[:, LANES:]
+
+    def pair_of(window, count):
+        return jnp.concatenate([shifted(window[c : c + 1], count) for c in range(2)], 0)
 
     turn = lane_sign((lags_local, LANES))
 
-    def step(q, total):
-        lanes = pl.ds(pl.multiple_of(q * BLOCK_LEN, BLOCK_LEN), 2 * BLOCK_LEN)
+    def step(n, total):
+        start = pl.multiple_of((first_block + n * BATCH) * BLOCK_LEN, BLOCK_LEN) + BLOCK_LEN - LANES
+        lanes = pl.ds(pl.multiple_of(start, LANES), BATCH * BLOCK_LEN + LANES)
         window, late = span_ref[:, lanes], late_ref[:, lanes]
-        taps_high, taps_low = halves(taps_of(window))
-        lag_rows = [shifted(late[c : c + 1, BLOCK_LEN - LANES :], lags_local) for c in range(2)]
-        pad = jnp.zeros((2 * SUBLANES - 2, BLOCK_LEN), jnp.float32)
-        lag_rows = jnp.concatenate(lag_rows + [window[:, BLOCK_LEN:], pad], 0)
+        taps_high, taps_low = halves(pair_of(window, TAPS))
+        pad = jnp.zeros((2 * SUBLANES - 2, BATCH * BLOCK_LEN), jnp.float32)
+        lag_rows = jnp.concatenate([pair_of(late, lags_local), window[:, LANES:], pad], 0)
         lags_high, lags_low = halves(lag_rows)
-        product = dot_nt(
-            jnp.concatenate([lags_high, lags_low], 0), jnp.concatenate([taps_high, taps_low], 0)
-        )
+        taps = jnp.concatenate([taps_high, taps_low], 0)
+        lags = jnp.concatenate([lags_high, lags_low], 0)
         count = lag_rows.shape[0]
-        product = product[:count, :LANES] + (product[:count, LANES:] + product[count:, :LANES])
-        by_real = product[:lags_local]
-        by_imag = product[lags_local : 2 * lags_local]
-        rows = pl.ds(pl.multiple_of(q * lags_local, lags_local), lags_local)
-        out_ref[rows, :] = by_real + turn * pltpu.roll(by_imag, TAPS, 1)
-        return total + product[2 * lags_local : 2 * lags_local + SUBLANES]
-
-    total = lax.fori_loop(0, blocks, step, jnp.zeros((SUBLANES, LANES), jnp.float32))
-
+        for b in range(BATCH):
+            cols = slice(b * BLOCK_LEN, (b + 1) * BLOCK_LEN)
+            product = dot_nt(lags[:, cols], taps[:, cols])
+            product = product[:count, :LANES] + (product[:count, LANES:] + product[count:, :LANES])
+            by_real = product[:lags_local]
+            by_imag = product[lags_local : 2 * lags_local]
+            rows = pl.ds(pl.multiple_of((n * BATCH + b) * lags_local, lags_local), lags_local)
+            out_ref[rows, :] = by_real + turn * pltpu.roll(by_imag, TAPS, 1)
+            total = total + product[2 * lags_local : 2 * lags_local + SUBLANES]
+        return total
+
+    total = lax.fori_loop(0, blocks // BATCH, step, jnp.zeros((SUBLANES, LANES), jnp.float32))
+    out_ref[blocks * lags_local :, :] = total
+    tail = pair_of(span_ref[:, samples + BLOCK_LEN - LANES :], TAPS)
+    tail_ref[...] = dot_nt(tail, tail, HIGHEST)
+
+
+def own_call(parts, lags_local):
+    length = parts[0].shape[2]
+    samples = length * sum(part.shape[0] for part in parts)
+    rows = samples // BLOCK_LEN // SHARES * lags_local
+    return pl.pallas_call(
+        functools.partial(own_kernel, lags_local),
+        out_shape=[
+            jax.ShapeDtypeStruct((rows + SUBLANES, 2 * TAPS), jnp.float32),
+            jax.ShapeDtypeStruct((2 * TAPS, 2 * TAPS), jnp.float32),
+        ],
+        scratch_shapes=[pltpu.VMEM((2, samples + 2 * BLOCK_LEN), jnp.float32)] * 2,
+        compiler_params=params(),
+        cost_estimate=pl.CostEstimate(
+            flops=24 * rows * BLOCK_LEN * 2 * TAPS, bytes_accessed=4 * rows * 2 * TAPS, transcendentals=0
+        ),
+        name="reference_products",
+    )(*parts)
+
+
+def as_factor(a):
+    return jnp.concatenate([a, -lane_sign(a.shape) * pltpu.roll(a, a.shape[0], 1)], 0)
+
+
+def dot_split(a, b):
+    (a_high, a_low), (b_high, b_low) = a, b
+    left = jnp.concatenate([a_high, a_low], 1)
+    right = jnp.concatenate([b_high, b_high], 0)
+    return jnp.dot(left, right, preferred_element_type=jnp.float32) + jnp.dot(
+        a_high, b_low, preferred_element_type=jnp.float32
+    )
+
+
+def solver_kernel(mine_ref, other_ref, tail_ref, gram_ref, solver_ref):
+    total = mine_ref[...] + other_ref[...]
     line = total[0:1] + lane_sign((1, LANES)) * pltpu.roll(total[1:2], TAPS, 1)
     low = lax.broadcasted_iota(jnp.int32, (1, LANES), 1) < TAPS
     line_r = jnp.where(low, line, 0.0)
     line_i = jnp.where(low, pltpu.roll(line, TAPS, 1), 0.0)
-    above = lax.broadcasted_iota(jnp.int32, (TAPS, TAPS), 1) > lax.broadcasted_iota(jnp.int32, (TAPS, TAPS), 0)
-    equal = lax.broadcasted_iota(jnp.int32, (TAPS, TAPS), 1) == lax.broadcasted_iota(jnp.int32, (TAPS, TAPS), 0)
+    cols = lax.broadcasted_iota(jnp.int32, (TAPS, TAPS), 1)
+    rows = lax.broadcasted_iota(jnp.int32, (TAPS, TAPS), 0)
+    above = cols > rows
 
     def upper(x):
         spread = pltpu.roll(jnp.broadcast_to(x, (TAPS, LANES)), 0, 1, stride=1, stride_axis=0)
@@ -293,37 +319,50 @@
     up_r = upper(line_r)
     up_i = jnp.where(above, upper(line_i), 0.0)
     strict_r = jnp.where(above, up_r, 0.0)
-    diag_r = jnp.where(equal, up_r, 0.0)
-    gram_r = strict_r + strict_r.T + diag_r
-    gram_i = up_i - up_i.T
-    tail = taps_of(span_ref[:, samples:])
-    tails = dot_nt(tail, tail, HIGHEST)
-    gram_r = gram_r - (tails[:TAPS, :TAPS] + tails[TAPS:, TAPS:])
-    gram_i = gram_i - (tails[:TAPS, TAPS:] - tails[TAPS:, :TAPS])
-
-    inverse = complex_inverse(jnp.concatenate([gram_r, gram_i], 1))
-    lower = -lane_sign(inverse.shape) * pltpu.roll(inverse, TAPS, 1)
-    solver = jnp.concatenate([inverse, lower], 0)
-    out_ref[...] = jnp.dot(
-        out_ref[...], solver, precision=HIGHEST, preferred_element_type=jnp.float32
-    )
-
-
-def own_call(ref_all, lags_local):
-    owners, _, length = ref_all.shape
-    samples = owners * length
-    blocks = samples // BLOCK_LEN
-    shape = (blocks * lags_local, 2 * TAPS)
+    diag_r = jnp.where(cols == rows, up_r, 0.0)
+    tails = tail_ref[...]
+    gram_r = strict_r + strict_r.T + diag_r - (tails[:TAPS, :TAPS] + tails[TAPS:, TAPS:])
+    gram_i = up_i - up_i.T - (tails[:TAPS, TAPS:] - tails[TAPS:, :TAPS])
+    gram = jnp.concatenate([gram_r, gram_i], 1)
+    gram_factor = as_factor(gram)
+    gram_ref[...] = gram_factor
+    gram_halves = halves(gram_factor)
+    one = (
+        lax.broadcasted_iota(jnp.int32, gram.shape, 0) == lax.broadcasted_iota(jnp.int32, gram.shape, 1)
+    ).astype(jnp.float32)
+    bound = jnp.max(jnp.sum(jnp.abs(gram), axis=1, keepdims=True), axis=0, keepdims=True)
+
+    def again(state):
+        count, left, _ = state
+        return (count < 60) & (left > 1e-3)
+
+    def newton(state):
+        count, _, x = state
+        x_halves = halves(x)
+        seen = dot_split(x_halves, gram_halves)
+        left = jnp.max(jnp.abs(seen - one))
+        x = 2.0 * x - dot_split(halves(seen), halves(as_factor(x)))
+        return count + 1, left, x
+
+    start = (jnp.int32(0), jnp.float32(1.0), one * (1.0 / bound))
+    _, _, inverse = lax.while_loop(again, newton, start)
+    solver_ref[...] = as_factor(inverse)
+
+
+def solver_call(mine, other, tail):
+    last = mine.shape[0] // SUBLANES - 1
+    line = pl.BlockSpec((SUBLANES, LANES), lambda i: (last, 0))
+    whole = pl.BlockSpec(tail.shape, lambda i: (0, 0))
     return pl.pallas_call(
-        functools.partial(own_kernel, lags_local),
-        out_shape=jax.ShapeDtypeStruct(shape, jnp.float32),
-        scratch_shapes=[pltpu.VMEM((2, samples + 2 * BLOCK_LEN), jnp.float32)] * 2,
+        solver_kernel,
+        grid=(1,),
+        in_specs=[line, line, whole],
+        out_specs=[whole, whole],
+        out_shape=[jax.ShapeDtypeStruct(tail.shape, jnp.float32)] * 2,
         compiler_params=params(),
-        cost_estimate=pl.CostEstimate(
-            flops=12 * samples * 2 * TAPS * 4 * lags_local, bytes_accessed=4 * math.prod(shape), transcendentals=0
-        ),
-        name="reference_products",
-    )(ref_all)
+        cost_estimate=pl.CostEstimate(flops=500_000_000, bytes_accessed=200_000, transcendentals=0),
+        name="gram_inverse",
+    )(mine, other, tail)
 
 
 def doppler_table(block_count, scale):
@@ -334,36 +373,53 @@
     return (np.concatenate([upper, lower], 0) * scale).astype(np.float32)
 
 
-def map_kernel(groups, got_ref, own_ref, wave_ref, out_ref, held_ref):
-    owners, pieces = got_ref.shape[:2]
-    blocks = pieces - groups // 2
+def map_kernel(groups, owners, *refs):
+    got_refs = refs[:owners]
+    mine_ref, other_ref, gram_ref, solver_ref, wave_ref, out_ref, got_ref, held_ref = refs[owners:]
+    me = lax.axis_index("tm")
+    blocks = got_refs[0].shape[0] - groups // 2
     lags_local = LANES // groups
     total = owners * blocks
     left = lax.broadcasted_iota(jnp.int32, (SUBLANES, LANES), 1) < TAPS
     sign = row_sign((SUBLANES, LANES))
+    for e, ref in enumerate(got_refs):
+        start = pl.multiple_of((me ^ e) * blocks * SUBLANES, SUBLANES)
+        got_ref[pl.ds(start, blocks * SUBLANES), :] = ref[:blocks].reshape(blocks * SUBLANES, LANES)
     rows = [None] * groups
     for i in range(groups // 2):
-        tile = got_ref[0, blocks + i]
-        for owner in range(1, owners):
-            tile = tile + got_ref[owner, blocks + i]
+        tile = got_refs[0][blocks + i]
+        for ref in got_refs[1:]:
+            tile = tile + ref[blocks + i]
         swapped = pltpu.roll(tile, TAPS, 1)
         for part, here, there in ((i, tile, swapped), (i + groups // 2, swapped, tile)):
             other = -sign * pltpu.roll(there, SUBLANES // 2, 0)
             rows[part] = jnp.where(left, here, other)
     cross = jnp.concatenate(rows, 0)
-    clutter = dot_nt(cross, own_ref[...], HIGHEST)
-    for q in range(0, total, groups):
-        lanes = slice(q * lags_local, q * lags_local + LANES)
-        tiles = [clutter[r : r + SUBLANES, lanes] for r in range(0, groups * SUBLANES, SUBLANES)]
-        for j, tile in enumerate(swap_groups(tiles, groups)):
-            at = q + j
-            held_ref[at * SUBLANES : (at + 1) * SUBLANES, :] = got_ref[at // blocks, at % blocks] - tile
+    solver = solver_ref[...]
+    taps = jnp.dot(cross, solver, precision=HIGHEST, preferred_element_type=jnp.float32)
+    rest = cross - jnp.dot(taps, gram_ref[...], precision=HIGHEST, preferred_element_type=jnp.float32)
+    taps = taps + jnp.dot(rest, solver, precision=HIGHEST, preferred_element_type=jnp.float32)
+    taps_high, taps_low = halves(taps)
+    taps_both = jnp.concatenate([taps_high, taps_low], 1)
+    share = lax.rem(lax.axis_index("chan"), SHARES)
+    share_blocks = total // SHARES
+    for which, own_ref in enumerate((mine_ref, other_ref)):
+        first = (share ^ which) * share_blocks
+        for q in range(0, share_blocks, 2 * groups):
+            own_high, own_low = halves(own_ref[q * lags_local : (q + 2 * groups) * lags_local, :])
+            clutter = dot_nt(taps_both, jnp.concatenate([own_high, own_high], 1)) + dot_nt(taps_high, own_low)
+            for h in range(2):
+                lanes = slice(h * LANES, (h + 1) * LANES)
+                tiles = [clutter[r : r + SUBLANES, lanes] for r in range(0, groups * SUBLANES, SUBLANES)]
+                tiles = jnp.concatenate(swap_groups(tiles, groups), 0)
+                at = pl.multiple_of((first + q + h * groups) * SUBLANES, groups * SUBLANES)
+                at = pl.ds(at, groups * SUBLANES)
+                held_ref[at, :] = got_ref[at, :] - tiles
     half = SUBLANES // 2
-    wave = wave_ref[...]
+    wave = (wave_ref[0], wave_ref[1])
     for g in range(half):
         parts = [held_ref[pl.ds(c * half + g, total, stride=SUBLANES), :] for c in range(2)]
-        lagged = jnp.concatenate(parts, 0).T
-        spectrum = jnp.dot(lagged, wave, precision=HIGHEST, preferred_element_type=jnp.float32)
+        spectrum = dot_split(halves(jnp.concatenate(parts, 0).T), wave)
         for i in range(groups):
             for c in range(2):
                 out_ref[half * i + g, c] = spectrum[
@@ -371,21 +427,21 @@
                 ]
 
 
-def map_call(got, own, wave, groups, beams_local):
-    owners, pieces = got.shape[:2]
-    total = owners * (pieces - groups // 2)
+def map_call(got, mine, other, gram, solver, wave, groups, beams_local):
+    owners = len(got)
+    total = owners * (got[0].shape[0] - groups // 2)
     lags_local = LANES // groups
     shape = (beams_local, 2, lags_local, DOPPLER)
     return pl.pallas_call(
-        functools.partial(map_kernel, groups),
+        functools.partial(map_kernel, groups, owners),
         out_shape=jax.ShapeDtypeStruct(shape, jnp.float32),
-        scratch_shapes=[pltpu.VMEM((total * SUBLANES, LANES), jnp.float32)],
+        scratch_shapes=[pltpu.VMEM((total * SUBLANES, LANES), jnp.float32)] * 2,
         compiler_params=params(),
         cost_estimate=pl.CostEstimate(
             flops=12 * math.prod(shape) * total, bytes_accessed=4 * math.prod(shape), transcendentals=0
         ),
         name="range_doppler",
-    )(got, own, wave)
+    )(*got, mine, other, gram, solver, wave)
 
 
 def swap(x, axis, by):
@@ -401,9 +457,15 @@
     groups = LANES // lags_local
     samples = length * tm_count
 
-    ref_all = lax.all_to_all(
-        jnp.broadcast_to(ref_signal[None], (tm_count,) + ref_signal.shape), "tm", 0, 0, tiled=True
-    )
+    edge = lax.ppermute(
+        ref_signal[:, length - 2 * LANES :], "tm", [(i, i + 1) for i in range(tm_count - 1)]
+    )
+    ref_parts = [ref_signal[None]]
+    by = 1
+    while by < tm_count:
+        ref_parts.append(swap(jnp.concatenate(ref_parts, 0), "tm", by))
+        by *= 2
+
     even, odd = beam_call(steering, surveillance.reshape(2 * channels, length), chan_count, beams_local)
     rows = 2 * beams_local
     parts = [even.reshape(chan_count // 2, rows, length), swap(odd, "chan", 1).reshape(chan_count // 2, rows, length)]
@@ -414,12 +476,16 @@
             sent = sent + part[1::2]
         parts = [part[::2] for part in parts] + [swap(sent, "chan", by)]
         by *= 2
-    table = table_call(ref_all)
+    table = table_call(edge, ref_signal)
     pieces = lag_call([part[0] for part in parts], table, groups, tm_count)
-    got = lax.all_to_all(pieces, "tm", 0, 0, tiled=True)
-    own = own_call(ref_all, lags_local)
+    got = [pieces[0]] + [swap(piece, "tm", e) for e, piece in enumerate(pieces) if e]
+    mine, tail = own_call(ref_parts, lags_local)
+    other = swap(mine, "chan", 1)
+    gram, solver = solver_call(mine, other, tail)
     wave = doppler_table(samples // BLOCK_LEN, 0.125 / math.sqrt(samples))
-    return map_call(got, own, jnp.asarray(wave), groups, beams_local)
+    high = wave.astype(jnp.bfloat16)
+    wave = np.stack([high, (wave - high.astype(np.float32)).astype(jnp.bfloat16)])
+    return map_call(got, mine, other, gram, solver, jnp.asarray(wave), groups, beams_local)
 
 
 def lag_table(ref_ext, offset, lags):
@@ -497,6 +563,7 @@
         and beams_local * lags_local == LANES * SUBLANES // 2
         and chan_count > 1
         and chan_count & (chan_count - 1) == 0
+        and tm_count & (tm_count - 1) == 0
         and 2 * surveillance.shape[1] % LANES == 0
         and surveillance.shape[2] % (4 * BLOCK_LEN) == 0
     )

time: 63.4 us -> 54.4 us (0.86)
  Pallas kernels: 39.4 us -> 13.8 us
  starting transfers between devices: 6.88 us -> 22.9 us
  blocking collectives: 13 us -> 0 us
  waiting for transfers between devices: 1.54 us -> 12.7 us
  other arithmetic: 0.07 us -> 1.63 us
  local copies, waits for them, and re-layouts: 2.11 us -> 2.79 us
    pallas_call x3 -> x4, Pallas kernels: 36.8 us -> 11.2 us  [the longest x1 4.89 us: own_call(): pl.pallas_call(functools.partial(own_kernel, lags_local), out_shape=[jax....]
    ppermute x2 -> x13, starting transfers between devices: 3.44 us -> 20.5 us  [swap(): return lax.ppermute(x, axis, pairs)]
    all_to_all x1 -> x0, blocking collectives: 13 us -> none  [tiled_device(): lax.all_to_all(jnp.broadcast_to(ref_signal[None], (tm_count,) + ref_signa...]
    ppermute x2 -> x13, waiting for transfers between devices: 1.54 us -> 11.4 us  [swap(): return lax.ppermute(x, axis, pairs)]
    all_to_all x1 -> x0, starting transfers between devices: 3.43 us -> none  [tiled_device(): got = lax.all_to_all(pieces, 'tm', 0, 0, tiled=True)]
    ppermute x0 -> x1, starting transfers between devices: none -> 2.4 us  [tiled_device(): lax.ppermute(ref_signal[:, length - 2 * LANES:], 'tm', [(i, i + 1) for i...]
    concatenate x0 -> x2, other arithmetic: none -> 1.56 us  [tiled_device(): ref_parts.append(swap(jnp.concatenate(ref_parts, 0), 'tm', by))]
    ppermute x0 -> x1, waiting for transfers between devices: none -> 1.29 us  [tiled_device(): lax.ppermute(ref_signal[:, length - 2 * LANES:], 'tm', [(i, i + 1) for i...]
  transfers between devices with their start and end apart: 3 -> 14, of which waited for: 1 -> 5; matrix products, arithmetic and copies ran while one was open for 0% -> 3% of each run, Pallas kernels for 51% -> 20%
where the time goes in v2:
time: 54.4 us; the launch traced here: 54 us
  starting transfers between devices  22.9 us (42%)
  Pallas kernels  13.8 us (25%)
  waiting for transfers between devices  12.7 us (23%)
  local copies, waits for them, and re-layouts  2.79 us (5%)
  other arithmetic  1.63 us (3%)
    ppermute x13, starting transfers between devices, swap(): return lax.ppermute(x, axis, pairs)  20.5 us
    ppermute x13, waiting for transfers between devices, swap(): return lax.ppermute(x, axis, pairs)  11.4 us
    pallas_call x1, Pallas kernels, own_call(): pl.pallas_call(functools.partial(own_kernel, lags_local), out_shape=[jax....  4.89 us
    pallas_call x1, Pallas kernels, map_call(): pl.pallas_call(functools.partial(map_kernel, groups, owners), out_shape=j...  2.79 us
    unnamed x10, local copies, waits for them, and re-layouts  2.79 us
    ppermute x1, starting transfers between devices, tiled_device(): lax.ppermute(ref_signal[:, length - 2 * LANES:], 'tm', [(i, i + 1) for i...  2.4 us
    pallas_call x1, Pallas kernels, solver_call(): pl.pallas_call(solver_kernel, grid=(1,), in_specs=[line, line, whole], ou...  2.04 us
    pallas_call x1, Pallas kernels, beam_call(): pl.pallas_call(functools.partial(beam_kernel, chan_count, beams_local), g...  1.91 us
  transfers between devices with their start and end apart: 14, of which 5 were waited for; matrix products, arithmetic and copies ran while one was open for 3% of the time, Pallas kernels for 20%

profile of v2, /device:TPU:0, one launch (start us, length us, event | category | flops | bytes accessed | tf_op | source)
XLA Modules:
  0.0 54.0 jit_solution(18420331526169129406)
XLA Ops:
  0.0 3.0 %collective-permute-start.10 = (f32[1,2,2048]{2,1,0:T(2,128)}, f32[1,2,2048]{2,1,0:T(2,128)S(1)}, u32[]{:S(2)}, u32[]{:S(2)}) collective-permute-start(f32[1,2,2048]{2,1,0:T(2,128)} %bitcast.7), channel_id=1, source_target_pairs={{0,1},{1,0},{2,3},{3,2},{4,5},{5,4},{6,7},{7,6},{8,9},{9,8},{10,11... | collective-permute-start | bytes 49160 | tf_op jit(solution)/shard_map/ppermute | solution.py:449
  3.0 1.2 %copy-done = f32[2,64,2048]{2,1,0:T(8,128)S(1)} copy-done((f32[2,64,2048]{2,1,0:T(8,128)S(1)}, f32[2,64,2048]{2,1,0:T(8,128)}, u32[]{:S(2)}) %copy-start) | copy-done | bytes 1048600
  4.2 0.8 %copy-done.4 = f32[2,64,64]{2,1,0:T(8,128)S(1)} copy-done((f32[2,64,64]{2,1,0:T(8,128)S(1)}, f32[2,64,64]{2,1,0:T(8,128)}, u32[]{:S(2)}) %copy-start.4) | copy-done | bytes 32792
  5.0 1.9 %beams.1 = (f32[64,2048]{1,0:T(8,128)S(1)}, f32[64,2048]{1,0:T(8,128)S(1)}) custom-call(f32[2,64,64]{2,1,0:T(8,128)S(1)} %copy-done.4, f32[128,2048]{1,0:T(8,128)S(1)} %bitcast.5), custom_call_target="tpu_custom_call" | custom-call | flops 67108864 | bytes 2097152 | tf_op jit(solution)/shard_map/beams/pallas_call | solution.py:98
  7.0 0.7 %pad_maximum_fusion.1 = f32[2,2,2048]{2,1,0:T(2,128)S(1)} fusion(f32[1,2,2048]{2,1,0:T(2,128)S(1)} %collective-permute-done.10.refs_1_, f32[1,2,2048]{2,1,0:T(2,128)} %bitcast.8), kind=kLoop, calls=%fused_computation.3 | loop fusion | flops 8192 | bytes 65536 | tf_op jit(solution)/shard_map/concatenate | solution.py:466
  7.8 1.6 %collective-permute-start.11 = (f32[2,2,2048]{2,1,0:T(2,128)S(1)}, f32[2,2,2048]{2,1,0:T(2,128)S(1)}, u32[]{:S(2)}, u32[]{:S(2)}) collective-permute-start(f32[2,2,2048]{2,1,0:T(2,128)S(1)} %pad_maximum_fusion.1), channel_id=1, source_target_pairs={{0,2},{1,3},{2,0},{3,1},{4,6},{5,7},{6,4},{7,5},{8,10},{9,11},{10,... | collective-permute-start | bytes 98312 | tf_op jit(solution)/shard_map/ppermute | solution.py:449
  9.4 2.3 %collective-permute-done.11.refs_2_ = f32[2,2,2048]{2,1,0:T(2,128)S(1)} collective-permute-done((f32[2,2,2048]{2,1,0:T(2,128)S(1)}, f32[2,2,2048]{2,1,0:T(2,128)S(1)}, u32[]{:S(2)}, u32[]{:S(2)}) %collective-permute-start.11) | collective-permute-done | bytes 32800 | tf_op jit(solution)/shard_map/ppermute | solution.py:449
  11.8 0.8 %pad_maximum_fusion = f32[4,2,2048]{2,1,0:T(2,128)S(1)} fusion(f32[2,2,2048]{2,1,0:T(2,128)S(1)} %collective-permute-done.11.refs_2_, f32[1,2,2048]{2,1,0:T(2,128)S(1)} %collective-permute-done.10.refs_1_, f32[1,2,2048]{2,1,0:T(2,128)} %bitcast.9), kind=kLoop, calls=%fused_computation.2 | loop fusion | flops 32768 | bytes 131072 | tf_op jit(solution)/shard_map/concatenate | solution.py:466
  12.6 2.6 %collective-permute-start.12 = (f32[4,2,2048]{2,1,0:T(2,128)S(1)}, f32[4,2,2048]{2,1,0:T(2,128)S(1)}, u32[]{:S(2)}, u32[]{:S(2)}) collective-permute-start(f32[4,2,2048]{2,1,0:T(2,128)S(1)} %pad_maximum_fusion), channel_id=1, source_target_pairs={{0,4},{1,5},{2,6},{3,7},{4,0},{5,1},{6,2},{7,3},{8,12},{9,13},{10,... | collective-permute-start | bytes 196616 | tf_op jit(solution)/shard_map/ppermute | solution.py:449
  15.2 2.7 %collective-permute-done.12.refs_3_ = f32[4,2,2048]{2,1,0:T(2,128)S(1)} collective-permute-done((f32[4,2,2048]{2,1,0:T(2,128)S(1)}, f32[4,2,2048]{2,1,0:T(2,128)S(1)}, u32[]{:S(2)}, u32[]{:S(2)}) %collective-permute-start.12) | collective-permute-done | bytes 65568 | tf_op jit(solution)/shard_map/ppermute | solution.py:449
  18.6 4.9 %reference_products.1 = (f32[1032,128]{1,0:T(8,128)S(1)}, f32[128,128]{1,0:T(8,128)S(1)}) custom-call(f32[1,2,2048]{2,1,0:T(2,128)S(1)} %bitcast.10, f32[1,2,2048]{2,1,0:T(2,128)S(1)} %collective-permute-done.10.refs_1_, f32[2,2,2048]{2,1,0:T(2,128)S(1)} %collective-permute-done.11.refs_2_, f32[4,2,2048]{2,1,0:T(2,128)S(1)} %collective-permute-done.12.refs_3_), custom_call_target="tpu_custom_call" | custom-call | flops 805306368 | bytes 524288 | tf_op jit(solution)/shard_map/reference_products/pallas_call | solution.py:277
  23.7 1.6 %collective-permute-start.1 = (f32[1,32,2048]{2,1,0:T(8,128)S(1)}, f32[1,32,2048]{2,1,0:T(8,128)S(1)}, u32[]{:S(2)}, u32[]{:S(2)}) collective-permute-start(f32[1,32,2048]{2,1,0:T(8,128)S(1)} %get-tuple-element.33), channel_id=1, source_target_pairs={{0,16},{8,24},{16,0},{24,8},{1,17},{9,25},{17,1},{25,9},{2,18},{10... | collective-permute-start | bytes 786440 | tf_op jit(solution)/shard_map/ppermute | solution.py:449
  25.2 2.4 %collective-permute-start.2 = (f32[2,256]{1,0:T(2,128)S(1)}, f32[2,256]{1,0:T(2,128)S(1)}, u32[]{:S(2)}, u32[]{:S(2)}) collective-permute-start(f32[2,256]{1,0:T(2,128)S(1)} %slice.27), channel_id=1, source_target_pairs={{0,1},{1,2},{2,3},{3,4},{4,5},{5,6},{6,7},{8,9},{9,10},{10,11},{11... | collective-permute-start | bytes 6152 | tf_op jit(solution)/shard_map/ppermute | solution.py:460
  27.6 1.3 %collective-permute-done.2.edge_ref = f32[2,256]{1,0:T(2,128)S(1)} collective-permute-done((f32[2,256]{1,0:T(2,128)S(1)}, f32[2,256]{1,0:T(2,128)S(1)}, u32[]{:S(2)}, u32[]{:S(2)}) %collective-permute-start.2) | collective-permute-done | bytes 2080 | tf_op jit(solution)/shard_map/ppermute | solution.py:460
  29.6 2.8 %collective-permute-done.1 = f32[1,32,2048]{2,1,0:T(8,128)S(1)} collective-permute-done((f32[1,32,2048]{2,1,0:T(8,128)S(1)}, f32[1,32,2048]{2,1,0:T(8,128)S(1)}, u32[]{:S(2)}, u32[]{:S(2)}) %collective-permute-start.1) | collective-permute-done | bytes 262176 | tf_op jit(solution)/shard_map/ppermute | solution.py:449
  32.4 1.5 %lag_products.1 = (f32[10,8,128]{2,1,0:T(8,128)S(1)}, f32[10,8,128]{2,1,0:T(8,128)S(1)}, f32[10,8,128]{2,1,0:T(8,128)S(1)}, f32[10,8,128]{2,1,0:T(8,128)S(1)}, f...) custom-call(f32[32,2048]{1,0:T(8,128)S(1)} %get-tuple-element.34.ref, ...), custom_call_target="tpu_custom_call" | custom-call | flops 402653184 | bytes 2555904 | tf_op jit(solution)/shard_map/lag_products/pallas_call | solution.py:200
  34.5 1.5 %collective-permute-start.4 = (f32[10,8,128]{2,1,0:T(8,128)S(1)}, f32[10,8,128]{2,1,0:T(8,128)S(1)}, u32[]{:S(2)}, u32[]{:S(2)}) collective-permute-start(f32[10,8,128]{2,1,0:T(8,128)S(1)} %get-tuple-element.23), channel_id=1, source_target_pairs={{0,2},{1,3},{2,0},{3,1},{4,6},{5,7},{6,4},{7,5},{8,10},{9,11},{10,... | collective-permute-start | bytes 122888 | tf_op jit(solution)/shard_map/ppermute | solution.py:449
  36.0 1.5 %collective-permute-start.5 = (f32[10,8,128]{2,1,0:T(8,128)S(1)}, f32[10,8,128]{2,1,0:T(8,128)S(1)}, u32[]{:S(2)}, u32[]{:S(2)}) collective-permute-start(f32[10,8,128]{2,1,0:T(8,128)S(1)} %get-tuple-element.24), channel_id=1, source_target_pairs={{0,3},{1,2},{2,1},{3,0},{4,7},{5,6},{6,5},{7,4},{8,11},{9,10},{10,... | collective-permute-start | bytes 122888 | tf_op jit(solution)/shard_map/ppermute | solution.py:449
  37.5 2.6 %collective-permute-start.6 = (f32[10,8,128]{2,1,0:T(8,128)S(1)}, f32[10,8,128]{2,1,0:T(8,128)S(1)}, u32[]{:S(2)}, u32[]{:S(2)}) collective-permute-start(f32[10,8,128]{2,1,0:T(8,128)S(1)} %get-tuple-element.25), channel_id=1, source_target_pairs={{0,4},{1,5},{2,6},{3,7},{4,0},{5,1},{6,2},{7,3},{8,12},{9,13},{10,... | collective-permute-start | bytes 122888 | tf_op jit(solution)/shard_map/ppermute | solution.py:449
  40.4 4.1 %collective-permute-start.8 = (f32[10,8,128]{2,1,0:T(8,128)S(1)}, f32[10,8,128]{2,1,0:T(8,128)S(1)}, u32[]{:S(2)}, u32[]{:S(2)}) collective-permute-start(f32[10,8,128]{2,1,0:T(8,128)S(1)} %get-tuple-element.27), channel_id=1, source_target_pairs={{0,6},{1,7},{2,4},{3,5},{4,2},{5,3},{6,0},{7,1},{8,14},{9,15},{10,... | collective-permute-start | bytes 122888 | tf_op jit(solution)/shard_map/ppermute | solution.py:449
  44.5 1.0 %collective-permute-start.9 = (f32[10,8,128]{2,1,0:T(8,128)S(1)}, f32[10,8,128]{2,1,0:T(8,128)S(1)}, u32[]{:S(2)}, u32[]{:S(2)}) collective-permute-start(f32[10,8,128]{2,1,0:T(8,128)S(1)} %get-tuple-element.28), channel_id=1, source_target_pairs={{0,7},{1,6},{2,5},{3,4},{4,3},{5,2},{6,1},{7,0},{8,15},{9,14},{10,... | collective-permute-start | bytes 122888 | tf_op jit(solution)/shard_map/ppermute | solution.py:449
  45.5 2.0 %gram_inverse.1 = (f32[128,128]{1,0:T(8,128)S(1)}, f32[128,128]{1,0:T(8,128)S(1)}) custom-call(f32[1032,128]{1,0:T(8,128)S(1)} %get-tuple-element.29.mine_ref.refs_8_, f32[1032,128]{1,0:T(8,128)S(1)} %collective-permute-done.13.other_ref.refs_9_, f32[128,128]{1,0:T(8,128)S(1)} %get-tuple-element.30.tail_ref), custom_call_target="tpu_custom_call" | custom-call | flops 500000000 | bytes 200000 | tf_op jit(solution)/shard_map/gram_inverse/pallas_call | solution.py:356
  47.6 3.6 %collective-permute-done.9.refs_7_ = f32[10,8,128]{2,1,0:T(8,128)S(1)} collective-permute-done((f32[10,8,128]{2,1,0:T(8,128)S(1)}, f32[10,8,128]{2,1,0:T(8,128)S(1)}, u32[]{:S(2)}, u32[]{:S(2)}) %collective-permute-start.9) | collective-permute-done | bytes 40992 | tf_op jit(solution)/shard_map/ppermute | solution.py:449
  51.2 2.8 %range_doppler.1 = f32[16,2,32,256]{3,2,1,0:T(8,128)} custom-call(f32[10,8,128]{2,1,0:T(8,128)S(1)} %get-tuple-element.21.refs_0_, f32[10,8,128]{2,1,0:T(8,128)S(1)} %collective-permute-done.3.refs_1_, f32[10,8,128]{2,1,0:T(8,128)S(1)} %collective-permute-done.4.refs_2_, f32[10,8,128]{2,1,0:T(8,128)S(1)} %collective-permute-done.5.refs_3_, ...), custom_call_target="tpu_custom_call" | custom-call | flops 201326592 | bytes 1048576 | tf_op jit(solution)/shard_map/range_doppler/pallas_call | solution.py:435
  (24 shorter events, 2.4 us)
Async XLA Ops:
  0.0 7.0 %collective-permute-start.10 = (f32[1,2,2048]{2,1,0:T(2,128)}, f32[1,2,2048]{2,1,0:T(2,128)S(1)}, u32[]{:S(2)}, u32[]{:S(2)}) collective-permute-start(f32[1,2,2048]{2,1,0:T(2,128)} %bitcast.7), channel_id=1, source_target_pairs={{0,1},{1,0},{2,3},{3,2},{4,5},{5,4},{6,7},{7,6},{8,9},{9,8},{10,11... | collective-permute-start | bytes 49160 | tf_op jit(solution)/shard_map/ppermute | solution.py:449
  3.0 1.2 %copy-start = (f32[2,64,2048]{2,1,0:T(8,128)S(1)}, f32[2,64,2048]{2,1,0:T(8,128)}, u32[]{:S(2)}) copy-start(f32[2,64,2048]{2,1,0:T(8,128)} %param.5) | copy-start | bytes 3145732
  4.2 0.8 %copy-start.4 = (f32[2,64,64]{2,1,0:T(8,128)S(1)}, f32[2,64,64]{2,1,0:T(8,128)}, u32[]{:S(2)}) copy-start(f32[2,64,64]{2,1,0:T(8,128)} %w_ref.1) | copy-start | bytes 98308
  7.0 16.6 %collective-permute-start = (f32[64,2048]{1,0:T(8,128)S(1)}, f32[64,2048]{1,0:T(8,128)S(1)}, u32[]{:S(2)}, u32[]{:S(2)}) collective-permute-start(f32[64,2048]{1,0:T(8,128)S(1)} %get-tuple-element.20), channel_id=1, source_target_pairs={{0,8},{8,0},{16,24},{24,16},{1,9},{9,1},{17,25},{25,17},{2,10},{10... | collective-permute-start | bytes 1572872 | tf_op jit(solution)/shard_map/ppermute | solution.py:449
  7.8 4.0 %collective-permute-start.11 = (f32[2,2,2048]{2,1,0:T(2,128)S(1)}, f32[2,2,2048]{2,1,0:T(2,128)S(1)}, u32[]{:S(2)}, u32[]{:S(2)}) collective-permute-start(f32[2,2,2048]{2,1,0:T(2,128)S(1)} %pad_maximum_fusion.1), channel_id=1, source_target_pairs={{0,2},{1,3},{2,0},{3,1},{4,6},{5,7},{6,4},{7,5},{8,10},{9,11},{10,... | collective-permute-start | bytes 98312 | tf_op jit(solution)/shard_map/ppermute | solution.py:449
  11.8 17.2 %copy-start.3 = (f32[2,2048]{1,0:T(2,128)S(1)}, f32[2,2048]{1,0:T(2,128)}, u32[]{:S(2)}) copy-start(f32[2,2048]{1,0:T(2,128)} %ref_ref.1) | copy-start | bytes 49156
  12.6 5.3 %collective-permute-start.12 = (f32[4,2,2048]{2,1,0:T(2,128)S(1)}, f32[4,2,2048]{2,1,0:T(2,128)S(1)}, u32[]{:S(2)}, u32[]{:S(2)}) collective-permute-start(f32[4,2,2048]{2,1,0:T(2,128)S(1)} %pad_maximum_fusion), channel_id=1, source_target_pairs={{0,4},{1,5},{2,6},{3,7},{4,0},{5,1},{6,2},{7,3},{8,12},{9,13},{10,... | collective-permute-start | bytes 196616 | tf_op jit(solution)/shard_map/ppermute | solution.py:449
  17.9 0.7 %copy-start.2 = (f32[2,2048]{1,0:T(2,128)S(1)}, f32[2,2048]{1,0:T(2,128)}, u32[]{:S(2)}) copy-start(f32[2,2048]{1,0:T(2,128)} %ref_ref.1) | copy-start | bytes 49156
  23.5 16.6 %collective-permute-start.13 = (f32[1032,128]{1,0:T(8,128)S(1)}, f32[1032,128]{1,0:T(8,128)S(1)}, u32[]{:S(2)}, u32[]{:S(2)}) collective-permute-start(f32[1032,128]{1,0:T(8,128)S(1)} %get-tuple-element.29.mine_ref.refs_8_), channel_id=1, source_target_pairs={{0,8},{8,0},{16,24},{24,16},{1,9},{9,1},{17,25},{25,17},{2,10},{10... | collective-permute-start | bytes 1585160 | tf_op jit(solution)/shard_map/ppermute | solution.py:449
  23.7 8.8 %collective-permute-start.1 = (f32[1,32,2048]{2,1,0:T(8,128)S(1)}, f32[1,32,2048]{2,1,0:T(8,128)S(1)}, u32[]{:S(2)}, u32[]{:S(2)}) collective-permute-start(f32[1,32,2048]{2,1,0:T(8,128)S(1)} %get-tuple-element.33), channel_id=1, source_target_pairs={{0,16},{8,24},{16,0},{24,8},{1,17},{9,25},{17,1},{25,9},{2,18},{10... | collective-permute-start | bytes 786440 | tf_op jit(solution)/shard_map/ppermute | solution.py:449
  25.2 3.7 %collective-permute-start.2 = (f32[2,256]{1,0:T(2,128)S(1)}, f32[2,256]{1,0:T(2,128)S(1)}, u32[]{:S(2)}, u32[]{:S(2)}) collective-permute-start(f32[2,256]{1,0:T(2,128)S(1)} %slice.27), channel_id=1, source_target_pairs={{0,1},{1,2},{2,3},{3,4},{4,5},{5,6},{6,7},{8,9},{9,10},{10,11},{11... | collective-permute-start | bytes 6152 | tf_op jit(solution)/shard_map/ppermute | solution.py:460
  32.4 18.7 %copy-start.1 = (bf16[2,128,512]{2,1,0:T(8,128)(2,1)S(1)}, bf16[2,128,512]{2,1,0:T(8,128)(2,1)}, u32[]{:S(2)}) copy-start(bf16[2,128,512]{2,1,0:T(8,128)(2,1)} %constant.2.clone.refs_12_) | copy-start | bytes 786436
  33.9 6.4 %collective-permute-start.3 = (f32[10,8,128]{2,1,0:T(8,128)S(1)}, f32[10,8,128]{2,1,0:T(8,128)S(1)}, u32[]{:S(2)}, u32[]{:S(2)}) collective-permute-start(f32[10,8,128]{2,1,0:T(8,128)S(1)} %get-tuple-element.22), channel_id=1, source_target_pairs={{0,1},{1,0},{2,3},{3,2},{4,5},{5,4},{6,7},{7,6},{8,9},{9,8},{10,11... | collective-permute-start | bytes 122888 | tf_op jit(solution)/shard_map/ppermute | solution.py:449
  34.5 10.0 %collective-permute-start.4 = (f32[10,8,128]{2,1,0:T(8,128)S(1)}, f32[10,8,128]{2,1,0:T(8,128)S(1)}, u32[]{:S(2)}, u32[]{:S(2)}) collective-permute-start(f32[10,8,128]{2,1,0:T(8,128)S(1)} %get-tuple-element.23), channel_id=1, source_target_pairs={{0,2},{1,3},{2,0},{3,1},{4,6},{5,7},{6,4},{7,5},{8,10},{9,11},{10,... | collective-permute-start | bytes 122888 | tf_op jit(solution)/shard_map/ppermute | solution.py:449
  36.0 11.6 %collective-permute-start.5 = (f32[10,8,128]{2,1,0:T(8,128)S(1)}, f32[10,8,128]{2,1,0:T(8,128)S(1)}, u32[]{:S(2)}, u32[]{:S(2)}) collective-permute-start(f32[10,8,128]{2,1,0:T(8,128)S(1)} %get-tuple-element.24), channel_id=1, source_target_pairs={{0,3},{1,2},{2,1},{3,0},{4,7},{5,6},{6,5},{7,4},{8,11},{9,10},{10,... | collective-permute-start | bytes 122888 | tf_op jit(solution)/shard_map/ppermute | solution.py:449
  37.5 10.1 %collective-permute-start.6 = (f32[10,8,128]{2,1,0:T(8,128)S(1)}, f32[10,8,128]{2,1,0:T(8,128)S(1)}, u32[]{:S(2)}, u32[]{:S(2)}) collective-permute-start(f32[10,8,128]{2,1,0:T(8,128)S(1)} %get-tuple-element.25), channel_id=1, source_target_pairs={{0,4},{1,5},{2,6},{3,7},{4,0},{5,1},{6,2},{7,3},{8,12},{9,13},{10,... | collective-permute-start | bytes 122888 | tf_op jit(solution)/shard_map/ppermute | solution.py:449
  40.1 7.4 %collective-permute-start.7 = (f32[10,8,128]{2,1,0:T(8,128)S(1)}, f32[10,8,128]{2,1,0:T(8,128)S(1)}, u32[]{:S(2)}, u32[]{:S(2)}) collective-permute-start(f32[10,8,128]{2,1,0:T(8,128)S(1)} %get-tuple-element.26), channel_id=1, source_target_pairs={{0,5},{1,4},{2,7},{3,6},{4,1},{5,0},{6,3},{7,2},{8,13},{9,12},{10,... | collective-permute-start | bytes 122888 | tf_op jit(solution)/shard_map/ppermute | solution.py:449
  40.4 7.2 %collective-permute-start.8 = (f32[10,8,128]{2,1,0:T(8,128)S(1)}, f32[10,8,128]{2,1,0:T(8,128)S(1)}, u32[]{:S(2)}, u32[]{:S(2)}) collective-permute-start(f32[10,8,128]{2,1,0:T(8,128)S(1)} %get-tuple-element.27), channel_id=1, source_target_pairs={{0,6},{1,7},{2,4},{3,5},{4,2},{5,3},{6,0},{7,1},{8,14},{9,15},{10,... | collective-permute-start | bytes 122888 | tf_op jit(solution)/shard_map/ppermute | solution.py:449
  44.5 6.7 %collective-permute-start.9 = (f32[10,8,128]{2,1,0:T(8,128)S(1)}, f32[10,8,128]{2,1,0:T(8,128)S(1)}, u32[]{:S(2)}, u32[]{:S(2)}) collective-permute-start(f32[10,8,128]{2,1,0:T(8,128)S(1)} %get-tuple-element.28), channel_id=1, source_target_pairs={{0,7},{1,6},{2,5},{3,4},{4,3},{5,2},{6,1},{7,0},{8,15},{9,14},{10,... | collective-permute-start | bytes 122888 | tf_op jit(solution)/shard_map/ppermute | solution.py:449

commit v3 on v2

--- a/solution.py
+++ b/solution.py
@@ -32,6 +32,15 @@
 def dot_nt(a, b, precision=None):
     return lax.dot_general(
         a, b, (((1,), (1,)), ((), ())), precision=precision, preferred_element_type=jnp.float32
+    )
+
+
+def dot_split(a, b):
+    (a_high, a_low), (b_high, b_low) = a, b
+    left = jnp.concatenate([a_high, a_low], 1)
+    right = jnp.concatenate([b_high, b_high], 0)
+    return jnp.dot(left, right, preferred_element_type=jnp.float32) + jnp.dot(
+        a_high, b_low, preferred_element_type=jnp.float32
     )
 
 
@@ -59,61 +68,55 @@
     return outs
 
 
-def beam_kernel(chan_count, beams_local, w_ref, s_ref, even_ref, odd_ref):
+def beam_kernel(parity, chan_count, beams_local, w_ref, s_ref, out_ref):
     me = lax.axis_index("chan")
     half = SUBLANES // 2
     sub = lax.broadcasted_iota(jnp.int32, (SUBLANES, w_ref.shape[2]), 0)
     top = sub < half
-    parts = []
-    for parity in range(2):
-        rows = []
-        for e in range(parity, chan_count, 2):
-            base = (me ^ e) * beams_local
-            for tile in range(beams_local // SUBLANES):
-                start = pl.multiple_of(base + tile * SUBLANES, SUBLANES)
-                wr = w_ref[0, pl.ds(start, SUBLANES), :]
-                wi = w_ref[1, pl.ds(start, SUBLANES), :]
-                wr_s = pltpu.roll(wr, half, 0)
-                wi_s = pltpu.roll(wi, half, 0)
-                first = [jnp.where(top, wr, wi_s), jnp.where(top, -wi, wr_s)]
-                second = [jnp.where(top, wr_s, wi), jnp.where(top, -wi_s, wr)]
-                rows.append(jnp.concatenate(first, 1))
-                rows.append(jnp.concatenate(second, 1))
-        parts.append(jnp.concatenate(rows, 0))
-    weights = jnp.concatenate(parts, 0)
-    product = jnp.dot(
-        weights, s_ref[...], precision=HIGHEST, preferred_element_type=jnp.float32
-    )
-    mid = product.shape[0] // 2
-    even_ref[...] = product[:mid]
-    odd_ref[...] = product[mid:]
-
-
-def beam_call(steering, survey, chan_count, beams_local):
+    rows = []
+    for e in range(parity, chan_count, 2):
+        base = (me ^ e) * beams_local
+        for tile in range(beams_local // SUBLANES):
+            start = pl.multiple_of(base + tile * SUBLANES, SUBLANES)
+            wr = w_ref[0, pl.ds(start, SUBLANES), :]
+            wi = w_ref[1, pl.ds(start, SUBLANES), :]
+            wr_s = pltpu.roll(wr, half, 0)
+            wi_s = pltpu.roll(wi, half, 0)
+            first = [jnp.where(top, wr, wi_s), jnp.where(top, -wi, wr_s)]
+            second = [jnp.where(top, wr_s, wi), jnp.where(top, -wi_s, wr)]
+            rows.append(jnp.concatenate(first, 1))
+            rows.append(jnp.concatenate(second, 1))
+    weights = jnp.concatenate(rows, 0)
+    out_ref[...] = dot_split(halves(weights), halves(s_ref[...]))
+
+
+def beam_call(steering, survey, parity, chan_count, beams_local):
     depth, length = survey.shape
     rows = chan_count * beams_local
     steps = 4
     width = length // steps
-    out = jax.ShapeDtypeStruct((rows, length), jnp.float32)
     return pl.pallas_call(
-        functools.partial(beam_kernel, chan_count, beams_local),
+        functools.partial(beam_kernel, parity, chan_count, beams_local),
         grid=(steps,),
         in_specs=[
             pl.BlockSpec(steering.shape, lambda i: (0, 0, 0)),
             pl.BlockSpec((depth, width), lambda i: (0, i)),
         ],
-        out_specs=[pl.BlockSpec((rows, width), lambda i: (0, i))] * 2,
-        out_shape=[out, out],
-        compiler_params=params(),
+        out_specs=pl.BlockSpec((rows, width), lambda i: (0, i)),
+        out_shape=jax.ShapeDtypeStruct((rows, length), jnp.float32),
+        compiler_params=pltpu.CompilerParams(vmem_limit_bytes=60 * 1024 * 1024),
         cost_estimate=pl.CostEstimate(
-            flops=4 * rows * depth * length, bytes_accessed=4 * length * (depth + 2 * rows), transcendentals=0
+            flops=6 * rows * depth * length, bytes_accessed=4 * length * (depth + rows), transcendentals=0
         ),
-        name="beams",
+        name="beams_kept" if parity == 0 else "beams_sent",
     )(steering, survey)
 
 
-def table_kernel(edge_ref, ref_ref, out_ref):
-    span = jnp.concatenate([edge_ref[...], ref_ref[...]], 1)
+def table_kernel(ref_ref, out_ref):
+    me = lax.axis_index("tm")
+    edge = ref_ref[jnp.maximum(me - 1, 0), :, ref_ref.shape[2] - 2 * LANES :]
+    edge = jnp.where(me > 0, edge, jnp.zeros_like(edge))
+    span = jnp.concatenate([edge, ref_ref[me]], 1)
     for c in range(2):
         tiled = jnp.broadcast_to(span[c : c + 1], (LANES, span.shape[1]))
         shifted = pltpu.roll(tiled, 0, 1, stride=1, stride_axis=0)[:, LANES:]
@@ -122,8 +125,8 @@
         out_ref[1, c] = low
 
 
-def table_call(edge, ref):
-    shape = (2, 2, LANES, LANES + ref.shape[1])
+def table_call(ref_all):
+    shape = (2, 2, LANES, LANES + ref_all.shape[2])
     return pl.pallas_call(
         table_kernel,
         out_shape=jax.ShapeDtypeStruct(shape, jnp.bfloat16),
@@ -132,15 +135,11 @@
             flops=8 * math.prod(shape), bytes_accessed=2 * math.prod(shape), transcendentals=0
         ),
         name="shifted_reference",
-    )(edge, ref)
+    )(ref_all)
 
 
 def lag_kernel(groups, owners, *refs):
-    y_refs = refs[: -(owners + 2)]
-    table_ref = refs[-(owners + 2)]
-    out_refs = refs[-(owners + 1) : -1]
-    held_ref = refs[-1]
-    me = lax.axis_index("tm")
+    *y_refs, table_ref, out_ref = refs
     y = y_refs[0][...]
     for y_ref in y_refs[1:]:
         y = y + y_ref[...]
@@ -180,31 +179,28 @@
             lanes = slice(h * LANES, (h + 1) * LANES)
             tiles = [product[r : r + SUBLANES, lanes] for r in range(0, rows, SUBLANES)]
             for j, tile in enumerate(swap_groups(tiles, groups)):
-                held_ref[h * groups + j, q] = tile
+                out_ref[h * groups + j, q] = tile
     left = lax.broadcasted_iota(jnp.int32, (SUBLANES, LANES), 1) < TAPS
     for i in range(groups // 2):
         a = taps_sum[i * SUBLANES : (i + 1) * SUBLANES]
         other = i + groups // 2
         b = taps_sum[other * SUBLANES : (other + 1) * SUBLANES]
         tile = jnp.where(left, a, pltpu.roll(b, LANES - TAPS, 1))
-        for out_ref in out_refs:
-            out_ref[blocks + i] = tile
-    for e, out_ref in enumerate(out_refs):
-        out_ref[:blocks] = held_ref[me ^ e]
+        for owner in range(owners):
+            out_ref[owner, blocks + i] = tile
 
 
 def lag_call(ys, table, groups, owners):
     rows, length = ys[0].shape
     blocks = length // BLOCK_LEN
-    shape = (blocks + groups // 2, SUBLANES, LANES)
+    shape = (owners, blocks + groups // 2, SUBLANES, LANES)
     return pl.pallas_call(
         functools.partial(lag_kernel, groups, owners),
-        out_shape=[jax.ShapeDtypeStruct(shape, jnp.float32)] * owners,
-        scratch_shapes=[pltpu.VMEM((owners, blocks, SUBLANES, LANES), jnp.float32)],
+        out_shape=jax.ShapeDtypeStruct(shape, jnp.float32),
         compiler_params=params(),
         cost_estimate=pl.CostEstimate(
             flops=12 * rows * LAGS * 2 * length,
-            bytes_accessed=4 * owners * math.prod(shape) + 2 * math.prod(table.shape),
+            bytes_accessed=4 * math.prod(shape) + 2 * math.prod(table.shape),
             transcendentals=0,
         ),
         name="lag_products",
@@ -215,22 +211,16 @@
 BATCH = 4
 
 
-def own_kernel(lags_local, *refs):
-    *part_refs, out_ref, tail_ref, span_ref, late_ref = refs
+def own_kernel(lags_local, ref_ref, out_ref, tail_ref, span_ref, late_ref):
     me = lax.axis_index("tm")
-    length = part_refs[0].shape[2]
-    owners = sum(part_ref.shape[0] for part_ref in part_refs)
+    owners, _, length = ref_ref.shape
     samples = owners * length
     blocks = samples // BLOCK_LEN // SHARES
     first_block = lax.rem(lax.axis_index("chan"), SHARES) * blocks
     span_ref[:, :BLOCK_LEN] = jnp.zeros((2, BLOCK_LEN), jnp.float32)
     span_ref[:, BLOCK_LEN + samples :] = jnp.zeros((2, BLOCK_LEN), jnp.float32)
-    e = 0
-    for part_ref in part_refs:
-        for i in range(part_ref.shape[0]):
-            start = pl.multiple_of((me ^ e) * length + BLOCK_LEN, BLOCK_LEN)
-            span_ref[:, pl.ds(start, length)] = part_ref[i]
-            e += 1
+    for t in range(owners):
+        span_ref[:, BLOCK_LEN + t * length : BLOCK_LEN + (t + 1) * length] = ref_ref[t]
     late_ref[...] = pltpu.roll(span_ref[...], me * lags_local, 1)
 
     def shifted(window, count):
@@ -270,9 +260,8 @@
     tail_ref[...] = dot_nt(tail, tail, HIGHEST)
 
 
-def own_call(parts, lags_local):
-    length = parts[0].shape[2]
-    samples = length * sum(part.shape[0] for part in parts)
+def own_call(ref_all, lags_local):
+    samples = ref_all.shape[0] * ref_all.shape[2]
     rows = samples // BLOCK_LEN // SHARES * lags_local
     return pl.pallas_call(
         functools.partial(own_kernel, lags_local),
@@ -286,20 +275,11 @@
             flops=24 * rows * BLOCK_LEN * 2 * TAPS, bytes_accessed=4 * rows * 2 * TAPS, transcendentals=0
         ),
         name="reference_products",
-    )(*parts)
+    )(ref_all)
 
 
 def as_factor(a):
     return jnp.concatenate([a, -lane_sign(a.shape) * pltpu.roll(a, a.shape[0], 1)], 0)
-
-
-def dot_split(a, b):
-    (a_high, a_low), (b_high, b_low) = a, b
-    left = jnp.concatenate([a_high, a_low], 1)
-    right = jnp.concatenate([b_high, b_high], 0)
-    return jnp.dot(left, right, preferred_element_type=jnp.float32) + jnp.dot(
-        a_high, b_low, preferred_element_type=jnp.float32
-    )
 
 
 def solver_kernel(mine_ref, other_ref, tail_ref, gram_ref, solver_ref):
@@ -373,23 +353,18 @@
     return (np.concatenate([upper, lower], 0) * scale).astype(np.float32)
 
 
-def map_kernel(groups, owners, *refs):
-    got_refs = refs[:owners]
-    mine_ref, other_ref, gram_ref, solver_ref, wave_ref, out_ref, got_ref, held_ref = refs[owners:]
-    me = lax.axis_index("tm")
-    blocks = got_refs[0].shape[0] - groups // 2
+def map_kernel(groups, got_ref, mine_ref, other_ref, gram_ref, solver_ref, wave_ref, out_ref, held_ref):
+    owners, pieces = got_ref.shape[:2]
+    blocks = pieces - groups // 2
     lags_local = LANES // groups
     total = owners * blocks
     left = lax.broadcasted_iota(jnp.int32, (SUBLANES, LANES), 1) < TAPS
     sign = row_sign((SUBLANES, LANES))
-    for e, ref in enumerate(got_refs):
-        start = pl.multiple_of((me ^ e) * blocks * SUBLANES, SUBLANES)
-        got_ref[pl.ds(start, blocks * SUBLANES), :] = ref[:blocks].reshape(blocks * SUBLANES, LANES)
     rows = [None] * groups
     for i in range(groups // 2):
-        tile = got_refs[0][blocks + i]
-        for ref in got_refs[1:]:
-            tile = tile + ref[blocks + i]
+        tile = got_ref[0, blocks + i]
+        for owner in range(1, owners):
+            tile = tile + got_ref[owner, blocks + i]
         swapped = pltpu.roll(tile, TAPS, 1)
         for part, here, there in ((i, tile, swapped), (i + groups // 2, swapped, tile)):
             other = -sign * pltpu.roll(there, SUBLANES // 2, 0)
@@ -411,10 +386,10 @@
             for h in range(2):
                 lanes = slice(h * LANES, (h + 1) * LANES)
                 tiles = [clutter[r : r + SUBLANES, lanes] for r in range(0, groups * SUBLANES, SUBLANES)]
-                tiles = jnp.concatenate(swap_groups(tiles, groups), 0)
-                at = pl.multiple_of((first + q + h * groups) * SUBLANES, groups * SUBLANES)
-                at = pl.ds(at, groups * SUBLANES)
-                held_ref[at, :] = got_ref[at, :] - tiles
+                for j, tile in enumerate(swap_groups(tiles, groups)):
+                    at = first + q + h * groups + j
+                    here = pl.ds(pl.multiple_of(at * SUBLANES, SUBLANES), SUBLANES)
+                    held_ref[here, :] = got_ref[at // blocks, at % blocks] - tile
     half = SUBLANES // 2
     wave = (wave_ref[0], wave_ref[1])
     for g in range(half):
@@ -428,20 +403,19 @@
 
 
 def map_call(got, mine, other, gram, solver, wave, groups, beams_local):
-    owners = len(got)
-    total = owners * (got[0].shape[0] - groups // 2)
+    total = got.shape[0] * (got.shape[1] - groups // 2)
     lags_local = LANES // groups
     shape = (beams_local, 2, lags_local, DOPPLER)
     return pl.pallas_call(
-        functools.partial(map_kernel, groups, owners),
+        functools.partial(map_kernel, groups),
         out_shape=jax.ShapeDtypeStruct(shape, jnp.float32),
-        scratch_shapes=[pltpu.VMEM((total * SUBLANES, LANES), jnp.float32)] * 2,
+        scratch_shapes=[pltpu.VMEM((total * SUBLANES, LANES), jnp.float32)],
         compiler_params=params(),
         cost_estimate=pl.CostEstimate(
             flops=12 * math.prod(shape) * total, bytes_accessed=4 * math.prod(shape), transcendentals=0
         ),
         name="range_doppler",
-    )(*got, mine, other, gram, solver, wave)
+    )(got, mine, other, gram, solver, wave)
 
 
 def swap(x, axis, by):
@@ -457,29 +431,26 @@
     groups = LANES // lags_local
     samples = length * tm_count
 
-    edge = lax.ppermute(
-        ref_signal[:, length - 2 * LANES :], "tm", [(i, i + 1) for i in range(tm_count - 1)]
-    )
-    ref_parts = [ref_signal[None]]
-    by = 1
-    while by < tm_count:
-        ref_parts.append(swap(jnp.concatenate(ref_parts, 0), "tm", by))
-        by *= 2
-
-    even, odd = beam_call(steering, surveillance.reshape(2 * channels, length), chan_count, beams_local)
+    ref_all = lax.all_to_all(
+        jnp.broadcast_to(ref_signal[None], (tm_count,) + ref_signal.shape), "tm", 0, 0, tiled=True
+    )
+    survey = surveillance.reshape(2 * channels, length)
     rows = 2 * beams_local
-    parts = [even.reshape(chan_count // 2, rows, length), swap(odd, "chan", 1).reshape(chan_count // 2, rows, length)]
+    shape = (chan_count // 2, rows, length)
+    moved = swap(beam_call(steering, survey, 1, chan_count, beams_local), "chan", 1)
+    parts = [beam_call(steering, survey, 0, chan_count, beams_local).reshape(shape), moved.reshape(shape)]
     by = 2
     while by < chan_count:
         sent = parts[0][1::2]
         for part in parts[1:]:
             sent = sent + part[1::2]
+        ref_all, sent = lax.optimization_barrier((ref_all, sent))
         parts = [part[::2] for part in parts] + [swap(sent, "chan", by)]
         by *= 2
-    table = table_call(edge, ref_signal)
+    mine, tail = own_call(ref_all, lags_local)
+    table = table_call(ref_all)
     pieces = lag_call([part[0] for part in parts], table, groups, tm_count)
-    got = [pieces[0]] + [swap(piece, "tm", e) for e, piece in enumerate(pieces) if e]
-    mine, tail = own_call(ref_parts, lags_local)
+    got = lax.all_to_all(pieces, "tm", 0, 0, tiled=True)
     other = swap(mine, "chan", 1)
     gram, solver = solver_call(mine, other, tail)
     wave = doppler_table(samples // BLOCK_LEN, 0.125 / math.sqrt(samples))

time: 54.4 us -> 47.4 us (0.87)
  starting transfers between devices: 22.9 us -> 13.1 us
  Pallas kernels: 13.8 us -> 20.2 us
  waiting for transfers between devices: 12.7 us -> 11 us
  local copies, waits for them, and re-layouts: 2.79 us -> 1.4 us
    ppermute x13 -> x3, starting transfers between devices: 20.5 us -> 2.01 us  [swap(): return lax.ppermute(x, axis, pairs)]
    ppermute x13 -> x3, waiting for transfers between devices: 11.4 us -> 0.01 us  [swap(): return lax.ppermute(x, axis, pairs)]
    all_to_all x0 -> x2, starting transfers between devices: none -> 11.1 us  [the longest x1 6.83 us: tiled_device(): lax.all_to_all(jnp.broadcast_to(ref_signal[None], (tm_count,) + ref_signa...]
    all_to_all x0 -> x2, waiting for transfers between devices: none -> 11 us  [the longest x1 8.26 us: tiled_device(): got = lax.all_to_all(pieces, 'tm', 0, 0, tiled=True)]
    pallas_call x3 -> x4, Pallas kernels: 6.19 us -> 12.6 us  [the longest x2 7.55 us: beam_call(): pl.pallas_call(functools.partial(beam_kernel, parity, chan_count, beams_l...]
    unnamed x10 -> x2, local copies, waits for them, and re-layouts: 2.79 us -> 0.01 us
    ppermute x1 -> x0, starting transfers between devices: 2.4 us -> none  [tiled_device(): lax.ppermute(ref_signal[:, length - 2 * LANES:], 'tm', [(i, i + 1) for i...]
    concatenate x2 -> x0, other arithmetic: 1.56 us -> none  [tiled_device(): ref_parts.append(swap(jnp.concatenate(ref_parts, 0), 'tm', by))]
  transfers between devices with their start and end apart: 14 -> 5, of which waited for: 5 -> 2; matrix products, arithmetic and copies ran while one was open for 3% -> 5% of each run, Pallas kernels for 20% -> 29%
where the time goes in v3:
time: 47.4 us; the launch traced here: 46.9 us
  Pallas kernels  20.2 us (43%)
  starting transfers between devices  13.1 us (28%)
  waiting for transfers between devices  11 us (23%)
  local copies, waits for them, and re-layouts  1.4 us (3%)
  other arithmetic  1.09 us (2%)
    all_to_all x1, waiting for transfers between devices, tiled_device(): got = lax.all_to_all(pieces, 'tm', 0, 0, tiled=True)  8.26 us
    pallas_call x2, Pallas kernels, beam_call(): pl.pallas_call(functools.partial(beam_kernel, parity, chan_count, beams_l...  7.55 us
    all_to_all x1, starting transfers between devices, tiled_device(): lax.all_to_all(jnp.broadcast_to(ref_signal[None], (tm_count,) + ref_signa...  6.83 us
    pallas_call x1, Pallas kernels, own_call(): pl.pallas_call(functools.partial(own_kernel, lags_local), out_shape=[jax....  4.89 us
    all_to_all x1, starting transfers between devices, tiled_device(): got = lax.all_to_all(pieces, 'tm', 0, 0, tiled=True)  4.3 us
    pallas_call x1, Pallas kernels, map_call(): pl.pallas_call(functools.partial(map_kernel, groups), out_shape=jax.Shape...  2.82 us
    all_to_all x1, waiting for transfers between devices, tiled_device(): lax.all_to_all(jnp.broadcast_to(ref_signal[None], (tm_count,) + ref_signa...  2.74 us
    pallas_call x1, Pallas kernels, lag_call(): pl.pallas_call(functools.partial(lag_kernel, groups, owners), out_shape=j...  2.2 us
  transfers between devices with their start and end apart: 5, of which 2 were waited for; matrix products, arithmetic and copies ran while one was open for 5% of the time, Pallas kernels for 29%

profile of v3, /device:TPU:0, one launch (start us, length us, event | category | flops | bytes accessed | tf_op | source)
XLA Modules:
  0.0 46.9 jit_solution(11264487685539920747)
XLA Ops:
  0.0 3.7 %beams_sent.1 = f32[64,2048]{1,0:T(8,128)} custom-call(f32[2,64,64]{2,1,0:T(8,128)} %w_ref.3, f32[128,2048]{1,0:T(8,128)} %bitcast.5), custom_call_target="tpu_custom_call" | custom-call | flops 100663296 | bytes 1572864 | tf_op jit(solution)/shard_map/beams_sent/pallas_call | solution.py:98
  3.7 0.5 collective-permute-start
  4.2 1.4 %broadcast_in_dim.2 = f32[8,2,2048]{2,1,0:T(2,128)} broadcast(f32[2,2048]{1,0:T(2,128)} %param.4), dimensions={1,2} | broadcast | bytes 147456 | tf_op jit(solution)/shard_map/broadcast_in_dim | solution.py:435
  5.6 6.8 %all-to-all-start = ((f32[8,2,2048]{2,1,0:T(2,128)}), f32[8,2,2048]{2,1,0:T(2,128)S(1)}, u32[]{:S(2)}, u32[]{:S(2)}) async-start(f32[8,2,2048]{2,1,0:T(2,128)} %broadcast_in_dim.2), calls=%async_computation | async-start | bytes 262144 | tf_op jit(solution)/shard_map/all_to_all | solution.py:434
  12.4 3.8 %beams_kept.1 = f32[64,2048]{1,0:T(8,128)} custom-call(f32[2,64,64]{2,1,0:T(8,128)} %w_ref.3, f32[128,2048]{1,0:T(8,128)} %bitcast.6), custom_call_target="tpu_custom_call" | custom-call | flops 100663296 | bytes 1572864 | tf_op jit(solution)/shard_map/beams_kept/pallas_call | solution.py:98
  16.2 0.0 collective-permute-done
  16.2 1.1 %fusion = (f32[1,32,2048]{2,1,0:T(8,128)S(1)}, f32[32,2048]{1,0:T(8,128)S(1)}, f32[32,2048]{1,0:T(8,128)S(1)}) fusion(f32[64,2048]{1,0:T(8,128)S(1)} %collective-permute-done, f32[64,2048]{1,0:T(8,128)} %beams_kept.1), kind=kLoop, calls=%fused_computation.1 | loop fusion | flops 65536 | bytes 1835008 | tf_op jit(solution)/shard_map/add | solution.py:446
  17.3 2.7 %all-to-all-done.ref_ref = f32[8,2,2048]{2,1,0:T(2,128)S(1)} async-done(((f32[8,2,2048]{2,1,0:T(2,128)}), f32[8,2,2048]{2,1,0:T(2,128)S(1)}, u32[]{:S(2)}, u32[]{:S(2)}) %all-to-all-start) | async-done | bytes 131104 | tf_op jit(solution)/shard_map/all_to_all | solution.py:434
  20.1 1.5 %collective-permute-start.1 = (f32[1,32,2048]{2,1,0:T(8,128)S(1)}, f32[1,32,2048]{2,1,0:T(8,128)S(1)}, u32[]{:S(2)}, u32[]{:S(2)}) collective-permute-start(f32[1,32,2048]{2,1,0:T(8,128)S(1)} %get-tuple-element.11), channel_id=1, source_target_pairs={{0,16},{8,24},{16,0},{24,8},{1,17},{9,25},{17,1},{25,9},{2,18},{10... | collective-permute-start | bytes 786440 | tf_op jit(solution)/shard_map/ppermute | solution.py:423
  21.6 4.9 %reference_products.1 = (f32[1032,128]{1,0:T(8,128)S(1)}, f32[128,128]{1,0:T(8,128)S(1)}) custom-call(f32[8,2,2048]{2,1,0:T(2,128)S(1)} %all-to-all-done.ref_ref), custom_call_target="tpu_custom_call" | custom-call | flops 805306368 | bytes 524288 | tf_op jit(solution)/shard_map/reference_products/pallas_call | solution.py:266
  26.5 0.1 collective-permute-start.2
  26.5 0.7 %shifted_reference.1.refs_3_ = bf16[2,2,128,2176]{3,2,1,0:T(8,128)(2,1)S(1)} custom-call(f32[8,2,2048]{2,1,0:T(2,128)S(1)} %all-to-all-done.ref_ref), custom_call_target="tpu_custom_call" | custom-call | flops 8912896 | bytes 2228224 | tf_op jit(solution)/shard_map/shifted_reference/pallas_call | solution.py:130
  27.2 0.0 collective-permute-done.1
  27.2 0.0 copy-start
  27.3 2.2 %lag_products.1 = f32[8,10,8,128]{3,2,1,0:T(8,128)} custom-call(f32[32,2048]{1,0:T(8,128)S(1)} %get-tuple-element.18.refs_0_, f32[32,2048]{1,0:T(8,128)S(1)} %get-tuple-element.19.refs_1_, f32[32,2048]{1,0:T(8,128)S(1)} %bitcast.4, bf16[2,2,128,2176]{3,2,1,0:T(8,128)(2,1)S(1)} %shifted_reference.1.refs_3_), custom_call_target="tpu_custom_call" | custom-call | flops 402653184 | bytes 2555904 | tf_op jit(solution)/shard_map/lag_products/pallas_call | solution.py:197
  29.5 4.3 %all-to-all-start.1 = ((f32[8,10,8,128]{3,2,1,0:T(8,128)}), f32[8,10,8,128]{3,2,1,0:T(8,128)S(1)}, u32[]{:S(2)}, u32[]{:S(2)}) async-start(f32[8,10,8,128]{3,2,1,0:T(8,128)} %lag_products.1), calls=%async_computation.1 | async-start | bytes 655360 | tf_op jit(solution)/shard_map/all_to_all | solution.py:453
  33.8 0.0 collective-permute-done.2.other_ref
  33.8 2.0 %gram_inverse.1 = (f32[128,128]{1,0:T(8,128)S(1)}, f32[128,128]{1,0:T(8,128)S(1)}) custom-call(f32[1032,128]{1,0:T(8,128)S(1)} %get-tuple-element.13.mine_ref, f32[1032,128]{1,0:T(8,128)S(1)} %collective-permute-done.2.other_ref, f32[128,128]{1,0:T(8,128)S(1)} %get-tuple-element.14.tail_ref), custom_call_target="tpu_custom_call" | custom-call | flops 500000000 | bytes 200000 | tf_op jit(solution)/shard_map/gram_inverse/pallas_call | solution.py:336
  35.8 8.3 %all-to-all-done.1.got_ref = f32[8,10,8,128]{3,2,1,0:T(8,128)S(1)} async-done(((f32[8,10,8,128]{3,2,1,0:T(8,128)}), f32[8,10,8,128]{3,2,1,0:T(8,128)S(1)}, u32[]{:S(2)}, u32[]{:S(2)}) %all-to-all-start.1) | async-done | bytes 327712 | tf_op jit(solution)/shard_map/all_to_all | solution.py:453
  44.1 0.0 copy-done
  44.1 2.8 %range_doppler.1 = f32[16,2,32,256]{3,2,1,0:T(8,128)} custom-call(f32[8,10,8,128]{3,2,1,0:T(8,128)S(1)} %all-to-all-done.1.got_ref, f32[1032,128]{1,0:T(8,128)S(1)} %get-tuple-element.13.mine_ref, f32[1032,128]{1,0:T(8,128)S(1)} %collective-permute-done.2.other_ref, f32[128,128]{1,0:T(8,128)S(1)} %get-tuple-element.15.gram_ref, ...), custom_call_target="tpu_custom_call" | custom-call | flops 201326592 | bytes 1048576 | tf_op jit(solution)/shard_map/range_doppler/pallas_call | solution.py:409
Async XLA Ops:
  3.7 12.5 %collective-permute-start = (f32[64,2048]{1,0:T(8,128)}, f32[64,2048]{1,0:T(8,128)S(1)}, u32[]{:S(2)}, u32[]{:S(2)}) collective-permute-start(f32[64,2048]{1,0:T(8,128)} %beams_sent.1), channel_id=1, source_target_pairs={{0,8},{8,0},{16,24},{24,16},{1,9},{9,1},{17,25},{25,17},{2,10},{10... | collective-permute-start | bytes 1572872 | tf_op jit(solution)/shard_map/ppermute | solution.py:423
  5.6 14.5 %all-to-all-start = ((f32[8,2,2048]{2,1,0:T(2,128)}), f32[8,2,2048]{2,1,0:T(2,128)S(1)}, u32[]{:S(2)}, u32[]{:S(2)}) async-start(f32[8,2,2048]{2,1,0:T(2,128)} %broadcast_in_dim.2), calls=%async_computation | async-start | bytes 262144 | tf_op jit(solution)/shard_map/all_to_all | solution.py:434
  20.1 7.2 %collective-permute-start.1 = (f32[1,32,2048]{2,1,0:T(8,128)S(1)}, f32[1,32,2048]{2,1,0:T(8,128)S(1)}, u32[]{:S(2)}, u32[]{:S(2)}) collective-permute-start(f32[1,32,2048]{2,1,0:T(8,128)S(1)} %get-tuple-element.11), channel_id=1, source_target_pairs={{0,16},{8,24},{16,0},{24,8},{1,17},{9,25},{17,1},{25,9},{2,18},{10... | collective-permute-start | bytes 786440 | tf_op jit(solution)/shard_map/ppermute | solution.py:423
  26.5 7.3 %collective-permute-start.2 = (f32[1032,128]{1,0:T(8,128)S(1)}, f32[1032,128]{1,0:T(8,128)S(1)}, u32[]{:S(2)}, u32[]{:S(2)}) collective-permute-start(f32[1032,128]{1,0:T(8,128)S(1)} %get-tuple-element.13.mine_ref), channel_id=1, source_target_pairs={{0,8},{8,0},{16,24},{24,16},{1,9},{9,1},{17,25},{25,17},{2,10},{10... | collective-permute-start | bytes 1585160 | tf_op jit(solution)/shard_map/ppermute | solution.py:423
  27.2 16.8 %copy-start = (bf16[2,128,512]{2,1,0:T(8,128)(2,1)S(1)}, bf16[2,128,512]{2,1,0:T(8,128)(2,1)}, u32[]{:S(2)}) copy-start(bf16[2,128,512]{2,1,0:T(8,128)(2,1)} %constant.2.clone.wave_ref) | copy-start | bytes 786436
  29.5 14.6 %all-to-all-start.1 = ((f32[8,10,8,128]{3,2,1,0:T(8,128)}), f32[8,10,8,128]{3,2,1,0:T(8,128)S(1)}, u32[]{:S(2)}, u32[]{:S(2)}) async-start(f32[8,10,8,128]{3,2,1,0:T(8,128)} %lag_products.1), calls=%async_computation.1 | async-start | bytes 655360 | tf_op jit(solution)/shard_map/all_to_all | solution.py:453

commit v4 on v3

--- a/solution.py
+++ b/solution.py
@@ -68,48 +68,80 @@
     return outs
 
 
-def beam_kernel(parity, chan_count, beams_local, w_ref, s_ref, out_ref):
+CHUNKS = 4
+
+
+def beam_kernel(
+    chan_count, beams_local, w_hbm, s_hbm, ref_hbm, kept_ref, sent_ref, spread_hbm, w_ref, s_ref, w_sem, s_sem, ref_sem
+):
     me = lax.axis_index("chan")
+    depth, length = s_hbm.shape
+    width = length // CHUNKS
+    w_copy = pltpu.make_async_copy(w_hbm, w_ref, w_sem)
+    w_copy.start()
+    s_copies = []
+    for n in range(CHUNKS):
+        cols = pl.ds(n * width, width)
+        s_copies.append(pltpu.make_async_copy(s_hbm.at[:, cols], s_ref.at[:, cols], s_sem.at[n]))
+        s_copies[n].start()
+    ref_copies = []
+    for n in range(spread_hbm.shape[0]):
+        ref_copies.append(pltpu.make_async_copy(ref_hbm, spread_hbm.at[n], ref_sem.at[n]))
+        ref_copies[n].start()
     half = SUBLANES // 2
-    sub = lax.broadcasted_iota(jnp.int32, (SUBLANES, w_ref.shape[2]), 0)
+    sub = lax.broadcasted_iota(jnp.int32, (SUBLANES, w_hbm.shape[2]), 0)
     top = sub < half
+    w_copy.wait()
     rows = []
-    for e in range(parity, chan_count, 2):
-        base = (me ^ e) * beams_local
-        for tile in range(beams_local // SUBLANES):
-            start = pl.multiple_of(base + tile * SUBLANES, SUBLANES)
-            wr = w_ref[0, pl.ds(start, SUBLANES), :]
-            wi = w_ref[1, pl.ds(start, SUBLANES), :]
-            wr_s = pltpu.roll(wr, half, 0)
-            wi_s = pltpu.roll(wi, half, 0)
-            first = [jnp.where(top, wr, wi_s), jnp.where(top, -wi, wr_s)]
-            second = [jnp.where(top, wr_s, wi), jnp.where(top, -wi_s, wr)]
-            rows.append(jnp.concatenate(first, 1))
-            rows.append(jnp.concatenate(second, 1))
-    weights = jnp.concatenate(rows, 0)
-    out_ref[...] = dot_split(halves(weights), halves(s_ref[...]))
-
-
-def beam_call(steering, survey, parity, chan_count, beams_local):
+    for parity in range(2):
+        for e in range(parity, chan_count, 2):
+            base = (me ^ e) * beams_local
+            for tile in range(beams_local // SUBLANES):
+                start = pl.multiple_of(base + tile * SUBLANES, SUBLANES)
+                wr = w_ref[0, pl.ds(start, SUBLANES), :]
+                wi = w_ref[1, pl.ds(start, SUBLANES), :]
+                wr_s = pltpu.roll(wr, half, 0)
+                wi_s = pltpu.roll(wi, half, 0)
+                first = [jnp.where(top, wr, wi_s), jnp.where(top, -wi, wr_s)]
+                second = [jnp.where(top, wr_s, wi), jnp.where(top, -wi_s, wr)]
+                rows.append(jnp.concatenate(first, 1))
+                rows.append(jnp.concatenate(second, 1))
+    weights = halves(jnp.concatenate(rows, 0))
+    mid = weights[0].shape[0] // 2
+    for n in range(CHUNKS):
+        cols = slice(n * width, (n + 1) * width)
+        s_copies[n].wait()
+        product = dot_split(weights, halves(s_ref[:, cols]))
+        kept_ref[:, cols] = product[:mid]
+        sent_ref[:, cols] = product[mid:]
+    for copy in ref_copies:
+        copy.wait()
+
+
+def beam_call(steering, survey, ref, owners, chan_count, beams_local):
     depth, length = survey.shape
     rows = chan_count * beams_local
-    steps = 4
-    width = length // steps
+    out = jax.ShapeDtypeStruct((rows, length), jnp.float32)
+    hbm = pl.BlockSpec(memory_space=pltpu.HBM)
+    vmem = pl.BlockSpec(memory_space=pltpu.VMEM)
     return pl.pallas_call(
-        functools.partial(beam_kernel, parity, chan_count, beams_local),
-        grid=(steps,),
-        in_specs=[
-            pl.BlockSpec(steering.shape, lambda i: (0, 0, 0)),
-            pl.BlockSpec((depth, width), lambda i: (0, i)),
+        functools.partial(beam_kernel, chan_count, beams_local),
+        in_specs=[hbm, hbm, hbm],
+        out_specs=[vmem, vmem, hbm],
+        out_shape=[out, out, jax.ShapeDtypeStruct((owners,) + ref.shape, jnp.float32)],
+        scratch_shapes=[
+            pltpu.VMEM(steering.shape, jnp.float32),
+            pltpu.VMEM(survey.shape, jnp.float32),
+            pltpu.SemaphoreType.DMA,
+            pltpu.SemaphoreType.DMA((CHUNKS,)),
+            pltpu.SemaphoreType.DMA((owners,)),
         ],
-        out_specs=pl.BlockSpec((rows, width), lambda i: (0, i)),
-        out_shape=jax.ShapeDtypeStruct((rows, length), jnp.float32),
-        compiler_params=pltpu.CompilerParams(vmem_limit_bytes=60 * 1024 * 1024),
+        compiler_params=params(),
         cost_estimate=pl.CostEstimate(
-            flops=6 * rows * depth * length, bytes_accessed=4 * length * (depth + rows), transcendentals=0
+            flops=12 * rows * depth * length, bytes_accessed=4 * length * (depth + 2 * rows), transcendentals=0
         ),
-        name="beams_kept" if parity == 0 else "beams_sent",
-    )(steering, survey)
+        name="beams",
+    )(*(pltpu.with_memory_space_constraint(x, pltpu.HBM) for x in (steering, survey, ref)))
 
 
 def table_kernel(ref_ref, out_ref):
@@ -139,7 +171,14 @@
 
 
 def lag_kernel(groups, owners, *refs):
-    *y_refs, table_ref, out_ref = refs
+    *y_refs, table_ref, out_hbm, out_ref, out_sem = refs
+    copies = []
+
+    def send(first, count):
+        part = (slice(None), pl.ds(first, count))
+        copies.append(pltpu.make_async_copy(out_ref.at[part], out_hbm.at[part], out_sem.at[len(copies)]))
+        copies[-1].start()
+
     y = y_refs[0][...]
     for y_ref in y_refs[1:]:
         y = y + y_ref[...]
@@ -180,6 +219,8 @@
             tiles = [product[r : r + SUBLANES, lanes] for r in range(0, rows, SUBLANES)]
             for j, tile in enumerate(swap_groups(tiles, groups)):
                 out_ref[h * groups + j, q] = tile
+        if q % 2:
+            send(q - 1, 2)
     left = lax.broadcasted_iota(jnp.int32, (SUBLANES, LANES), 1) < TAPS
     for i in range(groups // 2):
         a = taps_sum[i * SUBLANES : (i + 1) * SUBLANES]
@@ -188,6 +229,9 @@
         tile = jnp.where(left, a, pltpu.roll(b, LANES - TAPS, 1))
         for owner in range(owners):
             out_ref[owner, blocks + i] = tile
+    send(blocks, groups // 2)
+    for copy in copies:
+        copy.wait()
 
 
 def lag_call(ys, table, groups, owners):
@@ -196,7 +240,10 @@
     shape = (owners, blocks + groups // 2, SUBLANES, LANES)
     return pl.pallas_call(
         functools.partial(lag_kernel, groups, owners),
+        in_specs=[pl.BlockSpec(memory_space=pltpu.VMEM)] * (len(ys) + 1),
+        out_specs=pl.BlockSpec(memory_space=pltpu.HBM),
         out_shape=jax.ShapeDtypeStruct(shape, jnp.float32),
+        scratch_shapes=[pltpu.VMEM(shape, jnp.float32), pltpu.SemaphoreType.DMA((blocks // 2 + 1,))],
         compiler_params=params(),
         cost_estimate=pl.CostEstimate(
             flops=12 * rows * LAGS * 2 * length,
@@ -353,7 +400,7 @@
     return (np.concatenate([upper, lower], 0) * scale).astype(np.float32)
 
 
-def map_kernel(groups, got_ref, mine_ref, other_ref, gram_ref, solver_ref, wave_ref, out_ref, held_ref):
+def map_kernel(groups, got_ref, mine_ref, other_ref, gram_ref, solver_ref, wave_ref, out_hbm, held_ref, out_ref, out_sem):
     owners, pieces = got_ref.shape[:2]
     blocks = pieces - groups // 2
     lags_local = LANES // groups
@@ -392,14 +439,18 @@
                     held_ref[here, :] = got_ref[at // blocks, at % blocks] - tile
     half = SUBLANES // 2
     wave = (wave_ref[0], wave_ref[1])
+    copies = []
     for g in range(half):
         parts = [held_ref[pl.ds(c * half + g, total, stride=SUBLANES), :] for c in range(2)]
         spectrum = dot_split(halves(jnp.concatenate(parts, 0).T), wave)
         for i in range(groups):
+            beam = half * i + g
             for c in range(2):
-                out_ref[half * i + g, c] = spectrum[
-                    i * lags_local : (i + 1) * lags_local, c * DOPPLER : (c + 1) * DOPPLER
-                ]
+                out_ref[beam, c] = spectrum[i * lags_local : (i + 1) * lags_local, c * DOPPLER : (c + 1) * DOPPLER]
+            copies.append(pltpu.make_async_copy(out_ref.at[beam], out_hbm.at[beam], out_sem.at[beam]))
+            copies[-1].start()
+    for copy in copies:
+        copy.wait()
 
 
 def map_call(got, mine, other, gram, solver, wave, groups, beams_local):
@@ -408,8 +459,14 @@
     shape = (beams_local, 2, lags_local, DOPPLER)
     return pl.pallas_call(
         functools.partial(map_kernel, groups),
+        in_specs=[pl.BlockSpec(memory_space=pltpu.VMEM)] * 6,
+        out_specs=pl.BlockSpec(memory_space=pltpu.HBM),
         out_shape=jax.ShapeDtypeStruct(shape, jnp.float32),
-        scratch_shapes=[pltpu.VMEM((total * SUBLANES, LANES), jnp.float32)],
+        scratch_shapes=[
+            pltpu.VMEM((total * SUBLANES, LANES), jnp.float32),
+            pltpu.VMEM(shape, jnp.float32),
+            pltpu.SemaphoreType.DMA((beams_local,)),
+        ],
         compiler_params=params(),
         cost_estimate=pl.CostEstimate(
             flops=12 * math.prod(shape) * total, bytes_accessed=4 * math.prod(shape), transcendentals=0
@@ -431,26 +488,24 @@
     groups = LANES // lags_local
     samples = length * tm_count
 
-    ref_all = lax.all_to_all(
-        jnp.broadcast_to(ref_signal[None], (tm_count,) + ref_signal.shape), "tm", 0, 0, tiled=True
-    )
     survey = surveillance.reshape(2 * channels, length)
-    rows = 2 * beams_local
-    shape = (chan_count // 2, rows, length)
-    moved = swap(beam_call(steering, survey, 1, chan_count, beams_local), "chan", 1)
-    parts = [beam_call(steering, survey, 0, chan_count, beams_local).reshape(shape), moved.reshape(shape)]
+    kept, moved, spread = beam_call(steering, survey, ref_signal, tm_count, chan_count, beams_local)
+    shape = (chan_count // 2, 2 * beams_local, length)
+    parts = [kept.reshape(shape), swap(moved, "chan", 1).reshape(shape)]
     by = 2
     while by < chan_count:
         sent = parts[0][1::2]
         for part in parts[1:]:
             sent = sent + part[1::2]
-        ref_all, sent = lax.optimization_barrier((ref_all, sent))
+        spread, sent = lax.optimization_barrier((spread, sent))
         parts = [part[::2] for part in parts] + [swap(sent, "chan", by)]
         by *= 2
-    mine, tail = own_call(ref_all, lags_local)
+    ref_all = lax.all_to_all(spread, "tm", 0, 0, tiled=True)
     table = table_call(ref_all)
     pieces = lag_call([part[0] for part in parts], table, groups, tm_count)
+    ref_all, pieces = lax.optimization_barrier((ref_all, pieces))
     got = lax.all_to_all(pieces, "tm", 0, 0, tiled=True)
+    mine, tail = own_call(ref_all, lags_local)
     other = swap(mine, "chan", 1)
     gram, solver = solver_call(mine, other, tail)
     wave = doppler_table(samples // BLOCK_LEN, 0.125 / math.sqrt(samples))

time: 47.4 us -> 45.8 us (0.966)
  blocking collectives: 0 us -> 13 us
  starting transfers between devices: 13.1 us -> 6.96 us
  Pallas kernels: 20.2 us -> 14.9 us
  local copies, waits for them, and re-layouts: 1.4 us -> 0.01 us
  other arithmetic: 1.09 us -> 0.06 us
    all_to_all x0 -> x1, blocking collectives: none -> 13 us  [tiled_device(): ref_all = lax.all_to_all(spread, 'tm', 0, 0, tiled=True)]
    all_to_all x1 -> x0, starting transfers between devices: 6.83 us -> none  [tiled_device(): lax.all_to_all(jnp.broadcast_to(ref_signal[None], (tm_count,) + ref_signa...]
    pallas_call x4 -> x3, Pallas kernels: 12.6 us -> 7.27 us  [the longest x1 2.78 us: map_call(): pl.pallas_call(functools.partial(map_kernel, groups), in_specs=[pl.BlockS...]
    all_to_all x1 -> x0, waiting for transfers between devices: 2.74 us -> none  [tiled_device(): lax.all_to_all(jnp.broadcast_to(ref_signal[None], (tm_count,) + ref_signa...]
    ppermute x3, waiting for transfers between devices: 0.01 us -> 1.54 us  [swap(): return lax.ppermute(x, axis, pairs)]
    ppermute x3, starting transfers between devices: 2.01 us -> 3.51 us  [swap(): return lax.ppermute(x, axis, pairs)]
    broadcast_in_dim x1 -> x0, local copies, waits for them, and re-layouts: 1.39 us -> none  [tiled_device(): jnp.broadcast_to(ref_signal[None], (tm_count,) + ref_signal.shape)]
    add x1 -> x0, other arithmetic: 1.09 us -> none  [tiled_device(): sent = sent + part[1::2]]
  transfers between devices with their start and end apart: 5 -> 4, of which waited for: 2 -> 2; matrix products, arithmetic and copies ran while one was open for 5% -> 0% of each run, Pallas kernels for 29% -> 6%
where the time goes in v4:
time: 45.8 us; the launch traced here: 45.6 us
  Pallas kernels  14.9 us (33%)
  blocking collectives  13 us (28%)
  waiting for transfers between devices  10.6 us (23%)
  starting transfers between devices  6.96 us (15%)
    all_to_all x1, blocking collectives, tiled_device(): ref_all = lax.all_to_all(spread, 'tm', 0, 0, tiled=True)  13 us
    all_to_all x1, waiting for transfers between devices, tiled_device(): got = lax.all_to_all(pieces, 'tm', 0, 0, tiled=True)  9.06 us
    pallas_call x1, Pallas kernels, own_call(): pl.pallas_call(functools.partial(own_kernel, lags_local), out_shape=[jax....  4.88 us
    ppermute x3, starting transfers between devices, swap(): return lax.ppermute(x, axis, pairs)  3.51 us
    all_to_all x1, starting transfers between devices, tiled_device(): got = lax.all_to_all(pieces, 'tm', 0, 0, tiled=True)  3.45 us
    pallas_call x1, Pallas kernels, map_call(): pl.pallas_call(functools.partial(map_kernel, groups), in_specs=[pl.BlockS...  2.78 us
    pallas_call x1, Pallas kernels, beam_call(): pl.pallas_call(functools.partial(beam_kernel, chan_count, beams_local), i...  2.33 us
    pallas_call x1, Pallas kernels, lag_call(): pl.pallas_call(functools.partial(lag_kernel, groups, owners), in_specs=[p...  2.16 us
  transfers between devices with their start and end apart: 4, of which 2 were waited for; matrix products, arithmetic and copies ran while one was open for 0% of the time, Pallas kernels for 6%

profile of v4, /device:TPU:0, one launch (start us, length us, event | category | flops | bytes accessed | tf_op | source)
XLA Modules:
  0.0 45.6 jit_solution(11851352637076231755)
XLA Ops:
  0.0 2.3 %beams.1 = (f32[64,2048]{1,0:T(8,128)S(1)}, f32[64,2048]{1,0:T(8,128)S(1)}, f32[8,2,2048]{2,1,0:T(2,128)S(1)}) custom-call(f32[2,64,64]{2,1,0:T(8,128)} %w_hbm.1, f32[128,2048]{1,0:T(8,128)} %bitcast.5, f32[2,2048]{1,0:T(2,128)} %ref_hbm.1), custom_call_target="tpu_custom_call" | custom-call | flops 201326592 | bytes 2097152 | tf_op jit(solution)/shard_map/beams/pallas_call | solution.py:127
  2.3 0.5 %collective-permute-start = (f32[64,2048]{1,0:T(8,128)S(1)}, f32[64,2048]{1,0:T(8,128)S(1)}, u32[]{:S(2)}, u32[]{:S(2)}) collective-permute-start(f32[64,2048]{1,0:T(8,128)S(1)} %get-tuple-element.18), channel_id=1, source_target_pairs={{0,8},{8,0},{16,24},{24,16},{1,9},{9,1},{17,25},{25,17},{2,10},{10... | collective-permute-start | bytes 1572872 | tf_op jit(solution)/shard_map/ppermute | solution.py:480
  2.9 1.5 %collective-permute-done = f32[64,2048]{1,0:T(8,128)S(1)} collective-permute-done((f32[64,2048]{1,0:T(8,128)S(1)}, f32[64,2048]{1,0:T(8,128)S(1)}, u32[]{:S(2)}, u32[]{:S(2)}) %collective-permute-start) | collective-permute-done | bytes 524320 | tf_op jit(solution)/shard_map/ppermute | solution.py:480
  4.4 0.1 fusion.1
  4.5 2.9 %collective-permute-start.1 = (f32[1,32,2048]{2,1,0:T(8,128)S(1)}, f32[1,32,2048]{2,1,0:T(8,128)S(1)}, u32[]{:S(2)}, u32[]{:S(2)}) collective-permute-start(f32[1,32,2048]{2,1,0:T(8,128)S(1)} %get-tuple-element.20), channel_id=1, source_target_pairs={{0,16},{8,24},{16,0},{24,8},{1,17},{9,25},{17,1},{25,9},{2,18},{10... | collective-permute-start | bytes 786440 | tf_op jit(solution)/shard_map/ppermute | solution.py:480
  7.4 13.0 %all_to_all.10.ref_ref = f32[8,2,2048]{2,1,0:T(2,128)S(1)} all-to-all(f32[8,2,2048]{2,1,0:T(2,128)S(1)} %get-tuple-element.19), channel_id=1, replica_groups=mesh['chan'=4,'tm'=8] {'tm'}, dimensions={0} | all-to-all | bytes 262144 | tf_op jit(solution)/shard_map/all_to_all | solution.py:503
  20.4 0.7 %shifted_reference.1.refs_3_ = bf16[2,2,128,2176]{3,2,1,0:T(8,128)(2,1)S(1)} custom-call(f32[8,2,2048]{2,1,0:T(2,128)S(1)} %all_to_all.10.ref_ref), custom_call_target="tpu_custom_call" | custom-call | flops 8912896 | bytes 2228224 | tf_op jit(solution)/shard_map/shifted_reference/pallas_call | solution.py:162
  21.0 0.0 collective-permute-done.1
  21.1 2.2 %lag_products.1 = f32[8,10,8,128]{3,2,1,0:T(8,128)} custom-call(f32[32,2048]{1,0:T(8,128)S(1)} %get-tuple-element.29.refs_0_, f32[32,2048]{1,0:T(8,128)S(1)} %get-tuple-element.27.refs_1_, f32[32,2048]{1,0:T(8,128)S(1)} %bitcast.4, bf16[2,2,128,2176]{3,2,1,0:T(8,128)(2,1)S(1)} %shifted_reference.1.refs_3_), custom_call_target="tpu_custom_call" | custom-call | flops 402653184 | bytes 2555904 | tf_op jit(solution)/shard_map/lag_products/pallas_call | solution.py:241
  23.2 0.0 copy-start
  23.2 4.9 %reference_products.1 = (f32[1032,128]{1,0:T(8,128)S(1)}, f32[128,128]{1,0:T(8,128)S(1)}) custom-call(f32[8,2,2048]{2,1,0:T(2,128)S(1)} %all_to_all.10.ref_ref), custom_call_target="tpu_custom_call" | custom-call | flops 805306368 | bytes 524288 | tf_op jit(solution)/shard_map/reference_products/pallas_call | solution.py:313
  28.1 0.1 collective-permute-start.2
  28.2 3.4 %all-to-all-start.1 = ((f32[8,10,8,128]{3,2,1,0:T(8,128)}), f32[8,10,8,128]{3,2,1,0:T(8,128)S(1)}, u32[]{:S(2)}, u32[]{:S(2)}) async-start(f32[8,10,8,128]{3,2,1,0:T(8,128)} %lag_products.1), calls=%async_computation.1 | async-start | bytes 655360 | tf_op jit(solution)/shard_map/all_to_all | solution.py:507
  31.7 0.0 collective-permute-done.2.other_ref
  31.7 2.0 %gram_inverse.1 = (f32[128,128]{1,0:T(8,128)S(1)}, f32[128,128]{1,0:T(8,128)S(1)}) custom-call(f32[1032,128]{1,0:T(8,128)S(1)} %get-tuple-element.23.mine_ref, f32[1032,128]{1,0:T(8,128)S(1)} %collective-permute-done.2.other_ref, f32[128,128]{1,0:T(8,128)S(1)} %get-tuple-element.24.tail_ref), custom_call_target="tpu_custom_call" | custom-call | flops 500000000 | bytes 200000 | tf_op jit(solution)/shard_map/gram_inverse/pallas_call | solution.py:383
  33.7 9.1 %all-to-all-done.1.got_ref = f32[8,10,8,128]{3,2,1,0:T(8,128)S(1)} async-done(((f32[8,10,8,128]{3,2,1,0:T(8,128)}), f32[8,10,8,128]{3,2,1,0:T(8,128)S(1)}, u32[]{:S(2)}, u32[]{:S(2)}) %all-to-all-start.1) | async-done | bytes 327712 | tf_op jit(solution)/shard_map/all_to_all | solution.py:507
  42.8 0.0 copy-done
  42.8 2.8 %range_doppler.1 = f32[16,2,32,256]{3,2,1,0:T(8,128)} custom-call(f32[8,10,8,128]{3,2,1,0:T(8,128)S(1)} %all-to-all-done.1.got_ref, f32[1032,128]{1,0:T(8,128)S(1)} %get-tuple-element.23.mine_ref, f32[1032,128]{1,0:T(8,128)S(1)} %collective-permute-done.2.other_ref, f32[128,128]{1,0:T(8,128)S(1)} %get-tuple-element.25.gram_ref, ...), custom_call_target="tpu_custom_call" | custom-call | flops 201326592 | bytes 1048576 | tf_op jit(solution)/shard_map/range_doppler/pallas_call | solution.py:460
Async XLA Ops:
  2.3 2.1 %collective-permute-start = (f32[64,2048]{1,0:T(8,128)S(1)}, f32[64,2048]{1,0:T(8,128)S(1)}, u32[]{:S(2)}, u32[]{:S(2)}) collective-permute-start(f32[64,2048]{1,0:T(8,128)S(1)} %get-tuple-element.18), channel_id=1, source_target_pairs={{0,8},{8,0},{16,24},{24,16},{1,9},{9,1},{17,25},{25,17},{2,10},{10... | collective-permute-start | bytes 1572872 | tf_op jit(solution)/shard_map/ppermute | solution.py:480
  4.5 16.6 %collective-permute-start.1 = (f32[1,32,2048]{2,1,0:T(8,128)S(1)}, f32[1,32,2048]{2,1,0:T(8,128)S(1)}, u32[]{:S(2)}, u32[]{:S(2)}) collective-permute-start(f32[1,32,2048]{2,1,0:T(8,128)S(1)} %get-tuple-element.20), channel_id=1, source_target_pairs={{0,16},{8,24},{16,0},{24,8},{1,17},{9,25},{17,1},{25,9},{2,18},{10... | collective-permute-start | bytes 786440 | tf_op jit(solution)/shard_map/ppermute | solution.py:480
  23.2 19.6 %copy-start = (bf16[2,128,512]{2,1,0:T(8,128)(2,1)S(1)}, bf16[2,128,512]{2,1,0:T(8,128)(2,1)}, u32[]{:S(2)}) copy-start(bf16[2,128,512]{2,1,0:T(8,128)(2,1)} %constant.2.clone.wave_ref) | copy-start | bytes 786436
  28.1 3.5 %collective-permute-start.2 = (f32[1032,128]{1,0:T(8,128)S(1)}, f32[1032,128]{1,0:T(8,128)S(1)}, u32[]{:S(2)}, u32[]{:S(2)}) collective-permute-start(f32[1032,128]{1,0:T(8,128)S(1)} %get-tuple-element.23.mine_ref), channel_id=1, source_target_pairs={{0,8},{8,0},{16,24},{24,16},{1,9},{9,1},{17,25},{25,17},{2,10},{10... | collective-permute-start | bytes 1585160 | tf_op jit(solution)/shard_map/ppermute | solution.py:480
  28.2 14.6 %all-to-all-start.1 = ((f32[8,10,8,128]{3,2,1,0:T(8,128)}), f32[8,10,8,128]{3,2,1,0:T(8,128)S(1)}, u32[]{:S(2)}, u32[]{:S(2)}) async-start(f32[8,10,8,128]{3,2,1,0:T(8,128)} %lag_products.1), calls=%async_computation.1 | async-start | bytes 655360 | tf_op jit(solution)/shard_map/all_to_all | solution.py:507

commit v5 on v4

--- a/solution.py
+++ b/solution.py
@@ -72,7 +72,7 @@
 
 
 def beam_kernel(
-    chan_count, beams_local, w_hbm, s_hbm, ref_hbm, kept_ref, sent_ref, spread_hbm, w_ref, s_ref, w_sem, s_sem, ref_sem
+    chan_count, beams_local, w_hbm, s_hbm, ref_hbm, kept_ref, sent_ref, tiles_ref, w_ref, s_ref, ref_ref, w_sem, s_sem, ref_sem
 ):
     me = lax.axis_index("chan")
     depth, length = s_hbm.shape
@@ -84,10 +84,8 @@
         cols = pl.ds(n * width, width)
         s_copies.append(pltpu.make_async_copy(s_hbm.at[:, cols], s_ref.at[:, cols], s_sem.at[n]))
         s_copies[n].start()
-    ref_copies = []
-    for n in range(spread_hbm.shape[0]):
-        ref_copies.append(pltpu.make_async_copy(ref_hbm, spread_hbm.at[n], ref_sem.at[n]))
-        ref_copies[n].start()
+    ref_copy = pltpu.make_async_copy(ref_hbm, ref_ref, ref_sem)
+    ref_copy.start()
     half = SUBLANES // 2
     sub = lax.broadcasted_iota(jnp.int32, (SUBLANES, w_hbm.shape[2]), 0)
     top = sub < half
@@ -114,11 +112,13 @@
         product = dot_split(weights, halves(s_ref[:, cols]))
         kept_ref[:, cols] = product[:mid]
         sent_ref[:, cols] = product[mid:]
-    for copy in ref_copies:
-        copy.wait()
-
-
-def beam_call(steering, survey, ref, owners, chan_count, beams_local):
+    ref_copy.wait()
+    for c in range(2):
+        for n in range(length // LANES):
+            tiles_ref[0, c, n : n + 1, :] = ref_ref[c : c + 1, n * LANES : (n + 1) * LANES]
+
+
+def beam_call(steering, survey, ref, chan_count, beams_local):
     depth, length = survey.shape
     rows = chan_count * beams_local
     out = jax.ShapeDtypeStruct((rows, length), jnp.float32)
@@ -127,14 +127,15 @@
     return pl.pallas_call(
         functools.partial(beam_kernel, chan_count, beams_local),
         in_specs=[hbm, hbm, hbm],
-        out_specs=[vmem, vmem, hbm],
-        out_shape=[out, out, jax.ShapeDtypeStruct((owners,) + ref.shape, jnp.float32)],
+        out_specs=[vmem, vmem, vmem],
+        out_shape=[out, out, jax.ShapeDtypeStruct((1, 2, length // LANES, LANES), jnp.float32)],
         scratch_shapes=[
             pltpu.VMEM(steering.shape, jnp.float32),
             pltpu.VMEM(survey.shape, jnp.float32),
+            pltpu.VMEM(ref.shape, jnp.float32),
             pltpu.SemaphoreType.DMA,
             pltpu.SemaphoreType.DMA((CHUNKS,)),
-            pltpu.SemaphoreType.DMA((owners,)),
+            pltpu.SemaphoreType.DMA,
         ],
         compiler_params=params(),
         cost_estimate=pl.CostEstimate(
@@ -144,21 +145,27 @@
     )(*(pltpu.with_memory_space_constraint(x, pltpu.HBM) for x in (steering, survey, ref)))
 
 
-def table_kernel(ref_ref, out_ref):
+def table_kernel(*refs):
+    *part_refs, out_ref = refs
     me = lax.axis_index("tm")
-    edge = ref_ref[jnp.maximum(me - 1, 0), :, ref_ref.shape[2] - 2 * LANES :]
-    edge = jnp.where(me > 0, edge, jnp.zeros_like(edge))
-    span = jnp.concatenate([edge, ref_ref[me]], 1)
+    own = part_refs[0][0]
+    rows = own.shape[1]
+    edge = jnp.zeros((2, 2, LANES), jnp.float32)
+    for n, part_ref in enumerate(part_refs[1:], 1):
+        last = part_ref[part_ref.shape[0] - 1, :, rows - 2 :, :]
+        edge = jnp.where((me > 0) & ((me ^ (me - 1)) == 2**n - 1), last, edge)
     for c in range(2):
-        tiled = jnp.broadcast_to(span[c : c + 1], (LANES, span.shape[1]))
-        shifted = pltpu.roll(tiled, 0, 1, stride=1, stride_axis=0)[:, LANES:]
-        high, low = halves(shifted)
-        out_ref[0, c] = high
-        out_ref[1, c] = low
-
-
-def table_call(ref_all):
-    shape = (2, 2, LANES, LANES + ref_all.shape[2])
+        line = [edge[c, n : n + 1] for n in range(2)] + [own[c, n : n + 1] for n in range(rows)]
+        line = jnp.concatenate(line, 1)
+        for g in range(0, LANES, 2 * SUBLANES):
+            tiled = jnp.broadcast_to(line, (2 * SUBLANES, line.shape[1]))
+            high, low = halves(pltpu.roll(tiled, g, 1, stride=1, stride_axis=0)[:, LANES:])
+            out_ref[0, c, g : g + 2 * SUBLANES] = high
+            out_ref[1, c, g : g + 2 * SUBLANES] = low
+
+
+def table_call(parts):
+    shape = (2, 2, LANES, LANES * (parts[0].shape[2] + 1))
     return pl.pallas_call(
         table_kernel,
         out_shape=jax.ShapeDtypeStruct(shape, jnp.bfloat16),
@@ -167,7 +174,7 @@
             flops=8 * math.prod(shape), bytes_accessed=2 * math.prod(shape), transcendentals=0
         ),
         name="shifted_reference",
-    )(ref_all)
+    )(*parts)
 
 
 def lag_kernel(groups, owners, *refs):
@@ -254,83 +261,126 @@
     )(*ys, table)
 
 
-SHARES = 2
 BATCH = 4
-
-
-def own_kernel(lags_local, ref_ref, out_ref, tail_ref, span_ref, late_ref):
+EDGE = 2
+
+
+def own_kernel(lags_local, *refs):
+    *part_refs, out_ref, line_ref, tail_ref, span_ref, late_ref, taps_a, lags_a, taps_b, lags_b = refs
     me = lax.axis_index("tm")
-    owners, _, length = ref_ref.shape
-    samples = owners * length
-    blocks = samples // BLOCK_LEN // SHARES
-    first_block = lax.rem(lax.axis_index("chan"), SHARES) * blocks
-    span_ref[:, :BLOCK_LEN] = jnp.zeros((2, BLOCK_LEN), jnp.float32)
-    span_ref[:, BLOCK_LEN + samples :] = jnp.zeros((2, BLOCK_LEN), jnp.float32)
-    for t in range(owners):
-        span_ref[:, BLOCK_LEN + t * length : BLOCK_LEN + (t + 1) * length] = ref_ref[t]
-    late_ref[...] = pltpu.roll(span_ref[...], me * lags_local, 1)
-
-    def shifted(window, count):
-        tiled = jnp.broadcast_to(window, (count, window.shape[1]))
-        return pltpu.roll(tiled, 0, 1, stride=1, stride_axis=0)[:, LANES:]
-
-    def pair_of(window, count):
-        return jnp.concatenate([shifted(window[c : c + 1], count) for c in range(2)], 0)
+    part_rows = part_refs[0].shape[2]
+    owners = sum(part_ref.shape[0] for part_ref in part_refs)
+    samples = owners * part_rows * LANES
+    steps = samples // BLOCK_LEN // BATCH
+    total_rows = span_ref.shape[1]
+    block_rows = BLOCK_LEN // LANES
+
+    span_ref[...] = jnp.zeros_like(span_ref)
+    e = 0
+    for part_ref in part_refs:
+        for i in range(part_ref.shape[0]):
+            span_ref[:, pl.ds(EDGE + (me ^ e) * part_rows, part_rows), :] = part_ref[i]
+            e += 1
+    late_rows = (me * lags_local) // LANES
+    late_lanes = lax.rem(me * lags_local, LANES)
+    turned = [pltpu.roll(span_ref[c], late_lanes, 1) for c in range(2)]
+    before = [pltpu.roll(x, 1, 0) for x in turned]
+    lanes = lax.broadcasted_iota(jnp.int32, (total_rows, LANES), 1)
+    for c in range(2):
+        late_ref[c] = pltpu.roll(jnp.where(lanes < late_lanes, before[c], turned[c]), late_rows, 0)
+
+    def line_of(ref, c, first, count):
+        return jnp.concatenate([ref[c, pl.ds(first + n, 1), :] for n in range(count)], 1)
+
+    def shifted(line, by):
+        tiled = jnp.broadcast_to(line, (2 * SUBLANES, line.shape[1]))
+        return pltpu.roll(tiled, by, 1, stride=1, stride_axis=0)[:, LANES:]
+
+    def keep(ref, row, value):
+        high, low = halves(value)
+        half = ref.shape[0] // 2
+        ref[row : row + 2 * SUBLANES, :] = high
+        ref[half + row : half + row + 2 * SUBLANES, :] = low
+
+    def build(n, taps_ref, lags_ref):
+        first = EDGE - 1 + n * BATCH * block_rows
+        count = BATCH * block_rows + 1
+        lines = [line_of(span_ref, c, first, count) for c in range(2)]
+        for c in range(2):
+            for g in range(0, TAPS, 2 * SUBLANES):
+                keep(taps_ref, c * TAPS + g, shifted(lines[c], g))
+            late = line_of(late_ref, c, first, count)
+            for g in range(0, lags_local, 2 * SUBLANES):
+                keep(lags_ref, c * lags_local + g, shifted(late, g))
+        pad = jnp.zeros((2 * SUBLANES - 2, BATCH * BLOCK_LEN), jnp.float32)
+        keep(lags_ref, 2 * lags_local, jnp.concatenate([line[:, LANES:] for line in lines] + [pad], 0))
 
     turn = lane_sign((lags_local, LANES))
 
-    def step(n, total):
-        start = pl.multiple_of((first_block + n * BATCH) * BLOCK_LEN, BLOCK_LEN) + BLOCK_LEN - LANES
-        lanes = pl.ds(pl.multiple_of(start, LANES), BATCH * BLOCK_LEN + LANES)
-        window, late = span_ref[:, lanes], late_ref[:, lanes]
-        taps_high, taps_low = halves(pair_of(window, TAPS))
-        pad = jnp.zeros((2 * SUBLANES - 2, BATCH * BLOCK_LEN), jnp.float32)
-        lag_rows = jnp.concatenate([pair_of(late, lags_local), window[:, LANES:], pad], 0)
-        lags_high, lags_low = halves(lag_rows)
-        taps = jnp.concatenate([taps_high, taps_low], 0)
-        lags = jnp.concatenate([lags_high, lags_low], 0)
-        count = lag_rows.shape[0]
+    def use(n, taps_ref, lags_ref):
+        count = lags_ref.shape[0] // 2
         for b in range(BATCH):
             cols = slice(b * BLOCK_LEN, (b + 1) * BLOCK_LEN)
-            product = dot_nt(lags[:, cols], taps[:, cols])
+            product = dot_nt(lags_ref[:, cols], taps_ref[:, cols])
             product = product[:count, :LANES] + (product[:count, LANES:] + product[count:, :LANES])
             by_real = product[:lags_local]
             by_imag = product[lags_local : 2 * lags_local]
             rows = pl.ds(pl.multiple_of((n * BATCH + b) * lags_local, lags_local), lags_local)
-            out_ref[rows, :] = by_real + turn * pltpu.roll(by_imag, TAPS, 1)
-            total = total + product[2 * lags_local : 2 * lags_local + SUBLANES]
-        return total
-
-    total = lax.fori_loop(0, blocks // BATCH, step, jnp.zeros((SUBLANES, LANES), jnp.float32))
-    out_ref[blocks * lags_local :, :] = total
-    tail = pair_of(span_ref[:, samples + BLOCK_LEN - LANES :], TAPS)
+            high, low = halves(by_real + turn * pltpu.roll(by_imag, TAPS, 1))
+            out_ref[0, rows, :] = high
+            out_ref[1, rows, :] = low
+            line_ref[...] += product[2 * lags_local : 2 * lags_local + SUBLANES]
+
+    line_ref[...] = jnp.zeros_like(line_ref)
+    build(0, taps_a, lags_a)
+
+    def pair(m, carry):
+        build(2 * m + 1, taps_b, lags_b)
+        use(2 * m, taps_a, lags_a)
+        build(jnp.minimum(2 * m + 2, steps - 1), taps_a, lags_a)
+        use(2 * m + 1, taps_b, lags_b)
+        return carry
+
+    lax.fori_loop(0, steps // 2, pair, 0)
+    tail = []
+    for c in range(2):
+        line = line_of(span_ref, c, EDGE + owners * part_rows - 1, 2)
+        tail += [shifted(line, g) for g in range(0, TAPS, 2 * SUBLANES)]
+    tail = jnp.concatenate(tail, 0)
     tail_ref[...] = dot_nt(tail, tail, HIGHEST)
 
 
-def own_call(ref_all, lags_local):
-    samples = ref_all.shape[0] * ref_all.shape[2]
-    rows = samples // BLOCK_LEN // SHARES * lags_local
+def own_call(parts, lags_local):
+    part_rows = parts[0].shape[2]
+    span_rows = part_rows * sum(part.shape[0] for part in parts)
+    rows = span_rows * LANES // BLOCK_LEN * lags_local
+    held_rows = -(-(span_rows + 2 * EDGE) // SUBLANES) * SUBLANES
+    width = BATCH * BLOCK_LEN
+    taps = pltpu.VMEM((4 * TAPS, width), jnp.bfloat16)
+    lags = pltpu.VMEM((4 * lags_local + 4 * SUBLANES, width), jnp.bfloat16)
+    span = pltpu.VMEM((2, held_rows, LANES), jnp.float32)
     return pl.pallas_call(
         functools.partial(own_kernel, lags_local),
         out_shape=[
-            jax.ShapeDtypeStruct((rows + SUBLANES, 2 * TAPS), jnp.float32),
+            jax.ShapeDtypeStruct((2, rows, 2 * TAPS), jnp.bfloat16),
+            jax.ShapeDtypeStruct((SUBLANES, 2 * TAPS), jnp.float32),
             jax.ShapeDtypeStruct((2 * TAPS, 2 * TAPS), jnp.float32),
         ],
-        scratch_shapes=[pltpu.VMEM((2, samples + 2 * BLOCK_LEN), jnp.float32)] * 2,
+        scratch_shapes=[span, span, taps, lags, taps, lags],
         compiler_params=params(),
         cost_estimate=pl.CostEstimate(
             flops=24 * rows * BLOCK_LEN * 2 * TAPS, bytes_accessed=4 * rows * 2 * TAPS, transcendentals=0
         ),
         name="reference_products",
-    )(ref_all)
+    )(*parts)
 
 
 def as_factor(a):
     return jnp.concatenate([a, -lane_sign(a.shape) * pltpu.roll(a, a.shape[0], 1)], 0)
 
 
-def solver_kernel(mine_ref, other_ref, tail_ref, gram_ref, solver_ref):
-    total = mine_ref[...] + other_ref[...]
+def solver_kernel(line_ref, tail_ref, gram_ref, solver_ref):
+    total = line_ref[...]
     line = total[0:1] + lane_sign((1, LANES)) * pltpu.roll(total[1:2], TAPS, 1)
     low = lax.broadcasted_iota(jnp.int32, (1, LANES), 1) < TAPS
     line_r = jnp.where(low, line, 0.0)
@@ -351,9 +401,8 @@
     gram_r = strict_r + strict_r.T + diag_r - (tails[:TAPS, :TAPS] + tails[TAPS:, TAPS:])
     gram_i = up_i - up_i.T - (tails[:TAPS, TAPS:] - tails[TAPS:, :TAPS])
     gram = jnp.concatenate([gram_r, gram_i], 1)
-    gram_factor = as_factor(gram)
-    gram_ref[...] = gram_factor
-    gram_halves = halves(gram_factor)
+    gram_halves = halves(as_factor(gram))
+    gram_ref[0], gram_ref[1] = gram_halves
     one = (
         lax.broadcasted_iota(jnp.int32, gram.shape, 0) == lax.broadcasted_iota(jnp.int32, gram.shape, 1)
     ).astype(jnp.float32)
@@ -373,23 +422,18 @@
 
     start = (jnp.int32(0), jnp.float32(1.0), one * (1.0 / bound))
     _, _, inverse = lax.while_loop(again, newton, start)
-    solver_ref[...] = as_factor(inverse)
-
-
-def solver_call(mine, other, tail):
-    last = mine.shape[0] // SUBLANES - 1
-    line = pl.BlockSpec((SUBLANES, LANES), lambda i: (last, 0))
-    whole = pl.BlockSpec(tail.shape, lambda i: (0, 0))
+    solver_ref[0], solver_ref[1] = halves(as_factor(inverse))
+
+
+def solver_call(line, tail):
+    out = jax.ShapeDtypeStruct((2,) + tail.shape, jnp.bfloat16)
     return pl.pallas_call(
         solver_kernel,
-        grid=(1,),
-        in_specs=[line, line, whole],
-        out_specs=[whole, whole],
-        out_shape=[jax.ShapeDtypeStruct(tail.shape, jnp.float32)] * 2,
+        out_shape=[out, out],
         compiler_params=params(),
         cost_estimate=pl.CostEstimate(flops=500_000_000, bytes_accessed=200_000, transcendentals=0),
         name="gram_inverse",
-    )(mine, other, tail)
+    )(line, tail)
 
 
 def doppler_table(block_count, scale):
@@ -400,7 +444,7 @@
     return (np.concatenate([upper, lower], 0) * scale).astype(np.float32)
 
 
-def map_kernel(groups, got_ref, mine_ref, other_ref, gram_ref, solver_ref, wave_ref, out_hbm, held_ref, out_ref, out_sem):
+def map_kernel(groups, got_ref, own_ref, gram_ref, solver_ref, wave_ref, out_hbm, held_ref, out_ref, out_sem):
     owners, pieces = got_ref.shape[:2]
     blocks = pieces - groups // 2
     lags_local = LANES // groups
@@ -417,26 +461,22 @@
             other = -sign * pltpu.roll(there, SUBLANES // 2, 0)
             rows[part] = jnp.where(left, here, other)
     cross = jnp.concatenate(rows, 0)
-    solver = solver_ref[...]
-    taps = jnp.dot(cross, solver, precision=HIGHEST, preferred_element_type=jnp.float32)
-    rest = cross - jnp.dot(taps, gram_ref[...], precision=HIGHEST, preferred_element_type=jnp.float32)
-    taps = taps + jnp.dot(rest, solver, precision=HIGHEST, preferred_element_type=jnp.float32)
+    solver = (solver_ref[0], solver_ref[1])
+    taps = dot_split(halves(cross), solver)
+    rest = cross - dot_split(halves(taps), (gram_ref[0], gram_ref[1]))
+    taps = taps + dot_split(halves(rest), solver)
     taps_high, taps_low = halves(taps)
     taps_both = jnp.concatenate([taps_high, taps_low], 1)
-    share = lax.rem(lax.axis_index("chan"), SHARES)
-    share_blocks = total // SHARES
-    for which, own_ref in enumerate((mine_ref, other_ref)):
-        first = (share ^ which) * share_blocks
-        for q in range(0, share_blocks, 2 * groups):
-            own_high, own_low = halves(own_ref[q * lags_local : (q + 2 * groups) * lags_local, :])
-            clutter = dot_nt(taps_both, jnp.concatenate([own_high, own_high], 1)) + dot_nt(taps_high, own_low)
-            for h in range(2):
-                lanes = slice(h * LANES, (h + 1) * LANES)
-                tiles = [clutter[r : r + SUBLANES, lanes] for r in range(0, groups * SUBLANES, SUBLANES)]
-                for j, tile in enumerate(swap_groups(tiles, groups)):
-                    at = first + q + h * groups + j
-                    here = pl.ds(pl.multiple_of(at * SUBLANES, SUBLANES), SUBLANES)
-                    held_ref[here, :] = got_ref[at // blocks, at % blocks] - tile
+    for q in range(0, total, 2 * groups):
+        own = slice(q * lags_local, (q + 2 * groups) * lags_local)
+        own_high = own_ref[0, own, :]
+        clutter = dot_nt(taps_both, jnp.concatenate([own_high, own_high], 1)) + dot_nt(taps_high, own_ref[1, own, :])
+        for h in range(2):
+            lanes = slice(h * LANES, (h + 1) * LANES)
+            tiles = [clutter[r : r + SUBLANES, lanes] for r in range(0, groups * SUBLANES, SUBLANES)]
+            for j, tile in enumerate(swap_groups(tiles, groups)):
+                at = q + h * groups + j
+                held_ref[at * SUBLANES : (at + 1) * SUBLANES, :] = got_ref[at // blocks, at % blocks] - tile
     half = SUBLANES // 2
     wave = (wave_ref[0], wave_ref[1])
     copies = []
@@ -453,13 +493,13 @@
         copy.wait()
 
 
-def map_call(got, mine, other, gram, solver, wave, groups, beams_local):
+def map_call(got, own, gram, solver, wave, groups, beams_local):
     total = got.shape[0] * (got.shape[1] - groups // 2)
     lags_local = LANES // groups
     shape = (beams_local, 2, lags_local, DOPPLER)
     return pl.pallas_call(
         functools.partial(map_kernel, groups),
-        in_specs=[pl.BlockSpec(memory_space=pltpu.VMEM)] * 6,
+        in_specs=[pl.BlockSpec(memory_space=pltpu.VMEM)] * 5,
         out_specs=pl.BlockSpec(memory_space=pltpu.HBM),
         out_shape=jax.ShapeDtypeStruct(shape, jnp.float32),
         scratch_shapes=[
@@ -472,7 +512,7 @@
             flops=12 * math.prod(shape) * total, bytes_accessed=4 * math.prod(shape), transcendentals=0
         ),
         name="range_doppler",
-    )(got, mine, other, gram, solver, wave)
+    )(got, own, gram, solver, wave)
 
 
 def swap(x, axis, by):
@@ -489,29 +529,32 @@
     samples = length * tm_count
 
     survey = surveillance.reshape(2 * channels, length)
-    kept, moved, spread = beam_call(steering, survey, ref_signal, tm_count, chan_count, beams_local)
+    kept, moved, tiles = beam_call(steering, survey, ref_signal, chan_count, beams_local)
     shape = (chan_count // 2, 2 * beams_local, length)
     parts = [kept.reshape(shape), swap(moved, "chan", 1).reshape(shape)]
+    near = swap(tiles, "tm", 1)
     by = 2
     while by < chan_count:
         sent = parts[0][1::2]
         for part in parts[1:]:
             sent = sent + part[1::2]
-        spread, sent = lax.optimization_barrier((spread, sent))
+        tiles, sent = lax.optimization_barrier((tiles, sent))
         parts = [part[::2] for part in parts] + [swap(sent, "chan", by)]
         by *= 2
-    ref_all = lax.all_to_all(spread, "tm", 0, 0, tiled=True)
-    table = table_call(ref_all)
+    ref_parts = [tiles, near]
+    by = 2
+    while by < tm_count:
+        ref_parts.append(swap(jnp.concatenate(ref_parts, 0), "tm", by))
+        by *= 2
+    table = table_call(ref_parts)
     pieces = lag_call([part[0] for part in parts], table, groups, tm_count)
-    ref_all, pieces = lax.optimization_barrier((ref_all, pieces))
     got = lax.all_to_all(pieces, "tm", 0, 0, tiled=True)
-    mine, tail = own_call(ref_all, lags_local)
-    other = swap(mine, "chan", 1)
-    gram, solver = solver_call(mine, other, tail)
+    own, line, tail = own_call(ref_parts, lags_local)
+    gram, solver = solver_call(line, tail)
     wave = doppler_table(samples // BLOCK_LEN, 0.125 / math.sqrt(samples))
     high = wave.astype(jnp.bfloat16)
     wave = np.stack([high, (wave - high.astype(np.float32)).astype(jnp.bfloat16)])
-    return map_call(got, mine, other, gram, solver, jnp.asarray(wave), groups, beams_local)
+    return map_call(got, own, gram, solver, jnp.asarray(wave), groups, beams_local)
 
 
 def lag_table(ref_ext, offset, lags):
@@ -589,9 +632,10 @@
         and beams_local * lags_local == LANES * SUBLANES // 2
         and chan_count > 1
         and chan_count & (chan_count - 1) == 0
+        and tm_count > 1
         and tm_count & (tm_count - 1) == 0
         and 2 * surveillance.shape[1] % LANES == 0
-        and surveillance.shape[2] % (4 * BLOCK_LEN) == 0
+        and surveillance.shape[2] % (2 * BATCH * BLOCK_LEN) == 0
     )
     device = tiled_device if fills else plain_device
     return device(ref_signal, surveillance, steering)

time: 45.8 us -> 37.2 us (0.81)
  blocking collectives: 13 us -> 0 us
  starting transfers between devices: 6.96 us -> 16.4 us
  waiting for transfers between devices: 10.6 us -> 4.72 us
  Pallas kernels: 14.9 us -> 15.8 us
    all_to_all x1 -> x0, blocking collectives: 13 us -> none  [tiled_device(): ref_all = lax.all_to_all(spread, 'tm', 0, 0, tiled=True)]
    all_to_all x1, waiting for transfers between devices: 9.06 us -> 0.35 us  [tiled_device(): got = lax.all_to_all(pieces, 'tm', 0, 0, tiled=True)]
    ppermute x3 -> x5, starting transfers between devices: 3.51 us -> 9.69 us  [swap(): return lax.ppermute(x, axis, pairs)]
    all_to_all x1, starting transfers between devices: 3.45 us -> 6.71 us  [tiled_device(): got = lax.all_to_all(pieces, 'tm', 0, 0, tiled=True)]
    ppermute x3 -> x5, waiting for transfers between devices: 1.54 us -> 4.37 us  [swap(): return lax.ppermute(x, axis, pairs)]
    pallas_call x1, Pallas kernels: 4.88 us -> 6.25 us  [own_call(): pl.pallas_call(functools.partial(own_kernel, lags_local), out_shape=[jax....]
  transfers between devices with their start and end apart: 4 -> 6, of which waited for: 2 -> 3; matrix products, arithmetic and copies ran while one was open for 0% -> 0% of each run, Pallas kernels for 6% -> 24%
where the time goes in v5:
time: 37.2 us; the launch traced here: 37 us
  starting transfers between devices  16.4 us (44%)
  Pallas kernels  15.8 us (42%)
  waiting for transfers between devices  4.72 us (13%)
    ppermute x5, starting transfers between devices, swap(): return lax.ppermute(x, axis, pairs)  9.69 us
    all_to_all x1, starting transfers between devices, tiled_device(): got = lax.all_to_all(pieces, 'tm', 0, 0, tiled=True)  6.71 us
    pallas_call x1, Pallas kernels, own_call(): pl.pallas_call(functools.partial(own_kernel, lags_local), out_shape=[jax....  6.25 us
    ppermute x5, waiting for transfers between devices, swap(): return lax.ppermute(x, axis, pairs)  4.37 us
    pallas_call x1, Pallas kernels, map_call(): pl.pallas_call(functools.partial(map_kernel, groups), in_specs=[pl.BlockS...  2.46 us
    pallas_call x1, Pallas kernels, beam_call(): pl.pallas_call(functools.partial(beam_kernel, chan_count, beams_local), i...  2.16 us
    pallas_call x1, Pallas kernels, lag_call(): pl.pallas_call(functools.partial(lag_kernel, groups, owners), in_specs=[p...  2.16 us
    pallas_call x1, Pallas kernels, solver_call(): pl.pallas_call(solver_kernel, out_shape=[out, out], compiler_params=param...  2.06 us
  transfers between devices with their start and end apart: 6, of which 3 were waited for; matrix products, arithmetic and copies ran while one was open for 0% of the time, Pallas kernels for 24%

profile of v5, /device:TPU:0, one launch (start us, length us, event | category | flops | bytes accessed | tf_op | source)
XLA Modules:
  0.0 37.0 jit_solution(17439625554389192182)
XLA Ops:
  0.0 2.2 %beams.1 = (f32[64,2048]{1,0:T(8,128)S(1)}, f32[64,2048]{1,0:T(8,128)S(1)}, f32[1,2,16,128]{3,2,1,0:T(8,128)S(1)}) custom-call(f32[2,64,64]{2,1,0:T(8,128)} %w_hbm.1, f32[128,2048]{1,0:T(8,128)} %bitcast.5, f32[2,2048]{1,0:T(2,128)} %ref_hbm.1), custom_call_target="tpu_custom_call" | custom-call | flops 201326592 | bytes 2097152 | tf_op jit(solution)/shard_map/beams/pallas_call | solution.py:127
  2.2 0.5 %collective-permute-start = (f32[64,2048]{1,0:T(8,128)S(1)}, f32[64,2048]{1,0:T(8,128)S(1)}, u32[]{:S(2)}, u32[]{:S(2)}) collective-permute-start(f32[64,2048]{1,0:T(8,128)S(1)} %get-tuple-element.16), channel_id=1, source_target_pairs={{0,8},{8,0},{16,24},{24,16},{1,9},{9,1},{17,25},{25,17},{2,10},{10... | collective-permute-start | bytes 1572872 | tf_op jit(solution)/shard_map/ppermute | solution.py:520
  2.7 2.6 %collective-permute-start.2 = (f32[1,2,16,128]{3,2,1,0:T(8,128)S(1)}, f32[1,2,16,128]{3,2,1,0:T(8,128)S(1)}, u32[]{:S(2)}, u32[]{:S(2)}) collective-permute-start(f32[1,2,16,128]{3,2,1,0:T(8,128)S(1)} %get-tuple-element.19.refs_0_), channel_id=1, source_target_pairs={{0,1},{1,0},{2,3},{3,2},{4,5},{5,4},{6,7},{7,6},{8,9},{9,8},{10,11... | collective-permute-start | bytes 49160 | tf_op jit(solution)/shard_map/ppermute | solution.py:520
  5.3 0.0 collective-permute-done
  5.3 0.1 fusion
  5.4 1.9 %collective-permute-start.1 = (f32[1,32,2048]{2,1,0:T(8,128)S(1)}, f32[1,32,2048]{2,1,0:T(8,128)S(1)}, u32[]{:S(2)}, u32[]{:S(2)}) collective-permute-start(f32[1,32,2048]{2,1,0:T(8,128)S(1)} %get-tuple-element.18), channel_id=1, source_target_pairs={{0,16},{8,24},{16,0},{24,8},{1,17},{9,25},{17,1},{25,9},{2,18},{10... | collective-permute-start | bytes 786440 | tf_op jit(solution)/shard_map/ppermute | solution.py:520
  7.2 0.0 collective-permute-done.2.refs_1_
  7.2 1.9 %collective-permute-start.3 = (f32[2,2,16,128]{3,2,1,0:T(8,128)S(1)}, f32[2,2,16,128]{3,2,1,0:T(8,128)S(1)}, u32[]{:S(2)}, u32[]{:S(2)}) collective-permute-start(f32[2,2,16,128]{3,2,1,0:T(8,128)S(1)} %pad_maximum_fusion.1), channel_id=1, source_target_pairs={{0,2},{1,3},{2,0},{3,1},{4,6},{5,7},{6,4},{7,5},{8,10},{9,11},{10,... | collective-permute-start | bytes 98312 | tf_op jit(solution)/shard_map/ppermute | solution.py:520
  9.1 2.1 %collective-permute-done.3.refs_2_ = f32[2,2,16,128]{3,2,1,0:T(8,128)S(1)} collective-permute-done((f32[2,2,16,128]{3,2,1,0:T(8,128)S(1)}, f32[2,2,16,128]{3,2,1,0:T(8,128)S(1)}, u32[]{:S(2)}, u32[]{:S(2)}) %collective-permute-start.3) | collective-permute-done | bytes 32800 | tf_op jit(solution)/shard_map/ppermute | solution.py:520
  11.2 2.9 %collective-permute-start.4 = (f32[4,2,16,128]{3,2,1,0:T(8,128)S(1)}, f32[4,2,16,128]{3,2,1,0:T(8,128)S(1)}, u32[]{:S(2)}, u32[]{:S(2)}) collective-permute-start(f32[4,2,16,128]{3,2,1,0:T(8,128)S(1)} %pad_maximum_fusion), channel_id=1, source_target_pairs={{0,4},{1,5},{2,6},{3,7},{4,0},{5,1},{6,2},{7,3},{8,12},{9,13},{10,... | collective-permute-start | bytes 196616 | tf_op jit(solution)/shard_map/ppermute | solution.py:520
  14.0 2.3 %collective-permute-done.4.refs_3_ = f32[4,2,16,128]{3,2,1,0:T(8,128)S(1)} collective-permute-done((f32[4,2,16,128]{3,2,1,0:T(8,128)S(1)}, f32[4,2,16,128]{3,2,1,0:T(8,128)S(1)}, u32[]{:S(2)}, u32[]{:S(2)}) %collective-permute-start.4) | collective-permute-done | bytes 65568 | tf_op jit(solution)/shard_map/ppermute | solution.py:520
  16.3 0.7 %shifted_reference.1.refs_3_ = bf16[2,2,128,2176]{3,2,1,0:T(8,128)(2,1)S(1)} custom-call(f32[1,2,16,128]{3,2,1,0:T(8,128)S(1)} %get-tuple-element.19.refs_0_, f32[1,2,16,128]{3,2,1,0:T(8,128)S(1)} %collective-permute-done.2.refs_1_, f32[2,2,16,128]{3,2,1,0:T(8,128)S(1)} %collective-permute-done.3.refs_2_, f32[4,2,16,128]{3,2,1,0:T(8,128)S(1)} %collective-permute-done.4.refs_3_), custom_call_target="tpu_custom_call" | custom-call | flops 8912896 | bytes 2228224 | tf_op jit(solution)/shard_map/shifted_reference/pallas_call | solution.py:169
  17.0 0.0 collective-permute-done.1
  17.0 2.2 %lag_products.1 = f32[8,10,8,128]{3,2,1,0:T(8,128)} custom-call(f32[32,2048]{1,0:T(8,128)S(1)} %get-tuple-element.26.refs_0_, f32[32,2048]{1,0:T(8,128)S(1)} %get-tuple-element.27.refs_1_, f32[32,2048]{1,0:T(8,128)S(1)} %bitcast.4, bf16[2,2,128,2176]{3,2,1,0:T(8,128)(2,1)S(1)} %shifted_reference.1.refs_3_), custom_call_target="tpu_custom_call" | custom-call | flops 402653184 | bytes 2555904 | tf_op jit(solution)/shard_map/lag_products/pallas_call | solution.py:248
  19.2 6.7 %all-to-all-start = ((f32[8,10,8,128]{3,2,1,0:T(8,128)}), f32[8,10,8,128]{3,2,1,0:T(8,128)S(1)}, u32[]{:S(2)}, u32[]{:S(2)}) async-start(f32[8,10,8,128]{3,2,1,0:T(8,128)} %lag_products.1), calls=%async_computation | async-start | bytes 655360 | tf_op jit(solution)/shard_map/all_to_all | solution.py:551
  25.9 0.0 copy-start
  25.9 6.2 %reference_products.1 = (bf16[2,2048,128]{2,1,0:T(8,128)(2,1)S(1)}, f32[8,128]{1,0:T(8,128)S(1)}, f32[128,128]{1,0:T(8,128)S(1)}) custom-call(f32[1,2,16,128]{3,2,1,0:T(8,128)S(1)} %get-tuple-element.19.refs_0_, f32[1,2,16,128]{3,2,1,0:T(8,128)S(1)} %collective-permute-done.2.refs_1_, f32[2,2,16,128]{3,2,1,0:T(8,128)S(1)} %collective-permute-done.3.refs_2_, ...), custom_call_target="tpu_custom_call" | custom-call | flops 1610612736 | bytes 1048576 | tf_op jit(solution)/shard_map/reference_products/pallas_call | solution.py:362
  32.1 2.1 %gram_inverse.1 = (bf16[2,128,128]{2,1,0:T(8,128)(2,1)S(1)}, bf16[2,128,128]{2,1,0:T(8,128)(2,1)S(1)}) custom-call(f32[8,128]{1,0:T(8,128)S(1)} %get-tuple-element.21.line_ref, f32[128,128]{1,0:T(8,128)S(1)} %get-tuple-element.22.tail_ref), custom_call_target="tpu_custom_call" | custom-call | flops 500000000 | bytes 200000 | tf_op jit(solution)/shard_map/gram_inverse/pallas_call | solution.py:430
  34.2 0.3 all-to-all-done.got_ref
  34.6 0.0 copy-done
  34.6 2.5 %range_doppler.1 = f32[16,2,32,256]{3,2,1,0:T(8,128)} custom-call(f32[8,10,8,128]{3,2,1,0:T(8,128)S(1)} %all-to-all-done.got_ref, bf16[2,2048,128]{2,1,0:T(8,128)(2,1)S(1)} %get-tuple-element.20.own_ref, bf16[2,128,128]{2,1,0:T(8,128)(2,1)S(1)} %get-tuple-element.23.gram_ref, bf16[2,128,128]{2,1,0:T(8,128)(2,1)S(1)} %get-tuple-element.24.solver_ref, ...), custom_call_target="tpu_custom_call" | custom-call | flops 201326592 | bytes 1048576 | tf_op jit(solution)/shard_map/range_doppler/pallas_call | solution.py:500
  (2 shorter events, 0.0 us)
Async XLA Ops:
  2.2 3.1 %collective-permute-start = (f32[64,2048]{1,0:T(8,128)S(1)}, f32[64,2048]{1,0:T(8,128)S(1)}, u32[]{:S(2)}, u32[]{:S(2)}) collective-permute-start(f32[64,2048]{1,0:T(8,128)S(1)} %get-tuple-element.16), channel_id=1, source_target_pairs={{0,8},{8,0},{16,24},{24,16},{1,9},{9,1},{17,25},{25,17},{2,10},{10... | collective-permute-start | bytes 1572872 | tf_op jit(solution)/shard_map/ppermute | solution.py:520
  2.7 4.5 %collective-permute-start.2 = (f32[1,2,16,128]{3,2,1,0:T(8,128)S(1)}, f32[1,2,16,128]{3,2,1,0:T(8,128)S(1)}, u32[]{:S(2)}, u32[]{:S(2)}) collective-permute-start(f32[1,2,16,128]{3,2,1,0:T(8,128)S(1)} %get-tuple-element.19.refs_0_), channel_id=1, source_target_pairs={{0,1},{1,0},{2,3},{3,2},{4,5},{5,4},{6,7},{7,6},{8,9},{9,8},{10,11... | collective-permute-start | bytes 49160 | tf_op jit(solution)/shard_map/ppermute | solution.py:520
  5.4 11.6 %collective-permute-start.1 = (f32[1,32,2048]{2,1,0:T(8,128)S(1)}, f32[1,32,2048]{2,1,0:T(8,128)S(1)}, u32[]{:S(2)}, u32[]{:S(2)}) collective-permute-start(f32[1,32,2048]{2,1,0:T(8,128)S(1)} %get-tuple-element.18), channel_id=1, source_target_pairs={{0,16},{8,24},{16,0},{24,8},{1,17},{9,25},{17,1},{25,9},{2,18},{10... | collective-permute-start | bytes 786440 | tf_op jit(solution)/shard_map/ppermute | solution.py:520
  7.2 3.9 %collective-permute-start.3 = (f32[2,2,16,128]{3,2,1,0:T(8,128)S(1)}, f32[2,2,16,128]{3,2,1,0:T(8,128)S(1)}, u32[]{:S(2)}, u32[]{:S(2)}) collective-permute-start(f32[2,2,16,128]{3,2,1,0:T(8,128)S(1)} %pad_maximum_fusion.1), channel_id=1, source_target_pairs={{0,2},{1,3},{2,0},{3,1},{4,6},{5,7},{6,4},{7,5},{8,10},{9,11},{10,... | collective-permute-start | bytes 98312 | tf_op jit(solution)/shard_map/ppermute | solution.py:520
  11.2 5.2 %collective-permute-start.4 = (f32[4,2,16,128]{3,2,1,0:T(8,128)S(1)}, f32[4,2,16,128]{3,2,1,0:T(8,128)S(1)}, u32[]{:S(2)}, u32[]{:S(2)}) collective-permute-start(f32[4,2,16,128]{3,2,1,0:T(8,128)S(1)} %pad_maximum_fusion), channel_id=1, source_target_pairs={{0,4},{1,5},{2,6},{3,7},{4,0},{5,1},{6,2},{7,3},{8,12},{9,13},{10,... | collective-permute-start | bytes 196616 | tf_op jit(solution)/shard_map/ppermute | solution.py:520
  19.2 15.4 %all-to-all-start = ((f32[8,10,8,128]{3,2,1,0:T(8,128)}), f32[8,10,8,128]{3,2,1,0:T(8,128)S(1)}, u32[]{:S(2)}, u32[]{:S(2)}) async-start(f32[8,10,8,128]{3,2,1,0:T(8,128)} %lag_products.1), calls=%async_computation | async-start | bytes 655360 | tf_op jit(solution)/shard_map/all_to_all | solution.py:551
  25.9 8.7 %copy-start = (bf16[2,128,512]{2,1,0:T(8,128)(2,1)S(1)}, bf16[2,128,512]{2,1,0:T(8,128)(2,1)}, u32[]{:S(2)}) copy-start(bf16[2,128,512]{2,1,0:T(8,128)(2,1)} %constant.2.clone.wave_ref) | copy-start | bytes 786436

commit v6 on v5

--- a/solution.py
+++ b/solution.py
@@ -145,15 +145,31 @@
     )(*(pltpu.with_memory_space_constraint(x, pltpu.HBM) for x in (steering, survey, ref)))
 
 
+def pair_kernel(tiles_ref, near_ref, out_ref):
+    out_ref[0] = tiles_ref[0]
+    for c in range(2):
+        for n in range(tiles_ref.shape[2]):
+            out_ref[1, c, n : n + 1, :] = near_ref[c : c + 1, n * LANES : (n + 1) * LANES]
+
+
+def pair_call(tiles, near):
+    return pl.pallas_call(
+        pair_kernel,
+        out_shape=jax.ShapeDtypeStruct((2,) + tiles.shape[1:], jnp.float32),
+        compiler_params=params(),
+        cost_estimate=pl.CostEstimate(flops=0, bytes_accessed=16 * near.size, transcendentals=0),
+        name="reference_pair",
+    )(tiles, near)
+
+
 def table_kernel(*refs):
     *part_refs, out_ref = refs
     me = lax.axis_index("tm")
     own = part_refs[0][0]
     rows = own.shape[1]
     edge = jnp.zeros((2, 2, LANES), jnp.float32)
-    for n, part_ref in enumerate(part_refs[1:], 1):
-        last = part_ref[part_ref.shape[0] - 1, :, rows - 2 :, :]
-        edge = jnp.where((me > 0) & ((me ^ (me - 1)) == 2**n - 1), last, edge)
+    for n, part_ref in enumerate(part_refs):
+        edge = jnp.where((me > 0) & ((me ^ (me - 1)) == 2 * n + 1), part_ref[1, :, rows - 2 :, :], edge)
     for c in range(2):
         line = [edge[c, n : n + 1] for n in range(2)] + [own[c, n : n + 1] for n in range(rows)]
         line = jnp.concatenate(line, 1)
@@ -529,23 +545,20 @@
     samples = length * tm_count
 
     survey = surveillance.reshape(2 * channels, length)
+    near = swap(ref_signal, "tm", 1)
     kept, moved, tiles = beam_call(steering, survey, ref_signal, chan_count, beams_local)
     shape = (chan_count // 2, 2 * beams_local, length)
     parts = [kept.reshape(shape), swap(moved, "chan", 1).reshape(shape)]
-    near = swap(tiles, "tm", 1)
+    pair = pair_call(tiles, near)
     by = 2
     while by < chan_count:
         sent = parts[0][1::2]
         for part in parts[1:]:
             sent = sent + part[1::2]
-        tiles, sent = lax.optimization_barrier((tiles, sent))
+        pair, sent = lax.optimization_barrier((pair, sent))
         parts = [part[::2] for part in parts] + [swap(sent, "chan", by)]
         by *= 2
-    ref_parts = [tiles, near]
-    by = 2
-    while by < tm_count:
-        ref_parts.append(swap(jnp.concatenate(ref_parts, 0), "tm", by))
-        by *= 2
+    ref_parts = [pair] + [swap(pair, "tm", by) for by in range(2, tm_count, 2)]
     table = table_call(ref_parts)
     pieces = lag_call([part[0] for part in parts], table, groups, tm_count)
     got = lax.all_to_all(pieces, "tm", 0, 0, tiled=True)

time: 37.2 us -> 36.9 us (level)
  starting transfers between devices: 16.4 us -> 13 us
  waiting for transfers between devices: 4.72 us -> 7.71 us
    all_to_all x1, starting transfers between devices: 6.71 us -> 3.45 us  [tiled_device(): got = lax.all_to_all(pieces, 'tm', 0, 0, tiled=True)]
    ppermute x5 -> x6, waiting for transfers between devices: 4.37 us -> 7.43 us  [swap(): return lax.ppermute(x, axis, pairs)]
    ppermute x5 -> x6, starting transfers between devices: 9.69 us -> 9.55 us  [swap(): return lax.ppermute(x, axis, pairs)]
  transfers between devices with their start and end apart: 6 -> 7, of which waited for: 3 -> 4; matrix products, arithmetic and copies ran while one was open for 0% -> 0% of each run, Pallas kernels for 24% -> 25%
where the time goes in v6:
time: 36.9 us; the launch traced here: 36.6 us
  Pallas kernels  15.8 us (43%)
  starting transfers between devices  13 us (35%)
  waiting for transfers between devices  7.71 us (21%)
    ppermute x6, starting transfers between devices, swap(): return lax.ppermute(x, axis, pairs)  9.55 us
    ppermute x6, waiting for transfers between devices, swap(): return lax.ppermute(x, axis, pairs)  7.43 us
    pallas_call x1, Pallas kernels, own_call(): pl.pallas_call(functools.partial(own_kernel, lags_local), out_shape=[jax....  6.24 us
    all_to_all x1, starting transfers between devices, tiled_device(): got = lax.all_to_all(pieces, 'tm', 0, 0, tiled=True)  3.45 us
    pallas_call x1, Pallas kernels, map_call(): pl.pallas_call(functools.partial(map_kernel, groups), in_specs=[pl.BlockS...  2.46 us
    pallas_call x1, Pallas kernels, beam_call(): pl.pallas_call(functools.partial(beam_kernel, chan_count, beams_local), i...  2.16 us
    pallas_call x1, Pallas kernels, lag_call(): pl.pallas_call(functools.partial(lag_kernel, groups, owners), in_specs=[p...  2.16 us
    pallas_call x1, Pallas kernels, solver_call(): pl.pallas_call(solver_kernel, out_shape=[out, out], compiler_params=param...  2.06 us
  transfers between devices with their start and end apart: 7, of which 4 were waited for; matrix products, arithmetic and copies ran while one was open for 0% of the time, Pallas kernels for 25%

profile of v6, /device:TPU:0, one launch (start us, length us, event | category | flops | bytes accessed | tf_op | source)
XLA Modules:
  0.0 36.6 jit_solution(1009084748924694653)
XLA Ops:
  0.0 2.2 %beams.1 = (f32[64,2048]{1,0:T(8,128)S(1)}, f32[64,2048]{1,0:T(8,128)S(1)}, f32[1,2,16,128]{3,2,1,0:T(8,128)S(1)}) custom-call(f32[2,64,64]{2,1,0:T(8,128)} %w_hbm.1, f32[128,2048]{1,0:T(8,128)} %bitcast.5, f32[2,2048]{1,0:T(2,128)} %ref_hbm.1), custom_call_target="tpu_custom_call" | custom-call | flops 201326592 | bytes 2097152 | tf_op jit(solution)/shard_map/beams/pallas_call | solution.py:127
  2.2 0.5 %collective-permute-start = (f32[64,2048]{1,0:T(8,128)S(1)}, f32[64,2048]{1,0:T(8,128)S(1)}, u32[]{:S(2)}, u32[]{:S(2)}) collective-permute-start(f32[64,2048]{1,0:T(8,128)S(1)} %get-tuple-element.16), channel_id=1, source_target_pairs={{0,8},{8,0},{16,24},{24,16},{1,9},{9,1},{17,25},{25,17},{2,10},{10... | collective-permute-start | bytes 1572872 | tf_op jit(solution)/shard_map/ppermute | solution.py:536
  2.7 2.6 %collective-permute-start.1 = (f32[2,2048]{1,0:T(2,128)}, f32[2,2048]{1,0:T(2,128)S(1)}, u32[]{:S(2)}, u32[]{:S(2)}) collective-permute-start(f32[2,2048]{1,0:T(2,128)} %ref_hbm.1), channel_id=1, source_target_pairs={{0,1},{1,0},{2,3},{3,2},{4,5},{5,4},{6,7},{7,6},{8,9},{9,8},{10,11... | collective-permute-start | bytes 49160 | tf_op jit(solution)/shard_map/ppermute | solution.py:536
  5.3 1.9 %collective-permute-done.1.near_ref = f32[2,2048]{1,0:T(2,128)S(1)} collective-permute-done((f32[2,2048]{1,0:T(2,128)}, f32[2,2048]{1,0:T(2,128)S(1)}, u32[]{:S(2)}, u32[]{:S(2)}) %collective-permute-start.1) | collective-permute-done | bytes 16416 | tf_op jit(solution)/shard_map/ppermute | solution.py:536
  7.2 0.0 collective-permute-done
  7.2 0.1 fusion
  7.3 2.1 %collective-permute-start.2 = (f32[1,32,2048]{2,1,0:T(8,128)S(1)}, f32[1,32,2048]{2,1,0:T(8,128)S(1)}, u32[]{:S(2)}, u32[]{:S(2)}) collective-permute-start(f32[1,32,2048]{2,1,0:T(8,128)S(1)} %get-tuple-element.18), channel_id=1, source_target_pairs={{0,16},{8,24},{16,0},{24,8},{1,17},{9,25},{17,1},{25,9},{2,18},{10... | collective-permute-start | bytes 786440 | tf_op jit(solution)/shard_map/ppermute | solution.py:536
  9.4 1.6 %collective-permute-start.3 = (f32[2,2,16,128]{3,2,1,0:T(8,128)S(1)}, f32[2,2,16,128]{3,2,1,0:T(8,128)S(1)}, u32[]{:S(2)}, u32[]{:S(2)}) collective-permute-start(f32[2,2,16,128]{3,2,1,0:T(8,128)S(1)} %reference_pair.1.refs_0_), channel_id=1, source_target_pairs={{0,2},{1,3},{2,0},{3,1},{4,6},{5,7},{6,4},{7,5},{8,10},{9,11},{10,... | collective-permute-start | bytes 98312 | tf_op jit(solution)/shard_map/ppermute | solution.py:536
  10.9 2.6 %collective-permute-start.4 = (f32[2,2,16,128]{3,2,1,0:T(8,128)S(1)}, f32[2,2,16,128]{3,2,1,0:T(8,128)S(1)}, u32[]{:S(2)}, u32[]{:S(2)}) collective-permute-start(f32[2,2,16,128]{3,2,1,0:T(8,128)S(1)} %reference_pair.1.refs_0_), channel_id=1, source_target_pairs={{0,4},{1,5},{2,6},{3,7},{4,0},{5,1},{6,2},{7,3},{8,12},{9,13},{10,... | collective-permute-start | bytes 98312 | tf_op jit(solution)/shard_map/ppermute | solution.py:536
  13.5 0.2 collective-permute-start.5
  13.8 0.0 collective-permute-done.3.refs_1_
  13.8 2.3 %collective-permute-done.4.refs_2_ = f32[2,2,16,128]{3,2,1,0:T(8,128)S(1)} collective-permute-done((f32[2,2,16,128]{3,2,1,0:T(8,128)S(1)}, f32[2,2,16,128]{3,2,1,0:T(8,128)S(1)}, u32[]{:S(2)}, u32[]{:S(2)}) %collective-permute-start.4) | collective-permute-done | bytes 32800 | tf_op jit(solution)/shard_map/ppermute | solution.py:536
  16.0 3.2 %collective-permute-done.5.refs_3_ = f32[2,2,16,128]{3,2,1,0:T(8,128)S(1)} collective-permute-done((f32[2,2,16,128]{3,2,1,0:T(8,128)S(1)}, f32[2,2,16,128]{3,2,1,0:T(8,128)S(1)}, u32[]{:S(2)}, u32[]{:S(2)}) %collective-permute-start.5) | collective-permute-done | bytes 32800 | tf_op jit(solution)/shard_map/ppermute | solution.py:536
  19.3 0.7 %shifted_reference.1.refs_3_ = bf16[2,2,128,2176]{3,2,1,0:T(8,128)(2,1)S(1)} custom-call(f32[2,2,16,128]{3,2,1,0:T(8,128)S(1)} %reference_pair.1.refs_0_, f32[2,2,16,128]{3,2,1,0:T(8,128)S(1)} %collective-permute-done.3.refs_1_, f32[2,2,16,128]{3,2,1,0:T(8,128)S(1)} %collective-permute-done.4.refs_2_, f32[2,2,16,128]{3,2,1,0:T(8,128)S(1)} %collective-permute-done.5.refs_3_), custom_call_target="tpu_custom_call" | custom-call | flops 8912896 | bytes 2228224 | tf_op jit(solution)/shard_map/shifted_reference/pallas_call | solution.py:185
  19.9 0.0 collective-permute-done.2
  19.9 2.2 %lag_products.1 = f32[8,10,8,128]{3,2,1,0:T(8,128)} custom-call(f32[32,2048]{1,0:T(8,128)S(1)} %get-tuple-element.26.refs_0_, f32[32,2048]{1,0:T(8,128)S(1)} %get-tuple-element.27.refs_1_, f32[32,2048]{1,0:T(8,128)S(1)} %bitcast.4, bf16[2,2,128,2176]{3,2,1,0:T(8,128)(2,1)S(1)} %shifted_reference.1.refs_3_), custom_call_target="tpu_custom_call" | custom-call | flops 402653184 | bytes 2555904 | tf_op jit(solution)/shard_map/lag_products/pallas_call | solution.py:264
  22.1 3.4 %all-to-all-start = ((f32[8,10,8,128]{3,2,1,0:T(8,128)}), f32[8,10,8,128]{3,2,1,0:T(8,128)S(1)}, u32[]{:S(2)}, u32[]{:S(2)}) async-start(f32[8,10,8,128]{3,2,1,0:T(8,128)} %lag_products.1), calls=%async_computation | async-start | bytes 655360 | tf_op jit(solution)/shard_map/all_to_all | solution.py:564
  25.6 0.0 copy-start
  25.6 6.2 %reference_products.1 = (bf16[2,2048,128]{2,1,0:T(8,128)(2,1)S(1)}, f32[8,128]{1,0:T(8,128)S(1)}, f32[128,128]{1,0:T(8,128)S(1)}) custom-call(f32[2,2,16,128]{3,2,1,0:T(8,128)S(1)} %reference_pair.1.refs_0_, f32[2,2,16,128]{3,2,1,0:T(8,128)S(1)} %collective-permute-done.3.refs_1_, f32[2,2,16,128]{3,2,1,0:T(8,128)S(1)} %collective-permute-done.4.refs_2_, ...), custom_call_target="tpu_custom_call" | custom-call | flops 1610612736 | bytes 1048576 | tf_op jit(solution)/shard_map/reference_products/pallas_call | solution.py:378
  31.8 2.1 %gram_inverse.1 = (bf16[2,128,128]{2,1,0:T(8,128)(2,1)S(1)}, bf16[2,128,128]{2,1,0:T(8,128)(2,1)S(1)}) custom-call(f32[8,128]{1,0:T(8,128)S(1)} %get-tuple-element.21.line_ref, f32[128,128]{1,0:T(8,128)S(1)} %get-tuple-element.22.tail_ref), custom_call_target="tpu_custom_call" | custom-call | flops 500000000 | bytes 200000 | tf_op jit(solution)/shard_map/gram_inverse/pallas_call | solution.py:446
  33.9 0.3 all-to-all-done.got_ref
  34.2 0.0 copy-done
  34.2 2.5 %range_doppler.1 = f32[16,2,32,256]{3,2,1,0:T(8,128)} custom-call(f32[8,10,8,128]{3,2,1,0:T(8,128)S(1)} %all-to-all-done.got_ref, bf16[2,2048,128]{2,1,0:T(8,128)(2,1)S(1)} %get-tuple-element.20.own_ref, bf16[2,128,128]{2,1,0:T(8,128)(2,1)S(1)} %get-tuple-element.23.gram_ref, bf16[2,128,128]{2,1,0:T(8,128)(2,1)S(1)} %get-tuple-element.24.solver_ref, ...), custom_call_target="tpu_custom_call" | custom-call | flops 201326592 | bytes 1048576 | tf_op jit(solution)/shard_map/range_doppler/pallas_call | solution.py:516
  (1 shorter events, 0.0 us)
Async XLA Ops:
  2.2 5.1 %collective-permute-start = (f32[64,2048]{1,0:T(8,128)S(1)}, f32[64,2048]{1,0:T(8,128)S(1)}, u32[]{:S(2)}, u32[]{:S(2)}) collective-permute-start(f32[64,2048]{1,0:T(8,128)S(1)} %get-tuple-element.16), channel_id=1, source_target_pairs={{0,8},{8,0},{16,24},{24,16},{1,9},{9,1},{17,25},{25,17},{2,10},{10... | collective-permute-start | bytes 1572872 | tf_op jit(solution)/shard_map/ppermute | solution.py:536
  2.7 4.5 %collective-permute-start.1 = (f32[2,2048]{1,0:T(2,128)}, f32[2,2048]{1,0:T(2,128)S(1)}, u32[]{:S(2)}, u32[]{:S(2)}) collective-permute-start(f32[2,2048]{1,0:T(2,128)} %ref_hbm.1), channel_id=1, source_target_pairs={{0,1},{1,0},{2,3},{3,2},{4,5},{5,4},{6,7},{7,6},{8,9},{9,8},{10,11... | collective-permute-start | bytes 49160 | tf_op jit(solution)/shard_map/ppermute | solution.py:536
  7.3 12.6 %collective-permute-start.2 = (f32[1,32,2048]{2,1,0:T(8,128)S(1)}, f32[1,32,2048]{2,1,0:T(8,128)S(1)}, u32[]{:S(2)}, u32[]{:S(2)}) collective-permute-start(f32[1,32,2048]{2,1,0:T(8,128)S(1)} %get-tuple-element.18), channel_id=1, source_target_pairs={{0,16},{8,24},{16,0},{24,8},{1,17},{9,25},{17,1},{25,9},{2,18},{10... | collective-permute-start | bytes 786440 | tf_op jit(solution)/shard_map/ppermute | solution.py:536
  9.4 4.4 %collective-permute-start.3 = (f32[2,2,16,128]{3,2,1,0:T(8,128)S(1)}, f32[2,2,16,128]{3,2,1,0:T(8,128)S(1)}, u32[]{:S(2)}, u32[]{:S(2)}) collective-permute-start(f32[2,2,16,128]{3,2,1,0:T(8,128)S(1)} %reference_pair.1.refs_0_), channel_id=1, source_target_pairs={{0,2},{1,3},{2,0},{3,1},{4,6},{5,7},{6,4},{7,5},{8,10},{9,11},{10,... | collective-permute-start | bytes 98312 | tf_op jit(solution)/shard_map/ppermute | solution.py:536
  10.9 5.1 %collective-permute-start.4 = (f32[2,2,16,128]{3,2,1,0:T(8,128)S(1)}, f32[2,2,16,128]{3,2,1,0:T(8,128)S(1)}, u32[]{:S(2)}, u32[]{:S(2)}) collective-permute-start(f32[2,2,16,128]{3,2,1,0:T(8,128)S(1)} %reference_pair.1.refs_0_), channel_id=1, source_target_pairs={{0,4},{1,5},{2,6},{3,7},{4,0},{5,1},{6,2},{7,3},{8,12},{9,13},{10,... | collective-permute-start | bytes 98312 | tf_op jit(solution)/shard_map/ppermute | solution.py:536
  13.5 5.7 %collective-permute-start.5 = (f32[2,2,16,128]{3,2,1,0:T(8,128)S(1)}, f32[2,2,16,128]{3,2,1,0:T(8,128)S(1)}, u32[]{:S(2)}, u32[]{:S(2)}) collective-permute-start(f32[2,2,16,128]{3,2,1,0:T(8,128)S(1)} %reference_pair.1.refs_0_), channel_id=1, source_target_pairs={{0,6},{1,7},{2,4},{3,5},{4,2},{5,3},{6,0},{7,1},{8,14},{9,15},{10,... | collective-permute-start | bytes 98312 | tf_op jit(solution)/shard_map/ppermute | solution.py:536
  22.1 12.1 %all-to-all-start = ((f32[8,10,8,128]{3,2,1,0:T(8,128)}), f32[8,10,8,128]{3,2,1,0:T(8,128)S(1)}, u32[]{:S(2)}, u32[]{:S(2)}) async-start(f32[8,10,8,128]{3,2,1,0:T(8,128)} %lag_products.1), calls=%async_computation | async-start | bytes 655360 | tf_op jit(solution)/shard_map/all_to_all | solution.py:564
  25.6 8.6 %copy-start = (bf16[2,128,512]{2,1,0:T(8,128)(2,1)S(1)}, bf16[2,128,512]{2,1,0:T(8,128)(2,1)}, u32[]{:S(2)}) copy-start(bf16[2,128,512]{2,1,0:T(8,128)(2,1)} %constant.2.clone.wave_ref) | copy-start | bytes 786436

commit v7 on v6

--- a/solution.py
+++ b/solution.py
@@ -71,9 +71,7 @@
 CHUNKS = 4
 
 
-def beam_kernel(
-    chan_count, beams_local, w_hbm, s_hbm, ref_hbm, kept_ref, sent_ref, tiles_ref, w_ref, s_ref, ref_ref, w_sem, s_sem, ref_sem
-):
+def beam_sent_kernel(chan_count, beams_local, w_hbm, s_hbm, sent_ref, split_ref, kept_w_ref, w_ref, s_ref, w_sem, s_sem):
     me = lax.axis_index("chan")
     depth, length = s_hbm.shape
     width = length // CHUNKS
@@ -84,14 +82,12 @@
         cols = pl.ds(n * width, width)
         s_copies.append(pltpu.make_async_copy(s_hbm.at[:, cols], s_ref.at[:, cols], s_sem.at[n]))
         s_copies[n].start()
-    ref_copy = pltpu.make_async_copy(ref_hbm, ref_ref, ref_sem)
-    ref_copy.start()
     half = SUBLANES // 2
     sub = lax.broadcasted_iota(jnp.int32, (SUBLANES, w_hbm.shape[2]), 0)
     top = sub < half
-    w_copy.wait()
-    rows = []
-    for parity in range(2):
+
+    def weights(parity):
+        rows = []
         for e in range(parity, chan_count, 2):
             base = (me ^ e) * beams_local
             for tile in range(beams_local // SUBLANES):
@@ -104,58 +100,93 @@
                 second = [jnp.where(top, wr_s, wi), jnp.where(top, -wi_s, wr)]
                 rows.append(jnp.concatenate(first, 1))
                 rows.append(jnp.concatenate(second, 1))
-    weights = halves(jnp.concatenate(rows, 0))
-    mid = weights[0].shape[0] // 2
+        return halves(jnp.concatenate(rows, 0))
+
+    w_copy.wait()
+    kept_w_ref[0], kept_w_ref[1] = weights(0)
+    sent_w = weights(1)
     for n in range(CHUNKS):
         cols = slice(n * width, (n + 1) * width)
         s_copies[n].wait()
-        product = dot_split(weights, halves(s_ref[:, cols]))
-        kept_ref[:, cols] = product[:mid]
-        sent_ref[:, cols] = product[mid:]
+        samples = halves(s_ref[:, cols])
+        split_ref[0, :, cols], split_ref[1, :, cols] = samples
+        sent_ref[:, cols] = dot_split(sent_w, samples)
+
+
+def beam_sent_call(steering, survey, chan_count, beams_local):
+    depth, length = survey.shape
+    rows = chan_count * beams_local
+    hbm = pl.BlockSpec(memory_space=pltpu.HBM)
+    return pl.pallas_call(
+        functools.partial(beam_sent_kernel, chan_count, beams_local),
+        in_specs=[hbm, hbm],
+        out_specs=[pl.BlockSpec(memory_space=pltpu.VMEM)] * 3,
+        out_shape=[
+            jax.ShapeDtypeStruct((rows, length), jnp.float32),
+            jax.ShapeDtypeStruct((2, depth, length), jnp.bfloat16),
+            jax.ShapeDtypeStruct((2, rows, depth), jnp.bfloat16),
+        ],
+        scratch_shapes=[
+            pltpu.VMEM(steering.shape, jnp.float32),
+            pltpu.VMEM(survey.shape, jnp.float32),
+            pltpu.SemaphoreType.DMA,
+            pltpu.SemaphoreType.DMA((CHUNKS,)),
+        ],
+        compiler_params=params(),
+        cost_estimate=pl.CostEstimate(
+            flops=6 * rows * depth * length, bytes_accessed=4 * length * (depth + 2 * rows), transcendentals=0
+        ),
+        name="beams_sent",
+    )(*(pltpu.with_memory_space_constraint(x, pltpu.HBM) for x in (steering, survey)))
+
+
+def beam_kept_kernel(split_ref, w_ref, ref_hbm, kept_ref, tiles_ref, ref_ref, ref_sem):
+    ref_copy = pltpu.make_async_copy(ref_hbm, ref_ref, ref_sem)
+    ref_copy.start()
+    length = split_ref.shape[2]
+    width = length // CHUNKS
+    for n in range(CHUNKS):
+        cols = slice(n * width, (n + 1) * width)
+        kept_ref[:, cols] = dot_split((w_ref[0], w_ref[1]), (split_ref[0, :, cols], split_ref[1, :, cols]))
     ref_copy.wait()
     for c in range(2):
         for n in range(length // LANES):
-            tiles_ref[0, c, n : n + 1, :] = ref_ref[c : c + 1, n * LANES : (n + 1) * LANES]
-
-
-def beam_call(steering, survey, ref, chan_count, beams_local):
-    depth, length = survey.shape
-    rows = chan_count * beams_local
-    out = jax.ShapeDtypeStruct((rows, length), jnp.float32)
-    hbm = pl.BlockSpec(memory_space=pltpu.HBM)
+            cols = slice(n * LANES, (n + 1) * LANES)
+            tiles_ref[c, n : n + 1, :] = ref_ref[c : c + 1, cols]
+
+
+def beam_kept_call(split, weights, ref):
+    depth, length = split.shape[1:]
+    rows = weights.shape[1]
     vmem = pl.BlockSpec(memory_space=pltpu.VMEM)
     return pl.pallas_call(
-        functools.partial(beam_kernel, chan_count, beams_local),
-        in_specs=[hbm, hbm, hbm],
-        out_specs=[vmem, vmem, vmem],
-        out_shape=[out, out, jax.ShapeDtypeStruct((1, 2, length // LANES, LANES), jnp.float32)],
-        scratch_shapes=[
-            pltpu.VMEM(steering.shape, jnp.float32),
-            pltpu.VMEM(survey.shape, jnp.float32),
-            pltpu.VMEM(ref.shape, jnp.float32),
-            pltpu.SemaphoreType.DMA,
-            pltpu.SemaphoreType.DMA((CHUNKS,)),
-            pltpu.SemaphoreType.DMA,
+        beam_kept_kernel,
+        in_specs=[vmem, vmem, pl.BlockSpec(memory_space=pltpu.HBM)],
+        out_specs=[vmem, vmem],
+        out_shape=[
+            jax.ShapeDtypeStruct((rows, length), jnp.float32),
+            jax.ShapeDtypeStruct((2, length // LANES, LANES), jnp.float32),
         ],
+        scratch_shapes=[pltpu.VMEM(ref.shape, jnp.float32), pltpu.SemaphoreType.DMA],
         compiler_params=params(),
         cost_estimate=pl.CostEstimate(
-            flops=12 * rows * depth * length, bytes_accessed=4 * length * (depth + 2 * rows), transcendentals=0
+            flops=6 * rows * depth * length, bytes_accessed=4 * length * (depth + rows), transcendentals=0
         ),
-        name="beams",
-    )(*(pltpu.with_memory_space_constraint(x, pltpu.HBM) for x in (steering, survey, ref)))
+        name="beams_kept",
+    )(split, weights, pltpu.with_memory_space_constraint(ref, pltpu.HBM))
 
 
 def pair_kernel(tiles_ref, near_ref, out_ref):
-    out_ref[0] = tiles_ref[0]
+    out_ref[0] = tiles_ref[...]
     for c in range(2):
-        for n in range(tiles_ref.shape[2]):
+        for n in range(tiles_ref.shape[1]):
             out_ref[1, c, n : n + 1, :] = near_ref[c : c + 1, n * LANES : (n + 1) * LANES]
 
 
 def pair_call(tiles, near):
     return pl.pallas_call(
         pair_kernel,
-        out_shape=jax.ShapeDtypeStruct((2,) + tiles.shape[1:], jnp.float32),
+        out_shape=jax.ShapeDtypeStruct((2,) + tiles.shape, jnp.float32),
         compiler_params=params(),
         cost_estimate=pl.CostEstimate(flops=0, bytes_accessed=16 * near.size, transcendentals=0),
         name="reference_pair",
@@ -546,18 +577,21 @@
 
     survey = surveillance.reshape(2 * channels, length)
     near = swap(ref_signal, "tm", 1)
-    kept, moved, tiles = beam_call(steering, survey, ref_signal, chan_count, beams_local)
+    moved, split, weights = beam_sent_call(steering, survey, chan_count, beams_local)
     shape = (chan_count // 2, 2 * beams_local, length)
-    parts = [kept.reshape(shape), swap(moved, "chan", 1).reshape(shape)]
-    pair = pair_call(tiles, near)
+    moved = swap(moved, "chan", 1)
+    kept, tiles = beam_kept_call(split, weights, ref_signal)
+    near, moved = lax.optimization_barrier((near, moved))
+    parts = [kept.reshape(shape), moved.reshape(shape)]
     by = 2
     while by < chan_count:
         sent = parts[0][1::2]
         for part in parts[1:]:
             sent = sent + part[1::2]
-        pair, sent = lax.optimization_barrier((pair, sent))
+        tiles, sent = lax.optimization_barrier((tiles, sent))
         parts = [part[::2] for part in parts] + [swap(sent, "chan", by)]
         by *= 2
+    pair = pair_call(tiles, near)
     ref_parts = [pair] + [swap(pair, "tm", by) for by in range(2, tm_count, 2)]
     table = table_call(ref_parts)
     pieces = lag_call([part[0] for part in parts], table, groups, tm_count)

time: 36.9 us -> 36.9 us (level)
  waiting for transfers between devices: 7.71 us -> 6.93 us
  Pallas kernels: 15.8 us -> 16.5 us
    ppermute x6, waiting for transfers between devices: 7.43 us -> 6.65 us  [swap(): return lax.ppermute(x, axis, pairs)]
    pallas_call x1 -> x2, Pallas kernels: 2.16 us -> 2.86 us  [the longest x1 2.09 us: beam_sent_call(): pl.pallas_call(functools.partial(beam_sent_kernel, chan_count, beams_loca...]
  transfers between devices with their start and end apart: 7 -> 7, of which waited for: 4 -> 4; matrix products, arithmetic and copies ran while one was open for 0% -> 0% of each run, Pallas kernels for 25% -> 27%
where the time goes in v7:
time: 36.9 us; the launch traced here: 36.6 us
  Pallas kernels  16.5 us (45%)
  starting transfers between devices  13.1 us (36%)
  waiting for transfers between devices  6.93 us (19%)
    ppermute x6, starting transfers between devices, swap(): return lax.ppermute(x, axis, pairs)  9.62 us
    ppermute x6, waiting for transfers between devices, swap(): return lax.ppermute(x, axis, pairs)  6.65 us
    pallas_call x1, Pallas kernels, own_call(): pl.pallas_call(functools.partial(own_kernel, lags_local), out_shape=[jax....  6.24 us
    all_to_all x1, starting transfers between devices, tiled_device(): got = lax.all_to_all(pieces, 'tm', 0, 0, tiled=True)  3.45 us
    pallas_call x1, Pallas kernels, map_call(): pl.pallas_call(functools.partial(map_kernel, groups), in_specs=[pl.BlockS...  2.46 us
    pallas_call x1, Pallas kernels, lag_call(): pl.pallas_call(functools.partial(lag_kernel, groups, owners), in_specs=[p...  2.16 us
    pallas_call x1, Pallas kernels, beam_sent_call(): pl.pallas_call(functools.partial(beam_sent_kernel, chan_count, beams_loca...  2.09 us
    pallas_call x1, Pallas kernels, solver_call(): pl.pallas_call(solver_kernel, out_shape=[out, out], compiler_params=param...  2.06 us
  transfers between devices with their start and end apart: 7, of which 4 were waited for; matrix products, arithmetic and copies ran while one was open for 0% of the time, Pallas kernels for 27%

profile of v7, /device:TPU:0, one launch (start us, length us, event | category | flops | bytes accessed | tf_op | source)
XLA Modules:
  0.0 36.6 jit_solution(12070174002081814377)
XLA Ops:
  0.0 2.1 %beams_sent.1 = (f32[64,2048]{1,0:T(8,128)S(1)}, bf16[2,128,2048]{2,1,0:T(8,128)(2,1)S(1)}, bf16[2,64,128]{2,1,0:T(8,128)(2,1)S(1)}) custom-call(f32[2,64,64]{2,1,0:T(8,128)} %w_hbm.1, f32[128,2048]{1,0:T(8,128)} %bitcast.5), custom_call_target="tpu_custom_call" | custom-call | flops 100663296 | bytes 2097152 | tf_op jit(solution)/shard_map/beams_sent/pallas_call | solution.py:120
  2.1 0.5 %collective-permute-start.1 = (f32[64,2048]{1,0:T(8,128)S(1)}, f32[64,2048]{1,0:T(8,128)S(1)}, u32[]{:S(2)}, u32[]{:S(2)}) collective-permute-start(f32[64,2048]{1,0:T(8,128)S(1)} %get-tuple-element.22), channel_id=1, source_target_pairs={{0,8},{8,0},{16,24},{24,16},{1,9},{9,1},{17,25},{25,17},{2,10},{10... | collective-permute-start | bytes 1572872 | tf_op jit(solution)/shard_map/ppermute | solution.py:567
  2.6 2.6 %collective-permute-start = (f32[2,2048]{1,0:T(2,128)}, f32[2,2048]{1,0:T(2,128)S(1)}, u32[]{:S(2)}, u32[]{:S(2)}) collective-permute-start(f32[2,2048]{1,0:T(2,128)} %ref_hbm.1), channel_id=1, source_target_pairs={{0,1},{1,0},{2,3},{3,2},{4,5},{5,4},{6,7},{7,6},{8,9},{9,8},{10,11... | collective-permute-start | bytes 49160 | tf_op jit(solution)/shard_map/ppermute | solution.py:567
  5.2 0.8 %beams_kept.1 = (f32[64,2048]{1,0:T(8,128)S(1)}, f32[2,16,128]{2,1,0:T(8,128)S(1)}) custom-call(bf16[2,128,2048]{2,1,0:T(8,128)(2,1)S(1)} %get-tuple-element.19.split_ref, bf16[2,64,128]{2,1,0:T(8,128)(2,1)S(1)} %get-tuple-element.20.w_ref, f32[2,2048]{1,0:T(2,128)} %ref_hbm.1), custom_call_target="tpu_custom_call" | custom-call | flops 100663296 | bytes 1572864 | tf_op jit(solution)/shard_map/beams_kept/pallas_call | solution.py:162
  6.0 1.2 %collective-permute-done.near_ref = f32[2,2048]{1,0:T(2,128)S(1)} collective-permute-done((f32[2,2048]{1,0:T(2,128)}, f32[2,2048]{1,0:T(2,128)S(1)}, u32[]{:S(2)}, u32[]{:S(2)}) %collective-permute-start) | collective-permute-done | bytes 16416 | tf_op jit(solution)/shard_map/ppermute | solution.py:567
  7.1 0.0 collective-permute-done.1
  7.1 0.1 add_bitcast_fusion
  7.2 2.1 %collective-permute-start.2 = (f32[1,32,2048]{2,1,0:T(8,128)S(1)}, f32[1,32,2048]{2,1,0:T(8,128)S(1)}, u32[]{:S(2)}, u32[]{:S(2)}) collective-permute-start(f32[1,32,2048]{2,1,0:T(8,128)S(1)} %get-tuple-element.25), channel_id=1, source_target_pairs={{0,16},{8,24},{16,0},{24,8},{1,17},{9,25},{17,1},{25,9},{2,18},{10... | collective-permute-start | bytes 786440 | tf_op jit(solution)/shard_map/ppermute | solution.py:567
  9.3 1.6 %collective-permute-start.3 = (f32[2,2,16,128]{3,2,1,0:T(8,128)S(1)}, f32[2,2,16,128]{3,2,1,0:T(8,128)S(1)}, u32[]{:S(2)}, u32[]{:S(2)}) collective-permute-start(f32[2,2,16,128]{3,2,1,0:T(8,128)S(1)} %reference_pair.1.refs_0_), channel_id=1, source_target_pairs={{0,2},{1,3},{2,0},{3,1},{4,6},{5,7},{6,4},{7,5},{8,10},{9,11},{10,... | collective-permute-start | bytes 98312 | tf_op jit(solution)/shard_map/ppermute | solution.py:567
  10.9 2.6 %collective-permute-start.4 = (f32[2,2,16,128]{3,2,1,0:T(8,128)S(1)}, f32[2,2,16,128]{3,2,1,0:T(8,128)S(1)}, u32[]{:S(2)}, u32[]{:S(2)}) collective-permute-start(f32[2,2,16,128]{3,2,1,0:T(8,128)S(1)} %reference_pair.1.refs_0_), channel_id=1, source_target_pairs={{0,4},{1,5},{2,6},{3,7},{4,0},{5,1},{6,2},{7,3},{8,12},{9,13},{10,... | collective-permute-start | bytes 98312 | tf_op jit(solution)/shard_map/ppermute | solution.py:567
  13.5 0.2 collective-permute-start.5
  13.7 0.0 collective-permute-done.3.refs_1_
  13.7 2.3 %collective-permute-done.4.refs_2_ = f32[2,2,16,128]{3,2,1,0:T(8,128)S(1)} collective-permute-done((f32[2,2,16,128]{3,2,1,0:T(8,128)S(1)}, f32[2,2,16,128]{3,2,1,0:T(8,128)S(1)}, u32[]{:S(2)}, u32[]{:S(2)}) %collective-permute-start.4) | collective-permute-done | bytes 32800 | tf_op jit(solution)/shard_map/ppermute | solution.py:567
  16.0 3.2 %collective-permute-done.5.refs_3_ = f32[2,2,16,128]{3,2,1,0:T(8,128)S(1)} collective-permute-done((f32[2,2,16,128]{3,2,1,0:T(8,128)S(1)}, f32[2,2,16,128]{3,2,1,0:T(8,128)S(1)}, u32[]{:S(2)}, u32[]{:S(2)}) %collective-permute-start.5) | collective-permute-done | bytes 32800 | tf_op jit(solution)/shard_map/ppermute | solution.py:567
  19.2 0.7 %shifted_reference.1.refs_3_ = bf16[2,2,128,2176]{3,2,1,0:T(8,128)(2,1)S(1)} custom-call(f32[2,2,16,128]{3,2,1,0:T(8,128)S(1)} %reference_pair.1.refs_0_, f32[2,2,16,128]{3,2,1,0:T(8,128)S(1)} %collective-permute-done.3.refs_1_, f32[2,2,16,128]{3,2,1,0:T(8,128)S(1)} %collective-permute-done.4.refs_2_, f32[2,2,16,128]{3,2,1,0:T(8,128)S(1)} %collective-permute-done.5.refs_3_), custom_call_target="tpu_custom_call" | custom-call | flops 8912896 | bytes 2228224 | tf_op jit(solution)/shard_map/shifted_reference/pallas_call | solution.py:216
  19.9 0.0 collective-permute-done.2
  19.9 2.2 %lag_products.1 = f32[8,10,8,128]{3,2,1,0:T(8,128)} custom-call(f32[32,2048]{1,0:T(8,128)S(1)} %get-tuple-element.34.refs_0_, f32[32,2048]{1,0:T(8,128)S(1)} %get-tuple-element.35.refs_1_, f32[32,2048]{1,0:T(8,128)S(1)} %bitcast.4, bf16[2,2,128,2176]{3,2,1,0:T(8,128)(2,1)S(1)} %shifted_reference.1.refs_3_), custom_call_target="tpu_custom_call" | custom-call | flops 402653184 | bytes 2555904 | tf_op jit(solution)/shard_map/lag_products/pallas_call | solution.py:295
  22.1 3.4 %all-to-all-start = ((f32[8,10,8,128]{3,2,1,0:T(8,128)}), f32[8,10,8,128]{3,2,1,0:T(8,128)S(1)}, u32[]{:S(2)}, u32[]{:S(2)}) async-start(f32[8,10,8,128]{3,2,1,0:T(8,128)} %lag_products.1), calls=%async_computation | async-start | bytes 655360 | tf_op jit(solution)/shard_map/all_to_all | solution.py:598
  25.5 0.0 copy-start
  25.6 6.2 %reference_products.1 = (bf16[2,2048,128]{2,1,0:T(8,128)(2,1)S(1)}, f32[8,128]{1,0:T(8,128)S(1)}, f32[128,128]{1,0:T(8,128)S(1)}) custom-call(f32[2,2,16,128]{3,2,1,0:T(8,128)S(1)} %reference_pair.1.refs_0_, f32[2,2,16,128]{3,2,1,0:T(8,128)S(1)} %collective-permute-done.3.refs_1_, f32[2,2,16,128]{3,2,1,0:T(8,128)S(1)} %collective-permute-done.4.refs_2_, ...), custom_call_target="tpu_custom_call" | custom-call | flops 1610612736 | bytes 1048576 | tf_op jit(solution)/shard_map/reference_products/pallas_call | solution.py:409
  31.8 2.1 %gram_inverse.1 = (bf16[2,128,128]{2,1,0:T(8,128)(2,1)S(1)}, bf16[2,128,128]{2,1,0:T(8,128)(2,1)S(1)}) custom-call(f32[8,128]{1,0:T(8,128)S(1)} %get-tuple-element.29.line_ref, f32[128,128]{1,0:T(8,128)S(1)} %get-tuple-element.30.tail_ref), custom_call_target="tpu_custom_call" | custom-call | flops 500000000 | bytes 200000 | tf_op jit(solution)/shard_map/gram_inverse/pallas_call | solution.py:477
  33.9 0.3 all-to-all-done.got_ref
  34.1 0.0 copy-done
  34.1 2.5 %range_doppler.1 = f32[16,2,32,256]{3,2,1,0:T(8,128)} custom-call(f32[8,10,8,128]{3,2,1,0:T(8,128)S(1)} %all-to-all-done.got_ref, bf16[2,2048,128]{2,1,0:T(8,128)(2,1)S(1)} %get-tuple-element.28.own_ref, bf16[2,128,128]{2,1,0:T(8,128)(2,1)S(1)} %get-tuple-element.31.gram_ref, bf16[2,128,128]{2,1,0:T(8,128)(2,1)S(1)} %get-tuple-element.32.solver_ref, ...), custom_call_target="tpu_custom_call" | custom-call | flops 201326592 | bytes 1048576 | tf_op jit(solution)/shard_map/range_doppler/pallas_call | solution.py:547
  (1 shorter events, 0.0 us)
Async XLA Ops:
  2.1 5.0 %collective-permute-start.1 = (f32[64,2048]{1,0:T(8,128)S(1)}, f32[64,2048]{1,0:T(8,128)S(1)}, u32[]{:S(2)}, u32[]{:S(2)}) collective-permute-start(f32[64,2048]{1,0:T(8,128)S(1)} %get-tuple-element.22), channel_id=1, source_target_pairs={{0,8},{8,0},{16,24},{24,16},{1,9},{9,1},{17,25},{25,17},{2,10},{10... | collective-permute-start | bytes 1572872 | tf_op jit(solution)/shard_map/ppermute | solution.py:567
  2.6 4.5 %collective-permute-start = (f32[2,2048]{1,0:T(2,128)}, f32[2,2048]{1,0:T(2,128)S(1)}, u32[]{:S(2)}, u32[]{:S(2)}) collective-permute-start(f32[2,2048]{1,0:T(2,128)} %ref_hbm.1), channel_id=1, source_target_pairs={{0,1},{1,0},{2,3},{3,2},{4,5},{5,4},{6,7},{7,6},{8,9},{9,8},{10,11... | collective-permute-start | bytes 49160 | tf_op jit(solution)/shard_map/ppermute | solution.py:567
  7.2 12.7 %collective-permute-start.2 = (f32[1,32,2048]{2,1,0:T(8,128)S(1)}, f32[1,32,2048]{2,1,0:T(8,128)S(1)}, u32[]{:S(2)}, u32[]{:S(2)}) collective-permute-start(f32[1,32,2048]{2,1,0:T(8,128)S(1)} %get-tuple-element.25), channel_id=1, source_target_pairs={{0,16},{8,24},{16,0},{24,8},{1,17},{9,25},{17,1},{25,9},{2,18},{10... | collective-permute-start | bytes 786440 | tf_op jit(solution)/shard_map/ppermute | solution.py:567
  9.3 4.5 %collective-permute-start.3 = (f32[2,2,16,128]{3,2,1,0:T(8,128)S(1)}, f32[2,2,16,128]{3,2,1,0:T(8,128)S(1)}, u32[]{:S(2)}, u32[]{:S(2)}) collective-permute-start(f32[2,2,16,128]{3,2,1,0:T(8,128)S(1)} %reference_pair.1.refs_0_), channel_id=1, source_target_pairs={{0,2},{1,3},{2,0},{3,1},{4,6},{5,7},{6,4},{7,5},{8,10},{9,11},{10,... | collective-permute-start | bytes 98312 | tf_op jit(solution)/shard_map/ppermute | solution.py:567
  10.9 5.1 %collective-permute-start.4 = (f32[2,2,16,128]{3,2,1,0:T(8,128)S(1)}, f32[2,2,16,128]{3,2,1,0:T(8,128)S(1)}, u32[]{:S(2)}, u32[]{:S(2)}) collective-permute-start(f32[2,2,16,128]{3,2,1,0:T(8,128)S(1)} %reference_pair.1.refs_0_), channel_id=1, source_target_pairs={{0,4},{1,5},{2,6},{3,7},{4,0},{5,1},{6,2},{7,3},{8,12},{9,13},{10,... | collective-permute-start | bytes 98312 | tf_op jit(solution)/shard_map/ppermute | solution.py:567
  13.5 5.7 %collective-permute-start.5 = (f32[2,2,16,128]{3,2,1,0:T(8,128)S(1)}, f32[2,2,16,128]{3,2,1,0:T(8,128)S(1)}, u32[]{:S(2)}, u32[]{:S(2)}) collective-permute-start(f32[2,2,16,128]{3,2,1,0:T(8,128)S(1)} %reference_pair.1.refs_0_), channel_id=1, source_target_pairs={{0,6},{1,7},{2,4},{3,5},{4,2},{5,3},{6,0},{7,1},{8,14},{9,15},{10,... | collective-permute-start | bytes 98312 | tf_op jit(solution)/shard_map/ppermute | solution.py:567
  22.1 12.1 %all-to-all-start = ((f32[8,10,8,128]{3,2,1,0:T(8,128)}), f32[8,10,8,128]{3,2,1,0:T(8,128)S(1)}, u32[]{:S(2)}, u32[]{:S(2)}) async-start(f32[8,10,8,128]{3,2,1,0:T(8,128)} %lag_products.1), calls=%async_computation | async-start | bytes 655360 | tf_op jit(solution)/shard_map/all_to_all | solution.py:598
  25.5 8.6 %copy-start = (bf16[2,128,512]{2,1,0:T(8,128)(2,1)S(1)}, bf16[2,128,512]{2,1,0:T(8,128)(2,1)}, u32[]{:S(2)}) copy-start(bf16[2,128,512]{2,1,0:T(8,128)(2,1)} %constant.2.clone.wave_ref) | copy-start | bytes 786436

commit v8 on v6

--- a/solution.py
+++ b/solution.py
@@ -15,6 +15,7 @@
 BLOCK_LEN = 256
 LANES = 128
 SUBLANES = 8
+EDGE = 2
 
 HIGHEST = lax.Precision.HIGHEST
 VMEM_BYTES = 48 * 1024 * 1024
@@ -68,15 +69,16 @@
     return outs
 
 
-CHUNKS = 4
-
-
-def beam_kernel(
-    chan_count, beams_local, w_hbm, s_hbm, ref_hbm, kept_ref, sent_ref, tiles_ref, w_ref, s_ref, ref_ref, w_sem, s_sem, ref_sem
+SPANS = 2
+CHUNKS = 2
+
+
+def beam_first_kernel(
+    chan_count, beams_local, w_hbm, s_hbm, kept_ref, sent_ref, later_ref, weights_ref, w_ref, s_ref, w_sem, s_sem, later_sem
 ):
     me = lax.axis_index("chan")
-    depth, length = s_hbm.shape
-    width = length // CHUNKS
+    span = s_ref.shape[1]
+    width = span // CHUNKS
     w_copy = pltpu.make_async_copy(w_hbm, w_ref, w_sem)
     w_copy.start()
     s_copies = []
@@ -84,8 +86,8 @@
         cols = pl.ds(n * width, width)
         s_copies.append(pltpu.make_async_copy(s_hbm.at[:, cols], s_ref.at[:, cols], s_sem.at[n]))
         s_copies[n].start()
-    ref_copy = pltpu.make_async_copy(ref_hbm, ref_ref, ref_sem)
-    ref_copy.start()
+    later_copy = pltpu.make_async_copy(s_hbm.at[:, pl.ds(span, later_ref.shape[1])], later_ref, later_sem)
+    later_copy.start()
     half = SUBLANES // 2
     sub = lax.broadcasted_iota(jnp.int32, (SUBLANES, w_hbm.shape[2]), 0)
     top = sub < half
@@ -105,6 +107,7 @@
                 rows.append(jnp.concatenate(first, 1))
                 rows.append(jnp.concatenate(second, 1))
     weights = halves(jnp.concatenate(rows, 0))
+    weights_ref[0], weights_ref[1] = weights
     mid = weights[0].shape[0] // 2
     for n in range(CHUNKS):
         cols = slice(n * width, (n + 1) * width)
@@ -112,67 +115,107 @@
         product = dot_split(weights, halves(s_ref[:, cols]))
         kept_ref[:, cols] = product[:mid]
         sent_ref[:, cols] = product[mid:]
-    ref_copy.wait()
-    for c in range(2):
-        for n in range(length // LANES):
-            tiles_ref[0, c, n : n + 1, :] = ref_ref[c : c + 1, n * LANES : (n + 1) * LANES]
-
-
-def beam_call(steering, survey, ref, chan_count, beams_local):
+    later_copy.wait()
+
+
+def beam_first_call(steering, survey, chan_count, beams_local):
     depth, length = survey.shape
+    span = length // SPANS
     rows = chan_count * beams_local
-    out = jax.ShapeDtypeStruct((rows, length), jnp.float32)
+    out = jax.ShapeDtypeStruct((rows, span), jnp.float32)
     hbm = pl.BlockSpec(memory_space=pltpu.HBM)
-    vmem = pl.BlockSpec(memory_space=pltpu.VMEM)
     return pl.pallas_call(
-        functools.partial(beam_kernel, chan_count, beams_local),
-        in_specs=[hbm, hbm, hbm],
-        out_specs=[vmem, vmem, vmem],
-        out_shape=[out, out, jax.ShapeDtypeStruct((1, 2, length // LANES, LANES), jnp.float32)],
+        functools.partial(beam_first_kernel, chan_count, beams_local),
+        in_specs=[hbm, hbm],
+        out_specs=[pl.BlockSpec(memory_space=pltpu.VMEM)] * 4,
+        out_shape=[
+            out,
+            out,
+            jax.ShapeDtypeStruct((depth, length - span), jnp.float32),
+            jax.ShapeDtypeStruct((2, 2 * rows, depth), jnp.bfloat16),
+        ],
         scratch_shapes=[
             pltpu.VMEM(steering.shape, jnp.float32),
-            pltpu.VMEM(survey.shape, jnp.float32),
-            pltpu.VMEM(ref.shape, jnp.float32),
+            pltpu.VMEM((depth, span), jnp.float32),
             pltpu.SemaphoreType.DMA,
             pltpu.SemaphoreType.DMA((CHUNKS,)),
             pltpu.SemaphoreType.DMA,
         ],
         compiler_params=params(),
         cost_estimate=pl.CostEstimate(
-            flops=12 * rows * depth * length, bytes_accessed=4 * length * (depth + 2 * rows), transcendentals=0
+            flops=12 * rows * depth * span, bytes_accessed=4 * length * (depth + rows), transcendentals=0
         ),
-        name="beams",
-    )(*(pltpu.with_memory_space_constraint(x, pltpu.HBM) for x in (steering, survey, ref)))
-
-
-def pair_kernel(tiles_ref, near_ref, out_ref):
-    out_ref[0] = tiles_ref[0]
+        name="beams_first",
+    )(*(pltpu.with_memory_space_constraint(x, pltpu.HBM) for x in (steering, survey)))
+
+
+def beam_later_kernel(later_ref, weights_ref, ref_hbm, kept_ref, sent_ref, tiles_ref, edge_ref, ref_ref, ref_sem):
+    ref_copy = pltpu.make_async_copy(ref_hbm, ref_ref, ref_sem)
+    ref_copy.start()
+    product = dot_split((weights_ref[0], weights_ref[1]), halves(later_ref[...]))
+    mid = product.shape[0] // 2
+    kept_ref[...] = product[:mid]
+    sent_ref[...] = product[mid:]
+    ref_copy.wait()
+    edge_ref[...] = jnp.zeros_like(edge_ref)
+    count = tiles_ref.shape[1]
     for c in range(2):
-        for n in range(tiles_ref.shape[2]):
+        for n in range(count):
+            row = ref_ref[c : c + 1, n * LANES : (n + 1) * LANES]
+            tiles_ref[c, n : n + 1, :] = row
+            if n >= count - EDGE:
+                at = SUBLANES * c + n + EDGE - count
+                edge_ref[at : at + 1, :] = row
+
+
+def beam_later_call(later, weights, ref):
+    depth, span = later.shape
+    rows = weights.shape[1] // 2
+    vmem = pl.BlockSpec(memory_space=pltpu.VMEM)
+    out = jax.ShapeDtypeStruct((rows, span), jnp.float32)
+    return pl.pallas_call(
+        beam_later_kernel,
+        in_specs=[vmem, vmem, pl.BlockSpec(memory_space=pltpu.HBM)],
+        out_specs=[vmem] * 4,
+        out_shape=[
+            out,
+            out,
+            jax.ShapeDtypeStruct((2, ref.shape[1] // LANES, LANES), jnp.float32),
+            jax.ShapeDtypeStruct((2 * SUBLANES, LANES), jnp.float32),
+        ],
+        scratch_shapes=[pltpu.VMEM(ref.shape, jnp.float32), pltpu.SemaphoreType.DMA],
+        compiler_params=params(),
+        cost_estimate=pl.CostEstimate(
+            flops=12 * rows * depth * span, bytes_accessed=4 * span * (depth + 2 * rows), transcendentals=0
+        ),
+        name="beams_later",
+    )(later, weights, pltpu.with_memory_space_constraint(ref, pltpu.HBM))
+
+
+def pair_kernel(tiles_ref, near_ref, _, out_ref):
+    out_ref[0] = tiles_ref[...]
+    for c in range(2):
+        for n in range(tiles_ref.shape[1]):
             out_ref[1, c, n : n + 1, :] = near_ref[c : c + 1, n * LANES : (n + 1) * LANES]
 
 
-def pair_call(tiles, near):
+def pair_call(tiles, near, after):
+    vmem = pl.BlockSpec(memory_space=pltpu.VMEM)
     return pl.pallas_call(
         pair_kernel,
-        out_shape=jax.ShapeDtypeStruct((2,) + tiles.shape[1:], jnp.float32),
+        in_specs=[vmem, vmem, pl.BlockSpec(memory_space=pl.ANY)],
+        out_shape=jax.ShapeDtypeStruct((2,) + tiles.shape, jnp.float32),
         compiler_params=params(),
         cost_estimate=pl.CostEstimate(flops=0, bytes_accessed=16 * near.size, transcendentals=0),
         name="reference_pair",
-    )(tiles, near)
-
-
-def table_kernel(*refs):
-    *part_refs, out_ref = refs
-    me = lax.axis_index("tm")
-    own = part_refs[0][0]
-    rows = own.shape[1]
-    edge = jnp.zeros((2, 2, LANES), jnp.float32)
-    for n, part_ref in enumerate(part_refs):
-        edge = jnp.where((me > 0) & ((me ^ (me - 1)) == 2 * n + 1), part_ref[1, :, rows - 2 :, :], edge)
+    )(tiles, near, after)
+
+
+def table_kernel(edge_ref, tiles_ref, out_ref):
+    rows = tiles_ref.shape[1]
     for c in range(2):
-        line = [edge[c, n : n + 1] for n in range(2)] + [own[c, n : n + 1] for n in range(rows)]
-        line = jnp.concatenate(line, 1)
+        line = [edge_ref[SUBLANES * c + n : SUBLANES * c + n + 1, :] for n in range(EDGE)]
+        line = jnp.concatenate(line + [tiles_ref[c, n : n + 1, :] for n in range(rows)], 1)
         for g in range(0, LANES, 2 * SUBLANES):
             tiled = jnp.broadcast_to(line, (2 * SUBLANES, line.shape[1]))
             high, low = halves(pltpu.roll(tiled, g, 1, stride=1, stride_axis=0)[:, LANES:])
@@ -180,8 +223,8 @@
             out_ref[1, c, g : g + 2 * SUBLANES] = low
 
 
-def table_call(parts):
-    shape = (2, 2, LANES, LANES * (parts[0].shape[2] + 1))
+def table_call(edge, tiles):
+    shape = (2, 2, LANES, LANES * (tiles.shape[1] + 1))
     return pl.pallas_call(
         table_kernel,
         out_shape=jax.ShapeDtypeStruct(shape, jnp.bfloat16),
@@ -190,15 +233,18 @@
             flops=8 * math.prod(shape), bytes_accessed=2 * math.prod(shape), transcendentals=0
         ),
         name="shifted_reference",
-    )(*parts)
-
-
-def lag_kernel(groups, owners, *refs):
-    *y_refs, table_ref, out_hbm, out_ref, out_sem = refs
+    )(edge, tiles)
+
+
+def lag_kernel(groups, part_count, first, blocks, *refs):
+    y_refs, table_ref, refs = refs[:part_count], refs[part_count], refs[part_count + 1 :]
+    if first:
+        before_ref, _, *refs = refs
+    out_hbm, after_ref, out_ref, out_sem = refs
     copies = []
 
-    def send(first, count):
-        part = (slice(None), pl.ds(first, count))
+    def send(start, count):
+        part = (slice(None), pl.ds(start, count))
         copies.append(pltpu.make_async_copy(out_ref.at[part], out_hbm.at[part], out_sem.at[len(copies)]))
         copies[-1].start()
 
@@ -206,7 +252,7 @@
     for y_ref in y_refs[1:]:
         y = y + y_ref[...]
     rows, length = y.shape
-    blocks = length // BLOCK_LEN
+    count = length // BLOCK_LEN
     turned = jnp.concatenate(
         [pltpu.roll(y[r : r + SUBLANES], SUBLANES // 2, 0) for r in range(0, rows, SUBLANES)], 0
     )
@@ -215,11 +261,12 @@
     t_high, t_low = halves(turned)
     both = jnp.concatenate([y_high, y_low], 0)
     turned_both = jnp.concatenate([t_high, t_low], 0)
-    taps_sum = None
-    for q in range(blocks):
+    taps_sum = before_ref[...] if first else None
+    for n in range(count):
+        q = first + n
         near = slice(q * BLOCK_LEN + LANES, q * BLOCK_LEN + LANES + BLOCK_LEN)
         far = slice(q * BLOCK_LEN, (q + 1) * BLOCK_LEN)
-        cols = slice(q * BLOCK_LEN, (q + 1) * BLOCK_LEN)
+        cols = slice(n * BLOCK_LEN, (n + 1) * BLOCK_LEN)
         tables = []
         for h in range(2):
             tables.append(
@@ -242,31 +289,45 @@
             tiles = [product[r : r + SUBLANES, lanes] for r in range(0, rows, SUBLANES)]
             for j, tile in enumerate(swap_groups(tiles, groups)):
                 out_ref[h * groups + j, q] = tile
-        if q % 2:
+        if n % 2:
             send(q - 1, 2)
-    left = lax.broadcasted_iota(jnp.int32, (SUBLANES, LANES), 1) < TAPS
-    for i in range(groups // 2):
-        a = taps_sum[i * SUBLANES : (i + 1) * SUBLANES]
-        other = i + groups // 2
-        b = taps_sum[other * SUBLANES : (other + 1) * SUBLANES]
-        tile = jnp.where(left, a, pltpu.roll(b, LANES - TAPS, 1))
-        for owner in range(owners):
-            out_ref[owner, blocks + i] = tile
-    send(blocks, groups // 2)
+    after_ref[...] = taps_sum
+    if first + count == blocks:
+        left = lax.broadcasted_iota(jnp.int32, (SUBLANES, LANES), 1) < TAPS
+        for i in range(groups // 2):
+            a = taps_sum[i * SUBLANES : (i + 1) * SUBLANES]
+            other = i + groups // 2
+            b = taps_sum[other * SUBLANES : (other + 1) * SUBLANES]
+            tile = jnp.where(left, a, pltpu.roll(b, LANES - TAPS, 1))
+            for owner in range(out_ref.shape[0]):
+                out_ref[owner, blocks + i] = tile
+        send(blocks, groups // 2)
     for copy in copies:
         copy.wait()
 
 
-def lag_call(ys, table, groups, owners):
+def lag_call(ys, table, groups, owners, first, blocks, before=None):
     rows, length = ys[0].shape
-    blocks = length // BLOCK_LEN
     shape = (owners, blocks + groups // 2, SUBLANES, LANES)
+    vmem, hbm = pl.BlockSpec(memory_space=pltpu.VMEM), pl.BlockSpec(memory_space=pltpu.HBM)
+    operands = [*ys, table]
+    in_specs = [vmem] * len(operands)
+    aliases = {}
+    if before is not None:
+        pieces, taps_sum = before
+        operands += [taps_sum, pieces]
+        in_specs += [vmem, hbm]
+        aliases = {len(operands) - 1: 0}
     return pl.pallas_call(
-        functools.partial(lag_kernel, groups, owners),
-        in_specs=[pl.BlockSpec(memory_space=pltpu.VMEM)] * (len(ys) + 1),
-        out_specs=pl.BlockSpec(memory_space=pltpu.HBM),
-        out_shape=jax.ShapeDtypeStruct(shape, jnp.float32),
-        scratch_shapes=[pltpu.VMEM(shape, jnp.float32), pltpu.SemaphoreType.DMA((blocks // 2 + 1,))],
+        functools.partial(lag_kernel, groups, len(ys), first, blocks),
+        in_specs=in_specs,
+        out_specs=[hbm, vmem],
+        out_shape=[jax.ShapeDtypeStruct(shape, jnp.float32), jax.ShapeDtypeStruct((rows, LANES), jnp.float32)],
+        input_output_aliases=aliases,
+        scratch_shapes=[
+            pltpu.VMEM(shape, jnp.float32),
+            pltpu.SemaphoreType.DMA((length // BLOCK_LEN // 2 + 1,)),
+        ],
         compiler_params=params(),
         cost_estimate=pl.CostEstimate(
             flops=12 * rows * LAGS * 2 * length,
@@ -274,15 +335,14 @@
             transcendentals=0,
         ),
         name="lag_products",
-    )(*ys, table)
+    )(*operands)
 
 
 BATCH = 4
-EDGE = 2
 
 
 def own_kernel(lags_local, *refs):
-    *part_refs, out_ref, line_ref, tail_ref, span_ref, late_ref, taps_a, lags_a, taps_b, lags_b = refs
+    *part_refs, _, out_ref, line_ref, tail_ref, span_ref, late_ref, taps_a, lags_a, taps_b, lags_b = refs
     me = lax.axis_index("tm")
     part_rows = part_refs[0].shape[2]
     owners = sum(part_ref.shape[0] for part_ref in part_refs)
@@ -366,7 +426,7 @@
     tail_ref[...] = dot_nt(tail, tail, HIGHEST)
 
 
-def own_call(parts, lags_local):
+def own_call(parts, lags_local, after):
     part_rows = parts[0].shape[2]
     span_rows = part_rows * sum(part.shape[0] for part in parts)
     rows = span_rows * LANES // BLOCK_LEN * lags_local
@@ -377,6 +437,7 @@
     span = pltpu.VMEM((2, held_rows, LANES), jnp.float32)
     return pl.pallas_call(
         functools.partial(own_kernel, lags_local),
+        in_specs=[pl.BlockSpec(memory_space=pltpu.VMEM)] * len(parts) + [pl.BlockSpec(memory_space=pl.ANY)],
         out_shape=[
             jax.ShapeDtypeStruct((2, rows, 2 * TAPS), jnp.bfloat16),
             jax.ShapeDtypeStruct((SUBLANES, 2 * TAPS), jnp.float32),
@@ -388,7 +449,7 @@
             flops=24 * rows * BLOCK_LEN * 2 * TAPS, bytes_accessed=4 * rows * 2 * TAPS, transcendentals=0
         ),
         name="reference_products",
-    )(*parts)
+    )(*parts, after)
 
 
 def as_factor(a):
@@ -546,23 +607,29 @@
 
     survey = surveillance.reshape(2 * channels, length)
     near = swap(ref_signal, "tm", 1)
-    kept, moved, tiles = beam_call(steering, survey, ref_signal, chan_count, beams_local)
-    shape = (chan_count // 2, 2 * beams_local, length)
-    parts = [kept.reshape(shape), swap(moved, "chan", 1).reshape(shape)]
-    pair = pair_call(tiles, near)
-    by = 2
-    while by < chan_count:
-        sent = parts[0][1::2]
-        for part in parts[1:]:
-            sent = sent + part[1::2]
-        pair, sent = lax.optimization_barrier((pair, sent))
-        parts = [part[::2] for part in parts] + [swap(sent, "chan", by)]
-        by *= 2
+    kept_first, sent_first, later, weights = beam_first_call(steering, survey, chan_count, beams_local)
+    kept_later, sent_later, tiles, edge = beam_later_call(later, weights, ref_signal)
+    edge = lax.ppermute(edge, "tm", [(i, i + 1) for i in range(tm_count - 1)])
+    shape = (chan_count // 2, 2 * beams_local, length // SPANS)
+    spans = []
+    for kept, moved in ((kept_first, sent_first), (kept_later, sent_later)):
+        parts = [kept.reshape(shape), swap(moved, "chan", 1).reshape(shape)]
+        by = 2
+        while by < chan_count:
+            sent = parts[0][1::2]
+            for part in parts[1:]:
+                sent = sent + part[1::2]
+            parts = [part[::2] for part in parts] + [swap(sent, "chan", by)]
+            by *= 2
+        spans.append([part[0] for part in parts])
+    pair = pair_call(tiles, near, sent)
     ref_parts = [pair] + [swap(pair, "tm", by) for by in range(2, tm_count, 2)]
-    table = table_call(ref_parts)
-    pieces = lag_call([part[0] for part in parts], table, groups, tm_count)
+    table = table_call(edge, tiles)
+    blocks = length // BLOCK_LEN
+    before = lag_call(spans[0], table, groups, tm_count, 0, blocks)
+    pieces, taps_sum = lag_call(spans[1], table, groups, tm_count, blocks // SPANS, blocks, before)
     got = lax.all_to_all(pieces, "tm", 0, 0, tiled=True)
-    own, line, tail = own_call(ref_parts, lags_local)
+    own, line, tail = own_call(ref_parts, lags_local, taps_sum)
     gram, solver = solver_call(line, tail)
     wave = doppler_table(samples // BLOCK_LEN, 0.125 / math.sqrt(samples))
     high = wave.astype(jnp.bfloat16)

time: 36.9 us -> 46.7 us (1.27)
  starting transfers between devices: 13 us -> 21.1 us
  Pallas kernels: 15.8 us -> 16.8 us
  waiting for transfers between devices: 7.71 us -> 8.25 us
    ppermute x0 -> x1, starting transfers between devices: none -> 3.41 us  [tiled_device(): edge = lax.ppermute(edge, 'tm', [(i, i + 1) for i in range(tm_count - 1)])]
    all_to_all x1, starting transfers between devices: 3.45 us -> 6.61 us  [tiled_device(): got = lax.all_to_all(pieces, 'tm', 0, 0, tiled=True)]
    ppermute x6 -> x8, starting transfers between devices: 9.55 us -> 11.1 us  [swap(): return lax.ppermute(x, axis, pairs)]
    ppermute x0 -> x1, waiting for transfers between devices: none -> 1.35 us  [tiled_device(): edge = lax.ppermute(edge, 'tm', [(i, i + 1) for i in range(tm_count - 1)])]
    pallas_call x4 -> x6, Pallas kernels: 10.6 us -> 11.6 us  [the longest x1 6.25 us: own_call(): pl.pallas_call(functools.partial(own_kernel, lags_local), in_specs=[pl.Bl...]
    ppermute x6 -> x8, waiting for transfers between devices: 7.43 us -> 6.89 us  [swap(): return lax.ppermute(x, axis, pairs)]
  transfers between devices with their start and end apart: 7 -> 10, of which waited for: 4 -> 5; matrix products, arithmetic and copies ran while one was open for 0% -> 0% of each run, Pallas kernels for 25% -> 24%
where the time goes in v8:
time: 46.7 us; the launch traced here: 46.4 us
  starting transfers between devices  21.1 us (45%)
  Pallas kernels  16.8 us (36%)
  waiting for transfers between devices  8.25 us (18%)
    ppermute x8, starting transfers between devices, swap(): return lax.ppermute(x, axis, pairs)  11.1 us
    ppermute x8, waiting for transfers between devices, swap(): return lax.ppermute(x, axis, pairs)  6.89 us
    all_to_all x1, starting transfers between devices, tiled_device(): got = lax.all_to_all(pieces, 'tm', 0, 0, tiled=True)  6.61 us
    pallas_call x1, Pallas kernels, own_call(): pl.pallas_call(functools.partial(own_kernel, lags_local), in_specs=[pl.Bl...  6.25 us
    ppermute x1, starting transfers between devices, tiled_device(): edge = lax.ppermute(edge, 'tm', [(i, i + 1) for i in range(tm_count - 1)])  3.41 us
    pallas_call x2, Pallas kernels, lag_call(): pl.pallas_call(functools.partial(lag_kernel, groups, len(ys), first, bloc...  3.02 us
    pallas_call x1, Pallas kernels, map_call(): pl.pallas_call(functools.partial(map_kernel, groups), in_specs=[pl.BlockS...  2.46 us
    pallas_call x1, Pallas kernels, solver_call(): pl.pallas_call(solver_kernel, out_shape=[out, out], compiler_params=param...  2.06 us
  transfers between devices with their start and end apart: 10, of which 5 were waited for; matrix products, arithmetic and copies ran while one was open for 0% of the time, Pallas kernels for 24%

profile of v8, /device:TPU:0, one launch (start us, length us, event | category | flops | bytes accessed | tf_op | source)
XLA Modules:
  0.0 46.4 jit_solution(14703563215514132464)
XLA Ops:
  0.0 1.5 %beams_first.1 = (f32[64,1024]{1,0:T(8,128)S(1)}, f32[64,1024]{1,0:T(8,128)S(1)}, f32[128,1024]{1,0:T(8,128)S(1)}, bf16[2,128,128]{2,1,0:T(8,128)(2,1)S(1)}) custom-call(f32[2,64,64]{2,1,0:T(8,128)} %w_hbm.1, f32[128,2048]{1,0:T(8,128)} %bitcast.9), custom_call_target="tpu_custom_call" | custom-call | flops 100663296 | bytes 1572864 | tf_op jit(solution)/shard_map/beams_first/pallas_call | solution.py:127
  1.5 0.5 %collective-permute-start.3 = (f32[64,1024]{1,0:T(8,128)S(1)}, f32[64,1024]{1,0:T(8,128)S(1)}, u32[]{:S(2)}, u32[]{:S(2)}) collective-permute-start(f32[64,1024]{1,0:T(8,128)S(1)} %get-tuple-element.29), channel_id=1, source_target_pairs={{0,8},{8,0},{16,24},{24,16},{1,9},{9,1},{17,25},{25,17},{2,10},{10... | collective-permute-start | bytes 786440 | tf_op jit(solution)/shard_map/ppermute | solution.py:597
  2.0 0.8 %beams_later.1 = (f32[64,1024]{1,0:T(8,128)S(1)}, f32[64,1024]{1,0:T(8,128)S(1)}, f32[2,16,128]{2,1,0:T(8,128)S(1)}, f32[16,128]{1,0:T(8,128)S(1)}) custom-call(f32[128,1024]{1,0:T(8,128)S(1)} %get-tuple-element.22.later_ref, bf16[2,128,128]{2,1,0:T(8,128)(2,1)S(1)} %get-tuple-element.23.weights_ref, f32[2,2048]{1,0:T(2,128)} %ref_hbm.1), custom_call_target="tpu_custom_call" | custom-call | flops 100663296 | bytes 1048576 | tf_op jit(solution)/shard_map/beams_later/pallas_call | solution.py:176
  2.9 0.1 collective-permute-start
  3.0 0.2 collective-permute-done.3
  3.2 2.9 %collective-permute-start.4 = (f32[1,32,1024]{2,1,0:T(8,128)S(1)}, f32[1,32,1024]{2,1,0:T(8,128)S(1)}, u32[]{:S(2)}, u32[]{:S(2)}) collective-permute-start(f32[1,32,1024]{2,1,0:T(8,128)S(1)} %get-tuple-element.39), channel_id=1, source_target_pairs={{0,16},{8,24},{16,0},{24,8},{1,17},{9,25},{17,1},{25,9},{2,18},{10... | collective-permute-start | bytes 393224 | tf_op jit(solution)/shard_map/ppermute | solution.py:597
  6.2 1.0 %collective-permute-start.1 = (f32[1,32,1024]{2,1,0:T(8,128)S(1)}, f32[1,32,1024]{2,1,0:T(8,128)S(1)}, u32[]{:S(2)}, u32[]{:S(2)}) collective-permute-start(f32[1,32,1024]{2,1,0:T(8,128)S(1)} %get-tuple-element.42._), channel_id=1, source_target_pairs={{0,16},{8,24},{16,0},{24,8},{1,17},{9,25},{17,1},{25,9},{2,18},{10... | collective-permute-start | bytes 393224 | tf_op jit(solution)/shard_map/ppermute | solution.py:597
  7.2 3.4 %collective-permute-start.2 = (f32[16,128]{1,0:T(8,128)S(1)}, f32[16,128]{1,0:T(8,128)S(1)}, u32[]{:S(2)}, u32[]{:S(2)}) collective-permute-start(f32[16,128]{1,0:T(8,128)S(1)} %get-tuple-element.26), channel_id=1, source_target_pairs={{0,1},{1,2},{2,3},{3,4},{4,5},{5,6},{6,7},{8,9},{9,10},{10,11},{11... | collective-permute-start | bytes 24584 | tf_op jit(solution)/shard_map/ppermute | solution.py:612
  10.7 1.3 %collective-permute-done.2.edge_ref = f32[16,128]{1,0:T(8,128)S(1)} collective-permute-done((f32[16,128]{1,0:T(8,128)S(1)}, f32[16,128]{1,0:T(8,128)S(1)}, u32[]{:S(2)}, u32[]{:S(2)}) %collective-permute-start.2) | collective-permute-done | bytes 8224 | tf_op jit(solution)/shard_map/ppermute | solution.py:612
  12.0 0.7 %shifted_reference.1.refs_3_ = bf16[2,2,128,2176]{3,2,1,0:T(8,128)(2,1)S(1)} custom-call(f32[16,128]{1,0:T(8,128)S(1)} %collective-permute-done.2.edge_ref, f32[2,16,128]{2,1,0:T(8,128)S(1)} %get-tuple-element.27.tiles_ref), custom_call_target="tpu_custom_call" | custom-call | flops 8912896 | bytes 2228224 | tf_op jit(solution)/shard_map/shifted_reference/pallas_call | solution.py:228
  12.7 1.5 %lag_products.2 = (f32[8,10,8,128]{3,2,1,0:T(8,128)}, f32[32,128]{1,0:T(8,128)S(1)}) custom-call(f32[32,1024]{1,0:T(8,128)S(1)} %get-tuple-element.40.refs_0_, f32[32,1024]{1,0:T(8,128)S(1)} %get-tuple-element.41.refs_1_, f32[32,1024]{1,0:T(8,128)S(1)} %bitcast.7, bf16[2,2,128,2176]{3,2,1,0:T(8,128)(2,1)S(1)} %shifted_reference.1.refs_3_), custom_call_target="tpu_custom_call" | custom-call | flops 201326592 | bytes 2555904 | tf_op jit(solution)/shard_map/lag_products/pallas_call | solution.py:321
  14.2 0.0 copy-start.1
  14.2 1.5 %lag_products.3 = (f32[8,10,8,128]{3,2,1,0:T(8,128)}, f32[32,128]{1,0:T(8,128)S(1)}) custom-call(f32[32,1024]{1,0:T(8,128)S(1)} %get-tuple-element.43.refs_0_, f32[32,1024]{1,0:T(8,128)S(1)} %get-tuple-element.44.refs_1_, f32[32,1024]{1,0:T(8,128)S(1)} %bitcast.8, ...), custom_call_target="tpu_custom_call", output_to_operand_aliasing={{0}: (5, {})} | custom-call | flops 201326592 | bytes 2555904 | tf_op jit(solution)/shard_map/lag_products/pallas_call | solution.py:321
  15.8 6.6 %all-to-all-start = ((f32[8,10,8,128]{3,2,1,0:T(8,128)}), f32[8,10,8,128]{3,2,1,0:T(8,128)S(1)}, u32[]{:S(2)}, u32[]{:S(2)}) async-start(f32[8,10,8,128]{3,2,1,0:T(8,128)} %get-tuple-element.32), calls=%async_computation | async-start | bytes 655360 | tf_op jit(solution)/shard_map/all_to_all | solution.py:631
  22.4 2.0 %collective-permute-start.5 = (f32[2,2048]{1,0:T(2,128)S(1)}, f32[2,2048]{1,0:T(2,128)S(1)}, u32[]{:S(2)}, u32[]{:S(2)}) collective-permute-start(f32[2,2048]{1,0:T(2,128)S(1)} %copy-done.1), channel_id=1, source_target_pairs={{0,1},{1,0},{2,3},{3,2},{4,5},{5,4},{6,7},{7,6},{8,9},{9,8},{10,11... | collective-permute-start | bytes 49160 | tf_op jit(solution)/shard_map/ppermute | solution.py:597
  24.4 2.6 %collective-permute-done.5.near_ref = f32[2,2048]{1,0:T(2,128)S(1)} collective-permute-done((f32[2,2048]{1,0:T(2,128)S(1)}, f32[2,2048]{1,0:T(2,128)S(1)}, u32[]{:S(2)}, u32[]{:S(2)}) %collective-permute-start.5) | collective-permute-done | bytes 16416 | tf_op jit(solution)/shard_map/ppermute | solution.py:597
  27.0 3.8 %collective-permute-start.8 = (f32[2,2,16,128]{3,2,1,0:T(8,128)S(1)}, f32[2,2,16,128]{3,2,1,0:T(8,128)S(1)}, u32[]{:S(2)}, u32[]{:S(2)}) collective-permute-start(f32[2,2,16,128]{3,2,1,0:T(8,128)S(1)} %reference_pair.1.refs_0_), channel_id=1, source_target_pairs={{0,6},{1,7},{2,4},{3,5},{4,2},{5,3},{6,0},{7,1},{8,14},{9,15},{10,... | collective-permute-start | bytes 98312 | tf_op jit(solution)/shard_map/ppermute | solution.py:597
  30.8 0.1 collective-permute-start.7
  30.8 0.6 %collective-permute-start.6 = (f32[2,2,16,128]{3,2,1,0:T(8,128)S(1)}, f32[2,2,16,128]{3,2,1,0:T(8,128)S(1)}, u32[]{:S(2)}, u32[]{:S(2)}) collective-permute-start(f32[2,2,16,128]{3,2,1,0:T(8,128)S(1)} %reference_pair.1.refs_0_), channel_id=1, source_target_pairs={{0,2},{1,3},{2,0},{3,1},{4,6},{5,7},{6,4},{7,5},{8,10},{9,11},{10,... | collective-permute-start | bytes 98312 | tf_op jit(solution)/shard_map/ppermute | solution.py:597
  31.4 1.6 %collective-permute-done.8.refs_3_ = f32[2,2,16,128]{3,2,1,0:T(8,128)S(1)} collective-permute-done((f32[2,2,16,128]{3,2,1,0:T(8,128)S(1)}, f32[2,2,16,128]{3,2,1,0:T(8,128)S(1)}, u32[]{:S(2)}, u32[]{:S(2)}) %collective-permute-start.8) | collective-permute-done | bytes 32800 | tf_op jit(solution)/shard_map/ppermute | solution.py:597
  33.1 2.5 %collective-permute-done.7.refs_2_ = f32[2,2,16,128]{3,2,1,0:T(8,128)S(1)} collective-permute-done((f32[2,2,16,128]{3,2,1,0:T(8,128)S(1)}, f32[2,2,16,128]{3,2,1,0:T(8,128)S(1)}, u32[]{:S(2)}, u32[]{:S(2)}) %collective-permute-start.7) | collective-permute-done | bytes 32800 | tf_op jit(solution)/shard_map/ppermute | solution.py:597
  35.6 6.2 %reference_products.1 = (bf16[2,2048,128]{2,1,0:T(8,128)(2,1)S(1)}, f32[8,128]{1,0:T(8,128)S(1)}, f32[128,128]{1,0:T(8,128)S(1)}) custom-call(f32[2,2,16,128]{3,2,1,0:T(8,128)S(1)} %reference_pair.1.refs_0_, f32[2,2,16,128]{3,2,1,0:T(8,128)S(1)} %collective-permute-done.6.refs_1_, f32[2,2,16,128]{3,2,1,0:T(8,128)S(1)} %collective-permute-done.7.refs_2_, ...), custom_call_target="tpu_custom_call" | custom-call | flops 1610612736 | bytes 1048576 | tf_op jit(solution)/shard_map/reference_products/pallas_call | solution.py:438
  41.8 2.1 %gram_inverse.1 = (bf16[2,128,128]{2,1,0:T(8,128)(2,1)S(1)}, bf16[2,128,128]{2,1,0:T(8,128)(2,1)S(1)}) custom-call(f32[8,128]{1,0:T(8,128)S(1)} %get-tuple-element.35.line_ref, f32[128,128]{1,0:T(8,128)S(1)} %get-tuple-element.36.tail_ref), custom_call_target="tpu_custom_call" | custom-call | flops 500000000 | bytes 200000 | tf_op jit(solution)/shard_map/gram_inverse/pallas_call | solution.py:507
  43.9 2.5 %range_doppler.1 = f32[16,2,32,256]{3,2,1,0:T(8,128)} custom-call(f32[8,10,8,128]{3,2,1,0:T(8,128)S(1)} %all-to-all-done.got_ref, bf16[2,2048,128]{2,1,0:T(8,128)(2,1)S(1)} %get-tuple-element.34.own_ref, bf16[2,128,128]{2,1,0:T(8,128)(2,1)S(1)} %get-tuple-element.37.gram_ref, bf16[2,128,128]{2,1,0:T(8,128)(2,1)S(1)} %get-tuple-element.38.solver_ref, ...), custom_call_target="tpu_custom_call" | custom-call | flops 201326592 | bytes 1048576 | tf_op jit(solution)/shard_map/range_doppler/pallas_call | solution.py:577
  (11 shorter events, 0.1 us)
Async XLA Ops:
  1.5 1.7 %collective-permute-start.3 = (f32[64,1024]{1,0:T(8,128)S(1)}, f32[64,1024]{1,0:T(8,128)S(1)}, u32[]{:S(2)}, u32[]{:S(2)}) collective-permute-start(f32[64,1024]{1,0:T(8,128)S(1)} %get-tuple-element.29), channel_id=1, source_target_pairs={{0,8},{8,0},{16,24},{24,16},{1,9},{9,1},{17,25},{25,17},{2,10},{10... | collective-permute-start | bytes 786440 | tf_op jit(solution)/shard_map/ppermute | solution.py:597
  2.9 3.3 %collective-permute-start = (f32[64,1024]{1,0:T(8,128)S(1)}, f32[64,1024]{1,0:T(8,128)S(1)}, u32[]{:S(2)}, u32[]{:S(2)}) collective-permute-start(f32[64,1024]{1,0:T(8,128)S(1)} %get-tuple-element.25), channel_id=1, source_target_pairs={{0,8},{8,0},{16,24},{24,16},{1,9},{9,1},{17,25},{25,17},{2,10},{10... | collective-permute-start | bytes 786440 | tf_op jit(solution)/shard_map/ppermute | solution.py:597
  3.2 9.4 %collective-permute-start.4 = (f32[1,32,1024]{2,1,0:T(8,128)S(1)}, f32[1,32,1024]{2,1,0:T(8,128)S(1)}, u32[]{:S(2)}, u32[]{:S(2)}) collective-permute-start(f32[1,32,1024]{2,1,0:T(8,128)S(1)} %get-tuple-element.39), channel_id=1, source_target_pairs={{0,16},{8,24},{16,0},{24,8},{1,17},{9,25},{17,1},{25,9},{2,18},{10... | collective-permute-start | bytes 393224 | tf_op jit(solution)/shard_map/ppermute | solution.py:597
  6.2 8.0 %collective-permute-start.1 = (f32[1,32,1024]{2,1,0:T(8,128)S(1)}, f32[1,32,1024]{2,1,0:T(8,128)S(1)}, u32[]{:S(2)}, u32[]{:S(2)}) collective-permute-start(f32[1,32,1024]{2,1,0:T(8,128)S(1)} %get-tuple-element.42._), channel_id=1, source_target_pairs={{0,16},{8,24},{16,0},{24,8},{1,17},{9,25},{17,1},{25,9},{2,18},{10... | collective-permute-start | bytes 393224 | tf_op jit(solution)/shard_map/ppermute | solution.py:597
  7.2 4.8 %collective-permute-start.2 = (f32[16,128]{1,0:T(8,128)S(1)}, f32[16,128]{1,0:T(8,128)S(1)}, u32[]{:S(2)}, u32[]{:S(2)}) collective-permute-start(f32[16,128]{1,0:T(8,128)S(1)} %get-tuple-element.26), channel_id=1, source_target_pairs={{0,1},{1,2},{2,3},{3,4},{4,5},{5,6},{6,7},{8,9},{9,10},{10,11},{11... | collective-permute-start | bytes 24584 | tf_op jit(solution)/shard_map/ppermute | solution.py:612
  14.2 8.2 %copy-start.1 = (f32[2,2048]{1,0:T(2,128)S(1)}, f32[2,2048]{1,0:T(2,128)}, u32[]{:S(2)}) copy-start(f32[2,2048]{1,0:T(2,128)} %ref_hbm.1) | copy-start | bytes 49156
  15.8 28.1 %all-to-all-start = ((f32[8,10,8,128]{3,2,1,0:T(8,128)}), f32[8,10,8,128]{3,2,1,0:T(8,128)S(1)}, u32[]{:S(2)}, u32[]{:S(2)}) async-start(f32[8,10,8,128]{3,2,1,0:T(8,128)} %get-tuple-element.32), calls=%async_computation | async-start | bytes 655360 | tf_op jit(solution)/shard_map/all_to_all | solution.py:631
  22.4 4.6 %collective-permute-start.5 = (f32[2,2048]{1,0:T(2,128)S(1)}, f32[2,2048]{1,0:T(2,128)S(1)}, u32[]{:S(2)}, u32[]{:S(2)}) collective-permute-start(f32[2,2048]{1,0:T(2,128)S(1)} %copy-done.1), channel_id=1, source_target_pairs={{0,1},{1,0},{2,3},{3,2},{4,5},{5,4},{6,7},{7,6},{8,9},{9,8},{10,11... | collective-permute-start | bytes 49160 | tf_op jit(solution)/shard_map/ppermute | solution.py:597
  27.0 6.1 %collective-permute-start.8 = (f32[2,2,16,128]{3,2,1,0:T(8,128)S(1)}, f32[2,2,16,128]{3,2,1,0:T(8,128)S(1)}, u32[]{:S(2)}, u32[]{:S(2)}) collective-permute-start(f32[2,2,16,128]{3,2,1,0:T(8,128)S(1)} %reference_pair.1.refs_0_), channel_id=1, source_target_pairs={{0,6},{1,7},{2,4},{3,5},{4,2},{5,3},{6,0},{7,1},{8,14},{9,15},{10,... | collective-permute-start | bytes 98312 | tf_op jit(solution)/shard_map/ppermute | solution.py:597
  30.8 4.8 %collective-permute-start.7 = (f32[2,2,16,128]{3,2,1,0:T(8,128)S(1)}, f32[2,2,16,128]{3,2,1,0:T(8,128)S(1)}, u32[]{:S(2)}, u32[]{:S(2)}) collective-permute-start(f32[2,2,16,128]{3,2,1,0:T(8,128)S(1)} %reference_pair.1.refs_0_), channel_id=1, source_target_pairs={{0,4},{1,5},{2,6},{3,7},{4,0},{5,1},{6,2},{7,3},{8,12},{9,13},{10,... | collective-permute-start | bytes 98312 | tf_op jit(solution)/shard_map/ppermute | solution.py:597
  30.8 4.8 %collective-permute-start.6 = (f32[2,2,16,128]{3,2,1,0:T(8,128)S(1)}, f32[2,2,16,128]{3,2,1,0:T(8,128)S(1)}, u32[]{:S(2)}, u32[]{:S(2)}) collective-permute-start(f32[2,2,16,128]{3,2,1,0:T(8,128)S(1)} %reference_pair.1.refs_0_), channel_id=1, source_target_pairs={{0,2},{1,3},{2,0},{3,1},{4,6},{5,7},{6,4},{7,5},{8,10},{9,11},{10,... | collective-permute-start | bytes 98312 | tf_op jit(solution)/shard_map/ppermute | solution.py:597
  35.6 8.3 %copy-start = (bf16[2,128,512]{2,1,0:T(8,128)(2,1)S(1)}, bf16[2,128,512]{2,1,0:T(8,128)(2,1)}, u32[]{:S(2)}) copy-start(bf16[2,128,512]{2,1,0:T(8,128)(2,1)} %constant.2.clone.wave_ref) | copy-start | bytes 786436

commit v9 on v8

--- a/solution.py
+++ b/solution.py
@@ -23,6 +23,10 @@
 
 def params():
     return pltpu.CompilerParams(vmem_limit_bytes=VMEM_BYTES)
+
+
+def cost(us):
+    return pl.CostEstimate(flops=int(us * 1.15e9), bytes_accessed=0, transcendentals=0)
 
 
 def halves(x):
@@ -142,9 +146,7 @@
             pltpu.SemaphoreType.DMA,
         ],
         compiler_params=params(),
-        cost_estimate=pl.CostEstimate(
-            flops=12 * rows * depth * span, bytes_accessed=4 * length * (depth + rows), transcendentals=0
-        ),
+        cost_estimate=cost(1.5),
         name="beams_first",
     )(*(pltpu.with_memory_space_constraint(x, pltpu.HBM) for x in (steering, survey)))
 
@@ -185,18 +187,39 @@
         ],
         scratch_shapes=[pltpu.VMEM(ref.shape, jnp.float32), pltpu.SemaphoreType.DMA],
         compiler_params=params(),
-        cost_estimate=pl.CostEstimate(
-            flops=12 * rows * depth * span, bytes_accessed=4 * span * (depth + 2 * rows), transcendentals=0
-        ),
+        cost_estimate=cost(0.9),
         name="beams_later",
     )(later, weights, pltpu.with_memory_space_constraint(ref, pltpu.HBM))
 
 
+def sum_kernel(count, *refs):
+    kept_ref, sent_ref = refs[-2:]
+    for n in range(kept_ref.shape[0]):
+        for offset, out_ref in ((0, kept_ref), (1, sent_ref)):
+            total = refs[0][2 * n + offset]
+            for ref in refs[1:count]:
+                total = total + ref[2 * n + offset]
+            out_ref[n] = total
+
+
+def sum_call(parts, after):
+    shape = (parts[0].shape[0] // 2,) + parts[0].shape[1:]
+    out = jax.ShapeDtypeStruct(shape, jnp.float32)
+    vmem = pl.BlockSpec(memory_space=pltpu.VMEM)
+    return pl.pallas_call(
+        functools.partial(sum_kernel, len(parts)),
+        in_specs=[vmem] * len(parts) + [pl.BlockSpec(memory_space=pl.ANY)] * len(after),
+        out_specs=[vmem, vmem],
+        out_shape=[out, out],
+        compiler_params=params(),
+        cost_estimate=cost(0.1),
+        name="halves_summed",
+    )(*parts, *after)
+
+
 def pair_kernel(tiles_ref, near_ref, _, out_ref):
     out_ref[0] = tiles_ref[...]
-    for c in range(2):
-        for n in range(tiles_ref.shape[1]):
-            out_ref[1, c, n : n + 1, :] = near_ref[c : c + 1, n * LANES : (n + 1) * LANES]
+    out_ref[1] = near_ref[...]
 
 
 def pair_call(tiles, near, after):
@@ -206,7 +229,7 @@
         in_specs=[vmem, vmem, pl.BlockSpec(memory_space=pl.ANY)],
         out_shape=jax.ShapeDtypeStruct((2,) + tiles.shape, jnp.float32),
         compiler_params=params(),
-        cost_estimate=pl.CostEstimate(flops=0, bytes_accessed=16 * near.size, transcendentals=0),
+        cost_estimate=cost(0.1),
         name="reference_pair",
     )(tiles, near, after)
 
@@ -229,18 +252,13 @@
         table_kernel,
         out_shape=jax.ShapeDtypeStruct(shape, jnp.bfloat16),
         compiler_params=params(),
-        cost_estimate=pl.CostEstimate(
-            flops=8 * math.prod(shape), bytes_accessed=2 * math.prod(shape), transcendentals=0
-        ),
+        cost_estimate=cost(0.7),
         name="shifted_reference",
     )(edge, tiles)
 
 
-def lag_kernel(groups, part_count, first, blocks, *refs):
-    y_refs, table_ref, refs = refs[:part_count], refs[part_count], refs[part_count + 1 :]
-    if first:
-        before_ref, _, *refs = refs
-    out_hbm, after_ref, out_ref, out_sem = refs
+def lag_kernel(groups, spans, *refs):
+    *y_refs, table_ref, _, out_hbm, out_ref, out_sem = refs
     copies = []
 
     def send(start, count):
@@ -248,11 +266,16 @@
         copies.append(pltpu.make_async_copy(out_ref.at[part], out_hbm.at[part], out_sem.at[len(copies)]))
         copies[-1].start()
 
-    y = y_refs[0][...]
-    for y_ref in y_refs[1:]:
-        y = y + y_ref[...]
+    count = len(y_refs) // spans
+    parts = []
+    for n in range(spans):
+        part = y_refs[n * count][...]
+        for y_ref in y_refs[n * count + 1 : (n + 1) * count]:
+            part = part + y_ref[...]
+        parts.append(part)
+    y = jnp.concatenate(parts, 1)
     rows, length = y.shape
-    count = length // BLOCK_LEN
+    blocks = length // BLOCK_LEN
     turned = jnp.concatenate(
         [pltpu.roll(y[r : r + SUBLANES], SUBLANES // 2, 0) for r in range(0, rows, SUBLANES)], 0
     )
@@ -261,12 +284,11 @@
     t_high, t_low = halves(turned)
     both = jnp.concatenate([y_high, y_low], 0)
     turned_both = jnp.concatenate([t_high, t_low], 0)
-    taps_sum = before_ref[...] if first else None
-    for n in range(count):
-        q = first + n
+    taps_sum = None
+    for q in range(blocks):
         near = slice(q * BLOCK_LEN + LANES, q * BLOCK_LEN + LANES + BLOCK_LEN)
         far = slice(q * BLOCK_LEN, (q + 1) * BLOCK_LEN)
-        cols = slice(n * BLOCK_LEN, (n + 1) * BLOCK_LEN)
+        cols = slice(q * BLOCK_LEN, (q + 1) * BLOCK_LEN)
         tables = []
         for h in range(2):
             tables.append(
@@ -289,53 +311,35 @@
             tiles = [product[r : r + SUBLANES, lanes] for r in range(0, rows, SUBLANES)]
             for j, tile in enumerate(swap_groups(tiles, groups)):
                 out_ref[h * groups + j, q] = tile
-        if n % 2:
+        if q % 2:
             send(q - 1, 2)
-    after_ref[...] = taps_sum
-    if first + count == blocks:
-        left = lax.broadcasted_iota(jnp.int32, (SUBLANES, LANES), 1) < TAPS
-        for i in range(groups // 2):
-            a = taps_sum[i * SUBLANES : (i + 1) * SUBLANES]
-            other = i + groups // 2
-            b = taps_sum[other * SUBLANES : (other + 1) * SUBLANES]
-            tile = jnp.where(left, a, pltpu.roll(b, LANES - TAPS, 1))
-            for owner in range(out_ref.shape[0]):
-                out_ref[owner, blocks + i] = tile
-        send(blocks, groups // 2)
+    left = lax.broadcasted_iota(jnp.int32, (SUBLANES, LANES), 1) < TAPS
+    for i in range(groups // 2):
+        a = taps_sum[i * SUBLANES : (i + 1) * SUBLANES]
+        other = i + groups // 2
+        b = taps_sum[other * SUBLANES : (other + 1) * SUBLANES]
+        tile = jnp.where(left, a, pltpu.roll(b, LANES - TAPS, 1))
+        for owner in range(out_ref.shape[0]):
+            out_ref[owner, blocks + i] = tile
+    send(blocks, groups // 2)
     for copy in copies:
         copy.wait()
 
 
-def lag_call(ys, table, groups, owners, first, blocks, before=None):
-    rows, length = ys[0].shape
+def lag_call(ys, spans, table, after, groups, owners):
+    blocks = spans * ys[0].shape[1] // BLOCK_LEN
     shape = (owners, blocks + groups // 2, SUBLANES, LANES)
-    vmem, hbm = pl.BlockSpec(memory_space=pltpu.VMEM), pl.BlockSpec(memory_space=pltpu.HBM)
-    operands = [*ys, table]
-    in_specs = [vmem] * len(operands)
-    aliases = {}
-    if before is not None:
-        pieces, taps_sum = before
-        operands += [taps_sum, pieces]
-        in_specs += [vmem, hbm]
-        aliases = {len(operands) - 1: 0}
-    return pl.pallas_call(
-        functools.partial(lag_kernel, groups, len(ys), first, blocks),
-        in_specs=in_specs,
-        out_specs=[hbm, vmem],
-        out_shape=[jax.ShapeDtypeStruct(shape, jnp.float32), jax.ShapeDtypeStruct((rows, LANES), jnp.float32)],
-        input_output_aliases=aliases,
-        scratch_shapes=[
-            pltpu.VMEM(shape, jnp.float32),
-            pltpu.SemaphoreType.DMA((length // BLOCK_LEN // 2 + 1,)),
-        ],
-        compiler_params=params(),
-        cost_estimate=pl.CostEstimate(
-            flops=12 * rows * LAGS * 2 * length,
-            bytes_accessed=4 * math.prod(shape) + 2 * math.prod(table.shape),
-            transcendentals=0,
-        ),
+    vmem = pl.BlockSpec(memory_space=pltpu.VMEM)
+    return pl.pallas_call(
+        functools.partial(lag_kernel, groups, spans),
+        in_specs=[vmem] * (len(ys) + 1) + [pl.BlockSpec(memory_space=pl.ANY)],
+        out_specs=pl.BlockSpec(memory_space=pltpu.HBM),
+        out_shape=jax.ShapeDtypeStruct(shape, jnp.float32),
+        scratch_shapes=[pltpu.VMEM(shape, jnp.float32), pltpu.SemaphoreType.DMA((blocks // 2 + 1,))],
+        compiler_params=params(),
+        cost_estimate=cost(2.1),
         name="lag_products",
-    )(*operands)
+    )(*ys, table, after)
 
 
 BATCH = 4
@@ -445,9 +449,7 @@
         ],
         scratch_shapes=[span, span, taps, lags, taps, lags],
         compiler_params=params(),
-        cost_estimate=pl.CostEstimate(
-            flops=24 * rows * BLOCK_LEN * 2 * TAPS, bytes_accessed=4 * rows * 2 * TAPS, transcendentals=0
-        ),
+        cost_estimate=cost(6.2),
         name="reference_products",
     )(*parts, after)
 
@@ -508,7 +510,7 @@
         solver_kernel,
         out_shape=[out, out],
         compiler_params=params(),
-        cost_estimate=pl.CostEstimate(flops=500_000_000, bytes_accessed=200_000, transcendentals=0),
+        cost_estimate=cost(2.0),
         name="gram_inverse",
     )(line, tail)
 
@@ -585,9 +587,7 @@
             pltpu.SemaphoreType.DMA((beams_local,)),
         ],
         compiler_params=params(),
-        cost_estimate=pl.CostEstimate(
-            flops=12 * math.prod(shape) * total, bytes_accessed=4 * math.prod(shape), transcendentals=0
-        ),
+        cost_estimate=cost(2.5),
         name="range_doppler",
     )(got, own, gram, solver, wave)
 
@@ -606,30 +606,28 @@
     samples = length * tm_count
 
     survey = surveillance.reshape(2 * channels, length)
-    near = swap(ref_signal, "tm", 1)
     kept_first, sent_first, later, weights = beam_first_call(steering, survey, chan_count, beams_local)
     kept_later, sent_later, tiles, edge = beam_later_call(later, weights, ref_signal)
+    near = swap(tiles, "tm", 1)
     edge = lax.ppermute(edge, "tm", [(i, i + 1) for i in range(tm_count - 1)])
     shape = (chan_count // 2, 2 * beams_local, length // SPANS)
-    spans = []
+    ys = []
+    after = []
     for kept, moved in ((kept_first, sent_first), (kept_later, sent_later)):
-        parts = [kept.reshape(shape), swap(moved, "chan", 1).reshape(shape)]
+        kept, sent = kept.reshape(shape), swap(moved, "chan", 1).reshape(shape)
         by = 2
         while by < chan_count:
-            sent = parts[0][1::2]
-            for part in parts[1:]:
-                sent = sent + part[1::2]
-            parts = [part[::2] for part in parts] + [swap(sent, "chan", by)]
+            kept, moved = sum_call([kept, sent], after)
+            sent = swap(moved, "chan", by)
             by *= 2
-        spans.append([part[0] for part in parts])
-    pair = pair_call(tiles, near, sent)
+        after = [near, edge]
+        ys += [kept[0], sent[0]]
+    pair = pair_call(tiles, near, moved)
     ref_parts = [pair] + [swap(pair, "tm", by) for by in range(2, tm_count, 2)]
     table = table_call(edge, tiles)
-    blocks = length // BLOCK_LEN
-    before = lag_call(spans[0], table, groups, tm_count, 0, blocks)
-    pieces, taps_sum = lag_call(spans[1], table, groups, tm_count, blocks // SPANS, blocks, before)
+    pieces = lag_call(ys, SPANS, table, pair, groups, tm_count)
     got = lax.all_to_all(pieces, "tm", 0, 0, tiled=True)
-    own, line, tail = own_call(ref_parts, lags_local, taps_sum)
+    own, line, tail = own_call(ref_parts, lags_local, pieces)
     gram, solver = solver_call(line, tail)
     wave = doppler_table(samples // BLOCK_LEN, 0.125 / math.sqrt(samples))
     high = wave.astype(jnp.bfloat16)

time: 46.7 us -> 37.7 us (0.81)
  waiting for transfers between devices: 8.25 us -> 0.34 us
  Pallas kernels: 16.8 us -> 16 us
    ppermute x8, waiting for transfers between devices: 6.89 us -> 0.02 us  [swap(): return lax.ppermute(x, axis, pairs)]
    ppermute x8, starting transfers between devices: 11.1 us -> 13.9 us  [swap(): return lax.ppermute(x, axis, pairs)]
    ppermute x1, starting transfers between devices: 3.41 us -> 1.9 us  [tiled_device(): edge = lax.ppermute(edge, 'tm', [(i, i + 1) for i in range(tm_count - 1)])]
    all_to_all x1, starting transfers between devices: 6.61 us -> 5.11 us  [tiled_device(): got = lax.all_to_all(pieces, 'tm', 0, 0, tiled=True)]
    ppermute x1, waiting for transfers between devices: 1.35 us -> 0.01 us  [tiled_device(): edge = lax.ppermute(edge, 'tm', [(i, i + 1) for i in range(tm_count - 1)])]
    pallas_call x2 -> x3, Pallas kernels: 3.02 us -> 2.22 us  [the longest x1 2.16 us: lag_call(): pl.pallas_call(functools.partial(lag_kernel, groups, spans), in_specs=[vm...]
  transfers between devices with their start and end apart: 10 -> 10, of which waited for: 5 -> 1; matrix products, arithmetic and copies ran while one was open for 0% -> 0% of each run, Pallas kernels for 24% -> 32%
where the time goes in v9:
time: 37.7 us; the launch traced here: 37.4 us
  starting transfers between devices  20.9 us (55%)
  Pallas kernels  16 us (42%)
    ppermute x8, starting transfers between devices, swap(): return lax.ppermute(x, axis, pairs)  13.9 us
    pallas_call x1, Pallas kernels, own_call(): pl.pallas_call(functools.partial(own_kernel, lags_local), in_specs=[pl.Bl...  6.25 us
    all_to_all x1, starting transfers between devices, tiled_device(): got = lax.all_to_all(pieces, 'tm', 0, 0, tiled=True)  5.11 us
    pallas_call x1, Pallas kernels, map_call(): pl.pallas_call(functools.partial(map_kernel, groups), in_specs=[pl.BlockS...  2.47 us
    pallas_call x1, Pallas kernels, lag_call(): pl.pallas_call(functools.partial(lag_kernel, groups, spans), in_specs=[vm...  2.16 us
    pallas_call x1, Pallas kernels, solver_call(): pl.pallas_call(solver_kernel, out_shape=[out, out], compiler_params=param...  2.05 us
    ppermute x1, starting transfers between devices, tiled_device(): edge = lax.ppermute(edge, 'tm', [(i, i + 1) for i in range(tm_count - 1)])  1.9 us
    pallas_call x1, Pallas kernels, beam_first_call(): pl.pallas_call(functools.partial(beam_first_kernel, chan_count, beams_loc...  1.51 us
  transfers between devices with their start and end apart: 10, of which 1 were waited for; matrix products, arithmetic and copies ran while one was open for 0% of the time, Pallas kernels for 32%

profile of v9, /device:TPU:0, one launch (start us, length us, event | category | flops | bytes accessed | tf_op | source)
XLA Modules:
  0.0 37.4 jit_solution(8755799510733479584)
XLA Ops:
  0.0 1.5 %beams_first.1 = (f32[64,1024]{1,0:T(8,128)S(1)}, f32[64,1024]{1,0:T(8,128)S(1)}, f32[128,1024]{1,0:T(8,128)S(1)}, bf16[2,128,128]{2,1,0:T(8,128)(2,1)S(1)}) custom-call(f32[2,64,64]{2,1,0:T(8,128)} %w_hbm.1, f32[128,2048]{1,0:T(8,128)} %bitcast.17), custom_call_target="tpu_custom_call" | custom-call | flops 1724999936 | tf_op jit(solution)/shard_map/beams_first/pallas_call | solution.py:131
  1.5 0.5 %collective-permute-start = (f32[64,1024]{1,0:T(8,128)S(1)}, f32[64,1024]{1,0:T(8,128)S(1)}, u32[]{:S(2)}, u32[]{:S(2)}) collective-permute-start(f32[64,1024]{1,0:T(8,128)S(1)} %get-tuple-element.23), channel_id=1, source_target_pairs={{0,8},{8,0},{16,24},{24,16},{1,9},{9,1},{17,25},{25,17},{2,10},{10... | collective-permute-start | bytes 786440 | tf_op jit(solution)/shard_map/ppermute | solution.py:597
  2.0 0.8 %beams_later.1 = (f32[64,1024]{1,0:T(8,128)S(1)}, f32[64,1024]{1,0:T(8,128)S(1)}, f32[2,16,128]{2,1,0:T(8,128)S(1)}, f32[16,128]{1,0:T(8,128)S(1)}) custom-call(f32[128,1024]{1,0:T(8,128)S(1)} %get-tuple-element.26.later_ref, bf16[2,128,128]{2,1,0:T(8,128)(2,1)S(1)} %get-tuple-element.27.weights_ref, f32[2,2048]{1,0:T(2,128)} %ref_hbm.1), custom_call_target="tpu_custom_call" | custom-call | flops 1035000000 | tf_op jit(solution)/shard_map/beams_later/pallas_call | solution.py:178
  2.9 0.1 collective-permute-start.2
  3.0 3.0 %collective-permute-start.3 = (f32[2,16,128]{2,1,0:T(8,128)S(1)}, f32[2,16,128]{2,1,0:T(8,128)S(1)}, u32[]{:S(2)}, u32[]{:S(2)}) collective-permute-start(f32[2,16,128]{2,1,0:T(8,128)S(1)} %get-tuple-element.30.tiles_ref), channel_id=1, source_target_pairs={{0,1},{1,0},{2,3},{3,2},{4,5},{5,4},{6,7},{7,6},{8,9},{9,8},{10,11... | collective-permute-start | bytes 49160 | tf_op jit(solution)/shard_map/ppermute | solution.py:597
  6.0 1.9 %collective-permute-start.4 = (f32[16,128]{1,0:T(8,128)S(1)}, f32[16,128]{1,0:T(8,128)S(1)}, u32[]{:S(2)}, u32[]{:S(2)}) collective-permute-start(f32[16,128]{1,0:T(8,128)S(1)} %get-tuple-element.31), channel_id=1, source_target_pairs={{0,1},{1,2},{2,3},{3,4},{4,5},{5,6},{6,7},{8,9},{9,10},{10,11},{11... | collective-permute-start | bytes 24584 | tf_op jit(solution)/shard_map/ppermute | solution.py:612
  7.9 0.0 collective-permute-done
  7.9 2.1 %collective-permute-start.1 = (f32[1,32,1024]{2,1,0:T(8,128)S(1)}, f32[1,32,1024]{2,1,0:T(8,128)S(1)}, u32[]{:S(2)}, u32[]{:S(2)}) collective-permute-start(f32[1,32,1024]{2,1,0:T(8,128)S(1)} %get-tuple-element.25), channel_id=1, source_target_pairs={{0,16},{8,24},{16,0},{24,8},{1,17},{9,25},{17,1},{25,9},{2,18},{10... | collective-permute-start | bytes 393224 | tf_op jit(solution)/shard_map/ppermute | solution.py:597
  10.0 0.0 collective-permute-done.4.refs_3_.edge_ref
  10.0 0.0 collective-permute-done.3.refs_2_.near_ref
  10.0 0.0 collective-permute-done.2
  10.0 1.3 %collective-permute-start.5 = (f32[1,32,1024]{2,1,0:T(8,128)S(1)}, f32[1,32,1024]{2,1,0:T(8,128)S(1)}, u32[]{:S(2)}, u32[]{:S(2)}) collective-permute-start(f32[1,32,1024]{2,1,0:T(8,128)S(1)} %get-tuple-element.33._), channel_id=1, source_target_pairs={{0,16},{8,24},{16,0},{24,8},{1,17},{9,25},{17,1},{25,9},{2,18},{10... | collective-permute-start | bytes 393224 | tf_op jit(solution)/shard_map/ppermute | solution.py:597
  11.3 0.7 %shifted_reference.1.refs_4_ = bf16[2,2,128,2176]{3,2,1,0:T(8,128)(2,1)S(1)} custom-call(f32[16,128]{1,0:T(8,128)S(1)} %collective-permute-done.4.refs_3_.edge_ref, f32[2,16,128]{2,1,0:T(8,128)S(1)} %get-tuple-element.30.tiles_ref), custom_call_target="tpu_custom_call" | custom-call | flops 805000000 | tf_op jit(solution)/shard_map/shifted_reference/pallas_call | solution.py:251
  12.0 4.3 %collective-permute-start.6 = (f32[2,2,16,128]{3,2,1,0:T(8,128)S(1)}, f32[2,2,16,128]{3,2,1,0:T(8,128)S(1)}, u32[]{:S(2)}, u32[]{:S(2)}) collective-permute-start(f32[2,2,16,128]{3,2,1,0:T(8,128)S(1)} %reference_pair.1.refs_5_.refs_0_), channel_id=1, source_target_pairs={{0,2},{1,3},{2,0},{3,1},{4,6},{5,7},{6,4},{7,5},{8,10},{9,11},{10,... | collective-permute-start | bytes 98312 | tf_op jit(solution)/shard_map/ppermute | solution.py:597
  16.4 2.6 %collective-permute-start.7 = (f32[2,2,16,128]{3,2,1,0:T(8,128)S(1)}, f32[2,2,16,128]{3,2,1,0:T(8,128)S(1)}, u32[]{:S(2)}, u32[]{:S(2)}) collective-permute-start(f32[2,2,16,128]{3,2,1,0:T(8,128)S(1)} %reference_pair.1.refs_5_.refs_0_), channel_id=1, source_target_pairs={{0,4},{1,5},{2,6},{3,7},{4,0},{5,1},{6,2},{7,3},{8,12},{9,13},{10,... | collective-permute-start | bytes 98312 | tf_op jit(solution)/shard_map/ppermute | solution.py:597
  18.9 0.0 collective-permute-done.5
  19.0 2.2 %lag_products.1.refs_4_ = f32[8,10,8,128]{3,2,1,0:T(8,128)} custom-call(f32[32,1024]{1,0:T(8,128)S(1)} %bitcast.13, f32[32,1024]{1,0:T(8,128)S(1)} %bitcast.14, f32[32,1024]{1,0:T(8,128)S(1)} %bitcast.15, f32[32,1024]{1,0:T(8,128)S(1)} %bitcast.16, bf16[2,2,128,2176]{3,2,1,0:T(8,128)(2,1)S(1)} %shifted_reference.1.refs_4_, ...), custom_call_target="tpu_custom_call" | custom-call | flops 2415000064 | tf_op jit(solution)/shard_map/lag_products/pallas_call | solution.py:333
  21.1 5.1 %all-to-all-start = ((f32[8,10,8,128]{3,2,1,0:T(8,128)}), f32[8,10,8,128]{3,2,1,0:T(8,128)S(1)}, u32[]{:S(2)}, u32[]{:S(2)}) async-start(f32[8,10,8,128]{3,2,1,0:T(8,128)} %lag_products.1.refs_4_), calls=%async_computation | async-start | bytes 655360 | tf_op jit(solution)/shard_map/all_to_all | solution.py:629
  26.2 0.0 collective-permute-done.7.refs_2_
  26.3 6.3 %reference_products.1 = (bf16[2,2048,128]{2,1,0:T(8,128)(2,1)S(1)}, f32[8,128]{1,0:T(8,128)S(1)}, f32[128,128]{1,0:T(8,128)S(1)}) custom-call(f32[2,2,16,128]{3,2,1,0:T(8,128)S(1)} %reference_pair.1.refs_5_.refs_0_, f32[2,2,16,128]{3,2,1,0:T(8,128)S(1)} %collective-permute-done.6.refs_1_, f32[2,2,16,128]{3,2,1,0:T(8,128)S(1)} %collective-permute-done.7.refs_2_, ...), custom_call_target="tpu_custom_call" | custom-call | flops 7129999872 | tf_op jit(solution)/shard_map/reference_products/pallas_call | solution.py:442
  32.5 0.0 copy-start
  32.5 2.0 %gram_inverse.1 = (bf16[2,128,128]{2,1,0:T(8,128)(2,1)S(1)}, bf16[2,128,128]{2,1,0:T(8,128)(2,1)S(1)}) custom-call(f32[8,128]{1,0:T(8,128)S(1)} %get-tuple-element.35.line_ref, f32[128,128]{1,0:T(8,128)S(1)} %get-tuple-element.36.tail_ref), custom_call_target="tpu_custom_call" | custom-call | flops 2300000000 | tf_op jit(solution)/shard_map/gram_inverse/pallas_call | solution.py:509
  34.6 0.3 all-to-all-done.got_ref
  34.9 2.5 %range_doppler.1 = f32[16,2,32,256]{3,2,1,0:T(8,128)} custom-call(f32[8,10,8,128]{3,2,1,0:T(8,128)S(1)} %all-to-all-done.got_ref, bf16[2,2048,128]{2,1,0:T(8,128)(2,1)S(1)} %get-tuple-element.34.own_ref, bf16[2,128,128]{2,1,0:T(8,128)(2,1)S(1)} %get-tuple-element.37.gram_ref, bf16[2,128,128]{2,1,0:T(8,128)(2,1)S(1)} %get-tuple-element.38.solver_ref, ...), custom_call_target="tpu_custom_call" | custom-call | flops 2875000064 | tf_op jit(solution)/shard_map/range_doppler/pallas_call | solution.py:579
  (8 shorter events, 0.1 us)
Async XLA Ops:
  1.5 6.4 %collective-permute-start = (f32[64,1024]{1,0:T(8,128)S(1)}, f32[64,1024]{1,0:T(8,128)S(1)}, u32[]{:S(2)}, u32[]{:S(2)}) collective-permute-start(f32[64,1024]{1,0:T(8,128)S(1)} %get-tuple-element.23), channel_id=1, source_target_pairs={{0,8},{8,0},{16,24},{24,16},{1,9},{9,1},{17,25},{25,17},{2,10},{10... | collective-permute-start | bytes 786440 | tf_op jit(solution)/shard_map/ppermute | solution.py:597
  2.9 7.1 %collective-permute-start.2 = (f32[64,1024]{1,0:T(8,128)S(1)}, f32[64,1024]{1,0:T(8,128)S(1)}, u32[]{:S(2)}, u32[]{:S(2)}) collective-permute-start(f32[64,1024]{1,0:T(8,128)S(1)} %get-tuple-element.29), channel_id=1, source_target_pairs={{0,8},{8,0},{16,24},{24,16},{1,9},{9,1},{17,25},{25,17},{2,10},{10... | collective-permute-start | bytes 786440 | tf_op jit(solution)/shard_map/ppermute | solution.py:597
  3.0 7.0 %collective-permute-start.3 = (f32[2,16,128]{2,1,0:T(8,128)S(1)}, f32[2,16,128]{2,1,0:T(8,128)S(1)}, u32[]{:S(2)}, u32[]{:S(2)}) collective-permute-start(f32[2,16,128]{2,1,0:T(8,128)S(1)} %get-tuple-element.30.tiles_ref), channel_id=1, source_target_pairs={{0,1},{1,0},{2,3},{3,2},{4,5},{5,4},{6,7},{7,6},{8,9},{9,8},{10,11... | collective-permute-start | bytes 49160 | tf_op jit(solution)/shard_map/ppermute | solution.py:597
  6.0 4.0 %collective-permute-start.4 = (f32[16,128]{1,0:T(8,128)S(1)}, f32[16,128]{1,0:T(8,128)S(1)}, u32[]{:S(2)}, u32[]{:S(2)}) collective-permute-start(f32[16,128]{1,0:T(8,128)S(1)} %get-tuple-element.31), channel_id=1, source_target_pairs={{0,1},{1,2},{2,3},{3,4},{4,5},{5,6},{6,7},{8,9},{9,10},{10,11},{11... | collective-permute-start | bytes 24584 | tf_op jit(solution)/shard_map/ppermute | solution.py:612
  7.9 11.0 %collective-permute-start.1 = (f32[1,32,1024]{2,1,0:T(8,128)S(1)}, f32[1,32,1024]{2,1,0:T(8,128)S(1)}, u32[]{:S(2)}, u32[]{:S(2)}) collective-permute-start(f32[1,32,1024]{2,1,0:T(8,128)S(1)} %get-tuple-element.25), channel_id=1, source_target_pairs={{0,16},{8,24},{16,0},{24,8},{1,17},{9,25},{17,1},{25,9},{2,18},{10... | collective-permute-start | bytes 393224 | tf_op jit(solution)/shard_map/ppermute | solution.py:597
  10.0 8.9 %collective-permute-start.5 = (f32[1,32,1024]{2,1,0:T(8,128)S(1)}, f32[1,32,1024]{2,1,0:T(8,128)S(1)}, u32[]{:S(2)}, u32[]{:S(2)}) collective-permute-start(f32[1,32,1024]{2,1,0:T(8,128)S(1)} %get-tuple-element.33._), channel_id=1, source_target_pairs={{0,16},{8,24},{16,0},{24,8},{1,17},{9,25},{17,1},{25,9},{2,18},{10... | collective-permute-start | bytes 393224 | tf_op jit(solution)/shard_map/ppermute | solution.py:597
  12.0 14.2 %collective-permute-start.6 = (f32[2,2,16,128]{3,2,1,0:T(8,128)S(1)}, f32[2,2,16,128]{3,2,1,0:T(8,128)S(1)}, u32[]{:S(2)}, u32[]{:S(2)}) collective-permute-start(f32[2,2,16,128]{3,2,1,0:T(8,128)S(1)} %reference_pair.1.refs_5_.refs_0_), channel_id=1, source_target_pairs={{0,2},{1,3},{2,0},{3,1},{4,6},{5,7},{6,4},{7,5},{8,10},{9,11},{10,... | collective-permute-start | bytes 98312 | tf_op jit(solution)/shard_map/ppermute | solution.py:597
  16.4 9.9 %collective-permute-start.7 = (f32[2,2,16,128]{3,2,1,0:T(8,128)S(1)}, f32[2,2,16,128]{3,2,1,0:T(8,128)S(1)}, u32[]{:S(2)}, u32[]{:S(2)}) collective-permute-start(f32[2,2,16,128]{3,2,1,0:T(8,128)S(1)} %reference_pair.1.refs_5_.refs_0_), channel_id=1, source_target_pairs={{0,4},{1,5},{2,6},{3,7},{4,0},{5,1},{6,2},{7,3},{8,12},{9,13},{10,... | collective-permute-start | bytes 98312 | tf_op jit(solution)/shard_map/ppermute | solution.py:597
  18.9 7.3 %collective-permute-start.8 = (f32[2,2,16,128]{3,2,1,0:T(8,128)S(1)}, f32[2,2,16,128]{3,2,1,0:T(8,128)S(1)}, u32[]{:S(2)}, u32[]{:S(2)}) collective-permute-start(f32[2,2,16,128]{3,2,1,0:T(8,128)S(1)} %reference_pair.1.refs_5_.refs_0_), channel_id=1, source_target_pairs={{0,6},{1,7},{2,4},{3,5},{4,2},{5,3},{6,0},{7,1},{8,14},{9,15},{10,... | collective-permute-start | bytes 98312 | tf_op jit(solution)/shard_map/ppermute | solution.py:597
  21.1 13.8 %all-to-all-start = ((f32[8,10,8,128]{3,2,1,0:T(8,128)}), f32[8,10,8,128]{3,2,1,0:T(8,128)S(1)}, u32[]{:S(2)}, u32[]{:S(2)}) async-start(f32[8,10,8,128]{3,2,1,0:T(8,128)} %lag_products.1.refs_4_), calls=%async_computation | async-start | bytes 655360 | tf_op jit(solution)/shard_map/all_to_all | solution.py:629
  32.5 2.4 %copy-start = (bf16[2,128,512]{2,1,0:T(8,128)(2,1)S(1)}, bf16[2,128,512]{2,1,0:T(8,128)(2,1)}, u32[]{:S(2)}) copy-start(bf16[2,128,512]{2,1,0:T(8,128)(2,1)} %constant.2.clone.wave_ref) | copy-start | bytes 786436

commit v10 on v5

--- a/solution.py
+++ b/solution.py
@@ -15,6 +15,7 @@
 BLOCK_LEN = 256
 LANES = 128
 SUBLANES = 8
+EDGE = 2
 
 HIGHEST = lax.Precision.HIGHEST
 VMEM_BYTES = 48 * 1024 * 1024
@@ -22,6 +23,10 @@
 
 def params():
     return pltpu.CompilerParams(vmem_limit_bytes=VMEM_BYTES)
+
+
+def cost(us):
+    return pl.CostEstimate(flops=int(us * 1.15e9), bytes_accessed=0, transcendentals=0)
 
 
 def halves(x):
@@ -72,20 +77,21 @@
 
 
 def beam_kernel(
-    chan_count, beams_local, w_hbm, s_hbm, ref_hbm, kept_ref, sent_ref, tiles_ref, w_ref, s_ref, ref_ref, w_sem, s_sem, ref_sem
+    chan_count, beams_local, w_hbm, s_hbm, ref_hbm, kept_ref, sent_ref, tiles_ref, edge_ref, spread_hbm,
+    w_ref, s_ref, ref_ref, w_sem, s_sem, ref_sem, spread_sem,
 ):
     me = lax.axis_index("chan")
-    depth, length = s_hbm.shape
+    length = s_hbm.shape[1]
     width = length // CHUNKS
     w_copy = pltpu.make_async_copy(w_hbm, w_ref, w_sem)
     w_copy.start()
+    ref_copy = pltpu.make_async_copy(ref_hbm, ref_ref, ref_sem)
+    ref_copy.start()
     s_copies = []
     for n in range(CHUNKS):
         cols = pl.ds(n * width, width)
         s_copies.append(pltpu.make_async_copy(s_hbm.at[:, cols], s_ref.at[:, cols], s_sem.at[n]))
         s_copies[n].start()
-    ref_copy = pltpu.make_async_copy(ref_hbm, ref_ref, ref_sem)
-    ref_copy.start()
     half = SUBLANES // 2
     sub = lax.broadcasted_iota(jnp.int32, (SUBLANES, w_hbm.shape[2]), 0)
     top = sub < half
@@ -105,6 +111,20 @@
                 rows.append(jnp.concatenate(first, 1))
                 rows.append(jnp.concatenate(second, 1))
     weights = halves(jnp.concatenate(rows, 0))
+    ref_copy.wait()
+    edge_ref[...] = jnp.zeros_like(edge_ref)
+    count = tiles_ref.shape[1]
+    for c in range(2):
+        for n in range(count):
+            row = ref_ref[c : c + 1, n * LANES : (n + 1) * LANES]
+            tiles_ref[c, n : n + 1, :] = row
+            if n >= count - EDGE:
+                at = SUBLANES * c + n + EDGE - count
+                edge_ref[at : at + 1, :] = row
+    copies = []
+    for n in range(spread_hbm.shape[0]):
+        copies.append(pltpu.make_async_copy(tiles_ref, spread_hbm.at[n], spread_sem.at[n]))
+        copies[n].start()
     mid = weights[0].shape[0] // 2
     for n in range(CHUNKS):
         cols = slice(n * width, (n + 1) * width)
@@ -112,23 +132,27 @@
         product = dot_split(weights, halves(s_ref[:, cols]))
         kept_ref[:, cols] = product[:mid]
         sent_ref[:, cols] = product[mid:]
-    ref_copy.wait()
-    for c in range(2):
-        for n in range(length // LANES):
-            tiles_ref[0, c, n : n + 1, :] = ref_ref[c : c + 1, n * LANES : (n + 1) * LANES]
-
-
-def beam_call(steering, survey, ref, chan_count, beams_local):
+    for copy in copies:
+        copy.wait()
+
+
+def beam_call(steering, survey, ref, owners, chan_count, beams_local):
     depth, length = survey.shape
     rows = chan_count * beams_local
+    tiles = (2, length // LANES, LANES)
     out = jax.ShapeDtypeStruct((rows, length), jnp.float32)
-    hbm = pl.BlockSpec(memory_space=pltpu.HBM)
-    vmem = pl.BlockSpec(memory_space=pltpu.VMEM)
+    hbm, vmem = pl.BlockSpec(memory_space=pltpu.HBM), pl.BlockSpec(memory_space=pltpu.VMEM)
     return pl.pallas_call(
         functools.partial(beam_kernel, chan_count, beams_local),
-        in_specs=[hbm, hbm, hbm],
-        out_specs=[vmem, vmem, vmem],
-        out_shape=[out, out, jax.ShapeDtypeStruct((1, 2, length // LANES, LANES), jnp.float32)],
+        in_specs=[hbm] * 3,
+        out_specs=[vmem] * 4 + [hbm],
+        out_shape=[
+            out,
+            out,
+            jax.ShapeDtypeStruct(tiles, jnp.float32),
+            jax.ShapeDtypeStruct((2 * SUBLANES, LANES), jnp.float32),
+            jax.ShapeDtypeStruct((owners,) + tiles, jnp.float32),
+        ],
         scratch_shapes=[
             pltpu.VMEM(steering.shape, jnp.float32),
             pltpu.VMEM(survey.shape, jnp.float32),
@@ -136,27 +160,61 @@
             pltpu.SemaphoreType.DMA,
             pltpu.SemaphoreType.DMA((CHUNKS,)),
             pltpu.SemaphoreType.DMA,
+            pltpu.SemaphoreType.DMA((owners,)),
         ],
         compiler_params=params(),
-        cost_estimate=pl.CostEstimate(
-            flops=12 * rows * depth * length, bytes_accessed=4 * length * (depth + 2 * rows), transcendentals=0
-        ),
+        cost_estimate=cost(2.2),
         name="beams",
     )(*(pltpu.with_memory_space_constraint(x, pltpu.HBM) for x in (steering, survey, ref)))
 
 
-def table_kernel(*refs):
-    *part_refs, out_ref = refs
-    me = lax.axis_index("tm")
-    own = part_refs[0][0]
-    rows = own.shape[1]
-    edge = jnp.zeros((2, 2, LANES), jnp.float32)
-    for n, part_ref in enumerate(part_refs[1:], 1):
-        last = part_ref[part_ref.shape[0] - 1, :, rows - 2 :, :]
-        edge = jnp.where((me > 0) & ((me ^ (me - 1)) == 2**n - 1), last, edge)
+def hold_kernel(*refs):
+    del refs
+
+
+def hold_call(x, *after):
+    return pl.pallas_call(
+        hold_kernel,
+        in_specs=[pl.BlockSpec(memory_space=pltpu.HBM)] + [pl.BlockSpec(memory_space=pl.ANY)] * len(after),
+        out_specs=pl.BlockSpec(memory_space=pltpu.HBM),
+        out_shape=jax.ShapeDtypeStruct(x.shape, x.dtype),
+        input_output_aliases={0: 0},
+        compiler_params=params(),
+        cost_estimate=cost(0.1),
+        name="reference_held",
+    )(x, *after)
+
+
+def sum_kernel(count, *refs):
+    kept_ref, sent_ref = refs[-2:]
+    for n in range(kept_ref.shape[0]):
+        for offset, out_ref in ((0, kept_ref), (1, sent_ref)):
+            total = refs[0][2 * n + offset]
+            for ref in refs[1:count]:
+                total = total + ref[2 * n + offset]
+            out_ref[n] = total
+
+
+def sum_call(parts):
+    shape = (parts[0].shape[0] // 2,) + parts[0].shape[1:]
+    out = jax.ShapeDtypeStruct(shape, jnp.float32)
+    vmem = pl.BlockSpec(memory_space=pltpu.VMEM)
+    return pl.pallas_call(
+        functools.partial(sum_kernel, len(parts)),
+        in_specs=[vmem] * len(parts),
+        out_specs=[vmem, vmem],
+        out_shape=[out, out],
+        compiler_params=params(),
+        cost_estimate=cost(0.1),
+        name="halves_summed",
+    )(*parts)
+
+
+def table_kernel(edge_ref, tiles_ref, out_ref):
+    rows = tiles_ref.shape[1]
     for c in range(2):
-        line = [edge[c, n : n + 1] for n in range(2)] + [own[c, n : n + 1] for n in range(rows)]
-        line = jnp.concatenate(line, 1)
+        line = [edge_ref[SUBLANES * c + n : SUBLANES * c + n + 1, :] for n in range(EDGE)]
+        line = jnp.concatenate(line + [tiles_ref[c, n : n + 1, :] for n in range(rows)], 1)
         for g in range(0, LANES, 2 * SUBLANES):
             tiled = jnp.broadcast_to(line, (2 * SUBLANES, line.shape[1]))
             high, low = halves(pltpu.roll(tiled, g, 1, stride=1, stride_axis=0)[:, LANES:])
@@ -164,25 +222,23 @@
             out_ref[1, c, g : g + 2 * SUBLANES] = low
 
 
-def table_call(parts):
-    shape = (2, 2, LANES, LANES * (parts[0].shape[2] + 1))
+def table_call(edge, tiles):
+    shape = (2, 2, LANES, LANES * (tiles.shape[1] + 1))
     return pl.pallas_call(
         table_kernel,
         out_shape=jax.ShapeDtypeStruct(shape, jnp.bfloat16),
         compiler_params=params(),
-        cost_estimate=pl.CostEstimate(
-            flops=8 * math.prod(shape), bytes_accessed=2 * math.prod(shape), transcendentals=0
-        ),
+        cost_estimate=cost(0.7),
         name="shifted_reference",
-    )(*parts)
-
-
-def lag_kernel(groups, owners, *refs):
-    *y_refs, table_ref, out_hbm, out_ref, out_sem = refs
+    )(edge, tiles)
+
+
+def lag_kernel(groups, *refs):
+    *y_refs, table_ref, _, out_hbm, out_ref, out_sem = refs
     copies = []
 
-    def send(first, count):
-        part = (slice(None), pl.ds(first, count))
+    def send(start, count):
+        part = (slice(None), pl.ds(start, count))
         copies.append(pltpu.make_async_copy(out_ref.at[part], out_hbm.at[part], out_sem.at[len(copies)]))
         copies[-1].start()
 
@@ -234,53 +290,44 @@
         other = i + groups // 2
         b = taps_sum[other * SUBLANES : (other + 1) * SUBLANES]
         tile = jnp.where(left, a, pltpu.roll(b, LANES - TAPS, 1))
-        for owner in range(owners):
+        for owner in range(out_ref.shape[0]):
             out_ref[owner, blocks + i] = tile
     send(blocks, groups // 2)
     for copy in copies:
         copy.wait()
 
 
-def lag_call(ys, table, groups, owners):
-    rows, length = ys[0].shape
-    blocks = length // BLOCK_LEN
+def lag_call(ys, table, after, groups, owners):
+    blocks = ys[0].shape[1] // BLOCK_LEN
     shape = (owners, blocks + groups // 2, SUBLANES, LANES)
-    return pl.pallas_call(
-        functools.partial(lag_kernel, groups, owners),
-        in_specs=[pl.BlockSpec(memory_space=pltpu.VMEM)] * (len(ys) + 1),
+    vmem = pl.BlockSpec(memory_space=pltpu.VMEM)
+    return pl.pallas_call(
+        functools.partial(lag_kernel, groups),
+        in_specs=[vmem] * (len(ys) + 1) + [pl.BlockSpec(memory_space=pl.ANY)],
         out_specs=pl.BlockSpec(memory_space=pltpu.HBM),
         out_shape=jax.ShapeDtypeStruct(shape, jnp.float32),
         scratch_shapes=[pltpu.VMEM(shape, jnp.float32), pltpu.SemaphoreType.DMA((blocks // 2 + 1,))],
         compiler_params=params(),
-        cost_estimate=pl.CostEstimate(
-            flops=12 * rows * LAGS * 2 * length,
-            bytes_accessed=4 * math.prod(shape) + 2 * math.prod(table.shape),
-            transcendentals=0,
-        ),
+        cost_estimate=cost(2.1),
         name="lag_products",
-    )(*ys, table)
+    )(*ys, table, after)
 
 
 BATCH = 4
-EDGE = 2
 
 
 def own_kernel(lags_local, *refs):
-    *part_refs, out_ref, line_ref, tail_ref, span_ref, late_ref, taps_a, lags_a, taps_b, lags_b = refs
+    ref_ref, _, out_ref, line_ref, tail_ref, span_ref, late_ref, taps_a, lags_a, taps_b, lags_b = refs
     me = lax.axis_index("tm")
-    part_rows = part_refs[0].shape[2]
-    owners = sum(part_ref.shape[0] for part_ref in part_refs)
+    owners, _, part_rows, _ = ref_ref.shape
     samples = owners * part_rows * LANES
     steps = samples // BLOCK_LEN // BATCH
     total_rows = span_ref.shape[1]
     block_rows = BLOCK_LEN // LANES
 
     span_ref[...] = jnp.zeros_like(span_ref)
-    e = 0
-    for part_ref in part_refs:
-        for i in range(part_ref.shape[0]):
-            span_ref[:, pl.ds(EDGE + (me ^ e) * part_rows, part_rows), :] = part_ref[i]
-            e += 1
+    for t in range(owners):
+        span_ref[:, EDGE + t * part_rows : EDGE + (t + 1) * part_rows, :] = ref_ref[t]
     late_rows = (me * lags_local) // LANES
     late_lanes = lax.rem(me * lags_local, LANES)
     turned = [pltpu.roll(span_ref[c], late_lanes, 1) for c in range(2)]
@@ -350,9 +397,8 @@
     tail_ref[...] = dot_nt(tail, tail, HIGHEST)
 
 
-def own_call(parts, lags_local):
-    part_rows = parts[0].shape[2]
-    span_rows = part_rows * sum(part.shape[0] for part in parts)
+def own_call(ref_all, lags_local, after):
+    span_rows = ref_all.shape[0] * ref_all.shape[2]
     rows = span_rows * LANES // BLOCK_LEN * lags_local
     held_rows = -(-(span_rows + 2 * EDGE) // SUBLANES) * SUBLANES
     width = BATCH * BLOCK_LEN
@@ -361,6 +407,7 @@
     span = pltpu.VMEM((2, held_rows, LANES), jnp.float32)
     return pl.pallas_call(
         functools.partial(own_kernel, lags_local),
+        in_specs=[pl.BlockSpec(memory_space=pltpu.VMEM), pl.BlockSpec(memory_space=pl.ANY)],
         out_shape=[
             jax.ShapeDtypeStruct((2, rows, 2 * TAPS), jnp.bfloat16),
             jax.ShapeDtypeStruct((SUBLANES, 2 * TAPS), jnp.float32),
@@ -368,11 +415,9 @@
         ],
         scratch_shapes=[span, span, taps, lags, taps, lags],
         compiler_params=params(),
-        cost_estimate=pl.CostEstimate(
-            flops=24 * rows * BLOCK_LEN * 2 * TAPS, bytes_accessed=4 * rows * 2 * TAPS, transcendentals=0
-        ),
+        cost_estimate=cost(6.2),
         name="reference_products",
-    )(*parts)
+    )(ref_all, after)
 
 
 def as_factor(a):
@@ -431,7 +476,7 @@
         solver_kernel,
         out_shape=[out, out],
         compiler_params=params(),
-        cost_estimate=pl.CostEstimate(flops=500_000_000, bytes_accessed=200_000, transcendentals=0),
+        cost_estimate=cost(2.0),
         name="gram_inverse",
     )(line, tail)
 
@@ -508,9 +553,7 @@
             pltpu.SemaphoreType.DMA((beams_local,)),
         ],
         compiler_params=params(),
-        cost_estimate=pl.CostEstimate(
-            flops=12 * math.prod(shape) * total, bytes_accessed=4 * math.prod(shape), transcendentals=0
-        ),
+        cost_estimate=cost(2.5),
         name="range_doppler",
     )(got, own, gram, solver, wave)
 
@@ -529,27 +572,21 @@
     samples = length * tm_count
 
     survey = surveillance.reshape(2 * channels, length)
-    kept, moved, tiles = beam_call(steering, survey, ref_signal, chan_count, beams_local)
+    kept, moved, tiles, edge, spread = beam_call(steering, survey, ref_signal, tm_count, chan_count, beams_local)
+    edge = lax.ppermute(edge, "tm", [(i, i + 1) for i in range(tm_count - 1)])
     shape = (chan_count // 2, 2 * beams_local, length)
-    parts = [kept.reshape(shape), swap(moved, "chan", 1).reshape(shape)]
-    near = swap(tiles, "tm", 1)
+    kept, got = kept.reshape(shape), swap(moved, "chan", 1).reshape(shape)
     by = 2
     while by < chan_count:
-        sent = parts[0][1::2]
-        for part in parts[1:]:
-            sent = sent + part[1::2]
-        tiles, sent = lax.optimization_barrier((tiles, sent))
-        parts = [part[::2] for part in parts] + [swap(sent, "chan", by)]
+        kept, moved = sum_call([kept, got])
+        got = swap(moved, "chan", by)
         by *= 2
-    ref_parts = [tiles, near]
-    by = 2
-    while by < tm_count:
-        ref_parts.append(swap(jnp.concatenate(ref_parts, 0), "tm", by))
-        by *= 2
-    table = table_call(ref_parts)
-    pieces = lag_call([part[0] for part in parts], table, groups, tm_count)
+    spread = hold_call(spread, moved, edge)
+    ref_all = lax.all_to_all(spread, "tm", 0, 0, tiled=True)
+    table = table_call(edge, tiles)
+    pieces = lag_call([kept[0], got[0]], table, spread, groups, tm_count)
     got = lax.all_to_all(pieces, "tm", 0, 0, tiled=True)
-    own, line, tail = own_call(ref_parts, lags_local)
+    own, line, tail = own_call(ref_all, lags_local, pieces)
     gram, solver = solver_call(line, tail)
     wave = doppler_table(samples // BLOCK_LEN, 0.125 / math.sqrt(samples))
     high = wave.astype(jnp.bfloat16)

time: 37.2 us -> 40.9 us (1.099)
  waiting for transfers between devices: 4.72 us -> 7.67 us
  starting transfers between devices: 16.4 us -> 16.9 us
    all_to_all x0 -> x1, starting transfers between devices: none -> 6.6 us  [tiled_device(): ref_all = lax.all_to_all(spread, 'tm', 0, 0, tiled=True)]
    ppermute x5 -> x2, starting transfers between devices: 9.69 us -> 3.44 us  [swap(): return lax.ppermute(x, axis, pairs)]
    all_to_all x0 -> x1, waiting for transfers between devices: none -> 4.48 us  [tiled_device(): ref_all = lax.all_to_all(spread, 'tm', 0, 0, tiled=True)]
    ppermute x0 -> x1, starting transfers between devices: none -> 3.41 us  [tiled_device(): edge = lax.ppermute(edge, 'tm', [(i, i + 1) for i in range(tm_count - 1)])]
    all_to_all x1, starting transfers between devices: 6.71 us -> 3.43 us  [tiled_device(): got = lax.all_to_all(pieces, 'tm', 0, 0, tiled=True)]
    ppermute x5 -> x2, waiting for transfers between devices: 4.37 us -> 1.54 us  [swap(): return lax.ppermute(x, axis, pairs)]
    ppermute x0 -> x1, waiting for transfers between devices: none -> 1.35 us  [tiled_device(): edge = lax.ppermute(edge, 'tm', [(i, i + 1) for i in range(tm_count - 1)])]
    pallas_call x2 -> x4, Pallas kernels: 8.41 us -> 8.46 us  [the longest x1 6.24 us: own_call(): pl.pallas_call(functools.partial(own_kernel, lags_local), in_specs=[pl.Bl...]
  transfers between devices with their start and end apart: 6 -> 5, of which waited for: 3 -> 4; matrix products, arithmetic and copies ran while one was open for 0% -> 0% of each run, Pallas kernels for 24% -> 27%
where the time goes in v10:
time: 40.9 us; the launch traced here: 40.5 us
  starting transfers between devices  16.9 us (41%)
  Pallas kernels  15.9 us (39%)
  waiting for transfers between devices  7.67 us (19%)
    all_to_all x1, starting transfers between devices, tiled_device(): ref_all = lax.all_to_all(spread, 'tm', 0, 0, tiled=True)  6.6 us
    pallas_call x1, Pallas kernels, own_call(): pl.pallas_call(functools.partial(own_kernel, lags_local), in_specs=[pl.Bl...  6.24 us
    all_to_all x1, waiting for transfers between devices, tiled_device(): ref_all = lax.all_to_all(spread, 'tm', 0, 0, tiled=True)  4.48 us
    ppermute x2, starting transfers between devices, swap(): return lax.ppermute(x, axis, pairs)  3.44 us
    all_to_all x1, starting transfers between devices, tiled_device(): got = lax.all_to_all(pieces, 'tm', 0, 0, tiled=True)  3.43 us
    ppermute x1, starting transfers between devices, tiled_device(): edge = lax.ppermute(edge, 'tm', [(i, i + 1) for i in range(tm_count - 1)])  3.41 us
    pallas_call x1, Pallas kernels, map_call(): pl.pallas_call(functools.partial(map_kernel, groups), in_specs=[pl.BlockS...  2.46 us
    pallas_call x1, Pallas kernels, beam_call(): pl.pallas_call(functools.partial(beam_kernel, chan_count, beams_local), i...  2.25 us
  transfers between devices with their start and end apart: 5, of which 4 were waited for; matrix products, arithmetic and copies ran while one was open for 0% of the time, Pallas kernels for 27%

profile of v10, /device:TPU:0, one launch (start us, length us, event | category | flops | bytes accessed | tf_op | source)
XLA Modules:
  0.0 40.5 jit_solution(14869705067652275778)
XLA Ops:
  0.0 2.3 %beams.1 = (f32[64,2048]{1,0:T(8,128)S(1)}, f32[64,2048]{1,0:T(8,128)S(1)}, f32[2,16,128]{2,1,0:T(8,128)S(1)}, f32[16,128]{1,0:T(8,128)S(1)}, f32[8,2,16,128]{3,2,1,0:T(8,128)}) custom-call(f32[2,64,64]{2,1,0:T(8,128)} %w_hbm.1, f32[128,2048]{1,0:T(8,128)} %bitcast.9, f32[2,2048]{1,0:T(2,128)} %ref_hbm.1), custom_call_target="tpu_custom_call" | custom-call | flops 2529999872 | tf_op jit(solution)/shard_map/beams/pallas_call | solution.py:145
  2.3 0.5 %collective-permute-start = (f32[64,2048]{1,0:T(8,128)S(1)}, f32[64,2048]{1,0:T(8,128)S(1)}, u32[]{:S(2)}, u32[]{:S(2)}) collective-permute-start(f32[64,2048]{1,0:T(8,128)S(1)} %get-tuple-element.18), channel_id=1, source_target_pairs={{0,8},{8,0},{16,24},{24,16},{1,9},{9,1},{17,25},{25,17},{2,10},{10... | collective-permute-start | bytes 1572872 | tf_op jit(solution)/shard_map/ppermute | solution.py:563
  2.8 1.5 %collective-permute-done = f32[64,2048]{1,0:T(8,128)S(1)} collective-permute-done((f32[64,2048]{1,0:T(8,128)S(1)}, f32[64,2048]{1,0:T(8,128)S(1)}, u32[]{:S(2)}, u32[]{:S(2)}) %collective-permute-start) | collective-permute-done | bytes 524320 | tf_op jit(solution)/shard_map/ppermute | solution.py:563
  4.3 0.1 halves_summed.1
  4.4 2.9 %collective-permute-start.1 = (f32[1,32,2048]{2,1,0:T(8,128)S(1)}, f32[1,32,2048]{2,1,0:T(8,128)S(1)}, u32[]{:S(2)}, u32[]{:S(2)}) collective-permute-start(f32[1,32,2048]{2,1,0:T(8,128)S(1)} %get-tuple-element.20.refs_1_), channel_id=1, source_target_pairs={{0,16},{8,24},{16,0},{24,8},{1,17},{9,25},{17,1},{25,9},{2,18},{10... | collective-permute-start | bytes 786440 | tf_op jit(solution)/shard_map/ppermute | solution.py:563
  7.3 3.4 %collective-permute-start.2 = (f32[16,128]{1,0:T(8,128)S(1)}, f32[16,128]{1,0:T(8,128)S(1)}, u32[]{:S(2)}, u32[]{:S(2)}) collective-permute-start(f32[16,128]{1,0:T(8,128)S(1)} %get-tuple-element.21), channel_id=1, source_target_pairs={{0,1},{1,2},{2,3},{3,4},{4,5},{5,6},{6,7},{8,9},{9,10},{10,11},{11... | collective-permute-start | bytes 24584 | tf_op jit(solution)/shard_map/ppermute | solution.py:576
  10.7 1.3 %collective-permute-done.2.edge_ref.refs_2_ = f32[16,128]{1,0:T(8,128)S(1)} collective-permute-done((f32[16,128]{1,0:T(8,128)S(1)}, f32[16,128]{1,0:T(8,128)S(1)}, u32[]{:S(2)}, u32[]{:S(2)}) %collective-permute-start.2) | collective-permute-done | bytes 8224 | tf_op jit(solution)/shard_map/ppermute | solution.py:576
  12.1 6.6 %all-to-all-start.1 = ((f32[8,2,16,128]{3,2,1,0:T(8,128)}), f32[8,2,16,128]{3,2,1,0:T(8,128)S(1)}, u32[]{:S(2)}, u32[]{:S(2)}) async-start(f32[8,2,16,128]{3,2,1,0:T(8,128)} %reference_held.1.refs_3_), calls=%async_computation.1 | async-start | bytes 262144 | tf_op jit(solution)/shard_map/all_to_all | solution.py:585
  18.7 0.7 %shifted_reference.1.refs_2_ = bf16[2,2,128,2176]{3,2,1,0:T(8,128)(2,1)S(1)} custom-call(f32[16,128]{1,0:T(8,128)S(1)} %collective-permute-done.2.edge_ref.refs_2_, f32[2,16,128]{2,1,0:T(8,128)S(1)} %get-tuple-element.22.tiles_ref), custom_call_target="tpu_custom_call" | custom-call | flops 805000000 | tf_op jit(solution)/shard_map/shifted_reference/pallas_call | solution.py:227
  19.4 0.0 collective-permute-done.1
  19.4 2.2 %lag_products.1.refs_1_ = f32[8,10,8,128]{3,2,1,0:T(8,128)} custom-call(f32[32,2048]{1,0:T(8,128)S(1)} %bitcast.7, f32[32,2048]{1,0:T(8,128)S(1)} %bitcast.8, bf16[2,2,128,2176]{3,2,1,0:T(8,128)(2,1)S(1)} %shifted_reference.1.refs_2_, f32[8,2,16,128]{3,2,1,0:T(8,128)} %reference_held.1.refs_3_), custom_call_target="tpu_custom_call" | custom-call | flops 2415000064 | tf_op jit(solution)/shard_map/lag_products/pallas_call | solution.py:304
  21.5 4.5 %all-to-all-done.1.refs_0_ = f32[8,2,16,128]{3,2,1,0:T(8,128)S(1)} async-done(((f32[8,2,16,128]{3,2,1,0:T(8,128)}), f32[8,2,16,128]{3,2,1,0:T(8,128)S(1)}, u32[]{:S(2)}, u32[]{:S(2)}) %all-to-all-start.1) | async-done | bytes 131104 | tf_op jit(solution)/shard_map/all_to_all | solution.py:585
  26.0 3.4 %all-to-all-start = ((f32[8,10,8,128]{3,2,1,0:T(8,128)}), f32[8,10,8,128]{3,2,1,0:T(8,128)S(1)}, u32[]{:S(2)}, u32[]{:S(2)}) async-start(f32[8,10,8,128]{3,2,1,0:T(8,128)} %lag_products.1.refs_1_), calls=%async_computation | async-start | bytes 655360 | tf_op jit(solution)/shard_map/all_to_all | solution.py:588
  29.5 6.2 %reference_products.1 = (bf16[2,2048,128]{2,1,0:T(8,128)(2,1)S(1)}, f32[8,128]{1,0:T(8,128)S(1)}, f32[128,128]{1,0:T(8,128)S(1)}) custom-call(f32[8,2,16,128]{3,2,1,0:T(8,128)S(1)} %all-to-all-done.1.refs_0_, f32[8,10,8,128]{3,2,1,0:T(8,128)} %lag_products.1.refs_1_), custom_call_target="tpu_custom_call" | custom-call | flops 7129999872 | tf_op jit(solution)/shard_map/reference_products/pallas_call | solution.py:408
  35.7 0.0 copy-start
  35.7 2.0 %gram_inverse.1 = (bf16[2,128,128]{2,1,0:T(8,128)(2,1)S(1)}, bf16[2,128,128]{2,1,0:T(8,128)(2,1)S(1)}) custom-call(f32[8,128]{1,0:T(8,128)S(1)} %get-tuple-element.25.line_ref, f32[128,128]{1,0:T(8,128)S(1)} %get-tuple-element.26.tail_ref), custom_call_target="tpu_custom_call" | custom-call | flops 2300000000 | tf_op jit(solution)/shard_map/gram_inverse/pallas_call | solution.py:475
  37.8 0.3 all-to-all-done.got_ref
  38.1 0.0 copy-done
  38.1 2.5 %range_doppler.1 = f32[16,2,32,256]{3,2,1,0:T(8,128)} custom-call(f32[8,10,8,128]{3,2,1,0:T(8,128)S(1)} %all-to-all-done.got_ref, bf16[2,2048,128]{2,1,0:T(8,128)(2,1)S(1)} %get-tuple-element.24.own_ref, bf16[2,128,128]{2,1,0:T(8,128)(2,1)S(1)} %get-tuple-element.27.gram_ref, bf16[2,128,128]{2,1,0:T(8,128)(2,1)S(1)} %get-tuple-element.28.solver_ref, ...), custom_call_target="tpu_custom_call" | custom-call | flops 2875000064 | tf_op jit(solution)/shard_map/range_doppler/pallas_call | solution.py:545
  (1 shorter events, 0.0 us)
Async XLA Ops:
  2.3 2.1 %collective-permute-start = (f32[64,2048]{1,0:T(8,128)S(1)}, f32[64,2048]{1,0:T(8,128)S(1)}, u32[]{:S(2)}, u32[]{:S(2)}) collective-permute-start(f32[64,2048]{1,0:T(8,128)S(1)} %get-tuple-element.18), channel_id=1, source_target_pairs={{0,8},{8,0},{16,24},{24,16},{1,9},{9,1},{17,25},{25,17},{2,10},{10... | collective-permute-start | bytes 1572872 | tf_op jit(solution)/shard_map/ppermute | solution.py:563
  4.4 15.0 %collective-permute-start.1 = (f32[1,32,2048]{2,1,0:T(8,128)S(1)}, f32[1,32,2048]{2,1,0:T(8,128)S(1)}, u32[]{:S(2)}, u32[]{:S(2)}) collective-permute-start(f32[1,32,2048]{2,1,0:T(8,128)S(1)} %get-tuple-element.20.refs_1_), channel_id=1, source_target_pairs={{0,16},{8,24},{16,0},{24,8},{1,17},{9,25},{17,1},{25,9},{2,18},{10... | collective-permute-start | bytes 786440 | tf_op jit(solution)/shard_map/ppermute | solution.py:563
  7.3 4.8 %collective-permute-start.2 = (f32[16,128]{1,0:T(8,128)S(1)}, f32[16,128]{1,0:T(8,128)S(1)}, u32[]{:S(2)}, u32[]{:S(2)}) collective-permute-start(f32[16,128]{1,0:T(8,128)S(1)} %get-tuple-element.21), channel_id=1, source_target_pairs={{0,1},{1,2},{2,3},{3,4},{4,5},{5,6},{6,7},{8,9},{9,10},{10,11},{11... | collective-permute-start | bytes 24584 | tf_op jit(solution)/shard_map/ppermute | solution.py:576
  12.1 13.9 %all-to-all-start.1 = ((f32[8,2,16,128]{3,2,1,0:T(8,128)}), f32[8,2,16,128]{3,2,1,0:T(8,128)S(1)}, u32[]{:S(2)}, u32[]{:S(2)}) async-start(f32[8,2,16,128]{3,2,1,0:T(8,128)} %reference_held.1.refs_3_), calls=%async_computation.1 | async-start | bytes 262144 | tf_op jit(solution)/shard_map/all_to_all | solution.py:585
  26.0 12.0 %all-to-all-start = ((f32[8,10,8,128]{3,2,1,0:T(8,128)}), f32[8,10,8,128]{3,2,1,0:T(8,128)S(1)}, u32[]{:S(2)}, u32[]{:S(2)}) async-start(f32[8,10,8,128]{3,2,1,0:T(8,128)} %lag_products.1.refs_1_), calls=%async_computation | async-start | bytes 655360 | tf_op jit(solution)/shard_map/all_to_all | solution.py:588
  35.7 2.4 %copy-start = (bf16[2,128,512]{2,1,0:T(8,128)(2,1)S(1)}, bf16[2,128,512]{2,1,0:T(8,128)(2,1)}, u32[]{:S(2)}) copy-start(bf16[2,128,512]{2,1,0:T(8,128)(2,1)} %constant.2.clone.wave_ref) | copy-start | bytes 786436

commit v11 on v10

--- a/solution.py
+++ b/solution.py
@@ -77,8 +77,8 @@
 
 
 def beam_kernel(
-    chan_count, beams_local, w_hbm, s_hbm, ref_hbm, kept_ref, sent_ref, tiles_ref, edge_ref, spread_hbm,
-    w_ref, s_ref, ref_ref, w_sem, s_sem, ref_sem, spread_sem,
+    chan_count, beams_local, w_hbm, s_hbm, ref_hbm, kept_ref, sent_ref, tiles_ref, edge_ref,
+    w_ref, s_ref, ref_ref, w_sem, s_sem, ref_sem,
 ):
     me = lax.axis_index("chan")
     length = s_hbm.shape[1]
@@ -121,10 +121,6 @@
             if n >= count - EDGE:
                 at = SUBLANES * c + n + EDGE - count
                 edge_ref[at : at + 1, :] = row
-    copies = []
-    for n in range(spread_hbm.shape[0]):
-        copies.append(pltpu.make_async_copy(tiles_ref, spread_hbm.at[n], spread_sem.at[n]))
-        copies[n].start()
     mid = weights[0].shape[0] // 2
     for n in range(CHUNKS):
         cols = slice(n * width, (n + 1) * width)
@@ -132,11 +128,9 @@
         product = dot_split(weights, halves(s_ref[:, cols]))
         kept_ref[:, cols] = product[:mid]
         sent_ref[:, cols] = product[mid:]
-    for copy in copies:
-        copy.wait()
-
-
-def beam_call(steering, survey, ref, owners, chan_count, beams_local):
+
+
+def beam_call(steering, survey, ref, chan_count, beams_local):
     depth, length = survey.shape
     rows = chan_count * beams_local
     tiles = (2, length // LANES, LANES)
@@ -145,13 +139,12 @@
     return pl.pallas_call(
         functools.partial(beam_kernel, chan_count, beams_local),
         in_specs=[hbm] * 3,
-        out_specs=[vmem] * 4 + [hbm],
+        out_specs=[vmem] * 4,
         out_shape=[
             out,
             out,
             jax.ShapeDtypeStruct(tiles, jnp.float32),
             jax.ShapeDtypeStruct((2 * SUBLANES, LANES), jnp.float32),
-            jax.ShapeDtypeStruct((owners,) + tiles, jnp.float32),
         ],
         scratch_shapes=[
             pltpu.VMEM(steering.shape, jnp.float32),
@@ -160,29 +153,11 @@
             pltpu.SemaphoreType.DMA,
             pltpu.SemaphoreType.DMA((CHUNKS,)),
             pltpu.SemaphoreType.DMA,
-            pltpu.SemaphoreType.DMA((owners,)),
         ],
         compiler_params=params(),
         cost_estimate=cost(2.2),
         name="beams",
     )(*(pltpu.with_memory_space_constraint(x, pltpu.HBM) for x in (steering, survey, ref)))
-
-
-def hold_kernel(*refs):
-    del refs
-
-
-def hold_call(x, *after):
-    return pl.pallas_call(
-        hold_kernel,
-        in_specs=[pl.BlockSpec(memory_space=pltpu.HBM)] + [pl.BlockSpec(memory_space=pl.ANY)] * len(after),
-        out_specs=pl.BlockSpec(memory_space=pltpu.HBM),
-        out_shape=jax.ShapeDtypeStruct(x.shape, x.dtype),
-        input_output_aliases={0: 0},
-        compiler_params=params(),
-        cost_estimate=cost(0.1),
-        name="reference_held",
-    )(x, *after)
 
 
 def sum_kernel(count, *refs):
@@ -210,10 +185,35 @@
     )(*parts)
 
 
-def table_kernel(edge_ref, tiles_ref, out_ref):
+def join_kernel(first_ref, second_ref, *refs):
+    out_ref = refs[-1]
+    count = first_ref.shape[0]
+    out_ref[:count] = first_ref[...]
+    out_ref[count:] = second_ref[...]
+
+
+def join_call(first, second, *after):
+    vmem = pl.BlockSpec(memory_space=pltpu.VMEM)
+    return pl.pallas_call(
+        join_kernel,
+        in_specs=[vmem, vmem] + [pl.BlockSpec(memory_space=pl.ANY)] * len(after),
+        out_shape=jax.ShapeDtypeStruct((2 * first.shape[0],) + first.shape[1:], jnp.float32),
+        compiler_params=params(),
+        cost_estimate=cost(1.0),
+        name="reference_joined",
+    )(first, second, *after)
+
+
+def table_kernel(edge_ref, tiles_ref, *refs):
+    *round_refs, out_ref = refs
+    me = lax.axis_index("tm")
     rows = tiles_ref.shape[1]
     for c in range(2):
-        line = [edge_ref[SUBLANES * c + n : SUBLANES * c + n + 1, :] for n in range(EDGE)]
+        before = edge_ref[SUBLANES * c : SUBLANES * c + EDGE, :]
+        for n, round_ref in enumerate(round_refs):
+            last = round_ref[round_ref.shape[0] - 1, c, rows - EDGE :, :]
+            before = jnp.where((me > 0) & ((me ^ (me - 1)) == 2 ** (n + 1) - 1), last, before)
+        line = [before[n : n + 1] for n in range(EDGE)]
         line = jnp.concatenate(line + [tiles_ref[c, n : n + 1, :] for n in range(rows)], 1)
         for g in range(0, LANES, 2 * SUBLANES):
             tiled = jnp.broadcast_to(line, (2 * SUBLANES, line.shape[1]))
@@ -222,7 +222,7 @@
             out_ref[1, c, g : g + 2 * SUBLANES] = low
 
 
-def table_call(edge, tiles):
+def table_call(edge, tiles, rounds):
     shape = (2, 2, LANES, LANES * (tiles.shape[1] + 1))
     return pl.pallas_call(
         table_kernel,
@@ -230,7 +230,7 @@
         compiler_params=params(),
         cost_estimate=cost(0.7),
         name="shifted_reference",
-    )(edge, tiles)
+    )(edge, tiles, *rounds)
 
 
 def lag_kernel(groups, *refs):
@@ -317,17 +317,21 @@
 
 
 def own_kernel(lags_local, *refs):
-    ref_ref, _, out_ref, line_ref, tail_ref, span_ref, late_ref, taps_a, lags_a, taps_b, lags_b = refs
+    *part_refs, _, out_ref, line_ref, tail_ref, span_ref, late_ref, taps_a, lags_a, taps_b, lags_b = refs
     me = lax.axis_index("tm")
-    owners, _, part_rows, _ = ref_ref.shape
+    part_rows = part_refs[0].shape[2]
+    owners = sum(part_ref.shape[0] for part_ref in part_refs)
     samples = owners * part_rows * LANES
     steps = samples // BLOCK_LEN // BATCH
     total_rows = span_ref.shape[1]
     block_rows = BLOCK_LEN // LANES
 
     span_ref[...] = jnp.zeros_like(span_ref)
-    for t in range(owners):
-        span_ref[:, EDGE + t * part_rows : EDGE + (t + 1) * part_rows, :] = ref_ref[t]
+    e = 0
+    for part_ref in part_refs:
+        for i in range(part_ref.shape[0]):
+            span_ref[:, pl.ds(EDGE + (me ^ e) * part_rows, part_rows), :] = part_ref[i]
+            e += 1
     late_rows = (me * lags_local) // LANES
     late_lanes = lax.rem(me * lags_local, LANES)
     turned = [pltpu.roll(span_ref[c], late_lanes, 1) for c in range(2)]
@@ -397,8 +401,9 @@
     tail_ref[...] = dot_nt(tail, tail, HIGHEST)
 
 
-def own_call(ref_all, lags_local, after):
-    span_rows = ref_all.shape[0] * ref_all.shape[2]
+def own_call(parts, lags_local, after):
+    part_rows = parts[0].shape[2]
+    span_rows = part_rows * sum(part.shape[0] for part in parts)
     rows = span_rows * LANES // BLOCK_LEN * lags_local
     held_rows = -(-(span_rows + 2 * EDGE) // SUBLANES) * SUBLANES
     width = BATCH * BLOCK_LEN
@@ -407,7 +412,7 @@
     span = pltpu.VMEM((2, held_rows, LANES), jnp.float32)
     return pl.pallas_call(
         functools.partial(own_kernel, lags_local),
-        in_specs=[pl.BlockSpec(memory_space=pltpu.VMEM), pl.BlockSpec(memory_space=pl.ANY)],
+        in_specs=[pl.BlockSpec(memory_space=pltpu.VMEM)] * len(parts) + [pl.BlockSpec(memory_space=pl.ANY)],
         out_shape=[
             jax.ShapeDtypeStruct((2, rows, 2 * TAPS), jnp.bfloat16),
             jax.ShapeDtypeStruct((SUBLANES, 2 * TAPS), jnp.float32),
@@ -417,7 +422,7 @@
         compiler_params=params(),
         cost_estimate=cost(6.2),
         name="reference_products",
-    )(ref_all, after)
+    )(*parts, after)
 
 
 def as_factor(a):
@@ -572,8 +577,12 @@
     samples = length * tm_count
 
     survey = surveillance.reshape(2 * channels, length)
-    kept, moved, tiles, edge, spread = beam_call(steering, survey, ref_signal, tm_count, chan_count, beams_local)
-    edge = lax.ppermute(edge, "tm", [(i, i + 1) for i in range(tm_count - 1)])
+    kept, moved, tiles, edge = beam_call(steering, survey, ref_signal, chan_count, beams_local)
+    early = 1 if tm_count < 4 else 2
+    edge = lax.ppermute(
+        edge, "tm", [(i, i + 1) for i in range(tm_count - 1) if i ^ (i + 1) >= 1 << early]
+    )
+    near = swap(tiles[None], "tm", 1)
     shape = (chan_count // 2, 2 * beams_local, length)
     kept, got = kept.reshape(shape), swap(moved, "chan", 1).reshape(shape)
     by = 2
@@ -581,12 +590,17 @@
         kept, moved = sum_call([kept, got])
         got = swap(moved, "chan", by)
         by *= 2
-    spread = hold_call(spread, moved, edge)
-    ref_all = lax.all_to_all(spread, "tm", 0, 0, tiled=True)
-    table = table_call(edge, tiles)
-    pieces = lag_call([kept[0], got[0]], table, spread, groups, tm_count)
+    rounds = [near]
+    joined = join_call(tiles[None], near, moved)
+    while joined.shape[0] < tm_count:
+        rounds.append(swap(joined, "tm", joined.shape[0]))
+        if joined.shape[0] * 2 == tm_count:
+            break
+        joined = join_call(joined, rounds[-1])
+    table = table_call(edge, tiles, rounds[:early])
+    pieces = lag_call([kept[0], got[0]], table, joined, groups, tm_count)
     got = lax.all_to_all(pieces, "tm", 0, 0, tiled=True)
-    own, line, tail = own_call(ref_all, lags_local, pieces)
+    own, line, tail = own_call([tiles[None]] + rounds, lags_local, pieces)
     gram, solver = solver_call(line, tail)
     wave = doppler_table(samples // BLOCK_LEN, 0.125 / math.sqrt(samples))
     high = wave.astype(jnp.bfloat16)

time: 40.9 us -> 34.5 us (0.84)
  waiting for transfers between devices: 7.67 us -> 2.58 us
  starting transfers between devices: 16.9 us -> 15.8 us
    all_to_all x1 -> x0, starting transfers between devices: 6.6 us -> none  [tiled_device(): ref_all = lax.all_to_all(spread, 'tm', 0, 0, tiled=True)]
    ppermute x2 -> x5, starting transfers between devices: 3.44 us -> 9.72 us  [swap(): return lax.ppermute(x, axis, pairs)]
    all_to_all x1 -> x0, waiting for transfers between devices: 4.48 us -> none  [tiled_device(): ref_all = lax.all_to_all(spread, 'tm', 0, 0, tiled=True)]
    ppermute x1, starting transfers between devices: 3.41 us -> 0.65 us  [tiled_device(): lax.ppermute(edge, 'tm', [(i, i + 1) for i in range(tm_count - 1) if i ^...]
    all_to_all x1, starting transfers between devices: 3.43 us -> 5.46 us  [tiled_device(): got = lax.all_to_all(pieces, 'tm', 0, 0, tiled=True)]
    ppermute x1, waiting for transfers between devices: 1.35 us -> 0.01 us  [tiled_device(): lax.ppermute(edge, 'tm', [(i, i + 1) for i in range(tm_count - 1) if i ^...]
    all_to_all x1, waiting for transfers between devices: 0.29 us -> 1.18 us  [tiled_device(): got = lax.all_to_all(pieces, 'tm', 0, 0, tiled=True)]
    ppermute x2 -> x5, waiting for transfers between devices: 1.54 us -> 1.4 us  [swap(): return lax.ppermute(x, axis, pairs)]
  transfers between devices with their start and end apart: 5 -> 7, of which waited for: 4 -> 2; matrix products, arithmetic and copies ran while one was open for 0% -> 0% of each run, Pallas kernels for 27% -> 33%
where the time goes in v11:
time: 34.5 us; the launch traced here: 34.3 us
  Pallas kernels  15.8 us (46%)
  starting transfers between devices  15.8 us (46%)
  waiting for transfers between devices  2.58 us (7%)
    ppermute x5, starting transfers between devices, swap(): return lax.ppermute(x, axis, pairs)  9.72 us
    pallas_call x1, Pallas kernels, own_call(): pl.pallas_call(functools.partial(own_kernel, lags_local), in_specs=[pl.Bl...  6.25 us
    all_to_all x1, starting transfers between devices, tiled_device(): got = lax.all_to_all(pieces, 'tm', 0, 0, tiled=True)  5.46 us
    pallas_call x1, Pallas kernels, map_call(): pl.pallas_call(functools.partial(map_kernel, groups), in_specs=[pl.BlockS...  2.47 us
    pallas_call x1, Pallas kernels, beam_call(): pl.pallas_call(functools.partial(beam_kernel, chan_count, beams_local), i...  2.17 us
    pallas_call x1, Pallas kernels, lag_call(): pl.pallas_call(functools.partial(lag_kernel, groups), in_specs=[vmem] * (...  2.16 us
    pallas_call x1, Pallas kernels, solver_call(): pl.pallas_call(solver_kernel, out_shape=[out, out], compiler_params=param...  2.05 us
    ppermute x5, waiting for transfers between devices, swap(): return lax.ppermute(x, axis, pairs)  1.4 us
  transfers between devices with their start and end apart: 7, of which 2 were waited for; matrix products, arithmetic and copies ran while one was open for 0% of the time, Pallas kernels for 33%

profile of v11, /device:TPU:0, one launch (start us, length us, event | category | flops | bytes accessed | tf_op | source)
XLA Modules:
  0.0 34.3 jit_solution(1485716856845934431)
XLA Ops:
  0.0 2.2 %beams.1 = (f32[64,2048]{1,0:T(8,128)S(1)}, f32[64,2048]{1,0:T(8,128)S(1)}, f32[2,16,128]{2,1,0:T(8,128)S(1)}, f32[16,128]{1,0:T(8,128)S(1)}) custom-call(f32[2,64,64]{2,1,0:T(8,128)} %w_hbm.1, f32[128,2048]{1,0:T(8,128)} %bitcast.13, f32[2,2048]{1,0:T(2,128)} %ref_hbm.1), custom_call_target="tpu_custom_call" | custom-call | flops 2529999872 | tf_op jit(solution)/shard_map/beams/pallas_call | solution.py:139
  2.2 0.5 %collective-permute-start = (f32[64,2048]{1,0:T(8,128)S(1)}, f32[64,2048]{1,0:T(8,128)S(1)}, u32[]{:S(2)}, u32[]{:S(2)}) collective-permute-start(f32[64,2048]{1,0:T(8,128)S(1)} %get-tuple-element.17), channel_id=1, source_target_pairs={{0,8},{8,0},{16,24},{24,16},{1,9},{9,1},{17,25},{25,17},{2,10},{10... | collective-permute-start | bytes 1572872 | tf_op jit(solution)/shard_map/ppermute | solution.py:568
  2.7 2.6 %collective-permute-start.3 = (f32[1,2,16,128]{3,2,1,0:T(8,128)S(1)}, f32[1,2,16,128]{3,2,1,0:T(8,128)S(1)}, u32[]{:S(2)}, u32[]{:S(2)}) collective-permute-start(f32[1,2,16,128]{3,2,1,0:T(8,128)S(1)} %bitcast.10), channel_id=1, source_target_pairs={{0,1},{1,0},{2,3},{3,2},{4,5},{5,4},{6,7},{7,6},{8,9},{9,8},{10,11... | collective-permute-start | bytes 49160 | tf_op jit(solution)/shard_map/ppermute | solution.py:568
  5.3 0.0 collective-permute-done
  5.3 0.1 halves_summed.1
  5.3 1.9 %collective-permute-start.1 = (f32[1,32,2048]{2,1,0:T(8,128)S(1)}, f32[1,32,2048]{2,1,0:T(8,128)S(1)}, u32[]{:S(2)}, u32[]{:S(2)}) collective-permute-start(f32[1,32,2048]{2,1,0:T(8,128)S(1)} %get-tuple-element.19.refs_0_), channel_id=1, source_target_pairs={{0,16},{8,24},{16,0},{24,8},{1,17},{9,25},{17,1},{25,9},{2,18},{10... | collective-permute-start | bytes 786440 | tf_op jit(solution)/shard_map/ppermute | solution.py:568
  7.2 0.0 collective-permute-done.3.second_ref.refs_0_.refs_1_
  7.2 1.9 %collective-permute-start.4 = (f32[2,2,16,128]{3,2,1,0:T(8,128)S(1)}, f32[2,2,16,128]{3,2,1,0:T(8,128)S(1)}, u32[]{:S(2)}, u32[]{:S(2)}) collective-permute-start(f32[2,2,16,128]{3,2,1,0:T(8,128)S(1)} %reference_joined.2.first_ref), channel_id=1, source_target_pairs={{0,2},{1,3},{2,0},{3,1},{4,6},{5,7},{6,4},{7,5},{8,10},{9,11},{10,... | collective-permute-start | bytes 98312 | tf_op jit(solution)/shard_map/ppermute | solution.py:568
  9.1 0.6 %collective-permute-start.2 = (f32[16,128]{1,0:T(8,128)S(1)}, f32[16,128]{1,0:T(8,128)S(1)}, u32[]{:S(2)}, u32[]{:S(2)}) collective-permute-start(f32[16,128]{1,0:T(8,128)S(1)} %get-tuple-element.20), channel_id=1, source_target_pairs={{3,4},{11,12},{19,20},{27,28}} | collective-permute-start | bytes 24584 | tf_op jit(solution)/shard_map/ppermute | solution.py:582
  9.7 1.4 %collective-permute-done.4.refs_1_.second_ref.refs_2_ = f32[2,2,16,128]{3,2,1,0:T(8,128)S(1)} collective-permute-done((f32[2,2,16,128]{3,2,1,0:T(8,128)S(1)}, f32[2,2,16,128]{3,2,1,0:T(8,128)S(1)}, u32[]{:S(2)}, u32[]{:S(2)}) %collective-permute-start.4) | collective-permute-done | bytes 32800 | tf_op jit(solution)/shard_map/ppermute | solution.py:568
  11.1 2.9 %collective-permute-start.5 = (f32[4,2,16,128]{3,2,1,0:T(8,128)S(1)}, f32[4,2,16,128]{3,2,1,0:T(8,128)S(1)}, u32[]{:S(2)}, u32[]{:S(2)}) collective-permute-start(f32[4,2,16,128]{3,2,1,0:T(8,128)S(1)} %reference_joined.3.refs_3_), channel_id=1, source_target_pairs={{0,4},{1,5},{2,6},{3,7},{4,0},{5,1},{6,2},{7,3},{8,12},{9,13},{10,... | collective-permute-start | bytes 196616 | tf_op jit(solution)/shard_map/ppermute | solution.py:568
  14.0 0.0 collective-permute-done.2.edge_ref
  14.0 0.7 %shifted_reference.1.refs_2_ = bf16[2,2,128,2176]{3,2,1,0:T(8,128)(2,1)S(1)} custom-call(f32[16,128]{1,0:T(8,128)S(1)} %collective-permute-done.2.edge_ref, f32[2,16,128]{2,1,0:T(8,128)S(1)} %get-tuple-element.21.tiles_ref, f32[1,2,16,128]{3,2,1,0:T(8,128)S(1)} %collective-permute-done.3.second_ref.refs_0_.refs_1_, ...), custom_call_target="tpu_custom_call" | custom-call | flops 805000000 | tf_op jit(solution)/shard_map/shifted_reference/pallas_call | solution.py:227
  14.7 0.0 collective-permute-done.1
  14.7 2.2 %lag_products.1.refs_4_ = f32[8,10,8,128]{3,2,1,0:T(8,128)} custom-call(f32[32,2048]{1,0:T(8,128)S(1)} %bitcast.8, f32[32,2048]{1,0:T(8,128)S(1)} %bitcast.9, bf16[2,2,128,2176]{3,2,1,0:T(8,128)(2,1)S(1)} %shifted_reference.1.refs_2_, f32[4,2,16,128]{3,2,1,0:T(8,128)S(1)} %reference_joined.3.refs_3_), custom_call_target="tpu_custom_call" | custom-call | flops 2415000064 | tf_op jit(solution)/shard_map/lag_products/pallas_call | solution.py:304
  16.9 5.5 %all-to-all-start = ((f32[8,10,8,128]{3,2,1,0:T(8,128)}), f32[8,10,8,128]{3,2,1,0:T(8,128)S(1)}, u32[]{:S(2)}, u32[]{:S(2)}) async-start(f32[8,10,8,128]{3,2,1,0:T(8,128)} %lag_products.1.refs_4_), calls=%async_computation | async-start | bytes 655360 | tf_op jit(solution)/shard_map/all_to_all | solution.py:602
  22.3 0.0 collective-permute-done.5.refs_3_
  22.4 6.2 %reference_products.1 = (bf16[2,2048,128]{2,1,0:T(8,128)(2,1)S(1)}, f32[8,128]{1,0:T(8,128)S(1)}, f32[128,128]{1,0:T(8,128)S(1)}) custom-call(f32[1,2,16,128]{3,2,1,0:T(8,128)S(1)} %bitcast.12, f32[1,2,16,128]{3,2,1,0:T(8,128)S(1)} %collective-permute-done.3.second_ref.refs_0_.refs_1_, ...), custom_call_target="tpu_custom_call" | custom-call | flops 7129999872 | tf_op jit(solution)/shard_map/reference_products/pallas_call | solution.py:413
  28.6 0.0 copy-start
  28.6 2.0 %gram_inverse.1 = (bf16[2,128,128]{2,1,0:T(8,128)(2,1)S(1)}, bf16[2,128,128]{2,1,0:T(8,128)(2,1)S(1)}) custom-call(f32[8,128]{1,0:T(8,128)S(1)} %get-tuple-element.23.line_ref, f32[128,128]{1,0:T(8,128)S(1)} %get-tuple-element.24.tail_ref), custom_call_target="tpu_custom_call" | custom-call | flops 2300000000 | tf_op jit(solution)/shard_map/gram_inverse/pallas_call | solution.py:480
  30.7 1.2 %all-to-all-done.got_ref = f32[8,10,8,128]{3,2,1,0:T(8,128)S(1)} async-done(((f32[8,10,8,128]{3,2,1,0:T(8,128)}), f32[8,10,8,128]{3,2,1,0:T(8,128)S(1)}, u32[]{:S(2)}, u32[]{:S(2)}) %all-to-all-start) | async-done | bytes 327712 | tf_op jit(solution)/shard_map/all_to_all | solution.py:602
  31.8 0.0 copy-done
  31.8 2.5 %range_doppler.1 = f32[16,2,32,256]{3,2,1,0:T(8,128)} custom-call(f32[8,10,8,128]{3,2,1,0:T(8,128)S(1)} %all-to-all-done.got_ref, bf16[2,2048,128]{2,1,0:T(8,128)(2,1)S(1)} %get-tuple-element.22.own_ref, bf16[2,128,128]{2,1,0:T(8,128)(2,1)S(1)} %get-tuple-element.25.gram_ref, bf16[2,128,128]{2,1,0:T(8,128)(2,1)S(1)} %get-tuple-element.26.solver_ref, ...), custom_call_target="tpu_custom_call" | custom-call | flops 2875000064 | tf_op jit(solution)/shard_map/range_doppler/pallas_call | solution.py:550
  (2 shorter events, 0.0 us)
Async XLA Ops:
  2.2 3.1 %collective-permute-start = (f32[64,2048]{1,0:T(8,128)S(1)}, f32[64,2048]{1,0:T(8,128)S(1)}, u32[]{:S(2)}, u32[]{:S(2)}) collective-permute-start(f32[64,2048]{1,0:T(8,128)S(1)} %get-tuple-element.17), channel_id=1, source_target_pairs={{0,8},{8,0},{16,24},{24,16},{1,9},{9,1},{17,25},{25,17},{2,10},{10... | collective-permute-start | bytes 1572872 | tf_op jit(solution)/shard_map/ppermute | solution.py:568
  2.7 4.5 %collective-permute-start.3 = (f32[1,2,16,128]{3,2,1,0:T(8,128)S(1)}, f32[1,2,16,128]{3,2,1,0:T(8,128)S(1)}, u32[]{:S(2)}, u32[]{:S(2)}) collective-permute-start(f32[1,2,16,128]{3,2,1,0:T(8,128)S(1)} %bitcast.10), channel_id=1, source_target_pairs={{0,1},{1,0},{2,3},{3,2},{4,5},{5,4},{6,7},{7,6},{8,9},{9,8},{10,11... | collective-permute-start | bytes 49160 | tf_op jit(solution)/shard_map/ppermute | solution.py:568
  5.3 9.4 %collective-permute-start.1 = (f32[1,32,2048]{2,1,0:T(8,128)S(1)}, f32[1,32,2048]{2,1,0:T(8,128)S(1)}, u32[]{:S(2)}, u32[]{:S(2)}) collective-permute-start(f32[1,32,2048]{2,1,0:T(8,128)S(1)} %get-tuple-element.19.refs_0_), channel_id=1, source_target_pairs={{0,16},{8,24},{16,0},{24,8},{1,17},{9,25},{17,1},{25,9},{2,18},{10... | collective-permute-start | bytes 786440 | tf_op jit(solution)/shard_map/ppermute | solution.py:568
  7.2 3.9 %collective-permute-start.4 = (f32[2,2,16,128]{3,2,1,0:T(8,128)S(1)}, f32[2,2,16,128]{3,2,1,0:T(8,128)S(1)}, u32[]{:S(2)}, u32[]{:S(2)}) collective-permute-start(f32[2,2,16,128]{3,2,1,0:T(8,128)S(1)} %reference_joined.2.first_ref), channel_id=1, source_target_pairs={{0,2},{1,3},{2,0},{3,1},{4,6},{5,7},{6,4},{7,5},{8,10},{9,11},{10,... | collective-permute-start | bytes 98312 | tf_op jit(solution)/shard_map/ppermute | solution.py:568
  9.1 4.9 %collective-permute-start.2 = (f32[16,128]{1,0:T(8,128)S(1)}, f32[16,128]{1,0:T(8,128)S(1)}, u32[]{:S(2)}, u32[]{:S(2)}) collective-permute-start(f32[16,128]{1,0:T(8,128)S(1)} %get-tuple-element.20), channel_id=1, source_target_pairs={{3,4},{11,12},{19,20},{27,28}} | collective-permute-start | bytes 24584 | tf_op jit(solution)/shard_map/ppermute | solution.py:582
  11.1 11.2 %collective-permute-start.5 = (f32[4,2,16,128]{3,2,1,0:T(8,128)S(1)}, f32[4,2,16,128]{3,2,1,0:T(8,128)S(1)}, u32[]{:S(2)}, u32[]{:S(2)}) collective-permute-start(f32[4,2,16,128]{3,2,1,0:T(8,128)S(1)} %reference_joined.3.refs_3_), channel_id=1, source_target_pairs={{0,4},{1,5},{2,6},{3,7},{4,0},{5,1},{6,2},{7,3},{8,12},{9,13},{10,... | collective-permute-start | bytes 196616 | tf_op jit(solution)/shard_map/ppermute | solution.py:568
  16.9 14.9 %all-to-all-start = ((f32[8,10,8,128]{3,2,1,0:T(8,128)}), f32[8,10,8,128]{3,2,1,0:T(8,128)S(1)}, u32[]{:S(2)}, u32[]{:S(2)}) async-start(f32[8,10,8,128]{3,2,1,0:T(8,128)} %lag_products.1.refs_4_), calls=%async_computation | async-start | bytes 655360 | tf_op jit(solution)/shard_map/all_to_all | solution.py:602
  28.6 3.2 %copy-start = (bf16[2,128,512]{2,1,0:T(8,128)(2,1)S(1)}, bf16[2,128,512]{2,1,0:T(8,128)(2,1)}, u32[]{:S(2)}) copy-start(bf16[2,128,512]{2,1,0:T(8,128)(2,1)} %constant.2.clone.wave_ref) | copy-start | bytes 786436

commit v12 on v11

--- a/solution.py
+++ b/solution.py
@@ -77,7 +77,7 @@
 
 
 def beam_kernel(
-    chan_count, beams_local, w_hbm, s_hbm, ref_hbm, kept_ref, sent_ref, tiles_ref, edge_ref,
+    chan_count, beams_local, w_hbm, s_hbm, ref_hbm, kept_ref, sent_ref, tiles_ref,
     w_ref, s_ref, ref_ref, w_sem, s_sem, ref_sem,
 ):
     me = lax.axis_index("chan")
@@ -112,15 +112,9 @@
                 rows.append(jnp.concatenate(second, 1))
     weights = halves(jnp.concatenate(rows, 0))
     ref_copy.wait()
-    edge_ref[...] = jnp.zeros_like(edge_ref)
-    count = tiles_ref.shape[1]
     for c in range(2):
-        for n in range(count):
-            row = ref_ref[c : c + 1, n * LANES : (n + 1) * LANES]
-            tiles_ref[c, n : n + 1, :] = row
-            if n >= count - EDGE:
-                at = SUBLANES * c + n + EDGE - count
-                edge_ref[at : at + 1, :] = row
+        for n in range(tiles_ref.shape[1]):
+            tiles_ref[c, n : n + 1, :] = ref_ref[c : c + 1, n * LANES : (n + 1) * LANES]
     mid = weights[0].shape[0] // 2
     for n in range(CHUNKS):
         cols = slice(n * width, (n + 1) * width)
@@ -139,12 +133,11 @@
     return pl.pallas_call(
         functools.partial(beam_kernel, chan_count, beams_local),
         in_specs=[hbm] * 3,
-        out_specs=[vmem] * 4,
+        out_specs=[vmem] * 3,
         out_shape=[
             out,
             out,
             jax.ShapeDtypeStruct(tiles, jnp.float32),
-            jax.ShapeDtypeStruct((2 * SUBLANES, LANES), jnp.float32),
         ],
         scratch_shapes=[
             pltpu.VMEM(steering.shape, jnp.float32),
@@ -204,38 +197,77 @@
     )(first, second, *after)
 
 
-def table_kernel(edge_ref, tiles_ref, *refs):
-    *round_refs, out_ref = refs
+def edge_kernel(blocks_ref, out_ref):
+    rows = blocks_ref.shape[2]
+    out_ref[...] = jnp.zeros_like(out_ref)
+    for c in range(2):
+        out_ref[SUBLANES * c : SUBLANES * c + EDGE, :] = blocks_ref[0, c, rows - EDGE :, :]
+
+
+def edge_call(blocks):
+    return pl.pallas_call(
+        edge_kernel,
+        out_shape=jax.ShapeDtypeStruct((2 * SUBLANES, LANES), jnp.float32),
+        compiler_params=params(),
+        cost_estimate=cost(0.1),
+        name="reference_edge",
+    )(blocks)
+
+
+def spread_line(line, keep):
+    for g in range(0, LANES, 2 * SUBLANES):
+        tiled = jnp.broadcast_to(line, (2 * SUBLANES, line.shape[1]))
+        for h, value in enumerate(halves(pltpu.roll(tiled, g, 1, stride=1, stride_axis=0)[:, LANES:])):
+            keep(h, g, value)
+
+
+def table_kernel(tiles_ref, out_ref):
+    for c in range(2):
+        line = jnp.concatenate([tiles_ref[c, n : n + 1, :] for n in range(tiles_ref.shape[1])], 1)
+
+        def keep(h, g, value):
+            out_ref[h, c, g : g + 2 * SUBLANES] = value
+
+        spread_line(line, keep)
+
+
+def table_call(tiles):
+    shape = (2, 2, LANES, LANES * (tiles.shape[1] - 1))
+    return pl.pallas_call(
+        table_kernel,
+        out_shape=jax.ShapeDtypeStruct(shape, jnp.bfloat16),
+        compiler_params=params(),
+        cost_estimate=cost(0.7),
+        name="shifted_reference",
+    )(tiles)
+
+
+def lag_kernel(groups, part_count, *refs):
+    y_refs, refs = refs[:part_count], refs[part_count:]
+    table_ref, edge_ref, tiles_ref, *round_refs, _, out_hbm, out_ref, out_sem, first_ref = refs
+    copies = []
+
     me = lax.axis_index("tm")
-    rows = tiles_ref.shape[1]
     for c in range(2):
         before = edge_ref[SUBLANES * c : SUBLANES * c + EDGE, :]
         for n, round_ref in enumerate(round_refs):
-            last = round_ref[round_ref.shape[0] - 1, c, rows - EDGE :, :]
+            last = round_ref[round_ref.shape[0] - 1, c, round_ref.shape[2] - EDGE :, :]
             before = jnp.where((me > 0) & ((me ^ (me - 1)) == 2 ** (n + 1) - 1), last, before)
-        line = [before[n : n + 1] for n in range(EDGE)]
-        line = jnp.concatenate(line + [tiles_ref[c, n : n + 1, :] for n in range(rows)], 1)
-        for g in range(0, LANES, 2 * SUBLANES):
-            tiled = jnp.broadcast_to(line, (2 * SUBLANES, line.shape[1]))
-            high, low = halves(pltpu.roll(tiled, g, 1, stride=1, stride_axis=0)[:, LANES:])
-            out_ref[0, c, g : g + 2 * SUBLANES] = high
-            out_ref[1, c, g : g + 2 * SUBLANES] = low
-
-
-def table_call(edge, tiles, rounds):
-    shape = (2, 2, LANES, LANES * (tiles.shape[1] + 1))
-    return pl.pallas_call(
-        table_kernel,
-        out_shape=jax.ShapeDtypeStruct(shape, jnp.bfloat16),
-        compiler_params=params(),
-        cost_estimate=cost(0.7),
-        name="shifted_reference",
-    )(edge, tiles, *rounds)
-
-
-def lag_kernel(groups, *refs):
-    *y_refs, table_ref, _, out_hbm, out_ref, out_sem = refs
-    copies = []
+        line = jnp.concatenate([before[n : n + 1] for n in range(EDGE)] + [tiles_ref[c, 0:1, :]], 1)
+
+        def keep(h, g, value):
+            first_ref[h, c, g : g + 2 * SUBLANES] = value
+
+        spread_line(line, keep)
+
+    def tiles_at(h, c, start):
+        known = first_ref.shape[3]
+        if start >= known:
+            return table_ref[h, c, :, start - known : start - known + BLOCK_LEN]
+        if start + BLOCK_LEN <= known:
+            return first_ref[h, c, :, start : start + BLOCK_LEN]
+        rest = start + BLOCK_LEN - known
+        return jnp.concatenate([first_ref[h, c, :, start:], table_ref[h, c, :, :rest]], 1)
 
     def send(start, count):
         part = (slice(None), pl.ds(start, count))
@@ -257,20 +289,13 @@
     turned_both = jnp.concatenate([t_high, t_low], 0)
     taps_sum = None
     for q in range(blocks):
-        near = slice(q * BLOCK_LEN + LANES, q * BLOCK_LEN + LANES + BLOCK_LEN)
-        far = slice(q * BLOCK_LEN, (q + 1) * BLOCK_LEN)
         cols = slice(q * BLOCK_LEN, (q + 1) * BLOCK_LEN)
         tables = []
         for h in range(2):
-            tables.append(
-                jnp.concatenate(
-                    [
-                        jnp.concatenate([table_ref[h, 0, :, near], table_ref[h, 1, :, near]], 1),
-                        jnp.concatenate([table_ref[h, 0, :, far], table_ref[h, 1, :, far]], 1),
-                    ],
-                    0,
-                )
-            )
+            rows_of = []
+            for start in (q * BLOCK_LEN + LANES, q * BLOCK_LEN):
+                rows_of.append(jnp.concatenate([tiles_at(h, c, start) for c in range(2)], 1))
+            tables.append(jnp.concatenate(rows_of, 0))
         lhs = jnp.concatenate([both[:, cols], turned_both[:, cols]], 1)
         by_high = dot_nt(lhs, tables[0])
         by_low = dot_nt(lhs[:rows], tables[1])
@@ -297,20 +322,24 @@
         copy.wait()
 
 
-def lag_call(ys, table, after, groups, owners):
+def lag_call(ys, table, edge, tiles, rounds, after, groups, owners):
     blocks = ys[0].shape[1] // BLOCK_LEN
     shape = (owners, blocks + groups // 2, SUBLANES, LANES)
     vmem = pl.BlockSpec(memory_space=pltpu.VMEM)
     return pl.pallas_call(
-        functools.partial(lag_kernel, groups),
-        in_specs=[vmem] * (len(ys) + 1) + [pl.BlockSpec(memory_space=pl.ANY)],
+        functools.partial(lag_kernel, groups, len(ys)),
+        in_specs=[vmem] * (len(ys) + 3 + len(rounds)) + [pl.BlockSpec(memory_space=pl.ANY)],
         out_specs=pl.BlockSpec(memory_space=pltpu.HBM),
         out_shape=jax.ShapeDtypeStruct(shape, jnp.float32),
-        scratch_shapes=[pltpu.VMEM(shape, jnp.float32), pltpu.SemaphoreType.DMA((blocks // 2 + 1,))],
+        scratch_shapes=[
+            pltpu.VMEM(shape, jnp.float32),
+            pltpu.SemaphoreType.DMA((blocks // 2 + 1,)),
+            pltpu.VMEM((2, 2, LANES, 2 * LANES), jnp.bfloat16),
+        ],
         compiler_params=params(),
         cost_estimate=cost(2.1),
         name="lag_products",
-    )(*ys, table, after)
+    )(*ys, table, edge, tiles, *rounds, after)
 
 
 BATCH = 4
@@ -530,13 +559,16 @@
     half = SUBLANES // 2
     wave = (wave_ref[0], wave_ref[1])
     copies = []
-    for g in range(half):
-        parts = [held_ref[pl.ds(c * half + g, total, stride=SUBLANES), :] for c in range(2)]
-        spectrum = dot_split(halves(jnp.concatenate(parts, 0).T), wave)
-        for i in range(groups):
-            beam = half * i + g
+    for first in range(0, half, 2):
+        lagged = []
+        for g in (first, first + 1):
+            parts = [held_ref[pl.ds(c * half + g, total, stride=SUBLANES), :] for c in range(2)]
+            lagged.append(jnp.concatenate(parts, 0).T)
+        spectrum = dot_split(halves(jnp.concatenate(lagged, 0)), wave)
+        for n in range(2 * groups):
+            beam = half * (n % groups) + first + n // groups
             for c in range(2):
-                out_ref[beam, c] = spectrum[i * lags_local : (i + 1) * lags_local, c * DOPPLER : (c + 1) * DOPPLER]
+                out_ref[beam, c] = spectrum[n * lags_local : (n + 1) * lags_local, c * DOPPLER : (c + 1) * DOPPLER]
             copies.append(pltpu.make_async_copy(out_ref.at[beam], out_hbm.at[beam], out_sem.at[beam]))
             copies[-1].start()
     for copy in copies:
@@ -577,11 +609,7 @@
     samples = length * tm_count
 
     survey = surveillance.reshape(2 * channels, length)
-    kept, moved, tiles, edge = beam_call(steering, survey, ref_signal, chan_count, beams_local)
-    early = 1 if tm_count < 4 else 2
-    edge = lax.ppermute(
-        edge, "tm", [(i, i + 1) for i in range(tm_count - 1) if i ^ (i + 1) >= 1 << early]
-    )
+    kept, moved, tiles = beam_call(steering, survey, ref_signal, chan_count, beams_local)
     near = swap(tiles[None], "tm", 1)
     shape = (chan_count // 2, 2 * beams_local, length)
     kept, got = kept.reshape(shape), swap(moved, "chan", 1).reshape(shape)
@@ -592,13 +620,17 @@
         by *= 2
     rounds = [near]
     joined = join_call(tiles[None], near, moved)
+    early = 1 if tm_count < 4 else 2
+    edge = lax.ppermute(
+        edge_call(joined), "tm", [(i, i + 1) for i in range(tm_count - 1) if i ^ (i + 1) >= 1 << early]
+    )
     while joined.shape[0] < tm_count:
         rounds.append(swap(joined, "tm", joined.shape[0]))
         if joined.shape[0] * 2 == tm_count:
             break
         joined = join_call(joined, rounds[-1])
-    table = table_call(edge, tiles, rounds[:early])
-    pieces = lag_call([kept[0], got[0]], table, joined, groups, tm_count)
+    table = table_call(tiles)
+    pieces = lag_call([kept[0], got[0]], table, edge, tiles, rounds[:early], joined, groups, tm_count)
     got = lax.all_to_all(pieces, "tm", 0, 0, tiled=True)
     own, line, tail = own_call([tiles[None]] + rounds, lags_local, pieces)
     gram, solver = solver_call(line, tail)

time: 34.5 us -> 34.5 us (level)
  starting transfers between devices: 15.8 us -> 16.4 us
  waiting for transfers between devices: 2.58 us -> 2.08 us
    ppermute x5, waiting for transfers between devices: 1.4 us -> 0.77 us  [swap(): return lax.ppermute(x, axis, pairs)]
    all_to_all x1, starting transfers between devices: 5.46 us -> 6.01 us  [tiled_device(): got = lax.all_to_all(pieces, 'tm', 0, 0, tiled=True)]
    pallas_call x1 -> x2, Pallas kernels: 2.16 us -> 2.15 us  [the longest x1 2.14 us: lag_call(): pl.pallas_call(functools.partial(lag_kernel, groups, len(ys)), in_specs=[...]
  transfers between devices with their start and end apart: 7 -> 7, of which waited for: 2 -> 2; matrix products, arithmetic and copies ran while one was open for 0% -> 0% of each run, Pallas kernels for 33% -> 32%
where the time goes in v12:
time: 34.5 us; the launch traced here: 34.3 us
  starting transfers between devices  16.4 us (48%)
  Pallas kernels  15.8 us (46%)
  waiting for transfers between devices  2.08 us (6%)
    ppermute x5, starting transfers between devices, swap(): return lax.ppermute(x, axis, pairs)  9.72 us
    pallas_call x1, Pallas kernels, own_call(): pl.pallas_call(functools.partial(own_kernel, lags_local), in_specs=[pl.Bl...  6.25 us
    all_to_all x1, starting transfers between devices, tiled_device(): got = lax.all_to_all(pieces, 'tm', 0, 0, tiled=True)  6.01 us
    pallas_call x1, Pallas kernels, map_call(): pl.pallas_call(functools.partial(map_kernel, groups), in_specs=[pl.BlockS...  2.49 us
    pallas_call x1, Pallas kernels, beam_call(): pl.pallas_call(functools.partial(beam_kernel, chan_count, beams_local), i...  2.16 us
    pallas_call x1, Pallas kernels, lag_call(): pl.pallas_call(functools.partial(lag_kernel, groups, len(ys)), in_specs=[...  2.14 us
    pallas_call x1, Pallas kernels, solver_call(): pl.pallas_call(solver_kernel, out_shape=[out, out], compiler_params=param...  2.05 us
    all_to_all x1, waiting for transfers between devices, tiled_device(): got = lax.all_to_all(pieces, 'tm', 0, 0, tiled=True)  1.31 us
  transfers between devices with their start and end apart: 7, of which 2 were waited for; matrix products, arithmetic and copies ran while one was open for 0% of the time, Pallas kernels for 32%

profile of v12, /device:TPU:0, one launch (start us, length us, event | category | flops | bytes accessed | tf_op | source)
XLA Modules:
  0.0 34.3 jit_solution(11121670705283913245)
XLA Ops:
  0.0 2.2 %beams.1 = (f32[64,2048]{1,0:T(8,128)S(1)}, f32[64,2048]{1,0:T(8,128)S(1)}, f32[2,16,128]{2,1,0:T(8,128)S(1)}) custom-call(f32[2,64,64]{2,1,0:T(8,128)} %w_hbm.1, f32[128,2048]{1,0:T(8,128)} %bitcast.13, f32[2,2048]{1,0:T(2,128)} %ref_hbm.1), custom_call_target="tpu_custom_call" | custom-call | flops 2529999872 | tf_op jit(solution)/shard_map/beams/pallas_call | solution.py:133
  2.2 0.5 %collective-permute-start = (f32[64,2048]{1,0:T(8,128)S(1)}, f32[64,2048]{1,0:T(8,128)S(1)}, u32[]{:S(2)}, u32[]{:S(2)}) collective-permute-start(f32[64,2048]{1,0:T(8,128)S(1)} %get-tuple-element.16), channel_id=1, source_target_pairs={{0,8},{8,0},{16,24},{24,16},{1,9},{9,1},{17,25},{25,17},{2,10},{10... | collective-permute-start | bytes 1572872 | tf_op jit(solution)/shard_map/ppermute | solution.py:600
  2.7 2.6 %collective-permute-start.2 = (f32[1,2,16,128]{3,2,1,0:T(8,128)S(1)}, f32[1,2,16,128]{3,2,1,0:T(8,128)S(1)}, u32[]{:S(2)}, u32[]{:S(2)}) collective-permute-start(f32[1,2,16,128]{3,2,1,0:T(8,128)S(1)} %bitcast.10), channel_id=1, source_target_pairs={{0,1},{1,0},{2,3},{3,2},{4,5},{5,4},{6,7},{7,6},{8,9},{9,8},{10,11... | collective-permute-start | bytes 49160 | tf_op jit(solution)/shard_map/ppermute | solution.py:600
  5.3 0.0 collective-permute-done
  5.3 0.1 halves_summed.1
  5.3 1.9 %collective-permute-start.1 = (f32[1,32,2048]{2,1,0:T(8,128)S(1)}, f32[1,32,2048]{2,1,0:T(8,128)S(1)}, u32[]{:S(2)}, u32[]{:S(2)}) collective-permute-start(f32[1,32,2048]{2,1,0:T(8,128)S(1)} %get-tuple-element.18.refs_0_), channel_id=1, source_target_pairs={{0,16},{8,24},{16,0},{24,8},{1,17},{9,25},{17,1},{25,9},{2,18},{10... | collective-permute-start | bytes 786440 | tf_op jit(solution)/shard_map/ppermute | solution.py:600
  7.2 0.0 collective-permute-done.2.second_ref.refs_5_.refs_1_
  7.2 1.9 %collective-permute-start.4 = (f32[2,2,16,128]{3,2,1,0:T(8,128)S(1)}, f32[2,2,16,128]{3,2,1,0:T(8,128)S(1)}, u32[]{:S(2)}, u32[]{:S(2)}) collective-permute-start(f32[2,2,16,128]{3,2,1,0:T(8,128)S(1)} %reference_joined.2.blocks_ref.first_ref), channel_id=1, source_target_pairs={{0,2},{1,3},{2,0},{3,1},{4,6},{5,7},{6,4},{7,5},{8,10},{9,11},{10,... | collective-permute-start | bytes 98312 | tf_op jit(solution)/shard_map/ppermute | solution.py:600
  9.1 0.6 %shifted_reference.1.refs_2_ = bf16[2,2,128,1920]{3,2,1,0:T(8,128)(2,1)S(1)} custom-call(f32[2,16,128]{2,1,0:T(8,128)S(1)} %get-tuple-element.19.tiles_ref.refs_4_), custom_call_target="tpu_custom_call" | custom-call | flops 805000000 | tf_op jit(solution)/shard_map/shifted_reference/pallas_call | solution.py:236
  9.7 0.7 %collective-permute-start.3 = (f32[16,128]{1,0:T(8,128)S(1)}, f32[16,128]{1,0:T(8,128)S(1)}, u32[]{:S(2)}, u32[]{:S(2)}) collective-permute-start(f32[16,128]{1,0:T(8,128)S(1)} %reference_edge.1), channel_id=1, source_target_pairs={{3,4},{11,12},{19,20},{27,28}} | collective-permute-start | bytes 24584 | tf_op jit(solution)/shard_map/ppermute | solution.py:624
  10.4 0.8 %collective-permute-done.4.second_ref.refs_6_.refs_2_ = f32[2,2,16,128]{3,2,1,0:T(8,128)S(1)} collective-permute-done((f32[2,2,16,128]{3,2,1,0:T(8,128)S(1)}, f32[2,2,16,128]{3,2,1,0:T(8,128)S(1)}, u32[]{:S(2)}, u32[]{:S(2)}) %collective-permute-start.4) | collective-permute-done | bytes 32800 | tf_op jit(solution)/shard_map/ppermute | solution.py:600
  11.1 2.9 %collective-permute-start.5 = (f32[4,2,16,128]{3,2,1,0:T(8,128)S(1)}, f32[4,2,16,128]{3,2,1,0:T(8,128)S(1)}, u32[]{:S(2)}, u32[]{:S(2)}) collective-permute-start(f32[4,2,16,128]{3,2,1,0:T(8,128)S(1)} %reference_joined.3.refs_7_), channel_id=1, source_target_pairs={{0,4},{1,5},{2,6},{3,7},{4,0},{5,1},{6,2},{7,3},{8,12},{9,13},{10,... | collective-permute-start | bytes 196616 | tf_op jit(solution)/shard_map/ppermute | solution.py:600
  14.0 0.0 collective-permute-done.3.refs_3_
  14.0 0.0 collective-permute-done.1
  14.0 2.1 %lag_products.1.refs_4_ = f32[8,10,8,128]{3,2,1,0:T(8,128)} custom-call(f32[32,2048]{1,0:T(8,128)S(1)} %bitcast.8, f32[32,2048]{1,0:T(8,128)S(1)} %bitcast.9, bf16[2,2,128,1920]{3,2,1,0:T(8,128)(2,1)S(1)} %shifted_reference.1.refs_2_, f32[16,128]{1,0:T(8,128)S(1)} %collective-permute-done.3.refs_3_, f32[2,16,128]{2,1,0:T(8,128)S(1)} %get-tuple-element.19.tiles_ref.refs_4_, ...), custom_call_target="tpu_custom_call" | custom-call | flops 2415000064 | tf_op jit(solution)/shard_map/lag_products/pallas_call | solution.py:329
  16.2 6.0 %all-to-all-start = ((f32[8,10,8,128]{3,2,1,0:T(8,128)}), f32[8,10,8,128]{3,2,1,0:T(8,128)S(1)}, u32[]{:S(2)}, u32[]{:S(2)}) async-start(f32[8,10,8,128]{3,2,1,0:T(8,128)} %lag_products.1.refs_4_), calls=%async_computation | async-start | bytes 655360 | tf_op jit(solution)/shard_map/all_to_all | solution.py:634
  22.2 0.0 collective-permute-done.5.refs_3_
  22.2 6.2 %reference_products.1 = (bf16[2,2048,128]{2,1,0:T(8,128)(2,1)S(1)}, f32[8,128]{1,0:T(8,128)S(1)}, f32[128,128]{1,0:T(8,128)S(1)}) custom-call(f32[1,2,16,128]{3,2,1,0:T(8,128)S(1)} %bitcast.12, f32[1,2,16,128]{3,2,1,0:T(8,128)S(1)} %collective-permute-done.2.second_ref.refs_5_.refs_1_, ...), custom_call_target="tpu_custom_call" | custom-call | flops 7129999872 | tf_op jit(solution)/shard_map/reference_products/pallas_call | solution.py:442
  28.4 0.0 copy-start
  28.5 2.0 %gram_inverse.1 = (bf16[2,128,128]{2,1,0:T(8,128)(2,1)S(1)}, bf16[2,128,128]{2,1,0:T(8,128)(2,1)S(1)}) custom-call(f32[8,128]{1,0:T(8,128)S(1)} %get-tuple-element.21.line_ref, f32[128,128]{1,0:T(8,128)S(1)} %get-tuple-element.22.tail_ref), custom_call_target="tpu_custom_call" | custom-call | flops 2300000000 | tf_op jit(solution)/shard_map/gram_inverse/pallas_call | solution.py:509
  30.5 1.3 %all-to-all-done.got_ref = f32[8,10,8,128]{3,2,1,0:T(8,128)S(1)} async-done(((f32[8,10,8,128]{3,2,1,0:T(8,128)}), f32[8,10,8,128]{3,2,1,0:T(8,128)S(1)}, u32[]{:S(2)}, u32[]{:S(2)}) %all-to-all-start) | async-done | bytes 327712 | tf_op jit(solution)/shard_map/all_to_all | solution.py:634
  31.8 0.0 copy-done
  31.8 2.5 %range_doppler.1 = f32[16,2,32,256]{3,2,1,0:T(8,128)} custom-call(f32[8,10,8,128]{3,2,1,0:T(8,128)S(1)} %all-to-all-done.got_ref, bf16[2,2048,128]{2,1,0:T(8,128)(2,1)S(1)} %get-tuple-element.20.own_ref, bf16[2,128,128]{2,1,0:T(8,128)(2,1)S(1)} %get-tuple-element.23.gram_ref, bf16[2,128,128]{2,1,0:T(8,128)(2,1)S(1)} %get-tuple-element.24.solver_ref, ...), custom_call_target="tpu_custom_call" | custom-call | flops 2875000064 | tf_op jit(solution)/shard_map/range_doppler/pallas_call | solution.py:582
  (3 shorter events, 0.0 us)
Async XLA Ops:
  2.2 3.1 %collective-permute-start = (f32[64,2048]{1,0:T(8,128)S(1)}, f32[64,2048]{1,0:T(8,128)S(1)}, u32[]{:S(2)}, u32[]{:S(2)}) collective-permute-start(f32[64,2048]{1,0:T(8,128)S(1)} %get-tuple-element.16), channel_id=1, source_target_pairs={{0,8},{8,0},{16,24},{24,16},{1,9},{9,1},{17,25},{25,17},{2,10},{10... | collective-permute-start | bytes 1572872 | tf_op jit(solution)/shard_map/ppermute | solution.py:600
  2.7 4.5 %collective-permute-start.2 = (f32[1,2,16,128]{3,2,1,0:T(8,128)S(1)}, f32[1,2,16,128]{3,2,1,0:T(8,128)S(1)}, u32[]{:S(2)}, u32[]{:S(2)}) collective-permute-start(f32[1,2,16,128]{3,2,1,0:T(8,128)S(1)} %bitcast.10), channel_id=1, source_target_pairs={{0,1},{1,0},{2,3},{3,2},{4,5},{5,4},{6,7},{7,6},{8,9},{9,8},{10,11... | collective-permute-start | bytes 49160 | tf_op jit(solution)/shard_map/ppermute | solution.py:600
  5.3 8.7 %collective-permute-start.1 = (f32[1,32,2048]{2,1,0:T(8,128)S(1)}, f32[1,32,2048]{2,1,0:T(8,128)S(1)}, u32[]{:S(2)}, u32[]{:S(2)}) collective-permute-start(f32[1,32,2048]{2,1,0:T(8,128)S(1)} %get-tuple-element.18.refs_0_), channel_id=1, source_target_pairs={{0,16},{8,24},{16,0},{24,8},{1,17},{9,25},{17,1},{25,9},{2,18},{10... | collective-permute-start | bytes 786440 | tf_op jit(solution)/shard_map/ppermute | solution.py:600
  7.2 3.9 %collective-permute-start.4 = (f32[2,2,16,128]{3,2,1,0:T(8,128)S(1)}, f32[2,2,16,128]{3,2,1,0:T(8,128)S(1)}, u32[]{:S(2)}, u32[]{:S(2)}) collective-permute-start(f32[2,2,16,128]{3,2,1,0:T(8,128)S(1)} %reference_joined.2.blocks_ref.first_ref), channel_id=1, source_target_pairs={{0,2},{1,3},{2,0},{3,1},{4,6},{5,7},{6,4},{7,5},{8,10},{9,11},{10,... | collective-permute-start | bytes 98312 | tf_op jit(solution)/shard_map/ppermute | solution.py:600
  9.7 4.3 %collective-permute-start.3 = (f32[16,128]{1,0:T(8,128)S(1)}, f32[16,128]{1,0:T(8,128)S(1)}, u32[]{:S(2)}, u32[]{:S(2)}) collective-permute-start(f32[16,128]{1,0:T(8,128)S(1)} %reference_edge.1), channel_id=1, source_target_pairs={{3,4},{11,12},{19,20},{27,28}} | collective-permute-start | bytes 24584 | tf_op jit(solution)/shard_map/ppermute | solution.py:624
  11.1 11.0 %collective-permute-start.5 = (f32[4,2,16,128]{3,2,1,0:T(8,128)S(1)}, f32[4,2,16,128]{3,2,1,0:T(8,128)S(1)}, u32[]{:S(2)}, u32[]{:S(2)}) collective-permute-start(f32[4,2,16,128]{3,2,1,0:T(8,128)S(1)} %reference_joined.3.refs_7_), channel_id=1, source_target_pairs={{0,4},{1,5},{2,6},{3,7},{4,0},{5,1},{6,2},{7,3},{8,12},{9,13},{10,... | collective-permute-start | bytes 196616 | tf_op jit(solution)/shard_map/ppermute | solution.py:600
  16.2 15.6 %all-to-all-start = ((f32[8,10,8,128]{3,2,1,0:T(8,128)}), f32[8,10,8,128]{3,2,1,0:T(8,128)S(1)}, u32[]{:S(2)}, u32[]{:S(2)}) async-start(f32[8,10,8,128]{3,2,1,0:T(8,128)} %lag_products.1.refs_4_), calls=%async_computation | async-start | bytes 655360 | tf_op jit(solution)/shard_map/all_to_all | solution.py:634
  28.4 3.4 %copy-start = (bf16[2,128,512]{2,1,0:T(8,128)(2,1)S(1)}, bf16[2,128,512]{2,1,0:T(8,128)(2,1)}, u32[]{:S(2)}) copy-start(bf16[2,128,512]{2,1,0:T(8,128)(2,1)} %constant.2.clone.wave_ref) | copy-start | bytes 786436

commit v13 on v12

--- a/solution.py
+++ b/solution.py
@@ -458,7 +458,7 @@
     return jnp.concatenate([a, -lane_sign(a.shape) * pltpu.roll(a, a.shape[0], 1)], 0)
 
 
-def solver_kernel(line_ref, tail_ref, gram_ref, solver_ref):
+def solver_kernel(line_ref, tail_ref, solver_ref):
     total = line_ref[...]
     line = total[0:1] + lane_sign((1, LANES)) * pltpu.roll(total[1:2], TAPS, 1)
     low = lax.broadcasted_iota(jnp.int32, (1, LANES), 1) < TAPS
@@ -480,8 +480,8 @@
     gram_r = strict_r + strict_r.T + diag_r - (tails[:TAPS, :TAPS] + tails[TAPS:, TAPS:])
     gram_i = up_i - up_i.T - (tails[:TAPS, TAPS:] - tails[TAPS:, :TAPS])
     gram = jnp.concatenate([gram_r, gram_i], 1)
-    gram_halves = halves(as_factor(gram))
-    gram_ref[0], gram_ref[1] = gram_halves
+    gram_factor = as_factor(gram)
+    gram_halves = halves(gram_factor)
     one = (
         lax.broadcasted_iota(jnp.int32, gram.shape, 0) == lax.broadcasted_iota(jnp.int32, gram.shape, 1)
     ).astype(jnp.float32)
@@ -501,14 +501,17 @@
 
     start = (jnp.int32(0), jnp.float32(1.0), one * (1.0 / bound))
     _, _, inverse = lax.while_loop(again, newton, start)
-    solver_ref[0], solver_ref[1] = halves(as_factor(inverse))
+    seen = jnp.dot(inverse, gram_factor, precision=HIGHEST, preferred_element_type=jnp.float32)
+    inverse = inverse + jnp.dot(
+        one - seen, as_factor(inverse), precision=HIGHEST, preferred_element_type=jnp.float32
+    )
+    solver_ref[...] = as_factor(inverse)
 
 
 def solver_call(line, tail):
-    out = jax.ShapeDtypeStruct((2,) + tail.shape, jnp.bfloat16)
     return pl.pallas_call(
         solver_kernel,
-        out_shape=[out, out],
+        out_shape=jax.ShapeDtypeStruct(tail.shape, jnp.float32),
         compiler_params=params(),
         cost_estimate=cost(2.0),
         name="gram_inverse",
@@ -523,7 +526,7 @@
     return (np.concatenate([upper, lower], 0) * scale).astype(np.float32)
 
 
-def map_kernel(groups, got_ref, own_ref, gram_ref, solver_ref, wave_ref, out_hbm, held_ref, out_ref, out_sem):
+def map_kernel(groups, got_ref, own_ref, solver_ref, wave_ref, out_hbm, held_ref, out_ref, out_sem):
     owners, pieces = got_ref.shape[:2]
     blocks = pieces - groups // 2
     lags_local = LANES // groups
@@ -540,10 +543,7 @@
             other = -sign * pltpu.roll(there, SUBLANES // 2, 0)
             rows[part] = jnp.where(left, here, other)
     cross = jnp.concatenate(rows, 0)
-    solver = (solver_ref[0], solver_ref[1])
-    taps = dot_split(halves(cross), solver)
-    rest = cross - dot_split(halves(taps), (gram_ref[0], gram_ref[1]))
-    taps = taps + dot_split(halves(rest), solver)
+    taps = jnp.dot(cross, solver_ref[...], precision=HIGHEST, preferred_element_type=jnp.float32)
     taps_high, taps_low = halves(taps)
     taps_both = jnp.concatenate([taps_high, taps_low], 1)
     for q in range(0, total, 2 * groups):
@@ -575,13 +575,13 @@
         copy.wait()
 
 
-def map_call(got, own, gram, solver, wave, groups, beams_local):
+def map_call(got, own, solver, wave, groups, beams_local):
     total = got.shape[0] * (got.shape[1] - groups // 2)
     lags_local = LANES // groups
     shape = (beams_local, 2, lags_local, DOPPLER)
     return pl.pallas_call(
         functools.partial(map_kernel, groups),
-        in_specs=[pl.BlockSpec(memory_space=pltpu.VMEM)] * 5,
+        in_specs=[pl.BlockSpec(memory_space=pltpu.VMEM)] * 4,
         out_specs=pl.BlockSpec(memory_space=pltpu.HBM),
         out_shape=jax.ShapeDtypeStruct(shape, jnp.float32),
         scratch_shapes=[
@@ -592,7 +592,7 @@
         compiler_params=params(),
         cost_estimate=cost(2.5),
         name="range_doppler",
-    )(got, own, gram, solver, wave)
+    )(got, own, solver, wave)
 
 
 def swap(x, axis, by):
@@ -611,6 +611,10 @@
     survey = surveillance.reshape(2 * channels, length)
     kept, moved, tiles = beam_call(steering, survey, ref_signal, chan_count, beams_local)
     near = swap(tiles[None], "tm", 1)
+    early = 1 if tm_count < 4 else 2
+    edge = lax.ppermute(
+        edge_call(tiles[None]), "tm", [(i, i + 1) for i in range(tm_count - 1) if i ^ (i + 1) >= 1 << early]
+    )
     shape = (chan_count // 2, 2 * beams_local, length)
     kept, got = kept.reshape(shape), swap(moved, "chan", 1).reshape(shape)
     by = 2
@@ -619,11 +623,7 @@
         got = swap(moved, "chan", by)
         by *= 2
     rounds = [near]
-    joined = join_call(tiles[None], near, moved)
-    early = 1 if tm_count < 4 else 2
-    edge = lax.ppermute(
-        edge_call(joined), "tm", [(i, i + 1) for i in range(tm_count - 1) if i ^ (i + 1) >= 1 << early]
-    )
+    joined = join_call(tiles[None], near, moved, edge)
     while joined.shape[0] < tm_count:
         rounds.append(swap(joined, "tm", joined.shape[0]))
         if joined.shape[0] * 2 == tm_count:
@@ -633,11 +633,11 @@
     pieces = lag_call([kept[0], got[0]], table, edge, tiles, rounds[:early], joined, groups, tm_count)
     got = lax.all_to_all(pieces, "tm", 0, 0, tiled=True)
     own, line, tail = own_call([tiles[None]] + rounds, lags_local, pieces)
-    gram, solver = solver_call(line, tail)
+    solver = solver_call(line, tail)
     wave = doppler_table(samples // BLOCK_LEN, 0.125 / math.sqrt(samples))
     high = wave.astype(jnp.bfloat16)
     wave = np.stack([high, (wave - high.astype(np.float32)).astype(jnp.bfloat16)])
-    return map_call(got, own, gram, solver, jnp.asarray(wave), groups, beams_local)
+    return map_call(got, own, solver, jnp.asarray(wave), groups, beams_local)
 
 
 def lag_table(ref_ext, offset, lags):

time: 34.5 us -> 35.5 us (1.029)
  starting transfers between devices: 16.4 us -> 17.3 us
    ppermute x5, starting transfers between devices: 9.72 us -> 13.2 us  [swap(): return lax.ppermute(x, axis, pairs)]
    all_to_all x1, starting transfers between devices: 6.01 us -> 3.45 us  [tiled_device(): got = lax.all_to_all(pieces, 'tm', 0, 0, tiled=True)]
    all_to_all x1, waiting for transfers between devices: 1.31 us -> 0.16 us  [tiled_device(): got = lax.all_to_all(pieces, 'tm', 0, 0, tiled=True)]
    ppermute x5, waiting for transfers between devices: 0.77 us -> 1.73 us  [swap(): return lax.ppermute(x, axis, pairs)]
where the time goes in v13:
time: 35.5 us; the launch traced here: 35.2 us
  starting transfers between devices  17.3 us (49%)
  Pallas kernels  15.9 us (45%)
  waiting for transfers between devices  1.89 us (5%)
    ppermute x5, starting transfers between devices, swap(): return lax.ppermute(x, axis, pairs)  13.2 us
    pallas_call x1, Pallas kernels, own_call(): pl.pallas_call(functools.partial(own_kernel, lags_local), in_specs=[pl.Bl...  6.24 us
    all_to_all x1, starting transfers between devices, tiled_device(): got = lax.all_to_all(pieces, 'tm', 0, 0, tiled=True)  3.45 us
    pallas_call x1, Pallas kernels, map_call(): pl.pallas_call(functools.partial(map_kernel, groups), in_specs=[pl.BlockS...  2.46 us
    pallas_call x1, Pallas kernels, solver_call(): pl.pallas_call(solver_kernel, out_shape=jax.ShapeDtypeStruct(tail.shape,...  2.18 us
    pallas_call x1, Pallas kernels, beam_call(): pl.pallas_call(functools.partial(beam_kernel, chan_count, beams_local), i...  2.16 us
    pallas_call x1, Pallas kernels, lag_call(): pl.pallas_call(functools.partial(lag_kernel, groups, len(ys)), in_specs=[...  2.14 us
    ppermute x5, waiting for transfers between devices, swap(): return lax.ppermute(x, axis, pairs)  1.73 us
  transfers between devices with their start and end apart: 7, of which 2 were waited for; matrix products, arithmetic and copies ran while one was open for 0% of the time, Pallas kernels for 32%

profile of v13, /device:TPU:0, one launch (start us, length us, event | category | flops | bytes accessed | tf_op | source)
XLA Modules:
  0.0 35.2 jit_solution(17116680118691261247)
XLA Ops:
  0.0 2.2 %beams.1 = (f32[64,2048]{1,0:T(8,128)S(1)}, f32[64,2048]{1,0:T(8,128)S(1)}, f32[2,16,128]{2,1,0:T(8,128)S(1)}) custom-call(f32[2,64,64]{2,1,0:T(8,128)} %w_hbm.1, f32[128,2048]{1,0:T(8,128)} %bitcast.14, f32[2,2048]{1,0:T(2,128)} %ref_hbm.1), custom_call_target="tpu_custom_call" | custom-call | flops 2529999872 | tf_op jit(solution)/shard_map/beams/pallas_call | solution.py:133
  2.2 0.5 %collective-permute-start = (f32[64,2048]{1,0:T(8,128)S(1)}, f32[64,2048]{1,0:T(8,128)S(1)}, u32[]{:S(2)}, u32[]{:S(2)}) collective-permute-start(f32[64,2048]{1,0:T(8,128)S(1)} %get-tuple-element.14), channel_id=1, source_target_pairs={{0,8},{8,0},{16,24},{24,16},{1,9},{9,1},{17,25},{25,17},{2,10},{10... | collective-permute-start | bytes 1572872 | tf_op jit(solution)/shard_map/ppermute | solution.py:600
  2.7 2.6 %collective-permute-start.3 = (f32[1,2,16,128]{3,2,1,0:T(8,128)S(1)}, f32[1,2,16,128]{3,2,1,0:T(8,128)S(1)}, u32[]{:S(2)}, u32[]{:S(2)}) collective-permute-start(f32[1,2,16,128]{3,2,1,0:T(8,128)S(1)} %bitcast.10), channel_id=1, source_target_pairs={{0,1},{1,0},{2,3},{3,2},{4,5},{5,4},{6,7},{7,6},{8,9},{9,8},{10,11... | collective-permute-start | bytes 49160 | tf_op jit(solution)/shard_map/ppermute | solution.py:600
  5.3 0.6 %collective-permute-start.2 = (f32[16,128]{1,0:T(8,128)S(1)}, f32[16,128]{1,0:T(8,128)S(1)}, u32[]{:S(2)}, u32[]{:S(2)}) collective-permute-start(f32[16,128]{1,0:T(8,128)S(1)} %reference_edge.1), channel_id=1, source_target_pairs={{3,4},{11,12},{19,20},{27,28}} | collective-permute-start | bytes 24584 | tf_op jit(solution)/shard_map/ppermute | solution.py:615
  5.9 0.0 collective-permute-done
  6.0 0.1 halves_summed.1
  6.0 1.6 %collective-permute-start.1 = (f32[1,32,2048]{2,1,0:T(8,128)S(1)}, f32[1,32,2048]{2,1,0:T(8,128)S(1)}, u32[]{:S(2)}, u32[]{:S(2)}) collective-permute-start(f32[1,32,2048]{2,1,0:T(8,128)S(1)} %get-tuple-element.16.refs_0_), channel_id=1, source_target_pairs={{0,16},{8,24},{16,0},{24,8},{1,17},{9,25},{17,1},{25,9},{2,18},{10... | collective-permute-start | bytes 786440 | tf_op jit(solution)/shard_map/ppermute | solution.py:600
  7.6 0.0 collective-permute-done.2.refs_1_.refs_3_
  7.6 0.0 collective-permute-done.3.second_ref.refs_5_.refs_1_
  7.6 1.6 %collective-permute-start.4 = (f32[2,2,16,128]{3,2,1,0:T(8,128)S(1)}, f32[2,2,16,128]{3,2,1,0:T(8,128)S(1)}, u32[]{:S(2)}, u32[]{:S(2)}) collective-permute-start(f32[2,2,16,128]{3,2,1,0:T(8,128)S(1)} %reference_joined.2.first_ref), channel_id=1, source_target_pairs={{0,2},{1,3},{2,0},{3,1},{4,6},{5,7},{6,4},{7,5},{8,10},{9,11},{10,... | collective-permute-start | bytes 98312 | tf_op jit(solution)/shard_map/ppermute | solution.py:600
  9.2 0.6 %shifted_reference.1.refs_2_ = bf16[2,2,128,1920]{3,2,1,0:T(8,128)(2,1)S(1)} custom-call(f32[2,16,128]{2,1,0:T(8,128)S(1)} %get-tuple-element.17.tiles_ref.refs_4_), custom_call_target="tpu_custom_call" | custom-call | flops 805000000 | tf_op jit(solution)/shard_map/shifted_reference/pallas_call | solution.py:236
  9.8 1.7 %collective-permute-done.4.second_ref.refs_6_.refs_2_ = f32[2,2,16,128]{3,2,1,0:T(8,128)S(1)} collective-permute-done((f32[2,2,16,128]{3,2,1,0:T(8,128)S(1)}, f32[2,2,16,128]{3,2,1,0:T(8,128)S(1)}, u32[]{:S(2)}, u32[]{:S(2)}) %collective-permute-start.4) | collective-permute-done | bytes 32800 | tf_op jit(solution)/shard_map/ppermute | solution.py:600
  11.6 6.9 %collective-permute-start.5 = (f32[4,2,16,128]{3,2,1,0:T(8,128)S(1)}, f32[4,2,16,128]{3,2,1,0:T(8,128)S(1)}, u32[]{:S(2)}, u32[]{:S(2)}) collective-permute-start(f32[4,2,16,128]{3,2,1,0:T(8,128)S(1)} %reference_joined.3.refs_7_), channel_id=1, source_target_pairs={{0,4},{1,5},{2,6},{3,7},{4,0},{5,1},{6,2},{7,3},{8,12},{9,13},{10,... | collective-permute-start | bytes 196616 | tf_op jit(solution)/shard_map/ppermute | solution.py:600
  18.5 0.0 collective-permute-done.1
  18.5 2.1 %lag_products.1.refs_4_ = f32[8,10,8,128]{3,2,1,0:T(8,128)} custom-call(f32[32,2048]{1,0:T(8,128)S(1)} %bitcast.8, f32[32,2048]{1,0:T(8,128)S(1)} %bitcast.9, bf16[2,2,128,1920]{3,2,1,0:T(8,128)(2,1)S(1)} %shifted_reference.1.refs_2_, f32[16,128]{1,0:T(8,128)S(1)} %collective-permute-done.2.refs_1_.refs_3_, ...), custom_call_target="tpu_custom_call" | custom-call | flops 2415000064 | tf_op jit(solution)/shard_map/lag_products/pallas_call | solution.py:329
  20.6 3.4 %all-to-all-start = ((f32[8,10,8,128]{3,2,1,0:T(8,128)}), f32[8,10,8,128]{3,2,1,0:T(8,128)S(1)}, u32[]{:S(2)}, u32[]{:S(2)}) async-start(f32[8,10,8,128]{3,2,1,0:T(8,128)} %lag_products.1.refs_4_), calls=%async_computation | async-start | bytes 655360 | tf_op jit(solution)/shard_map/all_to_all | solution.py:634
  24.1 0.0 collective-permute-done.5.refs_3_
  24.1 6.2 %reference_products.1 = (bf16[2,2048,128]{2,1,0:T(8,128)(2,1)S(1)}, f32[8,128]{1,0:T(8,128)S(1)}, f32[128,128]{1,0:T(8,128)S(1)}) custom-call(f32[1,2,16,128]{3,2,1,0:T(8,128)S(1)} %bitcast.13, f32[1,2,16,128]{3,2,1,0:T(8,128)S(1)} %collective-permute-done.3.second_ref.refs_5_.refs_1_, ...), custom_call_target="tpu_custom_call" | custom-call | flops 7129999872 | tf_op jit(solution)/shard_map/reference_products/pallas_call | solution.py:442
  30.4 0.0 copy-start
  30.4 2.2 %gram_inverse.1.solver_ref = f32[128,128]{1,0:T(8,128)S(1)} custom-call(f32[8,128]{1,0:T(8,128)S(1)} %get-tuple-element.19.line_ref, f32[128,128]{1,0:T(8,128)S(1)} %get-tuple-element.20.tail_ref), custom_call_target="tpu_custom_call" | custom-call | flops 2300000000 | tf_op jit(solution)/shard_map/gram_inverse/pallas_call | solution.py:512
  32.5 0.2 all-to-all-done.got_ref
  32.7 0.0 copy-done
  32.7 2.5 %range_doppler.1 = f32[16,2,32,256]{3,2,1,0:T(8,128)} custom-call(f32[8,10,8,128]{3,2,1,0:T(8,128)S(1)} %all-to-all-done.got_ref, bf16[2,2048,128]{2,1,0:T(8,128)(2,1)S(1)} %get-tuple-element.18.own_ref, f32[128,128]{1,0:T(8,128)S(1)} %gram_inverse.1.solver_ref, bf16[2,128,512]{2,1,0:T(8,128)(2,1)S(1)} %copy-done), custom_call_target="tpu_custom_call" | custom-call | flops 2875000064 | tf_op jit(solution)/shard_map/range_doppler/pallas_call | solution.py:582
  (3 shorter events, 0.0 us)
Async XLA Ops:
  2.2 3.8 %collective-permute-start = (f32[64,2048]{1,0:T(8,128)S(1)}, f32[64,2048]{1,0:T(8,128)S(1)}, u32[]{:S(2)}, u32[]{:S(2)}) collective-permute-start(f32[64,2048]{1,0:T(8,128)S(1)} %get-tuple-element.14), channel_id=1, source_target_pairs={{0,8},{8,0},{16,24},{24,16},{1,9},{9,1},{17,25},{25,17},{2,10},{10... | collective-permute-start | bytes 1572872 | tf_op jit(solution)/shard_map/ppermute | solution.py:600
  2.7 4.9 %collective-permute-start.3 = (f32[1,2,16,128]{3,2,1,0:T(8,128)S(1)}, f32[1,2,16,128]{3,2,1,0:T(8,128)S(1)}, u32[]{:S(2)}, u32[]{:S(2)}) collective-permute-start(f32[1,2,16,128]{3,2,1,0:T(8,128)S(1)} %bitcast.10), channel_id=1, source_target_pairs={{0,1},{1,0},{2,3},{3,2},{4,5},{5,4},{6,7},{7,6},{8,9},{9,8},{10,11... | collective-permute-start | bytes 49160 | tf_op jit(solution)/shard_map/ppermute | solution.py:600
  5.3 2.3 %collective-permute-start.2 = (f32[16,128]{1,0:T(8,128)S(1)}, f32[16,128]{1,0:T(8,128)S(1)}, u32[]{:S(2)}, u32[]{:S(2)}) collective-permute-start(f32[16,128]{1,0:T(8,128)S(1)} %reference_edge.1), channel_id=1, source_target_pairs={{3,4},{11,12},{19,20},{27,28}} | collective-permute-start | bytes 24584 | tf_op jit(solution)/shard_map/ppermute | solution.py:615
  6.0 12.5 %collective-permute-start.1 = (f32[1,32,2048]{2,1,0:T(8,128)S(1)}, f32[1,32,2048]{2,1,0:T(8,128)S(1)}, u32[]{:S(2)}, u32[]{:S(2)}) collective-permute-start(f32[1,32,2048]{2,1,0:T(8,128)S(1)} %get-tuple-element.16.refs_0_), channel_id=1, source_target_pairs={{0,16},{8,24},{16,0},{24,8},{1,17},{9,25},{17,1},{25,9},{2,18},{10... | collective-permute-start | bytes 786440 | tf_op jit(solution)/shard_map/ppermute | solution.py:600
  7.6 4.0 %collective-permute-start.4 = (f32[2,2,16,128]{3,2,1,0:T(8,128)S(1)}, f32[2,2,16,128]{3,2,1,0:T(8,128)S(1)}, u32[]{:S(2)}, u32[]{:S(2)}) collective-permute-start(f32[2,2,16,128]{3,2,1,0:T(8,128)S(1)} %reference_joined.2.first_ref), channel_id=1, source_target_pairs={{0,2},{1,3},{2,0},{3,1},{4,6},{5,7},{6,4},{7,5},{8,10},{9,11},{10,... | collective-permute-start | bytes 98312 | tf_op jit(solution)/shard_map/ppermute | solution.py:600
  11.6 12.5 %collective-permute-start.5 = (f32[4,2,16,128]{3,2,1,0:T(8,128)S(1)}, f32[4,2,16,128]{3,2,1,0:T(8,128)S(1)}, u32[]{:S(2)}, u32[]{:S(2)}) collective-permute-start(f32[4,2,16,128]{3,2,1,0:T(8,128)S(1)} %reference_joined.3.refs_7_), channel_id=1, source_target_pairs={{0,4},{1,5},{2,6},{3,7},{4,0},{5,1},{6,2},{7,3},{8,12},{9,13},{10,... | collective-permute-start | bytes 196616 | tf_op jit(solution)/shard_map/ppermute | solution.py:600
  20.6 12.1 %all-to-all-start = ((f32[8,10,8,128]{3,2,1,0:T(8,128)}), f32[8,10,8,128]{3,2,1,0:T(8,128)S(1)}, u32[]{:S(2)}, u32[]{:S(2)}) async-start(f32[8,10,8,128]{3,2,1,0:T(8,128)} %lag_products.1.refs_4_), calls=%async_computation | async-start | bytes 655360 | tf_op jit(solution)/shard_map/all_to_all | solution.py:634
  30.4 2.3 %copy-start = (bf16[2,128,512]{2,1,0:T(8,128)(2,1)S(1)}, bf16[2,128,512]{2,1,0:T(8,128)(2,1)}, u32[]{:S(2)}) copy-start(bf16[2,128,512]{2,1,0:T(8,128)(2,1)} %constant.2.clone.wave_ref) | copy-start | bytes 786436

commit v14 on v12

--- a/solution.py
+++ b/solution.py
@@ -197,23 +197,6 @@
     )(first, second, *after)
 
 
-def edge_kernel(blocks_ref, out_ref):
-    rows = blocks_ref.shape[2]
-    out_ref[...] = jnp.zeros_like(out_ref)
-    for c in range(2):
-        out_ref[SUBLANES * c : SUBLANES * c + EDGE, :] = blocks_ref[0, c, rows - EDGE :, :]
-
-
-def edge_call(blocks):
-    return pl.pallas_call(
-        edge_kernel,
-        out_shape=jax.ShapeDtypeStruct((2 * SUBLANES, LANES), jnp.float32),
-        compiler_params=params(),
-        cost_estimate=cost(0.1),
-        name="reference_edge",
-    )(blocks)
-
-
 def spread_line(line, keep):
     for g in range(0, LANES, 2 * SUBLANES):
         tiled = jnp.broadcast_to(line, (2 * SUBLANES, line.shape[1]))
@@ -244,15 +227,13 @@
 
 def lag_kernel(groups, part_count, *refs):
     y_refs, refs = refs[:part_count], refs[part_count:]
-    table_ref, edge_ref, tiles_ref, *round_refs, _, out_hbm, out_ref, out_sem, first_ref = refs
+    table_ref, tiles_ref, *round_refs, _, out_hbm, out_ref, out_sem, first_ref = refs
     copies = []
 
     me = lax.axis_index("tm")
     for c in range(2):
-        before = edge_ref[SUBLANES * c : SUBLANES * c + EDGE, :]
-        for n, round_ref in enumerate(round_refs):
-            last = round_ref[round_ref.shape[0] - 1, c, round_ref.shape[2] - EDGE :, :]
-            before = jnp.where((me > 0) & ((me ^ (me - 1)) == 2 ** (n + 1) - 1), last, before)
+        tails = [ref[ref.shape[0] - 1, c, ref.shape[2] - EDGE :, :] for ref in round_refs]
+        before = jnp.where(me % 2 == 1, tails[0], jnp.where(me > 0, tails[-1], 0.0))
         line = jnp.concatenate([before[n : n + 1] for n in range(EDGE)] + [tiles_ref[c, 0:1, :]], 1)
 
         def keep(h, g, value):
@@ -322,13 +303,13 @@
         copy.wait()
 
 
-def lag_call(ys, table, edge, tiles, rounds, after, groups, owners):
+def lag_call(ys, table, tiles, rounds, after, groups, owners):
     blocks = ys[0].shape[1] // BLOCK_LEN
     shape = (owners, blocks + groups // 2, SUBLANES, LANES)
     vmem = pl.BlockSpec(memory_space=pltpu.VMEM)
     return pl.pallas_call(
         functools.partial(lag_kernel, groups, len(ys)),
-        in_specs=[vmem] * (len(ys) + 3 + len(rounds)) + [pl.BlockSpec(memory_space=pl.ANY)],
+        in_specs=[vmem] * (len(ys) + 2 + len(rounds)) + [pl.BlockSpec(memory_space=pl.ANY)],
         out_specs=pl.BlockSpec(memory_space=pltpu.HBM),
         out_shape=jax.ShapeDtypeStruct(shape, jnp.float32),
         scratch_shapes=[
@@ -339,7 +320,7 @@
         compiler_params=params(),
         cost_estimate=cost(2.1),
         name="lag_products",
-    )(*ys, table, edge, tiles, *rounds, after)
+    )(*ys, table, tiles, *rounds, after)
 
 
 BATCH = 4
@@ -356,11 +337,12 @@
     block_rows = BLOCK_LEN // LANES
 
     span_ref[...] = jnp.zeros_like(span_ref)
-    e = 0
+    n = 0
     for part_ref in part_refs:
         for i in range(part_ref.shape[0]):
-            span_ref[:, pl.ds(EDGE + (me ^ e) * part_rows, part_rows), :] = part_ref[i]
-            e += 1
+            block = lax.rem(me - (n // 2) * 2 + owners, owners) ^ (n % 2)
+            span_ref[:, pl.ds(EDGE + block * part_rows, part_rows), :] = part_ref[i]
+            n += 1
     late_rows = (me * lags_local) // LANES
     late_lanes = lax.rem(me * lags_local, LANES)
     turned = [pltpu.roll(span_ref[c], late_lanes, 1) for c in range(2)]
@@ -620,17 +602,14 @@
         by *= 2
     rounds = [near]
     joined = join_call(tiles[None], near, moved)
-    early = 1 if tm_count < 4 else 2
-    edge = lax.ppermute(
-        edge_call(joined), "tm", [(i, i + 1) for i in range(tm_count - 1) if i ^ (i + 1) >= 1 << early]
-    )
-    while joined.shape[0] < tm_count:
-        rounds.append(swap(joined, "tm", joined.shape[0]))
-        if joined.shape[0] * 2 == tm_count:
+    while True:
+        count = joined.shape[0]
+        rounds.append(lax.ppermute(joined, "tm", [(i, (i + count) % tm_count) for i in range(tm_count)]))
+        if count * 2 == tm_count:
             break
         joined = join_call(joined, rounds[-1])
     table = table_call(tiles)
-    pieces = lag_call([kept[0], got[0]], table, edge, tiles, rounds[:early], joined, groups, tm_count)
+    pieces = lag_call([kept[0], got[0]], table, tiles, rounds[:2], joined, groups, tm_count)
     got = lax.all_to_all(pieces, "tm", 0, 0, tiled=True)
     own, line, tail = own_call([tiles[None]] + rounds, lags_local, pieces)
     gram, solver = solver_call(line, tail)
@@ -715,7 +694,7 @@
         and beams_local * lags_local == LANES * SUBLANES // 2
         and chan_count > 1
         and chan_count & (chan_count - 1) == 0
-        and tm_count > 1
+        and tm_count > 2
         and tm_count & (tm_count - 1) == 0
         and 2 * surveillance.shape[1] % LANES == 0
         and surveillance.shape[2] % (2 * BATCH * BLOCK_LEN) == 0

time: 34.5 us -> 34.5 us (level)
  starting transfers between devices: 16.4 us -> 13.7 us
  waiting for transfers between devices: 2.08 us -> 4.74 us
    ppermute x5 -> x3, starting transfers between devices: 9.72 us -> 4.98 us  [swap(): return lax.ppermute(x, axis, pairs)]
    ppermute x1 -> x2, waiting for transfers between devices: 0.01 us -> 3.3 us  [tiled_device(): lax.ppermute(joined, 'tm', [(i, (i + count) % tm_count) for i in range(tm...]
    ppermute x1 -> x2, starting transfers between devices: 0.66 us -> 2.87 us  [tiled_device(): lax.ppermute(joined, 'tm', [(i, (i + count) % tm_count) for i in range(tm...]
    ppermute x5 -> x3, waiting for transfers between devices: 0.77 us -> 0.01 us  [swap(): return lax.ppermute(x, axis, pairs)]
  transfers between devices with their start and end apart: 7 -> 6, of which waited for: 2 -> 2; matrix products, arithmetic and copies ran while one was open for 0% -> 0% of each run, Pallas kernels for 32% -> 32%
where the time goes in v14:
time: 34.5 us; the launch traced here: 34.3 us
  Pallas kernels  15.8 us (46%)
  starting transfers between devices  13.7 us (40%)
  waiting for transfers between devices  4.74 us (14%)
    pallas_call x1, Pallas kernels, own_call(): pl.pallas_call(functools.partial(own_kernel, lags_local), in_specs=[pl.Bl...  6.25 us
    all_to_all x1, starting transfers between devices, tiled_device(): got = lax.all_to_all(pieces, 'tm', 0, 0, tiled=True)  5.89 us
    ppermute x3, starting transfers between devices, swap(): return lax.ppermute(x, axis, pairs)  4.98 us
    ppermute x2, waiting for transfers between devices, tiled_device(): lax.ppermute(joined, 'tm', [(i, (i + count) % tm_count) for i in range(tm...  3.3 us
    ppermute x2, starting transfers between devices, tiled_device(): lax.ppermute(joined, 'tm', [(i, (i + count) % tm_count) for i in range(tm...  2.87 us
    pallas_call x1, Pallas kernels, map_call(): pl.pallas_call(functools.partial(map_kernel, groups), in_specs=[pl.BlockS...  2.49 us
    pallas_call x1, Pallas kernels, beam_call(): pl.pallas_call(functools.partial(beam_kernel, chan_count, beams_local), i...  2.16 us
    pallas_call x1, Pallas kernels, lag_call(): pl.pallas_call(functools.partial(lag_kernel, groups, len(ys)), in_specs=[...  2.15 us
  transfers between devices with their start and end apart: 6, of which 2 were waited for; matrix products, arithmetic and copies ran while one was open for 0% of the time, Pallas kernels for 32%

profile of v14, /device:TPU:0, one launch (start us, length us, event | category | flops | bytes accessed | tf_op | source)
XLA Modules:
  0.0 34.3 jit_solution(13722533154311543788)
XLA Ops:
  0.0 2.2 %beams.1 = (f32[64,2048]{1,0:T(8,128)S(1)}, f32[64,2048]{1,0:T(8,128)S(1)}, f32[2,16,128]{2,1,0:T(8,128)S(1)}) custom-call(f32[2,64,64]{2,1,0:T(8,128)} %w_hbm.1, f32[128,2048]{1,0:T(8,128)} %bitcast.13, f32[2,2048]{1,0:T(2,128)} %ref_hbm.1), custom_call_target="tpu_custom_call" | custom-call | flops 2529999872 | tf_op jit(solution)/shard_map/beams/pallas_call | solution.py:133
  2.2 0.5 %collective-permute-start = (f32[64,2048]{1,0:T(8,128)S(1)}, f32[64,2048]{1,0:T(8,128)S(1)}, u32[]{:S(2)}, u32[]{:S(2)}) collective-permute-start(f32[64,2048]{1,0:T(8,128)S(1)} %get-tuple-element.16), channel_id=1, source_target_pairs={{0,8},{8,0},{16,24},{24,16},{1,9},{9,1},{17,25},{25,17},{2,10},{10... | collective-permute-start | bytes 1572872 | tf_op jit(solution)/shard_map/ppermute | solution.py:582
  2.7 2.6 %collective-permute-start.2 = (f32[1,2,16,128]{3,2,1,0:T(8,128)S(1)}, f32[1,2,16,128]{3,2,1,0:T(8,128)S(1)}, u32[]{:S(2)}, u32[]{:S(2)}) collective-permute-start(f32[1,2,16,128]{3,2,1,0:T(8,128)S(1)} %bitcast.10), channel_id=1, source_target_pairs={{0,1},{1,0},{2,3},{3,2},{4,5},{5,4},{6,7},{7,6},{8,9},{9,8},{10,11... | collective-permute-start | bytes 49160 | tf_op jit(solution)/shard_map/ppermute | solution.py:582
  5.3 0.0 collective-permute-done
  5.3 0.1 halves_summed.1
  5.3 1.9 %collective-permute-start.1 = (f32[1,32,2048]{2,1,0:T(8,128)S(1)}, f32[1,32,2048]{2,1,0:T(8,128)S(1)}, u32[]{:S(2)}, u32[]{:S(2)}) collective-permute-start(f32[1,32,2048]{2,1,0:T(8,128)S(1)} %get-tuple-element.18.refs_0_), channel_id=1, source_target_pairs={{0,16},{8,24},{16,0},{24,8},{1,17},{9,25},{17,1},{25,9},{2,18},{10... | collective-permute-start | bytes 786440 | tf_op jit(solution)/shard_map/ppermute | solution.py:582
  7.2 0.0 collective-permute-done.2.second_ref.refs_4_.refs_1_
  7.2 1.9 %collective-permute-start.3 = (f32[2,2,16,128]{3,2,1,0:T(8,128)S(1)}, f32[2,2,16,128]{3,2,1,0:T(8,128)S(1)}, u32[]{:S(2)}, u32[]{:S(2)}) collective-permute-start(f32[2,2,16,128]{3,2,1,0:T(8,128)S(1)} %reference_joined.2.first_ref), channel_id=1, source_target_pairs={{0,2},{1,3},{2,4},{3,5},{4,6},{5,7},{6,0},{7,1},{8,10},{9,11},{10,... | collective-permute-start | bytes 98312 | tf_op jit(solution)/shard_map/ppermute | solution.py:607
  9.1 0.6 %shifted_reference.1.refs_2_ = bf16[2,2,128,1920]{3,2,1,0:T(8,128)(2,1)S(1)} custom-call(f32[2,16,128]{2,1,0:T(8,128)S(1)} %get-tuple-element.19.tiles_ref.refs_3_), custom_call_target="tpu_custom_call" | custom-call | flops 805000000 | tf_op jit(solution)/shard_map/shifted_reference/pallas_call | solution.py:219
  9.7 3.3 %collective-permute-done.3.second_ref.refs_5_.refs_2_ = f32[2,2,16,128]{3,2,1,0:T(8,128)S(1)} collective-permute-done((f32[2,2,16,128]{3,2,1,0:T(8,128)S(1)}, f32[2,2,16,128]{3,2,1,0:T(8,128)S(1)}, u32[]{:S(2)}, u32[]{:S(2)}) %collective-permute-start.3) | collective-permute-done | bytes 32800 | tf_op jit(solution)/shard_map/ppermute | solution.py:607
  13.0 1.0 %collective-permute-start.4 = (f32[4,2,16,128]{3,2,1,0:T(8,128)S(1)}, f32[4,2,16,128]{3,2,1,0:T(8,128)S(1)}, u32[]{:S(2)}, u32[]{:S(2)}) collective-permute-start(f32[4,2,16,128]{3,2,1,0:T(8,128)S(1)} %reference_joined.3.refs_6_), channel_id=1, source_target_pairs={{0,4},{1,5},{2,6},{3,7},{4,0},{5,1},{6,2},{7,3},{8,12},{9,13},{10,... | collective-permute-start | bytes 196616 | tf_op jit(solution)/shard_map/ppermute | solution.py:607
  14.0 0.0 collective-permute-done.1
  14.0 2.1 %lag_products.1.refs_4_ = f32[8,10,8,128]{3,2,1,0:T(8,128)} custom-call(f32[32,2048]{1,0:T(8,128)S(1)} %bitcast.8, f32[32,2048]{1,0:T(8,128)S(1)} %bitcast.9, bf16[2,2,128,1920]{3,2,1,0:T(8,128)(2,1)S(1)} %shifted_reference.1.refs_2_, f32[2,16,128]{2,1,0:T(8,128)S(1)} %get-tuple-element.19.tiles_ref.refs_3_, ...), custom_call_target="tpu_custom_call" | custom-call | flops 2415000064 | tf_op jit(solution)/shard_map/lag_products/pallas_call | solution.py:310
  16.2 5.9 %all-to-all-start = ((f32[8,10,8,128]{3,2,1,0:T(8,128)}), f32[8,10,8,128]{3,2,1,0:T(8,128)S(1)}, u32[]{:S(2)}, u32[]{:S(2)}) async-start(f32[8,10,8,128]{3,2,1,0:T(8,128)} %lag_products.1.refs_4_), calls=%async_computation | async-start | bytes 655360 | tf_op jit(solution)/shard_map/all_to_all | solution.py:613
  22.1 0.0 collective-permute-done.4.refs_3_
  22.1 6.2 %reference_products.1 = (bf16[2,2048,128]{2,1,0:T(8,128)(2,1)S(1)}, f32[8,128]{1,0:T(8,128)S(1)}, f32[128,128]{1,0:T(8,128)S(1)}) custom-call(f32[1,2,16,128]{3,2,1,0:T(8,128)S(1)} %bitcast.12, f32[1,2,16,128]{3,2,1,0:T(8,128)S(1)} %collective-permute-done.2.second_ref.refs_4_.refs_1_, ...), custom_call_target="tpu_custom_call" | custom-call | flops 7129999872 | tf_op jit(solution)/shard_map/reference_products/pallas_call | solution.py:424
  28.3 0.0 copy-start
  28.3 2.0 %gram_inverse.1 = (bf16[2,128,128]{2,1,0:T(8,128)(2,1)S(1)}, bf16[2,128,128]{2,1,0:T(8,128)(2,1)S(1)}) custom-call(f32[8,128]{1,0:T(8,128)S(1)} %get-tuple-element.21.line_ref, f32[128,128]{1,0:T(8,128)S(1)} %get-tuple-element.22.tail_ref), custom_call_target="tpu_custom_call" | custom-call | flops 2300000000 | tf_op jit(solution)/shard_map/gram_inverse/pallas_call | solution.py:491
  30.4 1.4 %all-to-all-done.got_ref = f32[8,10,8,128]{3,2,1,0:T(8,128)S(1)} async-done(((f32[8,10,8,128]{3,2,1,0:T(8,128)}), f32[8,10,8,128]{3,2,1,0:T(8,128)S(1)}, u32[]{:S(2)}, u32[]{:S(2)}) %all-to-all-start) | async-done | bytes 327712 | tf_op jit(solution)/shard_map/all_to_all | solution.py:613
  31.8 0.0 copy-done
  31.8 2.5 %range_doppler.1 = f32[16,2,32,256]{3,2,1,0:T(8,128)} custom-call(f32[8,10,8,128]{3,2,1,0:T(8,128)S(1)} %all-to-all-done.got_ref, bf16[2,2048,128]{2,1,0:T(8,128)(2,1)S(1)} %get-tuple-element.20.own_ref, bf16[2,128,128]{2,1,0:T(8,128)(2,1)S(1)} %get-tuple-element.23.gram_ref, bf16[2,128,128]{2,1,0:T(8,128)(2,1)S(1)} %get-tuple-element.24.solver_ref, ...), custom_call_target="tpu_custom_call" | custom-call | flops 2875000064 | tf_op jit(solution)/shard_map/range_doppler/pallas_call | solution.py:564
  (2 shorter events, 0.0 us)
Async XLA Ops:
  2.2 3.1 %collective-permute-start = (f32[64,2048]{1,0:T(8,128)S(1)}, f32[64,2048]{1,0:T(8,128)S(1)}, u32[]{:S(2)}, u32[]{:S(2)}) collective-permute-start(f32[64,2048]{1,0:T(8,128)S(1)} %get-tuple-element.16), channel_id=1, source_target_pairs={{0,8},{8,0},{16,24},{24,16},{1,9},{9,1},{17,25},{25,17},{2,10},{10... | collective-permute-start | bytes 1572872 | tf_op jit(solution)/shard_map/ppermute | solution.py:582
  2.7 4.5 %collective-permute-start.2 = (f32[1,2,16,128]{3,2,1,0:T(8,128)S(1)}, f32[1,2,16,128]{3,2,1,0:T(8,128)S(1)}, u32[]{:S(2)}, u32[]{:S(2)}) collective-permute-start(f32[1,2,16,128]{3,2,1,0:T(8,128)S(1)} %bitcast.10), channel_id=1, source_target_pairs={{0,1},{1,0},{2,3},{3,2},{4,5},{5,4},{6,7},{7,6},{8,9},{9,8},{10,11... | collective-permute-start | bytes 49160 | tf_op jit(solution)/shard_map/ppermute | solution.py:582
  5.3 8.7 %collective-permute-start.1 = (f32[1,32,2048]{2,1,0:T(8,128)S(1)}, f32[1,32,2048]{2,1,0:T(8,128)S(1)}, u32[]{:S(2)}, u32[]{:S(2)}) collective-permute-start(f32[1,32,2048]{2,1,0:T(8,128)S(1)} %get-tuple-element.18.refs_0_), channel_id=1, source_target_pairs={{0,16},{8,24},{16,0},{24,8},{1,17},{9,25},{17,1},{25,9},{2,18},{10... | collective-permute-start | bytes 786440 | tf_op jit(solution)/shard_map/ppermute | solution.py:582
  7.2 5.8 %collective-permute-start.3 = (f32[2,2,16,128]{3,2,1,0:T(8,128)S(1)}, f32[2,2,16,128]{3,2,1,0:T(8,128)S(1)}, u32[]{:S(2)}, u32[]{:S(2)}) collective-permute-start(f32[2,2,16,128]{3,2,1,0:T(8,128)S(1)} %reference_joined.2.first_ref), channel_id=1, source_target_pairs={{0,2},{1,3},{2,4},{3,5},{4,6},{5,7},{6,0},{7,1},{8,10},{9,11},{10,... | collective-permute-start | bytes 98312 | tf_op jit(solution)/shard_map/ppermute | solution.py:607
  13.0 9.1 %collective-permute-start.4 = (f32[4,2,16,128]{3,2,1,0:T(8,128)S(1)}, f32[4,2,16,128]{3,2,1,0:T(8,128)S(1)}, u32[]{:S(2)}, u32[]{:S(2)}) collective-permute-start(f32[4,2,16,128]{3,2,1,0:T(8,128)S(1)} %reference_joined.3.refs_6_), channel_id=1, source_target_pairs={{0,4},{1,5},{2,6},{3,7},{4,0},{5,1},{6,2},{7,3},{8,12},{9,13},{10,... | collective-permute-start | bytes 196616 | tf_op jit(solution)/shard_map/ppermute | solution.py:607
  16.2 15.6 %all-to-all-start = ((f32[8,10,8,128]{3,2,1,0:T(8,128)}), f32[8,10,8,128]{3,2,1,0:T(8,128)S(1)}, u32[]{:S(2)}, u32[]{:S(2)}) async-start(f32[8,10,8,128]{3,2,1,0:T(8,128)} %lag_products.1.refs_4_), calls=%async_computation | async-start | bytes 655360 | tf_op jit(solution)/shard_map/all_to_all | solution.py:613
  28.3 3.5 %copy-start = (bf16[2,128,512]{2,1,0:T(8,128)(2,1)S(1)}, bf16[2,128,512]{2,1,0:T(8,128)(2,1)}, u32[]{:S(2)}) copy-start(bf16[2,128,512]{2,1,0:T(8,128)(2,1)} %constant.2.clone.wave_ref) | copy-start | bytes 786436

commit v15 on v14

--- a/solution.py
+++ b/solution.py
@@ -241,14 +241,13 @@
 
         spread_line(line, keep)
 
-    def tiles_at(h, c, start):
-        known = first_ref.shape[3]
-        if start >= known:
-            return table_ref[h, c, :, start - known : start - known + BLOCK_LEN]
-        if start + BLOCK_LEN <= known:
-            return first_ref[h, c, :, start : start + BLOCK_LEN]
-        rest = start + BLOCK_LEN - known
-        return jnp.concatenate([first_ref[h, c, :, start:], table_ref[h, c, :, :rest]], 1)
+    def table_tile(h, n):
+        parts = []
+        for c in range(2):
+            known = first_ref.shape[3] // LANES
+            ref, at = (first_ref, n) if n < known else (table_ref, n - known)
+            parts.append(ref[h, c, :, at * LANES : (at + 1) * LANES])
+        return jnp.concatenate(parts, 1)
 
     def send(start, count):
         part = (slice(None), pl.ds(start, count))
@@ -266,21 +265,31 @@
     turned = turned * row_sign(turned.shape)
     y_high, y_low = halves(y)
     t_high, t_low = halves(turned)
-    both = jnp.concatenate([y_high, y_low], 0)
-    turned_both = jnp.concatenate([t_high, t_low], 0)
+
+    def half_block(q, b):
+        cols = slice(q * BLOCK_LEN + b * LANES, q * BLOCK_LEN + (b + 1) * LANES)
+        return [jnp.concatenate([x[:, cols], t[:, cols]], 1) for x, t in ((y_high, t_high), (y_low, t_low))]
+
+    def products(stack, n, count):
+        high, low = (jnp.concatenate([table_tile(h, n + i) for i in range(count)], 0) for h in range(2))
+        by_high = dot_nt(jnp.concatenate([part for pair in stack for part in pair], 0), high)
+        by_low = dot_nt(jnp.concatenate([pair[0] for pair in stack], 0), low)
+        return [
+            by_high[2 * i * rows : (2 * i + 1) * rows]
+            + (by_high[(2 * i + 1) * rows : 2 * (i + 1) * rows] + by_low[i * rows : (i + 1) * rows])
+            for i in range(len(stack))
+        ]
+
     taps_sum = None
+    (far,) = products([half_block(0, 0)], 0, 1)
     for q in range(blocks):
-        cols = slice(q * BLOCK_LEN, (q + 1) * BLOCK_LEN)
-        tables = []
-        for h in range(2):
-            rows_of = []
-            for start in (q * BLOCK_LEN + LANES, q * BLOCK_LEN):
-                rows_of.append(jnp.concatenate([tiles_at(h, c, start) for c in range(2)], 1))
-            tables.append(jnp.concatenate(rows_of, 0))
-        lhs = jnp.concatenate([both[:, cols], turned_both[:, cols]], 1)
-        by_high = dot_nt(lhs, tables[0])
-        by_low = dot_nt(lhs[:rows], tables[1])
-        product = by_high[:rows] + (by_high[rows:] + by_low)
+        stack = [half_block(q, 0), half_block(q, 1)]
+        if q + 1 < blocks:
+            stack.append(half_block(q + 1, 0))
+        first, second, *after = products(stack, 2 * q + 1, 2)
+        product = jnp.concatenate([first[:, :LANES] + second[:, LANES:], second[:, :LANES] + far], 1)
+        if after:
+            far = after[0][:, LANES:]
         taps = product[:, :LANES]
         taps_sum = taps if taps_sum is None else taps_sum + taps
         for h in range(LAGS // LANES):

time: 34.5 us -> 34.2 us (level)
  Pallas kernels: 15.8 us -> 15.2 us
  transfers between devices with their start and end apart: 6 -> 6, of which waited for: 2 -> 2; matrix products, arithmetic and copies ran while one was open for 0% -> 0% of each run, Pallas kernels for 32% -> 31%
where the time goes in v15:
time: 34.2 us; the launch traced here: 34 us
  Pallas kernels  15.2 us (44%)
  starting transfers between devices  13.7 us (40%)
  waiting for transfers between devices  5.03 us (15%)
    pallas_call x1, Pallas kernels, own_call(): pl.pallas_call(functools.partial(own_kernel, lags_local), in_specs=[pl.Bl...  6.25 us
    all_to_all x1, starting transfers between devices, tiled_device(): got = lax.all_to_all(pieces, 'tm', 0, 0, tiled=True)  5.89 us
    ppermute x3, starting transfers between devices, swap(): return lax.ppermute(x, axis, pairs)  4.98 us
    ppermute x2, waiting for transfers between devices, tiled_device(): lax.ppermute(joined, 'tm', [(i, (i + count) % tm_count) for i in range(tm...  3.3 us
    ppermute x2, starting transfers between devices, tiled_device(): lax.ppermute(joined, 'tm', [(i, (i + count) % tm_count) for i in range(tm...  2.87 us
    pallas_call x1, Pallas kernels, map_call(): pl.pallas_call(functools.partial(map_kernel, groups), in_specs=[pl.BlockS...  2.49 us
    pallas_call x1, Pallas kernels, beam_call(): pl.pallas_call(functools.partial(beam_kernel, chan_count, beams_local), i...  2.16 us
    pallas_call x1, Pallas kernels, lag_call(): pl.pallas_call(functools.partial(lag_kernel, groups, len(ys)), in_specs=[...  1.81 us
  transfers between devices with their start and end apart: 6, of which 2 were waited for; matrix products, arithmetic and copies ran while one was open for 0% of the time, Pallas kernels for 31%

profile of v15, /device:TPU:0, one launch (start us, length us, event | category | flops | bytes accessed | tf_op | source)
XLA Modules:
  0.0 34.0 jit_solution(7124384623131110022)
XLA Ops:
  0.0 2.2 %beams.1 = (f32[64,2048]{1,0:T(8,128)S(1)}, f32[64,2048]{1,0:T(8,128)S(1)}, f32[2,16,128]{2,1,0:T(8,128)S(1)}) custom-call(f32[2,64,64]{2,1,0:T(8,128)} %w_hbm.1, f32[128,2048]{1,0:T(8,128)} %bitcast.13, f32[2,2048]{1,0:T(2,128)} %ref_hbm.1), custom_call_target="tpu_custom_call" | custom-call | flops 2529999872 | tf_op jit(solution)/shard_map/beams/pallas_call | solution.py:133
  2.2 0.5 %collective-permute-start = (f32[64,2048]{1,0:T(8,128)S(1)}, f32[64,2048]{1,0:T(8,128)S(1)}, u32[]{:S(2)}, u32[]{:S(2)}) collective-permute-start(f32[64,2048]{1,0:T(8,128)S(1)} %get-tuple-element.16), channel_id=1, source_target_pairs={{0,8},{8,0},{16,24},{24,16},{1,9},{9,1},{17,25},{25,17},{2,10},{10... | collective-permute-start | bytes 1572872 | tf_op jit(solution)/shard_map/ppermute | solution.py:591
  2.7 2.6 %collective-permute-start.2 = (f32[1,2,16,128]{3,2,1,0:T(8,128)S(1)}, f32[1,2,16,128]{3,2,1,0:T(8,128)S(1)}, u32[]{:S(2)}, u32[]{:S(2)}) collective-permute-start(f32[1,2,16,128]{3,2,1,0:T(8,128)S(1)} %bitcast.10), channel_id=1, source_target_pairs={{0,1},{1,0},{2,3},{3,2},{4,5},{5,4},{6,7},{7,6},{8,9},{9,8},{10,11... | collective-permute-start | bytes 49160 | tf_op jit(solution)/shard_map/ppermute | solution.py:591
  5.3 0.0 collective-permute-done
  5.3 0.1 halves_summed.1
  5.3 1.9 %collective-permute-start.1 = (f32[1,32,2048]{2,1,0:T(8,128)S(1)}, f32[1,32,2048]{2,1,0:T(8,128)S(1)}, u32[]{:S(2)}, u32[]{:S(2)}) collective-permute-start(f32[1,32,2048]{2,1,0:T(8,128)S(1)} %get-tuple-element.18.refs_0_), channel_id=1, source_target_pairs={{0,16},{8,24},{16,0},{24,8},{1,17},{9,25},{17,1},{25,9},{2,18},{10... | collective-permute-start | bytes 786440 | tf_op jit(solution)/shard_map/ppermute | solution.py:591
  7.2 0.0 collective-permute-done.2.second_ref.refs_4_.refs_1_
  7.2 1.9 %collective-permute-start.3 = (f32[2,2,16,128]{3,2,1,0:T(8,128)S(1)}, f32[2,2,16,128]{3,2,1,0:T(8,128)S(1)}, u32[]{:S(2)}, u32[]{:S(2)}) collective-permute-start(f32[2,2,16,128]{3,2,1,0:T(8,128)S(1)} %reference_joined.2.first_ref), channel_id=1, source_target_pairs={{0,2},{1,3},{2,4},{3,5},{4,6},{5,7},{6,0},{7,1},{8,10},{9,11},{10,... | collective-permute-start | bytes 98312 | tf_op jit(solution)/shard_map/ppermute | solution.py:616
  9.1 0.6 %shifted_reference.1.refs_2_ = bf16[2,2,128,1920]{3,2,1,0:T(8,128)(2,1)S(1)} custom-call(f32[2,16,128]{2,1,0:T(8,128)S(1)} %get-tuple-element.19.tiles_ref.refs_3_), custom_call_target="tpu_custom_call" | custom-call | flops 805000000 | tf_op jit(solution)/shard_map/shifted_reference/pallas_call | solution.py:219
  9.7 3.3 %collective-permute-done.3.second_ref.refs_5_.refs_2_ = f32[2,2,16,128]{3,2,1,0:T(8,128)S(1)} collective-permute-done((f32[2,2,16,128]{3,2,1,0:T(8,128)S(1)}, f32[2,2,16,128]{3,2,1,0:T(8,128)S(1)}, u32[]{:S(2)}, u32[]{:S(2)}) %collective-permute-start.3) | collective-permute-done | bytes 32800 | tf_op jit(solution)/shard_map/ppermute | solution.py:616
  13.0 1.0 %collective-permute-start.4 = (f32[4,2,16,128]{3,2,1,0:T(8,128)S(1)}, f32[4,2,16,128]{3,2,1,0:T(8,128)S(1)}, u32[]{:S(2)}, u32[]{:S(2)}) collective-permute-start(f32[4,2,16,128]{3,2,1,0:T(8,128)S(1)} %reference_joined.3.refs_6_), channel_id=1, source_target_pairs={{0,4},{1,5},{2,6},{3,7},{4,0},{5,1},{6,2},{7,3},{8,12},{9,13},{10,... | collective-permute-start | bytes 196616 | tf_op jit(solution)/shard_map/ppermute | solution.py:616
  14.0 0.0 collective-permute-done.1
  14.0 1.8 %lag_products.1.refs_4_ = f32[8,10,8,128]{3,2,1,0:T(8,128)} custom-call(f32[32,2048]{1,0:T(8,128)S(1)} %bitcast.8, f32[32,2048]{1,0:T(8,128)S(1)} %bitcast.9, bf16[2,2,128,1920]{3,2,1,0:T(8,128)(2,1)S(1)} %shifted_reference.1.refs_2_, f32[2,16,128]{2,1,0:T(8,128)S(1)} %get-tuple-element.19.tiles_ref.refs_3_, ...), custom_call_target="tpu_custom_call" | custom-call | flops 2415000064 | tf_op jit(solution)/shard_map/lag_products/pallas_call | solution.py:319
  15.8 5.9 %all-to-all-start = ((f32[8,10,8,128]{3,2,1,0:T(8,128)}), f32[8,10,8,128]{3,2,1,0:T(8,128)S(1)}, u32[]{:S(2)}, u32[]{:S(2)}) async-start(f32[8,10,8,128]{3,2,1,0:T(8,128)} %lag_products.1.refs_4_), calls=%async_computation | async-start | bytes 655360 | tf_op jit(solution)/shard_map/all_to_all | solution.py:622
  21.7 0.0 collective-permute-done.4.refs_3_
  21.7 6.2 %reference_products.1 = (bf16[2,2048,128]{2,1,0:T(8,128)(2,1)S(1)}, f32[8,128]{1,0:T(8,128)S(1)}, f32[128,128]{1,0:T(8,128)S(1)}) custom-call(f32[1,2,16,128]{3,2,1,0:T(8,128)S(1)} %bitcast.12, f32[1,2,16,128]{3,2,1,0:T(8,128)S(1)} %collective-permute-done.2.second_ref.refs_4_.refs_1_, ...), custom_call_target="tpu_custom_call" | custom-call | flops 7129999872 | tf_op jit(solution)/shard_map/reference_products/pallas_call | solution.py:433
  28.0 0.0 copy-start
  28.0 1.8 %gram_inverse.1 = (bf16[2,128,128]{2,1,0:T(8,128)(2,1)S(1)}, bf16[2,128,128]{2,1,0:T(8,128)(2,1)S(1)}) custom-call(f32[8,128]{1,0:T(8,128)S(1)} %get-tuple-element.21.line_ref, f32[128,128]{1,0:T(8,128)S(1)} %get-tuple-element.22.tail_ref), custom_call_target="tpu_custom_call" | custom-call | flops 2300000000 | tf_op jit(solution)/shard_map/gram_inverse/pallas_call | solution.py:500
  29.8 1.7 %all-to-all-done.got_ref = f32[8,10,8,128]{3,2,1,0:T(8,128)S(1)} async-done(((f32[8,10,8,128]{3,2,1,0:T(8,128)}), f32[8,10,8,128]{3,2,1,0:T(8,128)S(1)}, u32[]{:S(2)}, u32[]{:S(2)}) %all-to-all-start) | async-done | bytes 327712 | tf_op jit(solution)/shard_map/all_to_all | solution.py:622
  31.5 0.0 copy-done
  31.5 2.5 %range_doppler.1 = f32[16,2,32,256]{3,2,1,0:T(8,128)} custom-call(f32[8,10,8,128]{3,2,1,0:T(8,128)S(1)} %all-to-all-done.got_ref, bf16[2,2048,128]{2,1,0:T(8,128)(2,1)S(1)} %get-tuple-element.20.own_ref, bf16[2,128,128]{2,1,0:T(8,128)(2,1)S(1)} %get-tuple-element.23.gram_ref, bf16[2,128,128]{2,1,0:T(8,128)(2,1)S(1)} %get-tuple-element.24.solver_ref, ...), custom_call_target="tpu_custom_call" | custom-call | flops 2875000064 | tf_op jit(solution)/shard_map/range_doppler/pallas_call | solution.py:573
  (2 shorter events, 0.0 us)
Async XLA Ops:
  2.2 3.1 %collective-permute-start = (f32[64,2048]{1,0:T(8,128)S(1)}, f32[64,2048]{1,0:T(8,128)S(1)}, u32[]{:S(2)}, u32[]{:S(2)}) collective-permute-start(f32[64,2048]{1,0:T(8,128)S(1)} %get-tuple-element.16), channel_id=1, source_target_pairs={{0,8},{8,0},{16,24},{24,16},{1,9},{9,1},{17,25},{25,17},{2,10},{10... | collective-permute-start | bytes 1572872 | tf_op jit(solution)/shard_map/ppermute | solution.py:591
  2.7 4.5 %collective-permute-start.2 = (f32[1,2,16,128]{3,2,1,0:T(8,128)S(1)}, f32[1,2,16,128]{3,2,1,0:T(8,128)S(1)}, u32[]{:S(2)}, u32[]{:S(2)}) collective-permute-start(f32[1,2,16,128]{3,2,1,0:T(8,128)S(1)} %bitcast.10), channel_id=1, source_target_pairs={{0,1},{1,0},{2,3},{3,2},{4,5},{5,4},{6,7},{7,6},{8,9},{9,8},{10,11... | collective-permute-start | bytes 49160 | tf_op jit(solution)/shard_map/ppermute | solution.py:591
  5.3 8.7 %collective-permute-start.1 = (f32[1,32,2048]{2,1,0:T(8,128)S(1)}, f32[1,32,2048]{2,1,0:T(8,128)S(1)}, u32[]{:S(2)}, u32[]{:S(2)}) collective-permute-start(f32[1,32,2048]{2,1,0:T(8,128)S(1)} %get-tuple-element.18.refs_0_), channel_id=1, source_target_pairs={{0,16},{8,24},{16,0},{24,8},{1,17},{9,25},{17,1},{25,9},{2,18},{10... | collective-permute-start | bytes 786440 | tf_op jit(solution)/shard_map/ppermute | solution.py:591
  7.2 5.8 %collective-permute-start.3 = (f32[2,2,16,128]{3,2,1,0:T(8,128)S(1)}, f32[2,2,16,128]{3,2,1,0:T(8,128)S(1)}, u32[]{:S(2)}, u32[]{:S(2)}) collective-permute-start(f32[2,2,16,128]{3,2,1,0:T(8,128)S(1)} %reference_joined.2.first_ref), channel_id=1, source_target_pairs={{0,2},{1,3},{2,4},{3,5},{4,6},{5,7},{6,0},{7,1},{8,10},{9,11},{10,... | collective-permute-start | bytes 98312 | tf_op jit(solution)/shard_map/ppermute | solution.py:616
  13.0 8.7 %collective-permute-start.4 = (f32[4,2,16,128]{3,2,1,0:T(8,128)S(1)}, f32[4,2,16,128]{3,2,1,0:T(8,128)S(1)}, u32[]{:S(2)}, u32[]{:S(2)}) collective-permute-start(f32[4,2,16,128]{3,2,1,0:T(8,128)S(1)} %reference_joined.3.refs_6_), channel_id=1, source_target_pairs={{0,4},{1,5},{2,6},{3,7},{4,0},{5,1},{6,2},{7,3},{8,12},{9,13},{10,... | collective-permute-start | bytes 196616 | tf_op jit(solution)/shard_map/ppermute | solution.py:616
  15.8 15.6 %all-to-all-start = ((f32[8,10,8,128]{3,2,1,0:T(8,128)}), f32[8,10,8,128]{3,2,1,0:T(8,128)S(1)}, u32[]{:S(2)}, u32[]{:S(2)}) async-start(f32[8,10,8,128]{3,2,1,0:T(8,128)} %lag_products.1.refs_4_), calls=%async_computation | async-start | bytes 655360 | tf_op jit(solution)/shard_map/all_to_all | solution.py:622
  28.0 3.5 %copy-start = (bf16[2,128,512]{2,1,0:T(8,128)(2,1)S(1)}, bf16[2,128,512]{2,1,0:T(8,128)(2,1)}, u32[]{:S(2)}) copy-start(bf16[2,128,512]{2,1,0:T(8,128)(2,1)} %constant.2.clone.wave_ref) | copy-start | bytes 786436

commit v16 on v15

--- a/solution.py
+++ b/solution.py
@@ -536,11 +536,12 @@
     rest = cross - dot_split(halves(taps), (gram_ref[0], gram_ref[1]))
     taps = taps + dot_split(halves(rest), solver)
     taps_high, taps_low = halves(taps)
-    taps_both = jnp.concatenate([taps_high, taps_low], 1)
+    taps_both = jnp.concatenate([taps_high, taps_low], 0)
+    count = taps.shape[0]
     for q in range(0, total, 2 * groups):
         own = slice(q * lags_local, (q + 2 * groups) * lags_local)
-        own_high = own_ref[0, own, :]
-        clutter = dot_nt(taps_both, jnp.concatenate([own_high, own_high], 1)) + dot_nt(taps_high, own_ref[1, own, :])
+        by_high = dot_nt(taps_both, own_ref[0, own, :])
+        clutter = by_high[:count] + (by_high[count:] + dot_nt(taps_high, own_ref[1, own, :]))
         for h in range(2):
             lanes = slice(h * LANES, (h + 1) * LANES)
             tiles = [clutter[r : r + SUBLANES, lanes] for r in range(0, groups * SUBLANES, SUBLANES)]
@@ -557,11 +558,13 @@
             lagged.append(jnp.concatenate(parts, 0).T)
         spectrum = dot_split(halves(jnp.concatenate(lagged, 0)), wave)
         for n in range(2 * groups):
-            beam = half * (n % groups) + first + n // groups
             for c in range(2):
-                out_ref[beam, c] = spectrum[n * lags_local : (n + 1) * lags_local, c * DOPPLER : (c + 1) * DOPPLER]
-            copies.append(pltpu.make_async_copy(out_ref.at[beam], out_hbm.at[beam], out_sem.at[beam]))
-            copies[-1].start()
+                out_ref[n % groups, first + n // groups, c] = spectrum[
+                    n * lags_local : (n + 1) * lags_local, c * DOPPLER : (c + 1) * DOPPLER
+                ]
+        part = (slice(None), pl.ds(first, 2))
+        copies.append(pltpu.make_async_copy(out_ref.at[part], out_hbm.at[part], out_sem.at[first // 2]))
+        copies[-1].start()
     for copy in copies:
         copy.wait()
 
@@ -569,8 +572,9 @@
 def map_call(got, own, gram, solver, wave, groups, beams_local):
     total = got.shape[0] * (got.shape[1] - groups // 2)
     lags_local = LANES // groups
-    shape = (beams_local, 2, lags_local, DOPPLER)
-    return pl.pallas_call(
+    half = SUBLANES // 2
+    shape = (beams_local // half, half, 2, lags_local, DOPPLER)
+    out = pl.pallas_call(
         functools.partial(map_kernel, groups),
         in_specs=[pl.BlockSpec(memory_space=pltpu.VMEM)] * 5,
         out_specs=pl.BlockSpec(memory_space=pltpu.HBM),
@@ -578,12 +582,13 @@
         scratch_shapes=[
             pltpu.VMEM((total * SUBLANES, LANES), jnp.float32),
             pltpu.VMEM(shape, jnp.float32),
-            pltpu.SemaphoreType.DMA((beams_local,)),
+            pltpu.SemaphoreType.DMA((half // 2,)),
         ],
         compiler_params=params(),
         cost_estimate=cost(2.5),
         name="range_doppler",
     )(got, own, gram, solver, wave)
+    return out.reshape((beams_local,) + shape[2:])
 
 
 def swap(x, axis, by):

time: 34.2 us -> 34 us (level)
  transfers between devices with their start and end apart: 6 -> 6, of which waited for: 2 -> 2; matrix products, arithmetic and copies ran while one was open for 0% -> 0% of each run, Pallas kernels for 31% -> 32%
where the time goes in v16:
time: 34 us; the launch traced here: 33.8 us
  Pallas kernels  15.2 us (45%)
  starting transfers between devices  13.7 us (40%)
  waiting for transfers between devices  4.75 us (14%)
    pallas_call x1, Pallas kernels, own_call(): pl.pallas_call(functools.partial(own_kernel, lags_local), in_specs=[pl.Bl...  6.25 us
    all_to_all x1, starting transfers between devices, tiled_device(): got = lax.all_to_all(pieces, 'tm', 0, 0, tiled=True)  5.89 us
    ppermute x3, starting transfers between devices, swap(): return lax.ppermute(x, axis, pairs)  4.98 us
    ppermute x2, waiting for transfers between devices, tiled_device(): lax.ppermute(joined, 'tm', [(i, (i + count) % tm_count) for i in range(tm...  3.3 us
    ppermute x2, starting transfers between devices, tiled_device(): lax.ppermute(joined, 'tm', [(i, (i + count) % tm_count) for i in range(tm...  2.87 us
    pallas_call x1, Pallas kernels, map_call(): pl.pallas_call(functools.partial(map_kernel, groups), in_specs=[pl.BlockS...  2.3 us
    pallas_call x1, Pallas kernels, beam_call(): pl.pallas_call(functools.partial(beam_kernel, chan_count, beams_local), i...  2.16 us
    pallas_call x1, Pallas kernels, solver_call(): pl.pallas_call(solver_kernel, out_shape=[out, out], compiler_params=param...  2.05 us
  transfers between devices with their start and end apart: 6, of which 2 were waited for; matrix products, arithmetic and copies ran while one was open for 0% of the time, Pallas kernels for 32%

profile of v16, /device:TPU:0, one launch (start us, length us, event | category | flops | bytes accessed | tf_op | source)
XLA Modules:
  0.0 33.8 jit_solution(17818919830380212012)
XLA Ops:
  0.0 2.2 %beams.1 = (f32[64,2048]{1,0:T(8,128)S(1)}, f32[64,2048]{1,0:T(8,128)S(1)}, f32[2,16,128]{2,1,0:T(8,128)S(1)}) custom-call(f32[2,64,64]{2,1,0:T(8,128)} %w_hbm.1, f32[128,2048]{1,0:T(8,128)} %bitcast.14, f32[2,2048]{1,0:T(2,128)} %ref_hbm.1), custom_call_target="tpu_custom_call" | custom-call | flops 2529999872 | tf_op jit(solution)/shard_map/beams/pallas_call | solution.py:133
  2.2 0.5 %collective-permute-start = (f32[64,2048]{1,0:T(8,128)S(1)}, f32[64,2048]{1,0:T(8,128)S(1)}, u32[]{:S(2)}, u32[]{:S(2)}) collective-permute-start(f32[64,2048]{1,0:T(8,128)S(1)} %get-tuple-element.16), channel_id=1, source_target_pairs={{0,8},{8,0},{16,24},{24,16},{1,9},{9,1},{17,25},{25,17},{2,10},{10... | collective-permute-start | bytes 1572872 | tf_op jit(solution)/shard_map/ppermute | solution.py:596
  2.7 2.6 %collective-permute-start.2 = (f32[1,2,16,128]{3,2,1,0:T(8,128)S(1)}, f32[1,2,16,128]{3,2,1,0:T(8,128)S(1)}, u32[]{:S(2)}, u32[]{:S(2)}) collective-permute-start(f32[1,2,16,128]{3,2,1,0:T(8,128)S(1)} %bitcast.11), channel_id=1, source_target_pairs={{0,1},{1,0},{2,3},{3,2},{4,5},{5,4},{6,7},{7,6},{8,9},{9,8},{10,11... | collective-permute-start | bytes 49160 | tf_op jit(solution)/shard_map/ppermute | solution.py:596
  5.3 0.0 collective-permute-done
  5.3 0.1 halves_summed.1
  5.3 1.9 %collective-permute-start.1 = (f32[1,32,2048]{2,1,0:T(8,128)S(1)}, f32[1,32,2048]{2,1,0:T(8,128)S(1)}, u32[]{:S(2)}, u32[]{:S(2)}) collective-permute-start(f32[1,32,2048]{2,1,0:T(8,128)S(1)} %get-tuple-element.18.refs_0_), channel_id=1, source_target_pairs={{0,16},{8,24},{16,0},{24,8},{1,17},{9,25},{17,1},{25,9},{2,18},{10... | collective-permute-start | bytes 786440 | tf_op jit(solution)/shard_map/ppermute | solution.py:596
  7.2 0.0 collective-permute-done.2.second_ref.refs_4_.refs_1_
  7.2 1.9 %collective-permute-start.3 = (f32[2,2,16,128]{3,2,1,0:T(8,128)S(1)}, f32[2,2,16,128]{3,2,1,0:T(8,128)S(1)}, u32[]{:S(2)}, u32[]{:S(2)}) collective-permute-start(f32[2,2,16,128]{3,2,1,0:T(8,128)S(1)} %reference_joined.2.first_ref), channel_id=1, source_target_pairs={{0,2},{1,3},{2,4},{3,5},{4,6},{5,7},{6,0},{7,1},{8,10},{9,11},{10,... | collective-permute-start | bytes 98312 | tf_op jit(solution)/shard_map/ppermute | solution.py:621
  9.1 0.6 %shifted_reference.1.refs_2_ = bf16[2,2,128,1920]{3,2,1,0:T(8,128)(2,1)S(1)} custom-call(f32[2,16,128]{2,1,0:T(8,128)S(1)} %get-tuple-element.19.tiles_ref.refs_3_), custom_call_target="tpu_custom_call" | custom-call | flops 805000000 | tf_op jit(solution)/shard_map/shifted_reference/pallas_call | solution.py:219
  9.7 3.3 %collective-permute-done.3.second_ref.refs_5_.refs_2_ = f32[2,2,16,128]{3,2,1,0:T(8,128)S(1)} collective-permute-done((f32[2,2,16,128]{3,2,1,0:T(8,128)S(1)}, f32[2,2,16,128]{3,2,1,0:T(8,128)S(1)}, u32[]{:S(2)}, u32[]{:S(2)}) %collective-permute-start.3) | collective-permute-done | bytes 32800 | tf_op jit(solution)/shard_map/ppermute | solution.py:621
  13.0 1.0 %collective-permute-start.4 = (f32[4,2,16,128]{3,2,1,0:T(8,128)S(1)}, f32[4,2,16,128]{3,2,1,0:T(8,128)S(1)}, u32[]{:S(2)}, u32[]{:S(2)}) collective-permute-start(f32[4,2,16,128]{3,2,1,0:T(8,128)S(1)} %reference_joined.3.refs_6_), channel_id=1, source_target_pairs={{0,4},{1,5},{2,6},{3,7},{4,0},{5,1},{6,2},{7,3},{8,12},{9,13},{10,... | collective-permute-start | bytes 196616 | tf_op jit(solution)/shard_map/ppermute | solution.py:621
  14.0 0.0 collective-permute-done.1
  14.0 1.8 %lag_products.1.refs_4_ = f32[8,10,8,128]{3,2,1,0:T(8,128)} custom-call(f32[32,2048]{1,0:T(8,128)S(1)} %bitcast.9, f32[32,2048]{1,0:T(8,128)S(1)} %bitcast.10, bf16[2,2,128,1920]{3,2,1,0:T(8,128)(2,1)S(1)} %shifted_reference.1.refs_2_, f32[2,16,128]{2,1,0:T(8,128)S(1)} %get-tuple-element.19.tiles_ref.refs_3_, ...), custom_call_target="tpu_custom_call" | custom-call | flops 2415000064 | tf_op jit(solution)/shard_map/lag_products/pallas_call | solution.py:319
  15.8 5.9 %all-to-all-start = ((f32[8,10,8,128]{3,2,1,0:T(8,128)}), f32[8,10,8,128]{3,2,1,0:T(8,128)S(1)}, u32[]{:S(2)}, u32[]{:S(2)}) async-start(f32[8,10,8,128]{3,2,1,0:T(8,128)} %lag_products.1.refs_4_), calls=%async_computation | async-start | bytes 655360 | tf_op jit(solution)/shard_map/all_to_all | solution.py:627
  21.7 0.0 collective-permute-done.4.refs_3_
  21.7 6.2 %reference_products.1 = (bf16[2,2048,128]{2,1,0:T(8,128)(2,1)S(1)}, f32[8,128]{1,0:T(8,128)S(1)}, f32[128,128]{1,0:T(8,128)S(1)}) custom-call(f32[1,2,16,128]{3,2,1,0:T(8,128)S(1)} %bitcast.13, f32[1,2,16,128]{3,2,1,0:T(8,128)S(1)} %collective-permute-done.2.second_ref.refs_4_.refs_1_, ...), custom_call_target="tpu_custom_call" | custom-call | flops 7129999872 | tf_op jit(solution)/shard_map/reference_products/pallas_call | solution.py:433
  28.0 0.0 copy-start
  28.0 2.0 %gram_inverse.1 = (bf16[2,128,128]{2,1,0:T(8,128)(2,1)S(1)}, bf16[2,128,128]{2,1,0:T(8,128)(2,1)S(1)}) custom-call(f32[8,128]{1,0:T(8,128)S(1)} %get-tuple-element.21.line_ref, f32[128,128]{1,0:T(8,128)S(1)} %get-tuple-element.22.tail_ref), custom_call_target="tpu_custom_call" | custom-call | flops 2300000000 | tf_op jit(solution)/shard_map/gram_inverse/pallas_call | solution.py:500
  30.0 1.4 %all-to-all-done.got_ref = f32[8,10,8,128]{3,2,1,0:T(8,128)S(1)} async-done(((f32[8,10,8,128]{3,2,1,0:T(8,128)}), f32[8,10,8,128]{3,2,1,0:T(8,128)S(1)}, u32[]{:S(2)}, u32[]{:S(2)}) %all-to-all-start) | async-done | bytes 327712 | tf_op jit(solution)/shard_map/all_to_all | solution.py:627
  31.5 0.0 copy-done
  31.5 2.3 %range_doppler.1 = f32[4,4,2,32,256]{4,3,2,1,0:T(8,128)} custom-call(f32[8,10,8,128]{3,2,1,0:T(8,128)S(1)} %all-to-all-done.got_ref, bf16[2,2048,128]{2,1,0:T(8,128)(2,1)S(1)} %get-tuple-element.20.own_ref, bf16[2,128,128]{2,1,0:T(8,128)(2,1)S(1)} %get-tuple-element.23.gram_ref, bf16[2,128,128]{2,1,0:T(8,128)(2,1)S(1)} %get-tuple-element.24.solver_ref, ...), custom_call_target="tpu_custom_call" | custom-call | flops 2875000064 | tf_op jit(solution)/shard_map/range_doppler/pallas_call | solution.py:577
  (2 shorter events, 0.0 us)
Async XLA Ops:
  2.2 3.1 %collective-permute-start = (f32[64,2048]{1,0:T(8,128)S(1)}, f32[64,2048]{1,0:T(8,128)S(1)}, u32[]{:S(2)}, u32[]{:S(2)}) collective-permute-start(f32[64,2048]{1,0:T(8,128)S(1)} %get-tuple-element.16), channel_id=1, source_target_pairs={{0,8},{8,0},{16,24},{24,16},{1,9},{9,1},{17,25},{25,17},{2,10},{10... | collective-permute-start | bytes 1572872 | tf_op jit(solution)/shard_map/ppermute | solution.py:596
  2.7 4.5 %collective-permute-start.2 = (f32[1,2,16,128]{3,2,1,0:T(8,128)S(1)}, f32[1,2,16,128]{3,2,1,0:T(8,128)S(1)}, u32[]{:S(2)}, u32[]{:S(2)}) collective-permute-start(f32[1,2,16,128]{3,2,1,0:T(8,128)S(1)} %bitcast.11), channel_id=1, source_target_pairs={{0,1},{1,0},{2,3},{3,2},{4,5},{5,4},{6,7},{7,6},{8,9},{9,8},{10,11... | collective-permute-start | bytes 49160 | tf_op jit(solution)/shard_map/ppermute | solution.py:596
  5.3 8.7 %collective-permute-start.1 = (f32[1,32,2048]{2,1,0:T(8,128)S(1)}, f32[1,32,2048]{2,1,0:T(8,128)S(1)}, u32[]{:S(2)}, u32[]{:S(2)}) collective-permute-start(f32[1,32,2048]{2,1,0:T(8,128)S(1)} %get-tuple-element.18.refs_0_), channel_id=1, source_target_pairs={{0,16},{8,24},{16,0},{24,8},{1,17},{9,25},{17,1},{25,9},{2,18},{10... | collective-permute-start | bytes 786440 | tf_op jit(solution)/shard_map/ppermute | solution.py:596
  7.2 5.8 %collective-permute-start.3 = (f32[2,2,16,128]{3,2,1,0:T(8,128)S(1)}, f32[2,2,16,128]{3,2,1,0:T(8,128)S(1)}, u32[]{:S(2)}, u32[]{:S(2)}) collective-permute-start(f32[2,2,16,128]{3,2,1,0:T(8,128)S(1)} %reference_joined.2.first_ref), channel_id=1, source_target_pairs={{0,2},{1,3},{2,4},{3,5},{4,6},{5,7},{6,0},{7,1},{8,10},{9,11},{10,... | collective-permute-start | bytes 98312 | tf_op jit(solution)/shard_map/ppermute | solution.py:621
  13.0 8.7 %collective-permute-start.4 = (f32[4,2,16,128]{3,2,1,0:T(8,128)S(1)}, f32[4,2,16,128]{3,2,1,0:T(8,128)S(1)}, u32[]{:S(2)}, u32[]{:S(2)}) collective-permute-start(f32[4,2,16,128]{3,2,1,0:T(8,128)S(1)} %reference_joined.3.refs_6_), channel_id=1, source_target_pairs={{0,4},{1,5},{2,6},{3,7},{4,0},{5,1},{6,2},{7,3},{8,12},{9,13},{10,... | collective-permute-start | bytes 196616 | tf_op jit(solution)/shard_map/ppermute | solution.py:621
  15.8 15.6 %all-to-all-start = ((f32[8,10,8,128]{3,2,1,0:T(8,128)}), f32[8,10,8,128]{3,2,1,0:T(8,128)S(1)}, u32[]{:S(2)}, u32[]{:S(2)}) async-start(f32[8,10,8,128]{3,2,1,0:T(8,128)} %lag_products.1.refs_4_), calls=%async_computation | async-start | bytes 655360 | tf_op jit(solution)/shard_map/all_to_all | solution.py:627
  28.0 3.5 %copy-start = (bf16[2,128,512]{2,1,0:T(8,128)(2,1)S(1)}, bf16[2,128,512]{2,1,0:T(8,128)(2,1)}, u32[]{:S(2)}) copy-start(bf16[2,128,512]{2,1,0:T(8,128)(2,1)} %constant.2.clone.wave_ref) | copy-start | bytes 786436

commit v17 on v16

--- a/solution.py
+++ b/solution.py
@@ -73,7 +73,7 @@
     return outs
 
 
-CHUNKS = 4
+CHUNKS = 2
 
 
 def beam_kernel(
@@ -110,16 +110,20 @@
                 second = [jnp.where(top, wr_s, wi), jnp.where(top, -wi_s, wr)]
                 rows.append(jnp.concatenate(first, 1))
                 rows.append(jnp.concatenate(second, 1))
-    weights = halves(jnp.concatenate(rows, 0))
+    weights = jnp.concatenate(halves(jnp.concatenate(rows, 0)), 0)
+    count = weights.shape[0] // 2
     ref_copy.wait()
     for c in range(2):
         for n in range(tiles_ref.shape[1]):
             tiles_ref[c, n : n + 1, :] = ref_ref[c : c + 1, n * LANES : (n + 1) * LANES]
-    mid = weights[0].shape[0] // 2
+    mid = count // 2
     for n in range(CHUNKS):
         cols = slice(n * width, (n + 1) * width)
         s_copies[n].wait()
-        product = dot_split(weights, halves(s_ref[:, cols]))
+        high, low = halves(s_ref[:, cols])
+        by_high = jnp.dot(weights, high, preferred_element_type=jnp.float32)
+        by_low = jnp.dot(weights[:count], low, preferred_element_type=jnp.float32)
+        product = by_high[:count] + (by_high[count:] + by_low)
         kept_ref[:, cols] = product[:mid]
         sent_ref[:, cols] = product[mid:]
 
@@ -551,19 +555,14 @@
     half = SUBLANES // 2
     wave = (wave_ref[0], wave_ref[1])
     copies = []
-    for first in range(0, half, 2):
-        lagged = []
-        for g in (first, first + 1):
-            parts = [held_ref[pl.ds(c * half + g, total, stride=SUBLANES), :] for c in range(2)]
-            lagged.append(jnp.concatenate(parts, 0).T)
-        spectrum = dot_split(halves(jnp.concatenate(lagged, 0)), wave)
-        for n in range(2 * groups):
+    for g in range(half):
+        parts = [held_ref[pl.ds(c * half + g, total, stride=SUBLANES), :] for c in range(2)]
+        spectrum = dot_split(halves(jnp.concatenate(parts, 0).T), wave)
+        for i in range(groups):
             for c in range(2):
-                out_ref[n % groups, first + n // groups, c] = spectrum[
-                    n * lags_local : (n + 1) * lags_local, c * DOPPLER : (c + 1) * DOPPLER
-                ]
-        part = (slice(None), pl.ds(first, 2))
-        copies.append(pltpu.make_async_copy(out_ref.at[part], out_hbm.at[part], out_sem.at[first // 2]))
+                out_ref[i, g, c] = spectrum[i * lags_local : (i + 1) * lags_local, c * DOPPLER : (c + 1) * DOPPLER]
+        part = (slice(None), pl.ds(g, 1))
+        copies.append(pltpu.make_async_copy(out_ref.at[part], out_hbm.at[part], out_sem.at[g]))
         copies[-1].start()
     for copy in copies:
         copy.wait()
@@ -582,7 +581,7 @@
         scratch_shapes=[
             pltpu.VMEM((total * SUBLANES, LANES), jnp.float32),
             pltpu.VMEM(shape, jnp.float32),
-            pltpu.SemaphoreType.DMA((half // 2,)),
+            pltpu.SemaphoreType.DMA((half,)),
         ],
         compiler_params=params(),
         cost_estimate=cost(2.5),

time: 34 us -> 33.6 us (0.988)
  no operation moved by 1% of the time
where the time goes in v17:
time: 33.6 us; the launch traced here: 33.4 us
  Pallas kernels  14.9 us (44%)
  starting transfers between devices  13.7 us (41%)
  waiting for transfers between devices  4.74 us (14%)
    pallas_call x1, Pallas kernels, own_call(): pl.pallas_call(functools.partial(own_kernel, lags_local), in_specs=[pl.Bl...  6.26 us
    all_to_all x1, starting transfers between devices, tiled_device(): got = lax.all_to_all(pieces, 'tm', 0, 0, tiled=True)  5.89 us
    ppermute x3, starting transfers between devices, swap(): return lax.ppermute(x, axis, pairs)  4.97 us
    ppermute x2, waiting for transfers between devices, tiled_device(): lax.ppermute(joined, 'tm', [(i, (i + count) % tm_count) for i in range(tm...  3.31 us
    ppermute x2, starting transfers between devices, tiled_device(): lax.ppermute(joined, 'tm', [(i, (i + count) % tm_count) for i in range(tm...  2.87 us
    pallas_call x1, Pallas kernels, map_call(): pl.pallas_call(functools.partial(map_kernel, groups), in_specs=[pl.BlockS...  2.24 us
    pallas_call x1, Pallas kernels, solver_call(): pl.pallas_call(solver_kernel, out_shape=[out, out], compiler_params=param...  2.05 us
    pallas_call x1, Pallas kernels, beam_call(): pl.pallas_call(functools.partial(beam_kernel, chan_count, beams_local), i...  1.85 us
  transfers between devices with their start and end apart: 6, of which 2 were waited for; matrix products, arithmetic and copies ran while one was open for 0% of the time, Pallas kernels for 32%

profile of v17, /device:TPU:0, one launch (start us, length us, event | category | flops | bytes accessed | tf_op | source)
XLA Modules:
  0.0 33.4 jit_solution(15719665435690027394)
XLA Ops:
  0.0 1.8 %beams.1 = (f32[64,2048]{1,0:T(8,128)S(1)}, f32[64,2048]{1,0:T(8,128)S(1)}, f32[2,16,128]{2,1,0:T(8,128)S(1)}) custom-call(f32[2,64,64]{2,1,0:T(8,128)} %w_hbm.1, f32[128,2048]{1,0:T(8,128)} %bitcast.14, f32[2,2048]{1,0:T(2,128)} %ref_hbm.1), custom_call_target="tpu_custom_call" | custom-call | flops 2529999872 | tf_op jit(solution)/shard_map/beams/pallas_call | solution.py:137
  1.9 0.5 %collective-permute-start = (f32[64,2048]{1,0:T(8,128)S(1)}, f32[64,2048]{1,0:T(8,128)S(1)}, u32[]{:S(2)}, u32[]{:S(2)}) collective-permute-start(f32[64,2048]{1,0:T(8,128)S(1)} %get-tuple-element.16), channel_id=1, source_target_pairs={{0,8},{8,0},{16,24},{24,16},{1,9},{9,1},{17,25},{25,17},{2,10},{10... | collective-permute-start | bytes 1572872 | tf_op jit(solution)/shard_map/ppermute | solution.py:595
  2.4 2.6 %collective-permute-start.2 = (f32[1,2,16,128]{3,2,1,0:T(8,128)S(1)}, f32[1,2,16,128]{3,2,1,0:T(8,128)S(1)}, u32[]{:S(2)}, u32[]{:S(2)}) collective-permute-start(f32[1,2,16,128]{3,2,1,0:T(8,128)S(1)} %bitcast.11), channel_id=1, source_target_pairs={{0,1},{1,0},{2,3},{3,2},{4,5},{5,4},{6,7},{7,6},{8,9},{9,8},{10,11... | collective-permute-start | bytes 49160 | tf_op jit(solution)/shard_map/ppermute | solution.py:595
  5.0 0.0 collective-permute-done
  5.0 0.1 halves_summed.1
  5.0 1.9 %collective-permute-start.1 = (f32[1,32,2048]{2,1,0:T(8,128)S(1)}, f32[1,32,2048]{2,1,0:T(8,128)S(1)}, u32[]{:S(2)}, u32[]{:S(2)}) collective-permute-start(f32[1,32,2048]{2,1,0:T(8,128)S(1)} %get-tuple-element.18.refs_0_), channel_id=1, source_target_pairs={{0,16},{8,24},{16,0},{24,8},{1,17},{9,25},{17,1},{25,9},{2,18},{10... | collective-permute-start | bytes 786440 | tf_op jit(solution)/shard_map/ppermute | solution.py:595
  6.9 0.0 collective-permute-done.2.second_ref.refs_4_.refs_1_
  6.9 1.9 %collective-permute-start.3 = (f32[2,2,16,128]{3,2,1,0:T(8,128)S(1)}, f32[2,2,16,128]{3,2,1,0:T(8,128)S(1)}, u32[]{:S(2)}, u32[]{:S(2)}) collective-permute-start(f32[2,2,16,128]{3,2,1,0:T(8,128)S(1)} %reference_joined.2.first_ref), channel_id=1, source_target_pairs={{0,2},{1,3},{2,4},{3,5},{4,6},{5,7},{6,0},{7,1},{8,10},{9,11},{10,... | collective-permute-start | bytes 98312 | tf_op jit(solution)/shard_map/ppermute | solution.py:620
  8.8 0.6 %shifted_reference.1.refs_2_ = bf16[2,2,128,1920]{3,2,1,0:T(8,128)(2,1)S(1)} custom-call(f32[2,16,128]{2,1,0:T(8,128)S(1)} %get-tuple-element.19.tiles_ref.refs_3_), custom_call_target="tpu_custom_call" | custom-call | flops 805000000 | tf_op jit(solution)/shard_map/shifted_reference/pallas_call | solution.py:223
  9.4 3.3 %collective-permute-done.3.second_ref.refs_5_.refs_2_ = f32[2,2,16,128]{3,2,1,0:T(8,128)S(1)} collective-permute-done((f32[2,2,16,128]{3,2,1,0:T(8,128)S(1)}, f32[2,2,16,128]{3,2,1,0:T(8,128)S(1)}, u32[]{:S(2)}, u32[]{:S(2)}) %collective-permute-start.3) | collective-permute-done | bytes 32800 | tf_op jit(solution)/shard_map/ppermute | solution.py:620
  12.7 1.0 %collective-permute-start.4 = (f32[4,2,16,128]{3,2,1,0:T(8,128)S(1)}, f32[4,2,16,128]{3,2,1,0:T(8,128)S(1)}, u32[]{:S(2)}, u32[]{:S(2)}) collective-permute-start(f32[4,2,16,128]{3,2,1,0:T(8,128)S(1)} %reference_joined.3.refs_6_), channel_id=1, source_target_pairs={{0,4},{1,5},{2,6},{3,7},{4,0},{5,1},{6,2},{7,3},{8,12},{9,13},{10,... | collective-permute-start | bytes 196616 | tf_op jit(solution)/shard_map/ppermute | solution.py:620
  13.7 0.0 collective-permute-done.1
  13.7 1.8 %lag_products.1.refs_4_ = f32[8,10,8,128]{3,2,1,0:T(8,128)} custom-call(f32[32,2048]{1,0:T(8,128)S(1)} %bitcast.9, f32[32,2048]{1,0:T(8,128)S(1)} %bitcast.10, bf16[2,2,128,1920]{3,2,1,0:T(8,128)(2,1)S(1)} %shifted_reference.1.refs_2_, f32[2,16,128]{2,1,0:T(8,128)S(1)} %get-tuple-element.19.tiles_ref.refs_3_, ...), custom_call_target="tpu_custom_call" | custom-call | flops 2415000064 | tf_op jit(solution)/shard_map/lag_products/pallas_call | solution.py:323
  15.5 5.9 %all-to-all-start = ((f32[8,10,8,128]{3,2,1,0:T(8,128)}), f32[8,10,8,128]{3,2,1,0:T(8,128)S(1)}, u32[]{:S(2)}, u32[]{:S(2)}) async-start(f32[8,10,8,128]{3,2,1,0:T(8,128)} %lag_products.1.refs_4_), calls=%async_computation | async-start | bytes 655360 | tf_op jit(solution)/shard_map/all_to_all | solution.py:626
  21.4 0.0 collective-permute-done.4.refs_3_
  21.4 6.3 %reference_products.1 = (bf16[2,2048,128]{2,1,0:T(8,128)(2,1)S(1)}, f32[8,128]{1,0:T(8,128)S(1)}, f32[128,128]{1,0:T(8,128)S(1)}) custom-call(f32[1,2,16,128]{3,2,1,0:T(8,128)S(1)} %bitcast.13, f32[1,2,16,128]{3,2,1,0:T(8,128)S(1)} %collective-permute-done.2.second_ref.refs_4_.refs_1_, ...), custom_call_target="tpu_custom_call" | custom-call | flops 7129999872 | tf_op jit(solution)/shard_map/reference_products/pallas_call | solution.py:437
  27.7 0.0 copy-start
  27.7 2.0 %gram_inverse.1 = (bf16[2,128,128]{2,1,0:T(8,128)(2,1)S(1)}, bf16[2,128,128]{2,1,0:T(8,128)(2,1)S(1)}) custom-call(f32[8,128]{1,0:T(8,128)S(1)} %get-tuple-element.21.line_ref, f32[128,128]{1,0:T(8,128)S(1)} %get-tuple-element.22.tail_ref), custom_call_target="tpu_custom_call" | custom-call | flops 2300000000 | tf_op jit(solution)/shard_map/gram_inverse/pallas_call | solution.py:504
  29.7 1.4 %all-to-all-done.got_ref = f32[8,10,8,128]{3,2,1,0:T(8,128)S(1)} async-done(((f32[8,10,8,128]{3,2,1,0:T(8,128)}), f32[8,10,8,128]{3,2,1,0:T(8,128)S(1)}, u32[]{:S(2)}, u32[]{:S(2)}) %all-to-all-start) | async-done | bytes 327712 | tf_op jit(solution)/shard_map/all_to_all | solution.py:626
  31.2 0.0 copy-done
  31.2 2.2 %range_doppler.1 = f32[4,4,2,32,256]{4,3,2,1,0:T(8,128)} custom-call(f32[8,10,8,128]{3,2,1,0:T(8,128)S(1)} %all-to-all-done.got_ref, bf16[2,2048,128]{2,1,0:T(8,128)(2,1)S(1)} %get-tuple-element.20.own_ref, bf16[2,128,128]{2,1,0:T(8,128)(2,1)S(1)} %get-tuple-element.23.gram_ref, bf16[2,128,128]{2,1,0:T(8,128)(2,1)S(1)} %get-tuple-element.24.solver_ref, ...), custom_call_target="tpu_custom_call" | custom-call | flops 2875000064 | tf_op jit(solution)/shard_map/range_doppler/pallas_call | solution.py:576
  (2 shorter events, 0.0 us)
Async XLA Ops:
  1.9 3.1 %collective-permute-start = (f32[64,2048]{1,0:T(8,128)S(1)}, f32[64,2048]{1,0:T(8,128)S(1)}, u32[]{:S(2)}, u32[]{:S(2)}) collective-permute-start(f32[64,2048]{1,0:T(8,128)S(1)} %get-tuple-element.16), channel_id=1, source_target_pairs={{0,8},{8,0},{16,24},{24,16},{1,9},{9,1},{17,25},{25,17},{2,10},{10... | collective-permute-start | bytes 1572872 | tf_op jit(solution)/shard_map/ppermute | solution.py:595
  2.4 4.5 %collective-permute-start.2 = (f32[1,2,16,128]{3,2,1,0:T(8,128)S(1)}, f32[1,2,16,128]{3,2,1,0:T(8,128)S(1)}, u32[]{:S(2)}, u32[]{:S(2)}) collective-permute-start(f32[1,2,16,128]{3,2,1,0:T(8,128)S(1)} %bitcast.11), channel_id=1, source_target_pairs={{0,1},{1,0},{2,3},{3,2},{4,5},{5,4},{6,7},{7,6},{8,9},{9,8},{10,11... | collective-permute-start | bytes 49160 | tf_op jit(solution)/shard_map/ppermute | solution.py:595
  5.0 8.7 %collective-permute-start.1 = (f32[1,32,2048]{2,1,0:T(8,128)S(1)}, f32[1,32,2048]{2,1,0:T(8,128)S(1)}, u32[]{:S(2)}, u32[]{:S(2)}) collective-permute-start(f32[1,32,2048]{2,1,0:T(8,128)S(1)} %get-tuple-element.18.refs_0_), channel_id=1, source_target_pairs={{0,16},{8,24},{16,0},{24,8},{1,17},{9,25},{17,1},{25,9},{2,18},{10... | collective-permute-start | bytes 786440 | tf_op jit(solution)/shard_map/ppermute | solution.py:595
  6.9 5.8 %collective-permute-start.3 = (f32[2,2,16,128]{3,2,1,0:T(8,128)S(1)}, f32[2,2,16,128]{3,2,1,0:T(8,128)S(1)}, u32[]{:S(2)}, u32[]{:S(2)}) collective-permute-start(f32[2,2,16,128]{3,2,1,0:T(8,128)S(1)} %reference_joined.2.first_ref), channel_id=1, source_target_pairs={{0,2},{1,3},{2,4},{3,5},{4,6},{5,7},{6,0},{7,1},{8,10},{9,11},{10,... | collective-permute-start | bytes 98312 | tf_op jit(solution)/shard_map/ppermute | solution.py:620
  12.7 8.7 %collective-permute-start.4 = (f32[4,2,16,128]{3,2,1,0:T(8,128)S(1)}, f32[4,2,16,128]{3,2,1,0:T(8,128)S(1)}, u32[]{:S(2)}, u32[]{:S(2)}) collective-permute-start(f32[4,2,16,128]{3,2,1,0:T(8,128)S(1)} %reference_joined.3.refs_6_), channel_id=1, source_target_pairs={{0,4},{1,5},{2,6},{3,7},{4,0},{5,1},{6,2},{7,3},{8,12},{9,13},{10,... | collective-permute-start | bytes 196616 | tf_op jit(solution)/shard_map/ppermute | solution.py:620
  15.5 15.6 %all-to-all-start = ((f32[8,10,8,128]{3,2,1,0:T(8,128)}), f32[8,10,8,128]{3,2,1,0:T(8,128)S(1)}, u32[]{:S(2)}, u32[]{:S(2)}) async-start(f32[8,10,8,128]{3,2,1,0:T(8,128)} %lag_products.1.refs_4_), calls=%async_computation | async-start | bytes 655360 | tf_op jit(solution)/shard_map/all_to_all | solution.py:626
  27.7 3.5 %copy-start = (bf16[2,128,512]{2,1,0:T(8,128)(2,1)S(1)}, bf16[2,128,512]{2,1,0:T(8,128)(2,1)}, u32[]{:S(2)}) copy-start(bf16[2,128,512]{2,1,0:T(8,128)(2,1)} %constant.2.clone.wave_ref) | copy-start | bytes 786436

commit v18 on v17

--- a/solution.py
+++ b/solution.py
@@ -73,7 +73,7 @@
     return outs
 
 
-CHUNKS = 2
+CHUNKS = 4
 
 
 def beam_kernel(
@@ -553,11 +553,13 @@
                 at = q + h * groups + j
                 held_ref[at * SUBLANES : (at + 1) * SUBLANES, :] = got_ref[at // blocks, at % blocks] - tile
     half = SUBLANES // 2
-    wave = (wave_ref[0], wave_ref[1])
     copies = []
     for g in range(half):
         parts = [held_ref[pl.ds(c * half + g, total, stride=SUBLANES), :] for c in range(2)]
-        spectrum = dot_split(halves(jnp.concatenate(parts, 0).T), wave)
+        high, low = halves(jnp.concatenate(parts, 0).T)
+        by_high = jnp.dot(jnp.concatenate([high, low], 0), wave_ref[0], preferred_element_type=jnp.float32)
+        by_low = jnp.dot(high, wave_ref[1], preferred_element_type=jnp.float32)
+        spectrum = by_high[:LANES] + (by_high[LANES:] + by_low)
         for i in range(groups):
             for c in range(2):
                 out_ref[i, g, c] = spectrum[i * lags_local : (i + 1) * lags_local, c * DOPPLER : (c + 1) * DOPPLER]

time: 33.6 us -> 34.1 us (1.015)
  Pallas kernels: 14.9 us -> 15.3 us
    pallas_call x1, Pallas kernels: 1.85 us -> 2.24 us  [beam_call(): pl.pallas_call(functools.partial(beam_kernel, chan_count, beams_local), i...]
where the time goes in v18:
time: 34.1 us; the launch traced here: 33.9 us
  Pallas kernels  15.3 us (45%)
  starting transfers between devices  13.7 us (40%)
  waiting for transfers between devices  4.74 us (14%)
    pallas_call x1, Pallas kernels, own_call(): pl.pallas_call(functools.partial(own_kernel, lags_local), in_specs=[pl.Bl...  6.26 us
    all_to_all x1, starting transfers between devices, tiled_device(): got = lax.all_to_all(pieces, 'tm', 0, 0, tiled=True)  5.89 us
    ppermute x3, starting transfers between devices, swap(): return lax.ppermute(x, axis, pairs)  4.97 us
    ppermute x2, waiting for transfers between devices, tiled_device(): lax.ppermute(joined, 'tm', [(i, (i + count) % tm_count) for i in range(tm...  3.31 us
    ppermute x2, starting transfers between devices, tiled_device(): lax.ppermute(joined, 'tm', [(i, (i + count) % tm_count) for i in range(tm...  2.88 us
    pallas_call x1, Pallas kernels, map_call(): pl.pallas_call(functools.partial(map_kernel, groups), in_specs=[pl.BlockS...  2.33 us
    pallas_call x1, Pallas kernels, beam_call(): pl.pallas_call(functools.partial(beam_kernel, chan_count, beams_local), i...  2.24 us
    pallas_call x1, Pallas kernels, solver_call(): pl.pallas_call(solver_kernel, out_shape=[out, out], compiler_params=param...  2.05 us
  transfers between devices with their start and end apart: 6, of which 2 were waited for; matrix products, arithmetic and copies ran while one was open for 0% of the time, Pallas kernels for 32%

profile of v18, /device:TPU:0, one launch (start us, length us, event | category | flops | bytes accessed | tf_op | source)
XLA Modules:
  0.0 33.9 jit_solution(9901638985323628774)
XLA Ops:
  0.0 2.2 %beams.1 = (f32[64,2048]{1,0:T(8,128)S(1)}, f32[64,2048]{1,0:T(8,128)S(1)}, f32[2,16,128]{2,1,0:T(8,128)S(1)}) custom-call(f32[2,64,64]{2,1,0:T(8,128)} %w_hbm.1, f32[128,2048]{1,0:T(8,128)} %bitcast.14, f32[2,2048]{1,0:T(2,128)} %ref_hbm.1), custom_call_target="tpu_custom_call" | custom-call | flops 2529999872 | tf_op jit(solution)/shard_map/beams/pallas_call | solution.py:137
  2.2 0.5 %collective-permute-start = (f32[64,2048]{1,0:T(8,128)S(1)}, f32[64,2048]{1,0:T(8,128)S(1)}, u32[]{:S(2)}, u32[]{:S(2)}) collective-permute-start(f32[64,2048]{1,0:T(8,128)S(1)} %get-tuple-element.16), channel_id=1, source_target_pairs={{0,8},{8,0},{16,24},{24,16},{1,9},{9,1},{17,25},{25,17},{2,10},{10... | collective-permute-start | bytes 1572872 | tf_op jit(solution)/shard_map/ppermute | solution.py:597
  2.8 2.6 %collective-permute-start.2 = (f32[1,2,16,128]{3,2,1,0:T(8,128)S(1)}, f32[1,2,16,128]{3,2,1,0:T(8,128)S(1)}, u32[]{:S(2)}, u32[]{:S(2)}) collective-permute-start(f32[1,2,16,128]{3,2,1,0:T(8,128)S(1)} %bitcast.11), channel_id=1, source_target_pairs={{0,1},{1,0},{2,3},{3,2},{4,5},{5,4},{6,7},{7,6},{8,9},{9,8},{10,11... | collective-permute-start | bytes 49160 | tf_op jit(solution)/shard_map/ppermute | solution.py:597
  5.4 0.0 collective-permute-done
  5.4 0.1 halves_summed.1
  5.4 1.9 %collective-permute-start.1 = (f32[1,32,2048]{2,1,0:T(8,128)S(1)}, f32[1,32,2048]{2,1,0:T(8,128)S(1)}, u32[]{:S(2)}, u32[]{:S(2)}) collective-permute-start(f32[1,32,2048]{2,1,0:T(8,128)S(1)} %get-tuple-element.18.refs_0_), channel_id=1, source_target_pairs={{0,16},{8,24},{16,0},{24,8},{1,17},{9,25},{17,1},{25,9},{2,18},{10... | collective-permute-start | bytes 786440 | tf_op jit(solution)/shard_map/ppermute | solution.py:597
  7.3 0.0 collective-permute-done.2.second_ref.refs_4_.refs_1_
  7.3 1.9 %collective-permute-start.3 = (f32[2,2,16,128]{3,2,1,0:T(8,128)S(1)}, f32[2,2,16,128]{3,2,1,0:T(8,128)S(1)}, u32[]{:S(2)}, u32[]{:S(2)}) collective-permute-start(f32[2,2,16,128]{3,2,1,0:T(8,128)S(1)} %reference_joined.2.first_ref), channel_id=1, source_target_pairs={{0,2},{1,3},{2,4},{3,5},{4,6},{5,7},{6,0},{7,1},{8,10},{9,11},{10,... | collective-permute-start | bytes 98312 | tf_op jit(solution)/shard_map/ppermute | solution.py:622
  9.2 0.6 %shifted_reference.1.refs_2_ = bf16[2,2,128,1920]{3,2,1,0:T(8,128)(2,1)S(1)} custom-call(f32[2,16,128]{2,1,0:T(8,128)S(1)} %get-tuple-element.19.tiles_ref.refs_3_), custom_call_target="tpu_custom_call" | custom-call | flops 805000000 | tf_op jit(solution)/shard_map/shifted_reference/pallas_call | solution.py:223
  9.8 3.3 %collective-permute-done.3.second_ref.refs_5_.refs_2_ = f32[2,2,16,128]{3,2,1,0:T(8,128)S(1)} collective-permute-done((f32[2,2,16,128]{3,2,1,0:T(8,128)S(1)}, f32[2,2,16,128]{3,2,1,0:T(8,128)S(1)}, u32[]{:S(2)}, u32[]{:S(2)}) %collective-permute-start.3) | collective-permute-done | bytes 32800 | tf_op jit(solution)/shard_map/ppermute | solution.py:622
  13.1 1.0 %collective-permute-start.4 = (f32[4,2,16,128]{3,2,1,0:T(8,128)S(1)}, f32[4,2,16,128]{3,2,1,0:T(8,128)S(1)}, u32[]{:S(2)}, u32[]{:S(2)}) collective-permute-start(f32[4,2,16,128]{3,2,1,0:T(8,128)S(1)} %reference_joined.3.refs_6_), channel_id=1, source_target_pairs={{0,4},{1,5},{2,6},{3,7},{4,0},{5,1},{6,2},{7,3},{8,12},{9,13},{10,... | collective-permute-start | bytes 196616 | tf_op jit(solution)/shard_map/ppermute | solution.py:622
  14.1 0.0 collective-permute-done.1
  14.1 1.8 %lag_products.1.refs_4_ = f32[8,10,8,128]{3,2,1,0:T(8,128)} custom-call(f32[32,2048]{1,0:T(8,128)S(1)} %bitcast.9, f32[32,2048]{1,0:T(8,128)S(1)} %bitcast.10, bf16[2,2,128,1920]{3,2,1,0:T(8,128)(2,1)S(1)} %shifted_reference.1.refs_2_, f32[2,16,128]{2,1,0:T(8,128)S(1)} %get-tuple-element.19.tiles_ref.refs_3_, ...), custom_call_target="tpu_custom_call" | custom-call | flops 2415000064 | tf_op jit(solution)/shard_map/lag_products/pallas_call | solution.py:323
  15.9 5.9 %all-to-all-start = ((f32[8,10,8,128]{3,2,1,0:T(8,128)}), f32[8,10,8,128]{3,2,1,0:T(8,128)S(1)}, u32[]{:S(2)}, u32[]{:S(2)}) async-start(f32[8,10,8,128]{3,2,1,0:T(8,128)} %lag_products.1.refs_4_), calls=%async_computation | async-start | bytes 655360 | tf_op jit(solution)/shard_map/all_to_all | solution.py:628
  21.8 0.0 collective-permute-done.4.refs_3_
  21.8 6.3 %reference_products.1 = (bf16[2,2048,128]{2,1,0:T(8,128)(2,1)S(1)}, f32[8,128]{1,0:T(8,128)S(1)}, f32[128,128]{1,0:T(8,128)S(1)}) custom-call(f32[1,2,16,128]{3,2,1,0:T(8,128)S(1)} %bitcast.13, f32[1,2,16,128]{3,2,1,0:T(8,128)S(1)} %collective-permute-done.2.second_ref.refs_4_.refs_1_, ...), custom_call_target="tpu_custom_call" | custom-call | flops 7129999872 | tf_op jit(solution)/shard_map/reference_products/pallas_call | solution.py:437
  28.1 0.0 copy-start
  28.1 2.0 %gram_inverse.1 = (bf16[2,128,128]{2,1,0:T(8,128)(2,1)S(1)}, bf16[2,128,128]{2,1,0:T(8,128)(2,1)S(1)}) custom-call(f32[8,128]{1,0:T(8,128)S(1)} %get-tuple-element.21.line_ref, f32[128,128]{1,0:T(8,128)S(1)} %get-tuple-element.22.tail_ref), custom_call_target="tpu_custom_call" | custom-call | flops 2300000000 | tf_op jit(solution)/shard_map/gram_inverse/pallas_call | solution.py:504
  30.1 1.4 %all-to-all-done.got_ref = f32[8,10,8,128]{3,2,1,0:T(8,128)S(1)} async-done(((f32[8,10,8,128]{3,2,1,0:T(8,128)}), f32[8,10,8,128]{3,2,1,0:T(8,128)S(1)}, u32[]{:S(2)}, u32[]{:S(2)}) %all-to-all-start) | async-done | bytes 327712 | tf_op jit(solution)/shard_map/all_to_all | solution.py:628
  31.6 0.0 copy-done
  31.6 2.3 %range_doppler.1 = f32[4,4,2,32,256]{4,3,2,1,0:T(8,128)} custom-call(f32[8,10,8,128]{3,2,1,0:T(8,128)S(1)} %all-to-all-done.got_ref, bf16[2,2048,128]{2,1,0:T(8,128)(2,1)S(1)} %get-tuple-element.20.own_ref, bf16[2,128,128]{2,1,0:T(8,128)(2,1)S(1)} %get-tuple-element.23.gram_ref, bf16[2,128,128]{2,1,0:T(8,128)(2,1)S(1)} %get-tuple-element.24.solver_ref, ...), custom_call_target="tpu_custom_call" | custom-call | flops 2875000064 | tf_op jit(solution)/shard_map/range_doppler/pallas_call | solution.py:578
  (2 shorter events, 0.0 us)
Async XLA Ops:
  2.2 3.1 %collective-permute-start = (f32[64,2048]{1,0:T(8,128)S(1)}, f32[64,2048]{1,0:T(8,128)S(1)}, u32[]{:S(2)}, u32[]{:S(2)}) collective-permute-start(f32[64,2048]{1,0:T(8,128)S(1)} %get-tuple-element.16), channel_id=1, source_target_pairs={{0,8},{8,0},{16,24},{24,16},{1,9},{9,1},{17,25},{25,17},{2,10},{10... | collective-permute-start | bytes 1572872 | tf_op jit(solution)/shard_map/ppermute | solution.py:597
  2.8 4.5 %collective-permute-start.2 = (f32[1,2,16,128]{3,2,1,0:T(8,128)S(1)}, f32[1,2,16,128]{3,2,1,0:T(8,128)S(1)}, u32[]{:S(2)}, u32[]{:S(2)}) collective-permute-start(f32[1,2,16,128]{3,2,1,0:T(8,128)S(1)} %bitcast.11), channel_id=1, source_target_pairs={{0,1},{1,0},{2,3},{3,2},{4,5},{5,4},{6,7},{7,6},{8,9},{9,8},{10,11... | collective-permute-start | bytes 49160 | tf_op jit(solution)/shard_map/ppermute | solution.py:597
  5.4 8.7 %collective-permute-start.1 = (f32[1,32,2048]{2,1,0:T(8,128)S(1)}, f32[1,32,2048]{2,1,0:T(8,128)S(1)}, u32[]{:S(2)}, u32[]{:S(2)}) collective-permute-start(f32[1,32,2048]{2,1,0:T(8,128)S(1)} %get-tuple-element.18.refs_0_), channel_id=1, source_target_pairs={{0,16},{8,24},{16,0},{24,8},{1,17},{9,25},{17,1},{25,9},{2,18},{10... | collective-permute-start | bytes 786440 | tf_op jit(solution)/shard_map/ppermute | solution.py:597
  7.3 5.8 %collective-permute-start.3 = (f32[2,2,16,128]{3,2,1,0:T(8,128)S(1)}, f32[2,2,16,128]{3,2,1,0:T(8,128)S(1)}, u32[]{:S(2)}, u32[]{:S(2)}) collective-permute-start(f32[2,2,16,128]{3,2,1,0:T(8,128)S(1)} %reference_joined.2.first_ref), channel_id=1, source_target_pairs={{0,2},{1,3},{2,4},{3,5},{4,6},{5,7},{6,0},{7,1},{8,10},{9,11},{10,... | collective-permute-start | bytes 98312 | tf_op jit(solution)/shard_map/ppermute | solution.py:622
  13.1 8.7 %collective-permute-start.4 = (f32[4,2,16,128]{3,2,1,0:T(8,128)S(1)}, f32[4,2,16,128]{3,2,1,0:T(8,128)S(1)}, u32[]{:S(2)}, u32[]{:S(2)}) collective-permute-start(f32[4,2,16,128]{3,2,1,0:T(8,128)S(1)} %reference_joined.3.refs_6_), channel_id=1, source_target_pairs={{0,4},{1,5},{2,6},{3,7},{4,0},{5,1},{6,2},{7,3},{8,12},{9,13},{10,... | collective-permute-start | bytes 196616 | tf_op jit(solution)/shard_map/ppermute | solution.py:622
  15.9 15.6 %all-to-all-start = ((f32[8,10,8,128]{3,2,1,0:T(8,128)}), f32[8,10,8,128]{3,2,1,0:T(8,128)S(1)}, u32[]{:S(2)}, u32[]{:S(2)}) async-start(f32[8,10,8,128]{3,2,1,0:T(8,128)} %lag_products.1.refs_4_), calls=%async_computation | async-start | bytes 655360 | tf_op jit(solution)/shard_map/all_to_all | solution.py:628
  28.1 3.5 %copy-start = (bf16[2,128,512]{2,1,0:T(8,128)(2,1)S(1)}, bf16[2,128,512]{2,1,0:T(8,128)(2,1)}, u32[]{:S(2)}) copy-start(bf16[2,128,512]{2,1,0:T(8,128)(2,1)} %constant.2.clone.wave_ref) | copy-start | bytes 786436

commit v19 on v17

--- a/solution.py
+++ b/solution.py
@@ -73,7 +73,7 @@
     return outs
 
 
-CHUNKS = 2
+COPIES = 4
 
 
 def beam_kernel(
@@ -81,16 +81,15 @@
     w_ref, s_ref, ref_ref, w_sem, s_sem, ref_sem,
 ):
     me = lax.axis_index("chan")
-    length = s_hbm.shape[1]
-    width = length // CHUNKS
+    depth = s_hbm.shape[0] // COPIES
     w_copy = pltpu.make_async_copy(w_hbm, w_ref, w_sem)
     w_copy.start()
     ref_copy = pltpu.make_async_copy(ref_hbm, ref_ref, ref_sem)
     ref_copy.start()
     s_copies = []
-    for n in range(CHUNKS):
-        cols = pl.ds(n * width, width)
-        s_copies.append(pltpu.make_async_copy(s_hbm.at[:, cols], s_ref.at[:, cols], s_sem.at[n]))
+    for n in range(COPIES):
+        part = pl.ds(n * depth, depth)
+        s_copies.append(pltpu.make_async_copy(s_hbm.at[part], s_ref.at[part], s_sem.at[n]))
         s_copies[n].start()
     half = SUBLANES // 2
     sub = lax.broadcasted_iota(jnp.int32, (SUBLANES, w_hbm.shape[2]), 0)
@@ -117,15 +116,14 @@
         for n in range(tiles_ref.shape[1]):
             tiles_ref[c, n : n + 1, :] = ref_ref[c : c + 1, n * LANES : (n + 1) * LANES]
     mid = count // 2
-    for n in range(CHUNKS):
-        cols = slice(n * width, (n + 1) * width)
-        s_copies[n].wait()
-        high, low = halves(s_ref[:, cols])
-        by_high = jnp.dot(weights, high, preferred_element_type=jnp.float32)
-        by_low = jnp.dot(weights[:count], low, preferred_element_type=jnp.float32)
-        product = by_high[:count] + (by_high[count:] + by_low)
-        kept_ref[:, cols] = product[:mid]
-        sent_ref[:, cols] = product[mid:]
+    for copy in s_copies:
+        copy.wait()
+    high, low = halves(s_ref[...])
+    by_high = jnp.dot(weights, high, preferred_element_type=jnp.float32)
+    by_low = jnp.dot(weights[:count], low, preferred_element_type=jnp.float32)
+    product = by_high[:count] + (by_high[count:] + by_low)
+    kept_ref[...] = product[:mid]
+    sent_ref[...] = product[mid:]
 
 
 def beam_call(steering, survey, ref, chan_count, beams_local):
@@ -148,7 +146,7 @@
             pltpu.VMEM(survey.shape, jnp.float32),
             pltpu.VMEM(ref.shape, jnp.float32),
             pltpu.SemaphoreType.DMA,
-            pltpu.SemaphoreType.DMA((CHUNKS,)),
+            pltpu.SemaphoreType.DMA((COPIES,)),
             pltpu.SemaphoreType.DMA,
         ],
         compiler_params=params(),
@@ -301,8 +299,8 @@
             tiles = [product[r : r + SUBLANES, lanes] for r in range(0, rows, SUBLANES)]
             for j, tile in enumerate(swap_groups(tiles, groups)):
                 out_ref[h * groups + j, q] = tile
-        if q % 2:
-            send(q - 1, 2)
+        if q + 1 == blocks // 2:
+            send(0, blocks // 2)
     left = lax.broadcasted_iota(jnp.int32, (SUBLANES, LANES), 1) < TAPS
     for i in range(groups // 2):
         a = taps_sum[i * SUBLANES : (i + 1) * SUBLANES]
@@ -311,7 +309,7 @@
         tile = jnp.where(left, a, pltpu.roll(b, LANES - TAPS, 1))
         for owner in range(out_ref.shape[0]):
             out_ref[owner, blocks + i] = tile
-    send(blocks, groups // 2)
+    send(blocks // 2, blocks - blocks // 2 + groups // 2)
     for copy in copies:
         copy.wait()
 
@@ -327,7 +325,7 @@
         out_shape=jax.ShapeDtypeStruct(shape, jnp.float32),
         scratch_shapes=[
             pltpu.VMEM(shape, jnp.float32),
-            pltpu.SemaphoreType.DMA((blocks // 2 + 1,)),
+            pltpu.SemaphoreType.DMA((2,)),
             pltpu.VMEM((2, 2, LANES, 2 * LANES), jnp.bfloat16),
         ],
         compiler_params=params(),

time: 33.6 us -> 33.6 us (level)
  no operation moved by 1% of the time
where the time goes in v19:
time: 33.6 us; the launch traced here: 33.4 us
  Pallas kernels  14.9 us (44%)
  starting transfers between devices  13.7 us (41%)
  waiting for transfers between devices  4.74 us (14%)
    pallas_call x1, Pallas kernels, own_call(): pl.pallas_call(functools.partial(own_kernel, lags_local), in_specs=[pl.Bl...  6.25 us
    all_to_all x1, starting transfers between devices, tiled_device(): got = lax.all_to_all(pieces, 'tm', 0, 0, tiled=True)  5.89 us
    ppermute x3, starting transfers between devices, swap(): return lax.ppermute(x, axis, pairs)  4.97 us
    ppermute x2, waiting for transfers between devices, tiled_device(): lax.ppermute(joined, 'tm', [(i, (i + count) % tm_count) for i in range(tm...  3.3 us
    ppermute x2, starting transfers between devices, tiled_device(): lax.ppermute(joined, 'tm', [(i, (i + count) % tm_count) for i in range(tm...  2.88 us
    pallas_call x1, Pallas kernels, map_call(): pl.pallas_call(functools.partial(map_kernel, groups), in_specs=[pl.BlockS...  2.24 us
    pallas_call x1, Pallas kernels, solver_call(): pl.pallas_call(solver_kernel, out_shape=[out, out], compiler_params=param...  2.05 us
    pallas_call x1, Pallas kernels, beam_call(): pl.pallas_call(functools.partial(beam_kernel, chan_count, beams_local), i...  1.83 us
  transfers between devices with their start and end apart: 6, of which 2 were waited for; matrix products, arithmetic and copies ran while one was open for 0% of the time, Pallas kernels for 32%

profile of v19, /device:TPU:0, one launch (start us, length us, event | category | flops | bytes accessed | tf_op | source)
XLA Modules:
  0.0 33.4 jit_solution(3341839267201419780)
XLA Ops:
  0.0 1.8 %beams.1 = (f32[64,2048]{1,0:T(8,128)S(1)}, f32[64,2048]{1,0:T(8,128)S(1)}, f32[2,16,128]{2,1,0:T(8,128)S(1)}) custom-call(f32[2,64,64]{2,1,0:T(8,128)} %w_hbm.1, f32[128,2048]{1,0:T(8,128)} %bitcast.14, f32[2,2048]{1,0:T(2,128)} %ref_hbm.1), custom_call_target="tpu_custom_call" | custom-call | flops 2529999872 | tf_op jit(solution)/shard_map/beams/pallas_call | solution.py:135
  1.8 0.5 %collective-permute-start = (f32[64,2048]{1,0:T(8,128)S(1)}, f32[64,2048]{1,0:T(8,128)S(1)}, u32[]{:S(2)}, u32[]{:S(2)}) collective-permute-start(f32[64,2048]{1,0:T(8,128)S(1)} %get-tuple-element.16), channel_id=1, source_target_pairs={{0,8},{8,0},{16,24},{24,16},{1,9},{9,1},{17,25},{25,17},{2,10},{10... | collective-permute-start | bytes 1572872 | tf_op jit(solution)/shard_map/ppermute | solution.py:593
  2.4 2.6 %collective-permute-start.2 = (f32[1,2,16,128]{3,2,1,0:T(8,128)S(1)}, f32[1,2,16,128]{3,2,1,0:T(8,128)S(1)}, u32[]{:S(2)}, u32[]{:S(2)}) collective-permute-start(f32[1,2,16,128]{3,2,1,0:T(8,128)S(1)} %bitcast.11), channel_id=1, source_target_pairs={{0,1},{1,0},{2,3},{3,2},{4,5},{5,4},{6,7},{7,6},{8,9},{9,8},{10,11... | collective-permute-start | bytes 49160 | tf_op jit(solution)/shard_map/ppermute | solution.py:593
  5.0 0.0 collective-permute-done
  5.0 0.1 halves_summed.1
  5.0 1.9 %collective-permute-start.1 = (f32[1,32,2048]{2,1,0:T(8,128)S(1)}, f32[1,32,2048]{2,1,0:T(8,128)S(1)}, u32[]{:S(2)}, u32[]{:S(2)}) collective-permute-start(f32[1,32,2048]{2,1,0:T(8,128)S(1)} %get-tuple-element.18.refs_0_), channel_id=1, source_target_pairs={{0,16},{8,24},{16,0},{24,8},{1,17},{9,25},{17,1},{25,9},{2,18},{10... | collective-permute-start | bytes 786440 | tf_op jit(solution)/shard_map/ppermute | solution.py:593
  6.9 0.0 collective-permute-done.2.second_ref.refs_4_.refs_1_
  6.9 1.9 %collective-permute-start.3 = (f32[2,2,16,128]{3,2,1,0:T(8,128)S(1)}, f32[2,2,16,128]{3,2,1,0:T(8,128)S(1)}, u32[]{:S(2)}, u32[]{:S(2)}) collective-permute-start(f32[2,2,16,128]{3,2,1,0:T(8,128)S(1)} %reference_joined.2.first_ref), channel_id=1, source_target_pairs={{0,2},{1,3},{2,4},{3,5},{4,6},{5,7},{6,0},{7,1},{8,10},{9,11},{10,... | collective-permute-start | bytes 98312 | tf_op jit(solution)/shard_map/ppermute | solution.py:618
  8.8 0.6 %shifted_reference.1.refs_2_ = bf16[2,2,128,1920]{3,2,1,0:T(8,128)(2,1)S(1)} custom-call(f32[2,16,128]{2,1,0:T(8,128)S(1)} %get-tuple-element.19.tiles_ref.refs_3_), custom_call_target="tpu_custom_call" | custom-call | flops 805000000 | tf_op jit(solution)/shard_map/shifted_reference/pallas_call | solution.py:221
  9.4 3.3 %collective-permute-done.3.second_ref.refs_5_.refs_2_ = f32[2,2,16,128]{3,2,1,0:T(8,128)S(1)} collective-permute-done((f32[2,2,16,128]{3,2,1,0:T(8,128)S(1)}, f32[2,2,16,128]{3,2,1,0:T(8,128)S(1)}, u32[]{:S(2)}, u32[]{:S(2)}) %collective-permute-start.3) | collective-permute-done | bytes 32800 | tf_op jit(solution)/shard_map/ppermute | solution.py:618
  12.7 1.0 %collective-permute-start.4 = (f32[4,2,16,128]{3,2,1,0:T(8,128)S(1)}, f32[4,2,16,128]{3,2,1,0:T(8,128)S(1)}, u32[]{:S(2)}, u32[]{:S(2)}) collective-permute-start(f32[4,2,16,128]{3,2,1,0:T(8,128)S(1)} %reference_joined.3.refs_6_), channel_id=1, source_target_pairs={{0,4},{1,5},{2,6},{3,7},{4,0},{5,1},{6,2},{7,3},{8,12},{9,13},{10,... | collective-permute-start | bytes 196616 | tf_op jit(solution)/shard_map/ppermute | solution.py:618
  13.7 0.0 collective-permute-done.1
  13.7 1.8 %lag_products.1.refs_4_ = f32[8,10,8,128]{3,2,1,0:T(8,128)} custom-call(f32[32,2048]{1,0:T(8,128)S(1)} %bitcast.9, f32[32,2048]{1,0:T(8,128)S(1)} %bitcast.10, bf16[2,2,128,1920]{3,2,1,0:T(8,128)(2,1)S(1)} %shifted_reference.1.refs_2_, f32[2,16,128]{2,1,0:T(8,128)S(1)} %get-tuple-element.19.tiles_ref.refs_3_, ...), custom_call_target="tpu_custom_call" | custom-call | flops 2415000064 | tf_op jit(solution)/shard_map/lag_products/pallas_call | solution.py:321
  15.5 5.9 %all-to-all-start = ((f32[8,10,8,128]{3,2,1,0:T(8,128)}), f32[8,10,8,128]{3,2,1,0:T(8,128)S(1)}, u32[]{:S(2)}, u32[]{:S(2)}) async-start(f32[8,10,8,128]{3,2,1,0:T(8,128)} %lag_products.1.refs_4_), calls=%async_computation | async-start | bytes 655360 | tf_op jit(solution)/shard_map/all_to_all | solution.py:624
  21.4 0.0 collective-permute-done.4.refs_3_
  21.4 6.2 %reference_products.1 = (bf16[2,2048,128]{2,1,0:T(8,128)(2,1)S(1)}, f32[8,128]{1,0:T(8,128)S(1)}, f32[128,128]{1,0:T(8,128)S(1)}) custom-call(f32[1,2,16,128]{3,2,1,0:T(8,128)S(1)} %bitcast.13, f32[1,2,16,128]{3,2,1,0:T(8,128)S(1)} %collective-permute-done.2.second_ref.refs_4_.refs_1_, ...), custom_call_target="tpu_custom_call" | custom-call | flops 7129999872 | tf_op jit(solution)/shard_map/reference_products/pallas_call | solution.py:435
  27.7 0.0 copy-start
  27.7 2.0 %gram_inverse.1 = (bf16[2,128,128]{2,1,0:T(8,128)(2,1)S(1)}, bf16[2,128,128]{2,1,0:T(8,128)(2,1)S(1)}) custom-call(f32[8,128]{1,0:T(8,128)S(1)} %get-tuple-element.21.line_ref, f32[128,128]{1,0:T(8,128)S(1)} %get-tuple-element.22.tail_ref), custom_call_target="tpu_custom_call" | custom-call | flops 2300000000 | tf_op jit(solution)/shard_map/gram_inverse/pallas_call | solution.py:502
  29.7 1.4 %all-to-all-done.got_ref = f32[8,10,8,128]{3,2,1,0:T(8,128)S(1)} async-done(((f32[8,10,8,128]{3,2,1,0:T(8,128)}), f32[8,10,8,128]{3,2,1,0:T(8,128)S(1)}, u32[]{:S(2)}, u32[]{:S(2)}) %all-to-all-start) | async-done | bytes 327712 | tf_op jit(solution)/shard_map/all_to_all | solution.py:624
  31.1 0.0 copy-done
  31.2 2.2 %range_doppler.1 = f32[4,4,2,32,256]{4,3,2,1,0:T(8,128)} custom-call(f32[8,10,8,128]{3,2,1,0:T(8,128)S(1)} %all-to-all-done.got_ref, bf16[2,2048,128]{2,1,0:T(8,128)(2,1)S(1)} %get-tuple-element.20.own_ref, bf16[2,128,128]{2,1,0:T(8,128)(2,1)S(1)} %get-tuple-element.23.gram_ref, bf16[2,128,128]{2,1,0:T(8,128)(2,1)S(1)} %get-tuple-element.24.solver_ref, ...), custom_call_target="tpu_custom_call" | custom-call | flops 2875000064 | tf_op jit(solution)/shard_map/range_doppler/pallas_call | solution.py:574
  (2 shorter events, 0.0 us)
Async XLA Ops:
  1.8 3.1 %collective-permute-start = (f32[64,2048]{1,0:T(8,128)S(1)}, f32[64,2048]{1,0:T(8,128)S(1)}, u32[]{:S(2)}, u32[]{:S(2)}) collective-permute-start(f32[64,2048]{1,0:T(8,128)S(1)} %get-tuple-element.16), channel_id=1, source_target_pairs={{0,8},{8,0},{16,24},{24,16},{1,9},{9,1},{17,25},{25,17},{2,10},{10... | collective-permute-start | bytes 1572872 | tf_op jit(solution)/shard_map/ppermute | solution.py:593
  2.4 4.5 %collective-permute-start.2 = (f32[1,2,16,128]{3,2,1,0:T(8,128)S(1)}, f32[1,2,16,128]{3,2,1,0:T(8,128)S(1)}, u32[]{:S(2)}, u32[]{:S(2)}) collective-permute-start(f32[1,2,16,128]{3,2,1,0:T(8,128)S(1)} %bitcast.11), channel_id=1, source_target_pairs={{0,1},{1,0},{2,3},{3,2},{4,5},{5,4},{6,7},{7,6},{8,9},{9,8},{10,11... | collective-permute-start | bytes 49160 | tf_op jit(solution)/shard_map/ppermute | solution.py:593
  5.0 8.7 %collective-permute-start.1 = (f32[1,32,2048]{2,1,0:T(8,128)S(1)}, f32[1,32,2048]{2,1,0:T(8,128)S(1)}, u32[]{:S(2)}, u32[]{:S(2)}) collective-permute-start(f32[1,32,2048]{2,1,0:T(8,128)S(1)} %get-tuple-element.18.refs_0_), channel_id=1, source_target_pairs={{0,16},{8,24},{16,0},{24,8},{1,17},{9,25},{17,1},{25,9},{2,18},{10... | collective-permute-start | bytes 786440 | tf_op jit(solution)/shard_map/ppermute | solution.py:593
  6.9 5.8 %collective-permute-start.3 = (f32[2,2,16,128]{3,2,1,0:T(8,128)S(1)}, f32[2,2,16,128]{3,2,1,0:T(8,128)S(1)}, u32[]{:S(2)}, u32[]{:S(2)}) collective-permute-start(f32[2,2,16,128]{3,2,1,0:T(8,128)S(1)} %reference_joined.2.first_ref), channel_id=1, source_target_pairs={{0,2},{1,3},{2,4},{3,5},{4,6},{5,7},{6,0},{7,1},{8,10},{9,11},{10,... | collective-permute-start | bytes 98312 | tf_op jit(solution)/shard_map/ppermute | solution.py:618
  12.7 8.7 %collective-permute-start.4 = (f32[4,2,16,128]{3,2,1,0:T(8,128)S(1)}, f32[4,2,16,128]{3,2,1,0:T(8,128)S(1)}, u32[]{:S(2)}, u32[]{:S(2)}) collective-permute-start(f32[4,2,16,128]{3,2,1,0:T(8,128)S(1)} %reference_joined.3.refs_6_), channel_id=1, source_target_pairs={{0,4},{1,5},{2,6},{3,7},{4,0},{5,1},{6,2},{7,3},{8,12},{9,13},{10,... | collective-permute-start | bytes 196616 | tf_op jit(solution)/shard_map/ppermute | solution.py:618
  15.5 15.6 %all-to-all-start = ((f32[8,10,8,128]{3,2,1,0:T(8,128)}), f32[8,10,8,128]{3,2,1,0:T(8,128)S(1)}, u32[]{:S(2)}, u32[]{:S(2)}) async-start(f32[8,10,8,128]{3,2,1,0:T(8,128)} %lag_products.1.refs_4_), calls=%async_computation | async-start | bytes 655360 | tf_op jit(solution)/shard_map/all_to_all | solution.py:624
  27.7 3.5 %copy-start = (bf16[2,128,512]{2,1,0:T(8,128)(2,1)S(1)}, bf16[2,128,512]{2,1,0:T(8,128)(2,1)}, u32[]{:S(2)}) copy-start(bf16[2,128,512]{2,1,0:T(8,128)(2,1)} %constant.2.clone.wave_ref) | copy-start | bytes 786436

commit v20 on v19

--- a/solution.py
+++ b/solution.py
@@ -227,11 +227,8 @@
     )(tiles)
 
 
-def lag_kernel(groups, part_count, *refs):
-    y_refs, refs = refs[:part_count], refs[part_count:]
-    table_ref, tiles_ref, *round_refs, _, out_hbm, out_ref, out_sem, first_ref = refs
-    copies = []
-
+def first_kernel(tiles_ref, *refs):
+    *round_refs, out_ref = refs
     me = lax.axis_index("tm")
     for c in range(2):
         tails = [ref[ref.shape[0] - 1, c, ref.shape[2] - EDGE :, :] for ref in round_refs]
@@ -239,9 +236,25 @@
         line = jnp.concatenate([before[n : n + 1] for n in range(EDGE)] + [tiles_ref[c, 0:1, :]], 1)
 
         def keep(h, g, value):
-            first_ref[h, c, g : g + 2 * SUBLANES] = value
+            out_ref[h, c, g : g + 2 * SUBLANES] = value
 
         spread_line(line, keep)
+
+
+def first_call(tiles, rounds):
+    return pl.pallas_call(
+        first_kernel,
+        out_shape=jax.ShapeDtypeStruct((2, 2, LANES, 2 * LANES), jnp.bfloat16),
+        compiler_params=params(),
+        cost_estimate=cost(0.1),
+        name="shifted_first",
+    )(tiles, *rounds)
+
+
+def lag_kernel(groups, part_count, *refs):
+    y_refs, refs = refs[:part_count], refs[part_count:]
+    table_ref, first_ref, _, out_hbm, out_ref, out_sem = refs
+    copies = []
 
     def table_tile(h, n):
         parts = []
@@ -314,24 +327,23 @@
         copy.wait()
 
 
-def lag_call(ys, table, tiles, rounds, after, groups, owners):
+def lag_call(ys, table, first, after, groups, owners):
     blocks = ys[0].shape[1] // BLOCK_LEN
     shape = (owners, blocks + groups // 2, SUBLANES, LANES)
     vmem = pl.BlockSpec(memory_space=pltpu.VMEM)
     return pl.pallas_call(
         functools.partial(lag_kernel, groups, len(ys)),
-        in_specs=[vmem] * (len(ys) + 2 + len(rounds)) + [pl.BlockSpec(memory_space=pl.ANY)],
+        in_specs=[vmem] * (len(ys) + 2) + [pl.BlockSpec(memory_space=pl.ANY)],
         out_specs=pl.BlockSpec(memory_space=pltpu.HBM),
         out_shape=jax.ShapeDtypeStruct(shape, jnp.float32),
         scratch_shapes=[
             pltpu.VMEM(shape, jnp.float32),
             pltpu.SemaphoreType.DMA((2,)),
-            pltpu.VMEM((2, 2, LANES, 2 * LANES), jnp.bfloat16),
         ],
         compiler_params=params(),
         cost_estimate=cost(2.1),
         name="lag_products",
-    )(*ys, table, tiles, *rounds, after)
+    )(*ys, table, first, after)
 
 
 BATCH = 4
@@ -451,7 +463,7 @@
     return jnp.concatenate([a, -lane_sign(a.shape) * pltpu.roll(a, a.shape[0], 1)], 0)
 
 
-def solver_kernel(line_ref, tail_ref, gram_ref, solver_ref):
+def solver_kernel(line_ref, tail_ref, solver_ref):
     total = line_ref[...]
     line = total[0:1] + lane_sign((1, LANES)) * pltpu.roll(total[1:2], TAPS, 1)
     low = lax.broadcasted_iota(jnp.int32, (1, LANES), 1) < TAPS
@@ -473,8 +485,8 @@
     gram_r = strict_r + strict_r.T + diag_r - (tails[:TAPS, :TAPS] + tails[TAPS:, TAPS:])
     gram_i = up_i - up_i.T - (tails[:TAPS, TAPS:] - tails[TAPS:, :TAPS])
     gram = jnp.concatenate([gram_r, gram_i], 1)
-    gram_halves = halves(as_factor(gram))
-    gram_ref[0], gram_ref[1] = gram_halves
+    gram_factor = as_factor(gram)
+    gram_halves = halves(gram_factor)
     one = (
         lax.broadcasted_iota(jnp.int32, gram.shape, 0) == lax.broadcasted_iota(jnp.int32, gram.shape, 1)
     ).astype(jnp.float32)
@@ -494,14 +506,17 @@
 
     start = (jnp.int32(0), jnp.float32(1.0), one * (1.0 / bound))
     _, _, inverse = lax.while_loop(again, newton, start)
-    solver_ref[0], solver_ref[1] = halves(as_factor(inverse))
+    seen = jnp.dot(inverse, gram_factor, precision=HIGHEST, preferred_element_type=jnp.float32)
+    inverse = inverse + jnp.dot(
+        one - seen, as_factor(inverse), precision=HIGHEST, preferred_element_type=jnp.float32
+    )
+    solver_ref[...] = as_factor(inverse)
 
 
 def solver_call(line, tail):
-    out = jax.ShapeDtypeStruct((2,) + tail.shape, jnp.bfloat16)
     return pl.pallas_call(
         solver_kernel,
-        out_shape=[out, out],
+        out_shape=jax.ShapeDtypeStruct(tail.shape, jnp.float32),
         compiler_params=params(),
         cost_estimate=cost(2.0),
         name="gram_inverse",
@@ -516,7 +531,7 @@
     return (np.concatenate([upper, lower], 0) * scale).astype(np.float32)
 
 
-def map_kernel(groups, got_ref, own_ref, gram_ref, solver_ref, wave_ref, out_hbm, held_ref, out_ref, out_sem):
+def map_kernel(groups, got_ref, own_ref, solver_ref, wave_ref, out_hbm, held_ref, out_ref, out_sem):
     owners, pieces = got_ref.shape[:2]
     blocks = pieces - groups // 2
     lags_local = LANES // groups
@@ -533,10 +548,7 @@
             other = -sign * pltpu.roll(there, SUBLANES // 2, 0)
             rows[part] = jnp.where(left, here, other)
     cross = jnp.concatenate(rows, 0)
-    solver = (solver_ref[0], solver_ref[1])
-    taps = dot_split(halves(cross), solver)
-    rest = cross - dot_split(halves(taps), (gram_ref[0], gram_ref[1]))
-    taps = taps + dot_split(halves(rest), solver)
+    taps = jnp.dot(cross, solver_ref[...], precision=HIGHEST, preferred_element_type=jnp.float32)
     taps_high, taps_low = halves(taps)
     taps_both = jnp.concatenate([taps_high, taps_low], 0)
     count = taps.shape[0]
@@ -566,14 +578,14 @@
         copy.wait()
 
 
-def map_call(got, own, gram, solver, wave, groups, beams_local):
+def map_call(got, own, solver, wave, groups, beams_local):
     total = got.shape[0] * (got.shape[1] - groups // 2)
     lags_local = LANES // groups
     half = SUBLANES // 2
     shape = (beams_local // half, half, 2, lags_local, DOPPLER)
     out = pl.pallas_call(
         functools.partial(map_kernel, groups),
-        in_specs=[pl.BlockSpec(memory_space=pltpu.VMEM)] * 5,
+        in_specs=[pl.BlockSpec(memory_space=pltpu.VMEM)] * 4,
         out_specs=pl.BlockSpec(memory_space=pltpu.HBM),
         out_shape=jax.ShapeDtypeStruct(shape, jnp.float32),
         scratch_shapes=[
@@ -584,7 +596,7 @@
         compiler_params=params(),
         cost_estimate=cost(2.5),
         name="range_doppler",
-    )(got, own, gram, solver, wave)
+    )(got, own, solver, wave)
     return out.reshape((beams_local,) + shape[2:])
 
 
@@ -620,14 +632,15 @@
             break
         joined = join_call(joined, rounds[-1])
     table = table_call(tiles)
-    pieces = lag_call([kept[0], got[0]], table, tiles, rounds[:2], joined, groups, tm_count)
+    first = first_call(tiles, rounds[:2])
+    pieces = lag_call([kept[0], got[0]], table, first, joined, groups, tm_count)
     got = lax.all_to_all(pieces, "tm", 0, 0, tiled=True)
     own, line, tail = own_call([tiles[None]] + rounds, lags_local, pieces)
-    gram, solver = solver_call(line, tail)
+    solver = solver_call(line, tail)
     wave = doppler_table(samples // BLOCK_LEN, 0.125 / math.sqrt(samples))
     high = wave.astype(jnp.bfloat16)
     wave = np.stack([high, (wave - high.astype(np.float32)).astype(jnp.bfloat16)])
-    return map_call(got, own, gram, solver, jnp.asarray(wave), groups, beams_local)
+    return map_call(got, own, solver, jnp.asarray(wave), groups, beams_local)
 
 
 def lag_table(ref_ext, offset, lags):

time: 33.6 us -> 33.4 us (level)
  waiting for transfers between devices: 4.74 us -> 4.33 us
    pallas_call x1 -> x2, Pallas kernels: 2.05 us -> 2.63 us  [the longest x1 2.45 us: solver_call(): pl.pallas_call(solver_kernel, out_shape=jax.ShapeDtypeStruct(tail.shape,...]
    all_to_all x1, waiting for transfers between devices: 1.43 us -> 1.02 us  [tiled_device(): got = lax.all_to_all(pieces, 'tm', 0, 0, tiled=True)]
  transfers between devices with their start and end apart: 6 -> 6, of which waited for: 2 -> 2; matrix products, arithmetic and copies ran while one was open for 0% -> 0% of each run, Pallas kernels for 32% -> 34%
where the time goes in v20:
time: 33.4 us; the launch traced here: 33.2 us
  Pallas kernels  15.2 us (46%)
  starting transfers between devices  13.6 us (41%)
  waiting for transfers between devices  4.33 us (13%)
    pallas_call x1, Pallas kernels, own_call(): pl.pallas_call(functools.partial(own_kernel, lags_local), in_specs=[pl.Bl...  6.25 us
    all_to_all x1, starting transfers between devices, tiled_device(): got = lax.all_to_all(pieces, 'tm', 0, 0, tiled=True)  5.7 us
    ppermute x3, starting transfers between devices, swap(): return lax.ppermute(x, axis, pairs)  4.97 us
    ppermute x2, waiting for transfers between devices, tiled_device(): lax.ppermute(joined, 'tm', [(i, (i + count) % tm_count) for i in range(tm...  3.3 us
    ppermute x2, starting transfers between devices, tiled_device(): lax.ppermute(joined, 'tm', [(i, (i + count) % tm_count) for i in range(tm...  2.88 us
    pallas_call x1, Pallas kernels, solver_call(): pl.pallas_call(solver_kernel, out_shape=jax.ShapeDtypeStruct(tail.shape,...  2.45 us
    pallas_call x1, Pallas kernels, map_call(): pl.pallas_call(functools.partial(map_kernel, groups), in_specs=[pl.BlockS...  2.17 us
    pallas_call x1, Pallas kernels, beam_call(): pl.pallas_call(functools.partial(beam_kernel, chan_count, beams_local), i...  1.83 us
  transfers between devices with their start and end apart: 6, of which 2 were waited for; matrix products, arithmetic and copies ran while one was open for 0% of the time, Pallas kernels for 34%

profile of v20, /device:TPU:0, one launch (start us, length us, event | category | flops | bytes accessed | tf_op | source)
XLA Modules:
  0.0 33.2 jit_solution(11310417444828333849)
XLA Ops:
  0.0 1.8 %beams.1 = (f32[64,2048]{1,0:T(8,128)S(1)}, f32[64,2048]{1,0:T(8,128)S(1)}, f32[2,16,128]{2,1,0:T(8,128)S(1)}) custom-call(f32[2,64,64]{2,1,0:T(8,128)} %w_hbm.1, f32[128,2048]{1,0:T(8,128)} %bitcast.14, f32[2,2048]{1,0:T(2,128)} %ref_hbm.1), custom_call_target="tpu_custom_call" | custom-call | flops 2529999872 | tf_op jit(solution)/shard_map/beams/pallas_call | solution.py:135
  1.8 0.5 %collective-permute-start = (f32[64,2048]{1,0:T(8,128)S(1)}, f32[64,2048]{1,0:T(8,128)S(1)}, u32[]{:S(2)}, u32[]{:S(2)}) collective-permute-start(f32[64,2048]{1,0:T(8,128)S(1)} %get-tuple-element.14), channel_id=1, source_target_pairs={{0,8},{8,0},{16,24},{24,16},{1,9},{9,1},{17,25},{25,17},{2,10},{10... | collective-permute-start | bytes 1572872 | tf_op jit(solution)/shard_map/ppermute | solution.py:605
  2.4 2.6 %collective-permute-start.2 = (f32[1,2,16,128]{3,2,1,0:T(8,128)S(1)}, f32[1,2,16,128]{3,2,1,0:T(8,128)S(1)}, u32[]{:S(2)}, u32[]{:S(2)}) collective-permute-start(f32[1,2,16,128]{3,2,1,0:T(8,128)S(1)} %bitcast.11), channel_id=1, source_target_pairs={{0,1},{1,0},{2,3},{3,2},{4,5},{5,4},{6,7},{7,6},{8,9},{9,8},{10,11... | collective-permute-start | bytes 49160 | tf_op jit(solution)/shard_map/ppermute | solution.py:605
  5.0 0.0 collective-permute-done
  5.0 0.1 halves_summed.1
  5.0 1.9 %collective-permute-start.1 = (f32[1,32,2048]{2,1,0:T(8,128)S(1)}, f32[1,32,2048]{2,1,0:T(8,128)S(1)}, u32[]{:S(2)}, u32[]{:S(2)}) collective-permute-start(f32[1,32,2048]{2,1,0:T(8,128)S(1)} %get-tuple-element.16.refs_0_), channel_id=1, source_target_pairs={{0,16},{8,24},{16,0},{24,8},{1,17},{9,25},{17,1},{25,9},{2,18},{10... | collective-permute-start | bytes 786440 | tf_op jit(solution)/shard_map/ppermute | solution.py:605
  6.9 0.0 collective-permute-done.2.second_ref.refs_0_.refs_1_
  6.9 1.9 %collective-permute-start.3 = (f32[2,2,16,128]{3,2,1,0:T(8,128)S(1)}, f32[2,2,16,128]{3,2,1,0:T(8,128)S(1)}, u32[]{:S(2)}, u32[]{:S(2)}) collective-permute-start(f32[2,2,16,128]{3,2,1,0:T(8,128)S(1)} %reference_joined.2.first_ref), channel_id=1, source_target_pairs={{0,2},{1,3},{2,4},{3,5},{4,6},{5,7},{6,0},{7,1},{8,10},{9,11},{10,... | collective-permute-start | bytes 98312 | tf_op jit(solution)/shard_map/ppermute | solution.py:630
  8.8 0.6 %shifted_reference.1.refs_2_ = bf16[2,2,128,1920]{3,2,1,0:T(8,128)(2,1)S(1)} custom-call(f32[2,16,128]{2,1,0:T(8,128)S(1)} %get-tuple-element.17.tiles_ref), custom_call_target="tpu_custom_call" | custom-call | flops 805000000 | tf_op jit(solution)/shard_map/shifted_reference/pallas_call | solution.py:221
  9.4 3.3 %collective-permute-done.3.refs_1_.second_ref.refs_2_ = f32[2,2,16,128]{3,2,1,0:T(8,128)S(1)} collective-permute-done((f32[2,2,16,128]{3,2,1,0:T(8,128)S(1)}, f32[2,2,16,128]{3,2,1,0:T(8,128)S(1)}, u32[]{:S(2)}, u32[]{:S(2)}) %collective-permute-start.3) | collective-permute-done | bytes 32800 | tf_op jit(solution)/shard_map/ppermute | solution.py:630
  12.7 1.0 %collective-permute-start.4 = (f32[4,2,16,128]{3,2,1,0:T(8,128)S(1)}, f32[4,2,16,128]{3,2,1,0:T(8,128)S(1)}, u32[]{:S(2)}, u32[]{:S(2)}) collective-permute-start(f32[4,2,16,128]{3,2,1,0:T(8,128)S(1)} %reference_joined.3.refs_4_), channel_id=1, source_target_pairs={{0,4},{1,5},{2,6},{3,7},{4,0},{5,1},{6,2},{7,3},{8,12},{9,13},{10,... | collective-permute-start | bytes 196616 | tf_op jit(solution)/shard_map/ppermute | solution.py:630
  13.7 0.2 shifted_first.1.refs_3_
  13.9 0.0 collective-permute-done.1
  13.9 1.6 %lag_products.1.refs_4_ = f32[8,10,8,128]{3,2,1,0:T(8,128)} custom-call(f32[32,2048]{1,0:T(8,128)S(1)} %bitcast.9, f32[32,2048]{1,0:T(8,128)S(1)} %bitcast.10, bf16[2,2,128,1920]{3,2,1,0:T(8,128)(2,1)S(1)} %shifted_reference.1.refs_2_, bf16[2,2,128,256]{3,2,1,0:T(8,128)(2,1)S(1)} %shifted_first.1.refs_3_, f32[4,2,16,128]{3,2,1,0:T(8,128)S(1)} %reference_joined.3.refs_4_), custom_call_target="tpu_custom_call" | custom-call | flops 2415000064 | tf_op jit(solution)/shard_map/lag_products/pallas_call | solution.py:334
  15.5 5.7 %all-to-all-start = ((f32[8,10,8,128]{3,2,1,0:T(8,128)}), f32[8,10,8,128]{3,2,1,0:T(8,128)S(1)}, u32[]{:S(2)}, u32[]{:S(2)}) async-start(f32[8,10,8,128]{3,2,1,0:T(8,128)} %lag_products.1.refs_4_), calls=%async_computation | async-start | bytes 655360 | tf_op jit(solution)/shard_map/all_to_all | solution.py:637
  21.2 0.0 collective-permute-done.4.refs_3_
  21.2 6.3 %reference_products.1 = (bf16[2,2048,128]{2,1,0:T(8,128)(2,1)S(1)}, f32[8,128]{1,0:T(8,128)S(1)}, f32[128,128]{1,0:T(8,128)S(1)}) custom-call(f32[1,2,16,128]{3,2,1,0:T(8,128)S(1)} %bitcast.13, f32[1,2,16,128]{3,2,1,0:T(8,128)S(1)} %collective-permute-done.2.second_ref.refs_0_.refs_1_, ...), custom_call_target="tpu_custom_call" | custom-call | flops 7129999872 | tf_op jit(solution)/shard_map/reference_products/pallas_call | solution.py:447
  27.5 0.0 copy-start
  27.5 2.5 %gram_inverse.1.solver_ref = f32[128,128]{1,0:T(8,128)S(1)} custom-call(f32[8,128]{1,0:T(8,128)S(1)} %get-tuple-element.19.line_ref, f32[128,128]{1,0:T(8,128)S(1)} %get-tuple-element.20.tail_ref), custom_call_target="tpu_custom_call" | custom-call | flops 2300000000 | tf_op jit(solution)/shard_map/gram_inverse/pallas_call | solution.py:517
  30.0 1.0 %all-to-all-done.got_ref = f32[8,10,8,128]{3,2,1,0:T(8,128)S(1)} async-done(((f32[8,10,8,128]{3,2,1,0:T(8,128)}), f32[8,10,8,128]{3,2,1,0:T(8,128)S(1)}, u32[]{:S(2)}, u32[]{:S(2)}) %all-to-all-start) | async-done | bytes 327712 | tf_op jit(solution)/shard_map/all_to_all | solution.py:637
  31.0 0.0 copy-done
  31.0 2.2 %range_doppler.1 = f32[4,4,2,32,256]{4,3,2,1,0:T(8,128)} custom-call(f32[8,10,8,128]{3,2,1,0:T(8,128)S(1)} %all-to-all-done.got_ref, bf16[2,2048,128]{2,1,0:T(8,128)(2,1)S(1)} %get-tuple-element.18.own_ref, f32[128,128]{1,0:T(8,128)S(1)} %gram_inverse.1.solver_ref, bf16[2,128,512]{2,1,0:T(8,128)(2,1)S(1)} %copy-done), custom_call_target="tpu_custom_call" | custom-call | flops 2875000064 | tf_op jit(solution)/shard_map/range_doppler/pallas_call | solution.py:586
  (2 shorter events, 0.0 us)
Async XLA Ops:
  1.8 3.1 %collective-permute-start = (f32[64,2048]{1,0:T(8,128)S(1)}, f32[64,2048]{1,0:T(8,128)S(1)}, u32[]{:S(2)}, u32[]{:S(2)}) collective-permute-start(f32[64,2048]{1,0:T(8,128)S(1)} %get-tuple-element.14), channel_id=1, source_target_pairs={{0,8},{8,0},{16,24},{24,16},{1,9},{9,1},{17,25},{25,17},{2,10},{10... | collective-permute-start | bytes 1572872 | tf_op jit(solution)/shard_map/ppermute | solution.py:605
  2.4 4.5 %collective-permute-start.2 = (f32[1,2,16,128]{3,2,1,0:T(8,128)S(1)}, f32[1,2,16,128]{3,2,1,0:T(8,128)S(1)}, u32[]{:S(2)}, u32[]{:S(2)}) collective-permute-start(f32[1,2,16,128]{3,2,1,0:T(8,128)S(1)} %bitcast.11), channel_id=1, source_target_pairs={{0,1},{1,0},{2,3},{3,2},{4,5},{5,4},{6,7},{7,6},{8,9},{9,8},{10,11... | collective-permute-start | bytes 49160 | tf_op jit(solution)/shard_map/ppermute | solution.py:605
  5.0 8.9 %collective-permute-start.1 = (f32[1,32,2048]{2,1,0:T(8,128)S(1)}, f32[1,32,2048]{2,1,0:T(8,128)S(1)}, u32[]{:S(2)}, u32[]{:S(2)}) collective-permute-start(f32[1,32,2048]{2,1,0:T(8,128)S(1)} %get-tuple-element.16.refs_0_), channel_id=1, source_target_pairs={{0,16},{8,24},{16,0},{24,8},{1,17},{9,25},{17,1},{25,9},{2,18},{10... | collective-permute-start | bytes 786440 | tf_op jit(solution)/shard_map/ppermute | solution.py:605
  6.9 5.8 %collective-permute-start.3 = (f32[2,2,16,128]{3,2,1,0:T(8,128)S(1)}, f32[2,2,16,128]{3,2,1,0:T(8,128)S(1)}, u32[]{:S(2)}, u32[]{:S(2)}) collective-permute-start(f32[2,2,16,128]{3,2,1,0:T(8,128)S(1)} %reference_joined.2.first_ref), channel_id=1, source_target_pairs={{0,2},{1,3},{2,4},{3,5},{4,6},{5,7},{6,0},{7,1},{8,10},{9,11},{10,... | collective-permute-start | bytes 98312 | tf_op jit(solution)/shard_map/ppermute | solution.py:630
  12.7 8.6 %collective-permute-start.4 = (f32[4,2,16,128]{3,2,1,0:T(8,128)S(1)}, f32[4,2,16,128]{3,2,1,0:T(8,128)S(1)}, u32[]{:S(2)}, u32[]{:S(2)}) collective-permute-start(f32[4,2,16,128]{3,2,1,0:T(8,128)S(1)} %reference_joined.3.refs_4_), channel_id=1, source_target_pairs={{0,4},{1,5},{2,6},{3,7},{4,0},{5,1},{6,2},{7,3},{8,12},{9,13},{10,... | collective-permute-start | bytes 196616 | tf_op jit(solution)/shard_map/ppermute | solution.py:630
  15.5 15.4 %all-to-all-start = ((f32[8,10,8,128]{3,2,1,0:T(8,128)}), f32[8,10,8,128]{3,2,1,0:T(8,128)S(1)}, u32[]{:S(2)}, u32[]{:S(2)}) async-start(f32[8,10,8,128]{3,2,1,0:T(8,128)} %lag_products.1.refs_4_), calls=%async_computation | async-start | bytes 655360 | tf_op jit(solution)/shard_map/all_to_all | solution.py:637
  27.5 3.5 %copy-start = (bf16[2,128,512]{2,1,0:T(8,128)(2,1)S(1)}, bf16[2,128,512]{2,1,0:T(8,128)(2,1)}, u32[]{:S(2)}) copy-start(bf16[2,128,512]{2,1,0:T(8,128)(2,1)} %constant.2.clone.wave_ref) | copy-start | bytes 786436

commit v21 on v20

--- a/solution.py
+++ b/solution.py
@@ -73,7 +73,7 @@
     return outs
 
 
-COPIES = 4
+COPIES = 8
 
 
 def beam_kernel(
@@ -312,8 +312,8 @@
             tiles = [product[r : r + SUBLANES, lanes] for r in range(0, rows, SUBLANES)]
             for j, tile in enumerate(swap_groups(tiles, groups)):
                 out_ref[h * groups + j, q] = tile
-        if q + 1 == blocks // 2:
-            send(0, blocks // 2)
+        if q + 1 == blocks - 2:
+            send(0, q + 1)
     left = lax.broadcasted_iota(jnp.int32, (SUBLANES, LANES), 1) < TAPS
     for i in range(groups // 2):
         a = taps_sum[i * SUBLANES : (i + 1) * SUBLANES]
@@ -322,7 +322,7 @@
         tile = jnp.where(left, a, pltpu.roll(b, LANES - TAPS, 1))
         for owner in range(out_ref.shape[0]):
             out_ref[owner, blocks + i] = tile
-    send(blocks // 2, blocks - blocks // 2 + groups // 2)
+    send(blocks - 2, 2 + groups // 2)
     for copy in copies:
         copy.wait()
 

time: 33.4 us -> 33.5 us (level)
  no operation moved by 1% of the time
where the time goes in v21:
time: 33.5 us; the launch traced here: 33.3 us
  Pallas kernels  15.3 us (46%)
  starting transfers between devices  13.6 us (41%)
  waiting for transfers between devices  4.33 us (13%)
    pallas_call x1, Pallas kernels, own_call(): pl.pallas_call(functools.partial(own_kernel, lags_local), in_specs=[pl.Bl...  6.26 us
    all_to_all x1, starting transfers between devices, tiled_device(): got = lax.all_to_all(pieces, 'tm', 0, 0, tiled=True)  5.7 us
    ppermute x3, starting transfers between devices, swap(): return lax.ppermute(x, axis, pairs)  4.97 us
    ppermute x2, waiting for transfers between devices, tiled_device(): lax.ppermute(joined, 'tm', [(i, (i + count) % tm_count) for i in range(tm...  3.3 us
    ppermute x2, starting transfers between devices, tiled_device(): lax.ppermute(joined, 'tm', [(i, (i + count) % tm_count) for i in range(tm...  2.88 us
    pallas_call x1, Pallas kernels, solver_call(): pl.pallas_call(solver_kernel, out_shape=jax.ShapeDtypeStruct(tail.shape,...  2.45 us
    pallas_call x1, Pallas kernels, map_call(): pl.pallas_call(functools.partial(map_kernel, groups), in_specs=[pl.BlockS...  2.17 us
    pallas_call x1, Pallas kernels, beam_call(): pl.pallas_call(functools.partial(beam_kernel, chan_count, beams_local), i...  1.97 us
  transfers between devices with their start and end apart: 6, of which 2 were waited for; matrix products, arithmetic and copies ran while one was open for 0% of the time, Pallas kernels for 34%

profile of v21, /device:TPU:0, one launch (start us, length us, event | category | flops | bytes accessed | tf_op | source)
XLA Modules:
  0.0 33.3 jit_solution(1411844918275552105)
XLA Ops:
  0.0 2.0 %beams.1 = (f32[64,2048]{1,0:T(8,128)S(1)}, f32[64,2048]{1,0:T(8,128)S(1)}, f32[2,16,128]{2,1,0:T(8,128)S(1)}) custom-call(f32[2,64,64]{2,1,0:T(8,128)} %w_hbm.1, f32[128,2048]{1,0:T(8,128)} %bitcast.14, f32[2,2048]{1,0:T(2,128)} %ref_hbm.1), custom_call_target="tpu_custom_call" | custom-call | flops 2529999872 | tf_op jit(solution)/shard_map/beams/pallas_call | solution.py:135
  2.0 0.5 %collective-permute-start = (f32[64,2048]{1,0:T(8,128)S(1)}, f32[64,2048]{1,0:T(8,128)S(1)}, u32[]{:S(2)}, u32[]{:S(2)}) collective-permute-start(f32[64,2048]{1,0:T(8,128)S(1)} %get-tuple-element.14), channel_id=1, source_target_pairs={{0,8},{8,0},{16,24},{24,16},{1,9},{9,1},{17,25},{25,17},{2,10},{10... | collective-permute-start | bytes 1572872 | tf_op jit(solution)/shard_map/ppermute | solution.py:605
  2.5 2.6 %collective-permute-start.2 = (f32[1,2,16,128]{3,2,1,0:T(8,128)S(1)}, f32[1,2,16,128]{3,2,1,0:T(8,128)S(1)}, u32[]{:S(2)}, u32[]{:S(2)}) collective-permute-start(f32[1,2,16,128]{3,2,1,0:T(8,128)S(1)} %bitcast.11), channel_id=1, source_target_pairs={{0,1},{1,0},{2,3},{3,2},{4,5},{5,4},{6,7},{7,6},{8,9},{9,8},{10,11... | collective-permute-start | bytes 49160 | tf_op jit(solution)/shard_map/ppermute | solution.py:605
  5.1 0.0 collective-permute-done
  5.1 0.1 halves_summed.1
  5.2 1.9 %collective-permute-start.1 = (f32[1,32,2048]{2,1,0:T(8,128)S(1)}, f32[1,32,2048]{2,1,0:T(8,128)S(1)}, u32[]{:S(2)}, u32[]{:S(2)}) collective-permute-start(f32[1,32,2048]{2,1,0:T(8,128)S(1)} %get-tuple-element.16.refs_0_), channel_id=1, source_target_pairs={{0,16},{8,24},{16,0},{24,8},{1,17},{9,25},{17,1},{25,9},{2,18},{10... | collective-permute-start | bytes 786440 | tf_op jit(solution)/shard_map/ppermute | solution.py:605
  7.0 0.0 collective-permute-done.2.second_ref.refs_0_.refs_1_
  7.0 1.9 %collective-permute-start.3 = (f32[2,2,16,128]{3,2,1,0:T(8,128)S(1)}, f32[2,2,16,128]{3,2,1,0:T(8,128)S(1)}, u32[]{:S(2)}, u32[]{:S(2)}) collective-permute-start(f32[2,2,16,128]{3,2,1,0:T(8,128)S(1)} %reference_joined.2.first_ref), channel_id=1, source_target_pairs={{0,2},{1,3},{2,4},{3,5},{4,6},{5,7},{6,0},{7,1},{8,10},{9,11},{10,... | collective-permute-start | bytes 98312 | tf_op jit(solution)/shard_map/ppermute | solution.py:630
  8.9 0.6 %shifted_reference.1.refs_2_ = bf16[2,2,128,1920]{3,2,1,0:T(8,128)(2,1)S(1)} custom-call(f32[2,16,128]{2,1,0:T(8,128)S(1)} %get-tuple-element.17.tiles_ref), custom_call_target="tpu_custom_call" | custom-call | flops 805000000 | tf_op jit(solution)/shard_map/shifted_reference/pallas_call | solution.py:221
  9.5 3.3 %collective-permute-done.3.refs_1_.second_ref.refs_2_ = f32[2,2,16,128]{3,2,1,0:T(8,128)S(1)} collective-permute-done((f32[2,2,16,128]{3,2,1,0:T(8,128)S(1)}, f32[2,2,16,128]{3,2,1,0:T(8,128)S(1)}, u32[]{:S(2)}, u32[]{:S(2)}) %collective-permute-start.3) | collective-permute-done | bytes 32800 | tf_op jit(solution)/shard_map/ppermute | solution.py:630
  12.8 1.0 %collective-permute-start.4 = (f32[4,2,16,128]{3,2,1,0:T(8,128)S(1)}, f32[4,2,16,128]{3,2,1,0:T(8,128)S(1)}, u32[]{:S(2)}, u32[]{:S(2)}) collective-permute-start(f32[4,2,16,128]{3,2,1,0:T(8,128)S(1)} %reference_joined.3.refs_4_), channel_id=1, source_target_pairs={{0,4},{1,5},{2,6},{3,7},{4,0},{5,1},{6,2},{7,3},{8,12},{9,13},{10,... | collective-permute-start | bytes 196616 | tf_op jit(solution)/shard_map/ppermute | solution.py:630
  13.8 0.2 shifted_first.1.refs_3_
  14.0 0.0 collective-permute-done.1
  14.0 1.6 %lag_products.1.refs_4_ = f32[8,10,8,128]{3,2,1,0:T(8,128)} custom-call(f32[32,2048]{1,0:T(8,128)S(1)} %bitcast.9, f32[32,2048]{1,0:T(8,128)S(1)} %bitcast.10, bf16[2,2,128,1920]{3,2,1,0:T(8,128)(2,1)S(1)} %shifted_reference.1.refs_2_, bf16[2,2,128,256]{3,2,1,0:T(8,128)(2,1)S(1)} %shifted_first.1.refs_3_, f32[4,2,16,128]{3,2,1,0:T(8,128)S(1)} %reference_joined.3.refs_4_), custom_call_target="tpu_custom_call" | custom-call | flops 2415000064 | tf_op jit(solution)/shard_map/lag_products/pallas_call | solution.py:334
  15.6 5.7 %all-to-all-start = ((f32[8,10,8,128]{3,2,1,0:T(8,128)}), f32[8,10,8,128]{3,2,1,0:T(8,128)S(1)}, u32[]{:S(2)}, u32[]{:S(2)}) async-start(f32[8,10,8,128]{3,2,1,0:T(8,128)} %lag_products.1.refs_4_), calls=%async_computation | async-start | bytes 655360 | tf_op jit(solution)/shard_map/all_to_all | solution.py:637
  21.4 0.0 collective-permute-done.4.refs_3_
  21.4 6.3 %reference_products.1 = (bf16[2,2048,128]{2,1,0:T(8,128)(2,1)S(1)}, f32[8,128]{1,0:T(8,128)S(1)}, f32[128,128]{1,0:T(8,128)S(1)}) custom-call(f32[1,2,16,128]{3,2,1,0:T(8,128)S(1)} %bitcast.13, f32[1,2,16,128]{3,2,1,0:T(8,128)S(1)} %collective-permute-done.2.second_ref.refs_0_.refs_1_, ...), custom_call_target="tpu_custom_call" | custom-call | flops 7129999872 | tf_op jit(solution)/shard_map/reference_products/pallas_call | solution.py:447
  27.6 0.0 copy-start
  27.6 2.5 %gram_inverse.1.solver_ref = f32[128,128]{1,0:T(8,128)S(1)} custom-call(f32[8,128]{1,0:T(8,128)S(1)} %get-tuple-element.19.line_ref, f32[128,128]{1,0:T(8,128)S(1)} %get-tuple-element.20.tail_ref), custom_call_target="tpu_custom_call" | custom-call | flops 2300000000 | tf_op jit(solution)/shard_map/gram_inverse/pallas_call | solution.py:517
  30.1 1.0 %all-to-all-done.got_ref = f32[8,10,8,128]{3,2,1,0:T(8,128)S(1)} async-done(((f32[8,10,8,128]{3,2,1,0:T(8,128)}), f32[8,10,8,128]{3,2,1,0:T(8,128)S(1)}, u32[]{:S(2)}, u32[]{:S(2)}) %all-to-all-start) | async-done | bytes 327712 | tf_op jit(solution)/shard_map/all_to_all | solution.py:637
  31.1 0.0 copy-done
  31.1 2.2 %range_doppler.1 = f32[4,4,2,32,256]{4,3,2,1,0:T(8,128)} custom-call(f32[8,10,8,128]{3,2,1,0:T(8,128)S(1)} %all-to-all-done.got_ref, bf16[2,2048,128]{2,1,0:T(8,128)(2,1)S(1)} %get-tuple-element.18.own_ref, f32[128,128]{1,0:T(8,128)S(1)} %gram_inverse.1.solver_ref, bf16[2,128,512]{2,1,0:T(8,128)(2,1)S(1)} %copy-done), custom_call_target="tpu_custom_call" | custom-call | flops 2875000064 | tf_op jit(solution)/shard_map/range_doppler/pallas_call | solution.py:586
  (2 shorter events, 0.0 us)
Async XLA Ops:
  2.0 3.1 %collective-permute-start = (f32[64,2048]{1,0:T(8,128)S(1)}, f32[64,2048]{1,0:T(8,128)S(1)}, u32[]{:S(2)}, u32[]{:S(2)}) collective-permute-start(f32[64,2048]{1,0:T(8,128)S(1)} %get-tuple-element.14), channel_id=1, source_target_pairs={{0,8},{8,0},{16,24},{24,16},{1,9},{9,1},{17,25},{25,17},{2,10},{10... | collective-permute-start | bytes 1572872 | tf_op jit(solution)/shard_map/ppermute | solution.py:605
  2.5 4.5 %collective-permute-start.2 = (f32[1,2,16,128]{3,2,1,0:T(8,128)S(1)}, f32[1,2,16,128]{3,2,1,0:T(8,128)S(1)}, u32[]{:S(2)}, u32[]{:S(2)}) collective-permute-start(f32[1,2,16,128]{3,2,1,0:T(8,128)S(1)} %bitcast.11), channel_id=1, source_target_pairs={{0,1},{1,0},{2,3},{3,2},{4,5},{5,4},{6,7},{7,6},{8,9},{9,8},{10,11... | collective-permute-start | bytes 49160 | tf_op jit(solution)/shard_map/ppermute | solution.py:605
  5.2 8.9 %collective-permute-start.1 = (f32[1,32,2048]{2,1,0:T(8,128)S(1)}, f32[1,32,2048]{2,1,0:T(8,128)S(1)}, u32[]{:S(2)}, u32[]{:S(2)}) collective-permute-start(f32[1,32,2048]{2,1,0:T(8,128)S(1)} %get-tuple-element.16.refs_0_), channel_id=1, source_target_pairs={{0,16},{8,24},{16,0},{24,8},{1,17},{9,25},{17,1},{25,9},{2,18},{10... | collective-permute-start | bytes 786440 | tf_op jit(solution)/shard_map/ppermute | solution.py:605
  7.0 5.8 %collective-permute-start.3 = (f32[2,2,16,128]{3,2,1,0:T(8,128)S(1)}, f32[2,2,16,128]{3,2,1,0:T(8,128)S(1)}, u32[]{:S(2)}, u32[]{:S(2)}) collective-permute-start(f32[2,2,16,128]{3,2,1,0:T(8,128)S(1)} %reference_joined.2.first_ref), channel_id=1, source_target_pairs={{0,2},{1,3},{2,4},{3,5},{4,6},{5,7},{6,0},{7,1},{8,10},{9,11},{10,... | collective-permute-start | bytes 98312 | tf_op jit(solution)/shard_map/ppermute | solution.py:630
  12.8 8.5 %collective-permute-start.4 = (f32[4,2,16,128]{3,2,1,0:T(8,128)S(1)}, f32[4,2,16,128]{3,2,1,0:T(8,128)S(1)}, u32[]{:S(2)}, u32[]{:S(2)}) collective-permute-start(f32[4,2,16,128]{3,2,1,0:T(8,128)S(1)} %reference_joined.3.refs_4_), channel_id=1, source_target_pairs={{0,4},{1,5},{2,6},{3,7},{4,0},{5,1},{6,2},{7,3},{8,12},{9,13},{10,... | collective-permute-start | bytes 196616 | tf_op jit(solution)/shard_map/ppermute | solution.py:630
  15.6 15.4 %all-to-all-start = ((f32[8,10,8,128]{3,2,1,0:T(8,128)}), f32[8,10,8,128]{3,2,1,0:T(8,128)S(1)}, u32[]{:S(2)}, u32[]{:S(2)}) async-start(f32[8,10,8,128]{3,2,1,0:T(8,128)} %lag_products.1.refs_4_), calls=%async_computation | async-start | bytes 655360 | tf_op jit(solution)/shard_map/all_to_all | solution.py:637
  27.6 3.5 %copy-start = (bf16[2,128,512]{2,1,0:T(8,128)(2,1)S(1)}, bf16[2,128,512]{2,1,0:T(8,128)(2,1)}, u32[]{:S(2)}) copy-start(bf16[2,128,512]{2,1,0:T(8,128)(2,1)} %constant.2.clone.wave_ref) | copy-start | bytes 786436

commit v22 on v21

--- a/solution.py
+++ b/solution.py
@@ -73,7 +73,7 @@
     return outs
 
 
-COPIES = 8
+COPIES = 1
 
 
 def beam_kernel(
@@ -254,8 +254,6 @@
 def lag_kernel(groups, part_count, *refs):
     y_refs, refs = refs[:part_count], refs[part_count:]
     table_ref, first_ref, _, out_hbm, out_ref, out_sem = refs
-    copies = []
-
     def table_tile(h, n):
         parts = []
         for c in range(2):
@@ -263,11 +261,6 @@
             ref, at = (first_ref, n) if n < known else (table_ref, n - known)
             parts.append(ref[h, c, :, at * LANES : (at + 1) * LANES])
         return jnp.concatenate(parts, 1)
-
-    def send(start, count):
-        part = (slice(None), pl.ds(start, count))
-        copies.append(pltpu.make_async_copy(out_ref.at[part], out_hbm.at[part], out_sem.at[len(copies)]))
-        copies[-1].start()
 
     y = y_refs[0][...]
     for y_ref in y_refs[1:]:
@@ -312,8 +305,6 @@
             tiles = [product[r : r + SUBLANES, lanes] for r in range(0, rows, SUBLANES)]
             for j, tile in enumerate(swap_groups(tiles, groups)):
                 out_ref[h * groups + j, q] = tile
-        if q + 1 == blocks - 2:
-            send(0, q + 1)
     left = lax.broadcasted_iota(jnp.int32, (SUBLANES, LANES), 1) < TAPS
     for i in range(groups // 2):
         a = taps_sum[i * SUBLANES : (i + 1) * SUBLANES]
@@ -322,9 +313,9 @@
         tile = jnp.where(left, a, pltpu.roll(b, LANES - TAPS, 1))
         for owner in range(out_ref.shape[0]):
             out_ref[owner, blocks + i] = tile
-    send(blocks - 2, 2 + groups // 2)
-    for copy in copies:
-        copy.wait()
+    copy = pltpu.make_async_copy(out_ref, out_hbm, out_sem)
+    copy.start()
+    copy.wait()
 
 
 def lag_call(ys, table, first, after, groups, owners):
@@ -338,7 +329,7 @@
         out_shape=jax.ShapeDtypeStruct(shape, jnp.float32),
         scratch_shapes=[
             pltpu.VMEM(shape, jnp.float32),
-            pltpu.SemaphoreType.DMA((2,)),
+            pltpu.SemaphoreType.DMA,
         ],
         compiler_params=params(),
         cost_estimate=cost(2.1),

time: 33.5 us -> 33.5 us (level)
  no operation moved by 1% of the time
where the time goes in v22:
time: 33.5 us; the launch traced here: 33.2 us
  Pallas kernels  15.3 us (46%)
  starting transfers between devices  13.6 us (41%)
  waiting for transfers between devices  4.34 us (13%)
    pallas_call x1, Pallas kernels, own_call(): pl.pallas_call(functools.partial(own_kernel, lags_local), in_specs=[pl.Bl...  6.25 us
    all_to_all x1, starting transfers between devices, tiled_device(): got = lax.all_to_all(pieces, 'tm', 0, 0, tiled=True)  5.7 us
    ppermute x3, starting transfers between devices, swap(): return lax.ppermute(x, axis, pairs)  4.97 us
    ppermute x2, waiting for transfers between devices, tiled_device(): lax.ppermute(joined, 'tm', [(i, (i + count) % tm_count) for i in range(tm...  3.3 us
    ppermute x2, starting transfers between devices, tiled_device(): lax.ppermute(joined, 'tm', [(i, (i + count) % tm_count) for i in range(tm...  2.88 us
    pallas_call x1, Pallas kernels, solver_call(): pl.pallas_call(solver_kernel, out_shape=jax.ShapeDtypeStruct(tail.shape,...  2.45 us
    pallas_call x1, Pallas kernels, map_call(): pl.pallas_call(functools.partial(map_kernel, groups), in_specs=[pl.BlockS...  2.17 us
    pallas_call x1, Pallas kernels, beam_call(): pl.pallas_call(functools.partial(beam_kernel, chan_count, beams_local), i...  1.86 us
  transfers between devices with their start and end apart: 6, of which 2 were waited for; matrix products, arithmetic and copies ran while one was open for 0% of the time, Pallas kernels for 34%

profile of v22, /device:TPU:0, one launch (start us, length us, event | category | flops | bytes accessed | tf_op | source)
XLA Modules:
  0.0 33.2 jit_solution(16720663511449812211)
XLA Ops:
  0.0 1.9 %beams.1 = (f32[64,2048]{1,0:T(8,128)S(1)}, f32[64,2048]{1,0:T(8,128)S(1)}, f32[2,16,128]{2,1,0:T(8,128)S(1)}) custom-call(f32[2,64,64]{2,1,0:T(8,128)} %w_hbm.1, f32[128,2048]{1,0:T(8,128)} %bitcast.14, f32[2,2048]{1,0:T(2,128)} %ref_hbm.1), custom_call_target="tpu_custom_call" | custom-call | flops 2529999872 | tf_op jit(solution)/shard_map/beams/pallas_call | solution.py:135
  1.9 0.5 %collective-permute-start = (f32[64,2048]{1,0:T(8,128)S(1)}, f32[64,2048]{1,0:T(8,128)S(1)}, u32[]{:S(2)}, u32[]{:S(2)}) collective-permute-start(f32[64,2048]{1,0:T(8,128)S(1)} %get-tuple-element.14), channel_id=1, source_target_pairs={{0,8},{8,0},{16,24},{24,16},{1,9},{9,1},{17,25},{25,17},{2,10},{10... | collective-permute-start | bytes 1572872 | tf_op jit(solution)/shard_map/ppermute | solution.py:596
  2.4 2.6 %collective-permute-start.2 = (f32[1,2,16,128]{3,2,1,0:T(8,128)S(1)}, f32[1,2,16,128]{3,2,1,0:T(8,128)S(1)}, u32[]{:S(2)}, u32[]{:S(2)}) collective-permute-start(f32[1,2,16,128]{3,2,1,0:T(8,128)S(1)} %bitcast.11), channel_id=1, source_target_pairs={{0,1},{1,0},{2,3},{3,2},{4,5},{5,4},{6,7},{7,6},{8,9},{9,8},{10,11... | collective-permute-start | bytes 49160 | tf_op jit(solution)/shard_map/ppermute | solution.py:596
  5.0 0.0 collective-permute-done
  5.0 0.1 halves_summed.1
  5.0 1.9 %collective-permute-start.1 = (f32[1,32,2048]{2,1,0:T(8,128)S(1)}, f32[1,32,2048]{2,1,0:T(8,128)S(1)}, u32[]{:S(2)}, u32[]{:S(2)}) collective-permute-start(f32[1,32,2048]{2,1,0:T(8,128)S(1)} %get-tuple-element.16.refs_0_), channel_id=1, source_target_pairs={{0,16},{8,24},{16,0},{24,8},{1,17},{9,25},{17,1},{25,9},{2,18},{10... | collective-permute-start | bytes 786440 | tf_op jit(solution)/shard_map/ppermute | solution.py:596
  6.9 0.0 collective-permute-done.2.second_ref.refs_0_.refs_1_
  6.9 1.9 %collective-permute-start.3 = (f32[2,2,16,128]{3,2,1,0:T(8,128)S(1)}, f32[2,2,16,128]{3,2,1,0:T(8,128)S(1)}, u32[]{:S(2)}, u32[]{:S(2)}) collective-permute-start(f32[2,2,16,128]{3,2,1,0:T(8,128)S(1)} %reference_joined.2.first_ref), channel_id=1, source_target_pairs={{0,2},{1,3},{2,4},{3,5},{4,6},{5,7},{6,0},{7,1},{8,10},{9,11},{10,... | collective-permute-start | bytes 98312 | tf_op jit(solution)/shard_map/ppermute | solution.py:621
  8.8 0.6 %shifted_reference.1.refs_2_ = bf16[2,2,128,1920]{3,2,1,0:T(8,128)(2,1)S(1)} custom-call(f32[2,16,128]{2,1,0:T(8,128)S(1)} %get-tuple-element.17.tiles_ref), custom_call_target="tpu_custom_call" | custom-call | flops 805000000 | tf_op jit(solution)/shard_map/shifted_reference/pallas_call | solution.py:221
  9.4 3.3 %collective-permute-done.3.refs_1_.second_ref.refs_2_ = f32[2,2,16,128]{3,2,1,0:T(8,128)S(1)} collective-permute-done((f32[2,2,16,128]{3,2,1,0:T(8,128)S(1)}, f32[2,2,16,128]{3,2,1,0:T(8,128)S(1)}, u32[]{:S(2)}, u32[]{:S(2)}) %collective-permute-start.3) | collective-permute-done | bytes 32800 | tf_op jit(solution)/shard_map/ppermute | solution.py:621
  12.7 1.0 %collective-permute-start.4 = (f32[4,2,16,128]{3,2,1,0:T(8,128)S(1)}, f32[4,2,16,128]{3,2,1,0:T(8,128)S(1)}, u32[]{:S(2)}, u32[]{:S(2)}) collective-permute-start(f32[4,2,16,128]{3,2,1,0:T(8,128)S(1)} %reference_joined.3.refs_4_), channel_id=1, source_target_pairs={{0,4},{1,5},{2,6},{3,7},{4,0},{5,1},{6,2},{7,3},{8,12},{9,13},{10,... | collective-permute-start | bytes 196616 | tf_op jit(solution)/shard_map/ppermute | solution.py:621
  13.7 0.2 shifted_first.1.refs_3_
  13.9 0.0 collective-permute-done.1
  13.9 1.7 %lag_products.1.refs_4_ = f32[8,10,8,128]{3,2,1,0:T(8,128)} custom-call(f32[32,2048]{1,0:T(8,128)S(1)} %bitcast.9, f32[32,2048]{1,0:T(8,128)S(1)} %bitcast.10, bf16[2,2,128,1920]{3,2,1,0:T(8,128)(2,1)S(1)} %shifted_reference.1.refs_2_, bf16[2,2,128,256]{3,2,1,0:T(8,128)(2,1)S(1)} %shifted_first.1.refs_3_, f32[4,2,16,128]{3,2,1,0:T(8,128)S(1)} %reference_joined.3.refs_4_), custom_call_target="tpu_custom_call" | custom-call | flops 2415000064 | tf_op jit(solution)/shard_map/lag_products/pallas_call | solution.py:325
  15.6 5.7 %all-to-all-start = ((f32[8,10,8,128]{3,2,1,0:T(8,128)}), f32[8,10,8,128]{3,2,1,0:T(8,128)S(1)}, u32[]{:S(2)}, u32[]{:S(2)}) async-start(f32[8,10,8,128]{3,2,1,0:T(8,128)} %lag_products.1.refs_4_), calls=%async_computation | async-start | bytes 655360 | tf_op jit(solution)/shard_map/all_to_all | solution.py:628
  21.3 0.0 collective-permute-done.4.refs_3_
  21.3 6.2 %reference_products.1 = (bf16[2,2048,128]{2,1,0:T(8,128)(2,1)S(1)}, f32[8,128]{1,0:T(8,128)S(1)}, f32[128,128]{1,0:T(8,128)S(1)}) custom-call(f32[1,2,16,128]{3,2,1,0:T(8,128)S(1)} %bitcast.13, f32[1,2,16,128]{3,2,1,0:T(8,128)S(1)} %collective-permute-done.2.second_ref.refs_0_.refs_1_, ...), custom_call_target="tpu_custom_call" | custom-call | flops 7129999872 | tf_op jit(solution)/shard_map/reference_products/pallas_call | solution.py:438
  27.6 0.0 copy-start
  27.6 2.5 %gram_inverse.1.solver_ref = f32[128,128]{1,0:T(8,128)S(1)} custom-call(f32[8,128]{1,0:T(8,128)S(1)} %get-tuple-element.19.line_ref, f32[128,128]{1,0:T(8,128)S(1)} %get-tuple-element.20.tail_ref), custom_call_target="tpu_custom_call" | custom-call | flops 2300000000 | tf_op jit(solution)/shard_map/gram_inverse/pallas_call | solution.py:508
  30.0 1.0 %all-to-all-done.got_ref = f32[8,10,8,128]{3,2,1,0:T(8,128)S(1)} async-done(((f32[8,10,8,128]{3,2,1,0:T(8,128)}), f32[8,10,8,128]{3,2,1,0:T(8,128)S(1)}, u32[]{:S(2)}, u32[]{:S(2)}) %all-to-all-start) | async-done | bytes 327712 | tf_op jit(solution)/shard_map/all_to_all | solution.py:628
  31.1 0.0 copy-done
  31.1 2.2 %range_doppler.1 = f32[4,4,2,32,256]{4,3,2,1,0:T(8,128)} custom-call(f32[8,10,8,128]{3,2,1,0:T(8,128)S(1)} %all-to-all-done.got_ref, bf16[2,2048,128]{2,1,0:T(8,128)(2,1)S(1)} %get-tuple-element.18.own_ref, f32[128,128]{1,0:T(8,128)S(1)} %gram_inverse.1.solver_ref, bf16[2,128,512]{2,1,0:T(8,128)(2,1)S(1)} %copy-done), custom_call_target="tpu_custom_call" | custom-call | flops 2875000064 | tf_op jit(solution)/shard_map/range_doppler/pallas_call | solution.py:577
  (2 shorter events, 0.0 us)
Async XLA Ops:
  1.9 3.1 %collective-permute-start = (f32[64,2048]{1,0:T(8,128)S(1)}, f32[64,2048]{1,0:T(8,128)S(1)}, u32[]{:S(2)}, u32[]{:S(2)}) collective-permute-start(f32[64,2048]{1,0:T(8,128)S(1)} %get-tuple-element.14), channel_id=1, source_target_pairs={{0,8},{8,0},{16,24},{24,16},{1,9},{9,1},{17,25},{25,17},{2,10},{10... | collective-permute-start | bytes 1572872 | tf_op jit(solution)/shard_map/ppermute | solution.py:596
  2.4 4.5 %collective-permute-start.2 = (f32[1,2,16,128]{3,2,1,0:T(8,128)S(1)}, f32[1,2,16,128]{3,2,1,0:T(8,128)S(1)}, u32[]{:S(2)}, u32[]{:S(2)}) collective-permute-start(f32[1,2,16,128]{3,2,1,0:T(8,128)S(1)} %bitcast.11), channel_id=1, source_target_pairs={{0,1},{1,0},{2,3},{3,2},{4,5},{5,4},{6,7},{7,6},{8,9},{9,8},{10,11... | collective-permute-start | bytes 49160 | tf_op jit(solution)/shard_map/ppermute | solution.py:596
  5.0 8.9 %collective-permute-start.1 = (f32[1,32,2048]{2,1,0:T(8,128)S(1)}, f32[1,32,2048]{2,1,0:T(8,128)S(1)}, u32[]{:S(2)}, u32[]{:S(2)}) collective-permute-start(f32[1,32,2048]{2,1,0:T(8,128)S(1)} %get-tuple-element.16.refs_0_), channel_id=1, source_target_pairs={{0,16},{8,24},{16,0},{24,8},{1,17},{9,25},{17,1},{25,9},{2,18},{10... | collective-permute-start | bytes 786440 | tf_op jit(solution)/shard_map/ppermute | solution.py:596
  6.9 5.8 %collective-permute-start.3 = (f32[2,2,16,128]{3,2,1,0:T(8,128)S(1)}, f32[2,2,16,128]{3,2,1,0:T(8,128)S(1)}, u32[]{:S(2)}, u32[]{:S(2)}) collective-permute-start(f32[2,2,16,128]{3,2,1,0:T(8,128)S(1)} %reference_joined.2.first_ref), channel_id=1, source_target_pairs={{0,2},{1,3},{2,4},{3,5},{4,6},{5,7},{6,0},{7,1},{8,10},{9,11},{10,... | collective-permute-start | bytes 98312 | tf_op jit(solution)/shard_map/ppermute | solution.py:621
  12.7 8.6 %collective-permute-start.4 = (f32[4,2,16,128]{3,2,1,0:T(8,128)S(1)}, f32[4,2,16,128]{3,2,1,0:T(8,128)S(1)}, u32[]{:S(2)}, u32[]{:S(2)}) collective-permute-start(f32[4,2,16,128]{3,2,1,0:T(8,128)S(1)} %reference_joined.3.refs_4_), channel_id=1, source_target_pairs={{0,4},{1,5},{2,6},{3,7},{4,0},{5,1},{6,2},{7,3},{8,12},{9,13},{10,... | collective-permute-start | bytes 196616 | tf_op jit(solution)/shard_map/ppermute | solution.py:621
  15.6 15.4 %all-to-all-start = ((f32[8,10,8,128]{3,2,1,0:T(8,128)}), f32[8,10,8,128]{3,2,1,0:T(8,128)S(1)}, u32[]{:S(2)}, u32[]{:S(2)}) async-start(f32[8,10,8,128]{3,2,1,0:T(8,128)} %lag_products.1.refs_4_), calls=%async_computation | async-start | bytes 655360 | tf_op jit(solution)/shard_map/all_to_all | solution.py:628
  27.6 3.5 %copy-start = (bf16[2,128,512]{2,1,0:T(8,128)(2,1)S(1)}, bf16[2,128,512]{2,1,0:T(8,128)(2,1)}, u32[]{:S(2)}) copy-start(bf16[2,128,512]{2,1,0:T(8,128)(2,1)} %constant.2.clone.wave_ref) | copy-start | bytes 786436

commit v23 on v20

--- a/solution.py
+++ b/solution.py
@@ -32,6 +32,29 @@
 def halves(x):
     high = x.astype(jnp.bfloat16)
     return high, (x - high.astype(jnp.float32)).astype(jnp.bfloat16)
+
+
+def thirds(x):
+    high = x.astype(jnp.bfloat16)
+    rest = x - high.astype(jnp.float32)
+    return (high,) + halves(rest)
+
+
+def dot_parts(a, b, across=False):
+    rows = a[0].shape[0]
+    by_size = {}
+    for j, right in enumerate(b):
+        left = a[: max(3 - j, 1)]
+        left = left[0] if len(left) == 1 else jnp.concatenate(left, 0)
+        contract = (((1,), (1 if across else 0,)), ((), ()))
+        product = lax.dot_general(left, right, contract, preferred_element_type=jnp.float32)
+        for i in range(product.shape[0] // rows):
+            by_size.setdefault(i + j, []).append(product[i * rows : (i + 1) * rows])
+    total = None
+    for size in sorted(by_size, reverse=True):
+        for term in by_size[size]:
+            total = term if total is None else total + term
+    return total
 
 
 def dot_nt(a, b, precision=None):
@@ -109,19 +132,15 @@
                 second = [jnp.where(top, wr_s, wi), jnp.where(top, -wi_s, wr)]
                 rows.append(jnp.concatenate(first, 1))
                 rows.append(jnp.concatenate(second, 1))
-    weights = jnp.concatenate(halves(jnp.concatenate(rows, 0)), 0)
-    count = weights.shape[0] // 2
+    weights = halves(jnp.concatenate(rows, 0))
     ref_copy.wait()
     for c in range(2):
         for n in range(tiles_ref.shape[1]):
             tiles_ref[c, n : n + 1, :] = ref_ref[c : c + 1, n * LANES : (n + 1) * LANES]
-    mid = count // 2
     for copy in s_copies:
         copy.wait()
-    high, low = halves(s_ref[...])
-    by_high = jnp.dot(weights, high, preferred_element_type=jnp.float32)
-    by_low = jnp.dot(weights[:count], low, preferred_element_type=jnp.float32)
-    product = by_high[:count] + (by_high[count:] + by_low)
+    product = dot_parts(weights, thirds(s_ref[...]))
+    mid = product.shape[0] // 2
     kept_ref[...] = product[:mid]
     sent_ref[...] = product[mid:]
 
@@ -278,22 +297,16 @@
         [pltpu.roll(y[r : r + SUBLANES], SUBLANES // 2, 0) for r in range(0, rows, SUBLANES)], 0
     )
     turned = turned * row_sign(turned.shape)
-    y_high, y_low = halves(y)
-    t_high, t_low = halves(turned)
+    y_parts, t_parts = thirds(y), thirds(turned)
 
     def half_block(q, b):
         cols = slice(q * BLOCK_LEN + b * LANES, q * BLOCK_LEN + (b + 1) * LANES)
-        return [jnp.concatenate([x[:, cols], t[:, cols]], 1) for x, t in ((y_high, t_high), (y_low, t_low))]
+        return [jnp.concatenate([x[:, cols], t[:, cols]], 1) for x, t in zip(y_parts, t_parts)]
 
     def products(stack, n, count):
-        high, low = (jnp.concatenate([table_tile(h, n + i) for i in range(count)], 0) for h in range(2))
-        by_high = dot_nt(jnp.concatenate([part for pair in stack for part in pair], 0), high)
-        by_low = dot_nt(jnp.concatenate([pair[0] for pair in stack], 0), low)
-        return [
-            by_high[2 * i * rows : (2 * i + 1) * rows]
-            + (by_high[(2 * i + 1) * rows : 2 * (i + 1) * rows] + by_low[i * rows : (i + 1) * rows])
-            for i in range(len(stack))
-        ]
+        tiles = [jnp.concatenate([table_tile(h, n + i) for i in range(count)], 0) for h in range(2)]
+        product = dot_parts([jnp.concatenate(part, 0) for part in zip(*stack)], tiles, True)
+        return [product[i * rows : (i + 1) * rows] for i in range(len(stack))]
 
     taps_sum = None
     (far,) = products([half_block(0, 0)], 0, 1)
@@ -381,11 +394,10 @@
         tiled = jnp.broadcast_to(line, (2 * SUBLANES, line.shape[1]))
         return pltpu.roll(tiled, by, 1, stride=1, stride_axis=0)[:, LANES:]
 
-    def keep(ref, row, value):
-        high, low = halves(value)
-        half = ref.shape[0] // 2
-        ref[row : row + 2 * SUBLANES, :] = high
-        ref[half + row : half + row + 2 * SUBLANES, :] = low
+    def keep(ref, row, parts):
+        step = ref.shape[0] // len(parts)
+        for n, part in enumerate(parts):
+            ref[n * step + row : n * step + row + 2 * SUBLANES, :] = part
 
     def build(n, taps_ref, lags_ref):
         first = EDGE - 1 + n * BATCH * block_rows
@@ -393,12 +405,12 @@
         lines = [line_of(span_ref, c, first, count) for c in range(2)]
         for c in range(2):
             for g in range(0, TAPS, 2 * SUBLANES):
-                keep(taps_ref, c * TAPS + g, shifted(lines[c], g))
+                keep(taps_ref, c * TAPS + g, thirds(shifted(lines[c], g)))
             late = line_of(late_ref, c, first, count)
             for g in range(0, lags_local, 2 * SUBLANES):
-                keep(lags_ref, c * lags_local + g, shifted(late, g))
+                keep(lags_ref, c * lags_local + g, halves(shifted(late, g)))
         pad = jnp.zeros((2 * SUBLANES - 2, BATCH * BLOCK_LEN), jnp.float32)
-        keep(lags_ref, 2 * lags_local, jnp.concatenate([line[:, LANES:] for line in lines] + [pad], 0))
+        keep(lags_ref, 2 * lags_local, halves(jnp.concatenate([line[:, LANES:] for line in lines] + [pad], 0)))
 
     turn = lane_sign((lags_local, LANES))
 
@@ -406,14 +418,14 @@
         count = lags_ref.shape[0] // 2
         for b in range(BATCH):
             cols = slice(b * BLOCK_LEN, (b + 1) * BLOCK_LEN)
-            product = dot_nt(lags_ref[:, cols], taps_ref[:, cols])
-            product = product[:count, :LANES] + (product[:count, LANES:] + product[count:, :LANES])
+            product = dot_nt(lags_ref[:, cols], taps_ref[: 2 * LANES, cols])
+            least = dot_nt(lags_ref[:count, cols], taps_ref[2 * LANES :, cols]) + product[count:, LANES:]
+            product = product[:count, :LANES] + ((product[:count, LANES:] + product[count:, :LANES]) + least)
             by_real = product[:lags_local]
             by_imag = product[lags_local : 2 * lags_local]
             rows = pl.ds(pl.multiple_of((n * BATCH + b) * lags_local, lags_local), lags_local)
-            high, low = halves(by_real + turn * pltpu.roll(by_imag, TAPS, 1))
-            out_ref[0, rows, :] = high
-            out_ref[1, rows, :] = low
+            for part, value in enumerate(thirds(by_real + turn * pltpu.roll(by_imag, TAPS, 1))):
+                out_ref[part, rows, :] = value
             line_ref[...] += product[2 * lags_local : 2 * lags_local + SUBLANES]
 
     line_ref[...] = jnp.zeros_like(line_ref)
@@ -441,14 +453,14 @@
     rows = span_rows * LANES // BLOCK_LEN * lags_local
     held_rows = -(-(span_rows + 2 * EDGE) // SUBLANES) * SUBLANES
     width = BATCH * BLOCK_LEN
-    taps = pltpu.VMEM((4 * TAPS, width), jnp.bfloat16)
+    taps = pltpu.VMEM((6 * TAPS, width), jnp.bfloat16)
     lags = pltpu.VMEM((4 * lags_local + 4 * SUBLANES, width), jnp.bfloat16)
     span = pltpu.VMEM((2, held_rows, LANES), jnp.float32)
     return pl.pallas_call(
         functools.partial(own_kernel, lags_local),
         in_specs=[pl.BlockSpec(memory_space=pltpu.VMEM)] * len(parts) + [pl.BlockSpec(memory_space=pl.ANY)],
         out_shape=[
-            jax.ShapeDtypeStruct((2, rows, 2 * TAPS), jnp.bfloat16),
+            jax.ShapeDtypeStruct((3, rows, 2 * TAPS), jnp.bfloat16),
             jax.ShapeDtypeStruct((SUBLANES, 2 * TAPS), jnp.float32),
             jax.ShapeDtypeStruct((2 * TAPS, 2 * TAPS), jnp.float32),
         ],
@@ -463,7 +475,7 @@
     return jnp.concatenate([a, -lane_sign(a.shape) * pltpu.roll(a, a.shape[0], 1)], 0)
 
 
-def solver_kernel(line_ref, tail_ref, solver_ref):
+def solver_kernel(line_ref, tail_ref, gram_ref, solver_ref):
     total = line_ref[...]
     line = total[0:1] + lane_sign((1, LANES)) * pltpu.roll(total[1:2], TAPS, 1)
     low = lax.broadcasted_iota(jnp.int32, (1, LANES), 1) < TAPS
@@ -486,6 +498,7 @@
     gram_i = up_i - up_i.T - (tails[:TAPS, TAPS:] - tails[TAPS:, :TAPS])
     gram = jnp.concatenate([gram_r, gram_i], 1)
     gram_factor = as_factor(gram)
+    gram_ref[...] = gram_factor
     gram_halves = halves(gram_factor)
     one = (
         lax.broadcasted_iota(jnp.int32, gram.shape, 0) == lax.broadcasted_iota(jnp.int32, gram.shape, 1)
@@ -516,7 +529,7 @@
 def solver_call(line, tail):
     return pl.pallas_call(
         solver_kernel,
-        out_shape=jax.ShapeDtypeStruct(tail.shape, jnp.float32),
+        out_shape=[jax.ShapeDtypeStruct(tail.shape, jnp.float32)] * 2,
         compiler_params=params(),
         cost_estimate=cost(2.0),
         name="gram_inverse",
@@ -531,7 +544,7 @@
     return (np.concatenate([upper, lower], 0) * scale).astype(np.float32)
 
 
-def map_kernel(groups, got_ref, own_ref, solver_ref, wave_ref, out_hbm, held_ref, out_ref, out_sem):
+def map_kernel(groups, got_ref, own_ref, gram_ref, solver_ref, wave_ref, out_hbm, held_ref, out_ref, out_sem):
     owners, pieces = got_ref.shape[:2]
     blocks = pieces - groups // 2
     lags_local = LANES // groups
@@ -548,14 +561,16 @@
             other = -sign * pltpu.roll(there, SUBLANES // 2, 0)
             rows[part] = jnp.where(left, here, other)
     cross = jnp.concatenate(rows, 0)
-    taps = jnp.dot(cross, solver_ref[...], precision=HIGHEST, preferred_element_type=jnp.float32)
-    taps_high, taps_low = halves(taps)
-    taps_both = jnp.concatenate([taps_high, taps_low], 0)
-    count = taps.shape[0]
+
+    def exact(x, ref):
+        return jnp.dot(x, ref[...], precision=HIGHEST, preferred_element_type=jnp.float32)
+
+    taps = exact(cross, solver_ref)
+    taps = taps + exact(cross - exact(taps, gram_ref), solver_ref)
+    taps = thirds(taps)
     for q in range(0, total, 2 * groups):
         own = slice(q * lags_local, (q + 2 * groups) * lags_local)
-        by_high = dot_nt(taps_both, own_ref[0, own, :])
-        clutter = by_high[:count] + (by_high[count:] + dot_nt(taps_high, own_ref[1, own, :]))
+        clutter = dot_parts(taps, [own_ref[part, own, :] for part in range(3)], True)
         for h in range(2):
             lanes = slice(h * LANES, (h + 1) * LANES)
             tiles = [clutter[r : r + SUBLANES, lanes] for r in range(0, groups * SUBLANES, SUBLANES)]
@@ -578,14 +593,14 @@
         copy.wait()
 
 
-def map_call(got, own, solver, wave, groups, beams_local):
+def map_call(got, own, gram, solver, wave, groups, beams_local):
     total = got.shape[0] * (got.shape[1] - groups // 2)
     lags_local = LANES // groups
     half = SUBLANES // 2
     shape = (beams_local // half, half, 2, lags_local, DOPPLER)
     out = pl.pallas_call(
         functools.partial(map_kernel, groups),
-        in_specs=[pl.BlockSpec(memory_space=pltpu.VMEM)] * 4,
+        in_specs=[pl.BlockSpec(memory_space=pltpu.VMEM)] * 5,
         out_specs=pl.BlockSpec(memory_space=pltpu.HBM),
         out_shape=jax.ShapeDtypeStruct(shape, jnp.float32),
         scratch_shapes=[
@@ -596,7 +611,7 @@
         compiler_params=params(),
         cost_estimate=cost(2.5),
         name="range_doppler",
-    )(got, own, solver, wave)
+    )(got, own, gram, solver, wave)
     return out.reshape((beams_local,) + shape[2:])
 
 
@@ -636,11 +651,11 @@
     pieces = lag_call([kept[0], got[0]], table, first, joined, groups, tm_count)
     got = lax.all_to_all(pieces, "tm", 0, 0, tiled=True)
     own, line, tail = own_call([tiles[None]] + rounds, lags_local, pieces)
-    solver = solver_call(line, tail)
+    gram, solver = solver_call(line, tail)
     wave = doppler_table(samples // BLOCK_LEN, 0.125 / math.sqrt(samples))
     high = wave.astype(jnp.bfloat16)
     wave = np.stack([high, (wave - high.astype(np.float32)).astype(jnp.bfloat16)])
-    return map_call(got, own, solver, jnp.asarray(wave), groups, beams_local)
+    return map_call(got, own, gram, solver, jnp.asarray(wave), groups, beams_local)
 
 
 def lag_table(ref_ext, offset, lags):

time: 33.4 us -> 34.1 us (1.021)
  Pallas kernels: 15.2 us -> 16.2 us
    pallas_call x1, Pallas kernels: 2.17 us -> 2.69 us  [map_call(): pl.pallas_call(functools.partial(map_kernel, groups), in_specs=[pl.BlockS...]
where the time goes in v23:
time: 34.1 us; the launch traced here: 33.9 us
  Pallas kernels  16.2 us (48%)
  starting transfers between devices  13.6 us (40%)
  waiting for transfers between devices  4.09 us (12%)
    pallas_call x1, Pallas kernels, own_call(): pl.pallas_call(functools.partial(own_kernel, lags_local), in_specs=[pl.Bl...  6.49 us
    all_to_all x1, starting transfers between devices, tiled_device(): got = lax.all_to_all(pieces, 'tm', 0, 0, tiled=True)  5.7 us
    ppermute x3, starting transfers between devices, swap(): return lax.ppermute(x, axis, pairs)  4.97 us
    ppermute x2, waiting for transfers between devices, tiled_device(): lax.ppermute(joined, 'tm', [(i, (i + count) % tm_count) for i in range(tm...  3.3 us
    ppermute x2, starting transfers between devices, tiled_device(): lax.ppermute(joined, 'tm', [(i, (i + count) % tm_count) for i in range(tm...  2.88 us
    pallas_call x1, Pallas kernels, map_call(): pl.pallas_call(functools.partial(map_kernel, groups), in_specs=[pl.BlockS...  2.69 us
    pallas_call x1, Pallas kernels, solver_call(): pl.pallas_call(solver_kernel, out_shape=[jax.ShapeDtypeStruct(tail.shape,...  2.46 us
    pallas_call x1, Pallas kernels, beam_call(): pl.pallas_call(functools.partial(beam_kernel, chan_count, beams_local), i...  2.1 us
  transfers between devices with their start and end apart: 6, of which 2 were waited for; matrix products, arithmetic and copies ran while one was open for 0% of the time, Pallas kernels for 34%

profile of v23, /device:TPU:0, one launch (start us, length us, event | category | flops | bytes accessed | tf_op | source)
XLA Modules:
  0.0 33.9 jit_solution(4688438372637653778)
XLA Ops:
  0.0 2.1 %beams.1 = (f32[64,2048]{1,0:T(8,128)S(1)}, f32[64,2048]{1,0:T(8,128)S(1)}, f32[2,16,128]{2,1,0:T(8,128)S(1)}) custom-call(f32[2,64,64]{2,1,0:T(8,128)} %w_hbm.1, f32[128,2048]{1,0:T(8,128)} %bitcast.14, f32[2,2048]{1,0:T(2,128)} %ref_hbm.1), custom_call_target="tpu_custom_call" | custom-call | flops 2529999872 | tf_op jit(solution)/shard_map/beams/pallas_call | solution.py:154
  2.1 0.5 %collective-permute-start = (f32[64,2048]{1,0:T(8,128)S(1)}, f32[64,2048]{1,0:T(8,128)S(1)}, u32[]{:S(2)}, u32[]{:S(2)}) collective-permute-start(f32[64,2048]{1,0:T(8,128)S(1)} %get-tuple-element.16), channel_id=1, source_target_pairs={{0,8},{8,0},{16,24},{24,16},{1,9},{9,1},{17,25},{25,17},{2,10},{10... | collective-permute-start | bytes 1572872 | tf_op jit(solution)/shard_map/ppermute | solution.py:620
  2.6 2.6 %collective-permute-start.2 = (f32[1,2,16,128]{3,2,1,0:T(8,128)S(1)}, f32[1,2,16,128]{3,2,1,0:T(8,128)S(1)}, u32[]{:S(2)}, u32[]{:S(2)}) collective-permute-start(f32[1,2,16,128]{3,2,1,0:T(8,128)S(1)} %bitcast.11), channel_id=1, source_target_pairs={{0,1},{1,0},{2,3},{3,2},{4,5},{5,4},{6,7},{7,6},{8,9},{9,8},{10,11... | collective-permute-start | bytes 49160 | tf_op jit(solution)/shard_map/ppermute | solution.py:620
  5.2 0.0 collective-permute-done
  5.2 0.1 halves_summed.1
  5.3 1.9 %collective-permute-start.1 = (f32[1,32,2048]{2,1,0:T(8,128)S(1)}, f32[1,32,2048]{2,1,0:T(8,128)S(1)}, u32[]{:S(2)}, u32[]{:S(2)}) collective-permute-start(f32[1,32,2048]{2,1,0:T(8,128)S(1)} %get-tuple-element.18.refs_0_), channel_id=1, source_target_pairs={{0,16},{8,24},{16,0},{24,8},{1,17},{9,25},{17,1},{25,9},{2,18},{10... | collective-permute-start | bytes 786440 | tf_op jit(solution)/shard_map/ppermute | solution.py:620
  7.1 0.0 collective-permute-done.2.second_ref.refs_0_.refs_1_
  7.2 1.9 %collective-permute-start.3 = (f32[2,2,16,128]{3,2,1,0:T(8,128)S(1)}, f32[2,2,16,128]{3,2,1,0:T(8,128)S(1)}, u32[]{:S(2)}, u32[]{:S(2)}) collective-permute-start(f32[2,2,16,128]{3,2,1,0:T(8,128)S(1)} %reference_joined.2.first_ref), channel_id=1, source_target_pairs={{0,2},{1,3},{2,4},{3,5},{4,6},{5,7},{6,0},{7,1},{8,10},{9,11},{10,... | collective-permute-start | bytes 98312 | tf_op jit(solution)/shard_map/ppermute | solution.py:645
  9.0 0.6 %shifted_reference.1.refs_2_ = bf16[2,2,128,1920]{3,2,1,0:T(8,128)(2,1)S(1)} custom-call(f32[2,16,128]{2,1,0:T(8,128)S(1)} %get-tuple-element.19.tiles_ref), custom_call_target="tpu_custom_call" | custom-call | flops 805000000 | tf_op jit(solution)/shard_map/shifted_reference/pallas_call | solution.py:240
  9.6 3.3 %collective-permute-done.3.refs_1_.second_ref.refs_2_ = f32[2,2,16,128]{3,2,1,0:T(8,128)S(1)} collective-permute-done((f32[2,2,16,128]{3,2,1,0:T(8,128)S(1)}, f32[2,2,16,128]{3,2,1,0:T(8,128)S(1)}, u32[]{:S(2)}, u32[]{:S(2)}) %collective-permute-start.3) | collective-permute-done | bytes 32800 | tf_op jit(solution)/shard_map/ppermute | solution.py:645
  12.9 1.0 %collective-permute-start.4 = (f32[4,2,16,128]{3,2,1,0:T(8,128)S(1)}, f32[4,2,16,128]{3,2,1,0:T(8,128)S(1)}, u32[]{:S(2)}, u32[]{:S(2)}) collective-permute-start(f32[4,2,16,128]{3,2,1,0:T(8,128)S(1)} %reference_joined.3.refs_4_), channel_id=1, source_target_pairs={{0,4},{1,5},{2,6},{3,7},{4,0},{5,1},{6,2},{7,3},{8,12},{9,13},{10,... | collective-permute-start | bytes 196616 | tf_op jit(solution)/shard_map/ppermute | solution.py:645
  14.0 0.2 shifted_first.1.refs_3_
  14.1 0.0 collective-permute-done.1
  14.2 1.6 %lag_products.1.refs_4_ = f32[8,10,8,128]{3,2,1,0:T(8,128)} custom-call(f32[32,2048]{1,0:T(8,128)S(1)} %bitcast.9, f32[32,2048]{1,0:T(8,128)S(1)} %bitcast.10, bf16[2,2,128,1920]{3,2,1,0:T(8,128)(2,1)S(1)} %shifted_reference.1.refs_2_, bf16[2,2,128,256]{3,2,1,0:T(8,128)(2,1)S(1)} %shifted_first.1.refs_3_, f32[4,2,16,128]{3,2,1,0:T(8,128)S(1)} %reference_joined.3.refs_4_), custom_call_target="tpu_custom_call" | custom-call | flops 2415000064 | tf_op jit(solution)/shard_map/lag_products/pallas_call | solution.py:347
  15.7 5.7 %all-to-all-start = ((f32[8,10,8,128]{3,2,1,0:T(8,128)}), f32[8,10,8,128]{3,2,1,0:T(8,128)S(1)}, u32[]{:S(2)}, u32[]{:S(2)}) async-start(f32[8,10,8,128]{3,2,1,0:T(8,128)} %lag_products.1.refs_4_), calls=%async_computation | async-start | bytes 655360 | tf_op jit(solution)/shard_map/all_to_all | solution.py:652
  21.5 0.0 collective-permute-done.4.refs_3_
  21.5 6.5 %reference_products.1 = (bf16[3,2048,128]{2,1,0:T(8,128)(2,1)S(1)}, f32[8,128]{1,0:T(8,128)S(1)}, f32[128,128]{1,0:T(8,128)S(1)}) custom-call(f32[1,2,16,128]{3,2,1,0:T(8,128)S(1)} %bitcast.13, f32[1,2,16,128]{3,2,1,0:T(8,128)S(1)} %collective-permute-done.2.second_ref.refs_0_.refs_1_, ...), custom_call_target="tpu_custom_call" | custom-call | flops 7129999872 | tf_op jit(solution)/shard_map/reference_products/pallas_call | solution.py:459
  27.9 0.0 copy-start
  28.0 2.5 %gram_inverse.1 = (f32[128,128]{1,0:T(8,128)S(1)}, f32[128,128]{1,0:T(8,128)S(1)}) custom-call(f32[8,128]{1,0:T(8,128)S(1)} %get-tuple-element.21.line_ref, f32[128,128]{1,0:T(8,128)S(1)} %get-tuple-element.22.tail_ref), custom_call_target="tpu_custom_call" | custom-call | flops 2300000000 | tf_op jit(solution)/shard_map/gram_inverse/pallas_call | solution.py:530
  30.4 0.8 %all-to-all-done.got_ref = f32[8,10,8,128]{3,2,1,0:T(8,128)S(1)} async-done(((f32[8,10,8,128]{3,2,1,0:T(8,128)}), f32[8,10,8,128]{3,2,1,0:T(8,128)S(1)}, u32[]{:S(2)}, u32[]{:S(2)}) %all-to-all-start) | async-done | bytes 327712 | tf_op jit(solution)/shard_map/all_to_all | solution.py:652
  31.2 0.0 copy-done
  31.2 2.7 %range_doppler.1 = f32[4,4,2,32,256]{4,3,2,1,0:T(8,128)} custom-call(f32[8,10,8,128]{3,2,1,0:T(8,128)S(1)} %all-to-all-done.got_ref, bf16[3,2048,128]{2,1,0:T(8,128)(2,1)S(1)} %get-tuple-element.20.own_ref, f32[128,128]{1,0:T(8,128)S(1)} %get-tuple-element.23.gram_ref, f32[128,128]{1,0:T(8,128)S(1)} %get-tuple-element.24.solver_ref, ...), custom_call_target="tpu_custom_call" | custom-call | flops 2875000064 | tf_op jit(solution)/shard_map/range_doppler/pallas_call | solution.py:601
  (2 shorter events, 0.0 us)
Async XLA Ops:
  2.1 3.1 %collective-permute-start = (f32[64,2048]{1,0:T(8,128)S(1)}, f32[64,2048]{1,0:T(8,128)S(1)}, u32[]{:S(2)}, u32[]{:S(2)}) collective-permute-start(f32[64,2048]{1,0:T(8,128)S(1)} %get-tuple-element.16), channel_id=1, source_target_pairs={{0,8},{8,0},{16,24},{24,16},{1,9},{9,1},{17,25},{25,17},{2,10},{10... | collective-permute-start | bytes 1572872 | tf_op jit(solution)/shard_map/ppermute | solution.py:620
  2.6 4.5 %collective-permute-start.2 = (f32[1,2,16,128]{3,2,1,0:T(8,128)S(1)}, f32[1,2,16,128]{3,2,1,0:T(8,128)S(1)}, u32[]{:S(2)}, u32[]{:S(2)}) collective-permute-start(f32[1,2,16,128]{3,2,1,0:T(8,128)S(1)} %bitcast.11), channel_id=1, source_target_pairs={{0,1},{1,0},{2,3},{3,2},{4,5},{5,4},{6,7},{7,6},{8,9},{9,8},{10,11... | collective-permute-start | bytes 49160 | tf_op jit(solution)/shard_map/ppermute | solution.py:620
  5.3 8.9 %collective-permute-start.1 = (f32[1,32,2048]{2,1,0:T(8,128)S(1)}, f32[1,32,2048]{2,1,0:T(8,128)S(1)}, u32[]{:S(2)}, u32[]{:S(2)}) collective-permute-start(f32[1,32,2048]{2,1,0:T(8,128)S(1)} %get-tuple-element.18.refs_0_), channel_id=1, source_target_pairs={{0,16},{8,24},{16,0},{24,8},{1,17},{9,25},{17,1},{25,9},{2,18},{10... | collective-permute-start | bytes 786440 | tf_op jit(solution)/shard_map/ppermute | solution.py:620
  7.2 5.8 %collective-permute-start.3 = (f32[2,2,16,128]{3,2,1,0:T(8,128)S(1)}, f32[2,2,16,128]{3,2,1,0:T(8,128)S(1)}, u32[]{:S(2)}, u32[]{:S(2)}) collective-permute-start(f32[2,2,16,128]{3,2,1,0:T(8,128)S(1)} %reference_joined.2.first_ref), channel_id=1, source_target_pairs={{0,2},{1,3},{2,4},{3,5},{4,6},{5,7},{6,0},{7,1},{8,10},{9,11},{10,... | collective-permute-start | bytes 98312 | tf_op jit(solution)/shard_map/ppermute | solution.py:645
  12.9 8.5 %collective-permute-start.4 = (f32[4,2,16,128]{3,2,1,0:T(8,128)S(1)}, f32[4,2,16,128]{3,2,1,0:T(8,128)S(1)}, u32[]{:S(2)}, u32[]{:S(2)}) collective-permute-start(f32[4,2,16,128]{3,2,1,0:T(8,128)S(1)} %reference_joined.3.refs_4_), channel_id=1, source_target_pairs={{0,4},{1,5},{2,6},{3,7},{4,0},{5,1},{6,2},{7,3},{8,12},{9,13},{10,... | collective-permute-start | bytes 196616 | tf_op jit(solution)/shard_map/ppermute | solution.py:645
  15.7 15.4 %all-to-all-start = ((f32[8,10,8,128]{3,2,1,0:T(8,128)}), f32[8,10,8,128]{3,2,1,0:T(8,128)S(1)}, u32[]{:S(2)}, u32[]{:S(2)}) async-start(f32[8,10,8,128]{3,2,1,0:T(8,128)} %lag_products.1.refs_4_), calls=%async_computation | async-start | bytes 655360 | tf_op jit(solution)/shard_map/all_to_all | solution.py:652
  27.9 3.2 %copy-start = (bf16[2,128,512]{2,1,0:T(8,128)(2,1)S(1)}, bf16[2,128,512]{2,1,0:T(8,128)(2,1)}, u32[]{:S(2)}) copy-start(bf16[2,128,512]{2,1,0:T(8,128)(2,1)} %constant.2.clone.wave_ref) | copy-start | bytes 786436

commit v24 on v23

--- a/solution.py
+++ b/solution.py
@@ -498,7 +498,8 @@
     gram_i = up_i - up_i.T - (tails[:TAPS, TAPS:] - tails[TAPS:, :TAPS])
     gram = jnp.concatenate([gram_r, gram_i], 1)
     gram_factor = as_factor(gram)
-    gram_ref[...] = gram_factor
+    for part, value in enumerate(thirds(gram_factor)):
+        gram_ref[part] = value
     gram_halves = halves(gram_factor)
     one = (
         lax.broadcasted_iota(jnp.int32, gram.shape, 0) == lax.broadcasted_iota(jnp.int32, gram.shape, 1)
@@ -523,13 +524,14 @@
     inverse = inverse + jnp.dot(
         one - seen, as_factor(inverse), precision=HIGHEST, preferred_element_type=jnp.float32
     )
-    solver_ref[...] = as_factor(inverse)
+    for part, value in enumerate(thirds(as_factor(inverse))):
+        solver_ref[part] = value
 
 
 def solver_call(line, tail):
     return pl.pallas_call(
         solver_kernel,
-        out_shape=[jax.ShapeDtypeStruct(tail.shape, jnp.float32)] * 2,
+        out_shape=[jax.ShapeDtypeStruct((3,) + tail.shape, jnp.bfloat16)] * 2,
         compiler_params=params(),
         cost_estimate=cost(2.0),
         name="gram_inverse",
@@ -563,7 +565,7 @@
     cross = jnp.concatenate(rows, 0)
 
     def exact(x, ref):
-        return jnp.dot(x, ref[...], precision=HIGHEST, preferred_element_type=jnp.float32)
+        return dot_parts(thirds(x), [ref[part] for part in range(3)])
 
     taps = exact(cross, solver_ref)
     taps = taps + exact(cross - exact(taps, gram_ref), solver_ref)

time: 34.1 us -> 34 us (level)
  Pallas kernels: 16.2 us -> 15.8 us
  transfers between devices with their start and end apart: 6 -> 6, of which waited for: 2 -> 2; matrix products, arithmetic and copies ran while one was open for 0% -> 0% of each run, Pallas kernels for 34% -> 33%
where the time goes in v24:
time: 34 us; the launch traced here: 33.8 us
  Pallas kernels  15.8 us (46%)
  starting transfers between devices  13.6 us (40%)
  waiting for transfers between devices  4.34 us (13%)
    pallas_call x1, Pallas kernels, own_call(): pl.pallas_call(functools.partial(own_kernel, lags_local), in_specs=[pl.Bl...  6.49 us
    all_to_all x1, starting transfers between devices, tiled_device(): got = lax.all_to_all(pieces, 'tm', 0, 0, tiled=True)  5.7 us
    ppermute x3, starting transfers between devices, swap(): return lax.ppermute(x, axis, pairs)  4.97 us
    ppermute x2, waiting for transfers between devices, tiled_device(): lax.ppermute(joined, 'tm', [(i, (i + count) % tm_count) for i in range(tm...  3.3 us
    ppermute x2, starting transfers between devices, tiled_device(): lax.ppermute(joined, 'tm', [(i, (i + count) % tm_count) for i in range(tm...  2.88 us
    pallas_call x1, Pallas kernels, map_call(): pl.pallas_call(functools.partial(map_kernel, groups), in_specs=[pl.BlockS...  2.58 us
    pallas_call x1, Pallas kernels, solver_call(): pl.pallas_call(solver_kernel, out_shape=[jax.ShapeDtypeStruct((3,) + tail...  2.2 us
    pallas_call x1, Pallas kernels, beam_call(): pl.pallas_call(functools.partial(beam_kernel, chan_count, beams_local), i...  2.1 us
  transfers between devices with their start and end apart: 6, of which 2 were waited for; matrix products, arithmetic and copies ran while one was open for 0% of the time, Pallas kernels for 33%

profile of v24, /device:TPU:0, one launch (start us, length us, event | category | flops | bytes accessed | tf_op | source)
XLA Modules:
  0.0 33.8 jit_solution(11328003492747499556)
XLA Ops:
  0.0 2.1 %beams.1 = (f32[64,2048]{1,0:T(8,128)S(1)}, f32[64,2048]{1,0:T(8,128)S(1)}, f32[2,16,128]{2,1,0:T(8,128)S(1)}) custom-call(f32[2,64,64]{2,1,0:T(8,128)} %w_hbm.1, f32[128,2048]{1,0:T(8,128)} %bitcast.14, f32[2,2048]{1,0:T(2,128)} %ref_hbm.1), custom_call_target="tpu_custom_call" | custom-call | flops 2529999872 | tf_op jit(solution)/shard_map/beams/pallas_call | solution.py:154
  2.1 0.5 %collective-permute-start = (f32[64,2048]{1,0:T(8,128)S(1)}, f32[64,2048]{1,0:T(8,128)S(1)}, u32[]{:S(2)}, u32[]{:S(2)}) collective-permute-start(f32[64,2048]{1,0:T(8,128)S(1)} %get-tuple-element.16), channel_id=1, source_target_pairs={{0,8},{8,0},{16,24},{24,16},{1,9},{9,1},{17,25},{25,17},{2,10},{10... | collective-permute-start | bytes 1572872 | tf_op jit(solution)/shard_map/ppermute | solution.py:622
  2.6 2.6 %collective-permute-start.2 = (f32[1,2,16,128]{3,2,1,0:T(8,128)S(1)}, f32[1,2,16,128]{3,2,1,0:T(8,128)S(1)}, u32[]{:S(2)}, u32[]{:S(2)}) collective-permute-start(f32[1,2,16,128]{3,2,1,0:T(8,128)S(1)} %bitcast.11), channel_id=1, source_target_pairs={{0,1},{1,0},{2,3},{3,2},{4,5},{5,4},{6,7},{7,6},{8,9},{9,8},{10,11... | collective-permute-start | bytes 49160 | tf_op jit(solution)/shard_map/ppermute | solution.py:622
  5.2 0.0 collective-permute-done
  5.2 0.1 halves_summed.1
  5.3 1.9 %collective-permute-start.1 = (f32[1,32,2048]{2,1,0:T(8,128)S(1)}, f32[1,32,2048]{2,1,0:T(8,128)S(1)}, u32[]{:S(2)}, u32[]{:S(2)}) collective-permute-start(f32[1,32,2048]{2,1,0:T(8,128)S(1)} %get-tuple-element.18.refs_0_), channel_id=1, source_target_pairs={{0,16},{8,24},{16,0},{24,8},{1,17},{9,25},{17,1},{25,9},{2,18},{10... | collective-permute-start | bytes 786440 | tf_op jit(solution)/shard_map/ppermute | solution.py:622
  7.1 0.0 collective-permute-done.2.second_ref.refs_0_.refs_1_
  7.2 1.9 %collective-permute-start.3 = (f32[2,2,16,128]{3,2,1,0:T(8,128)S(1)}, f32[2,2,16,128]{3,2,1,0:T(8,128)S(1)}, u32[]{:S(2)}, u32[]{:S(2)}) collective-permute-start(f32[2,2,16,128]{3,2,1,0:T(8,128)S(1)} %reference_joined.2.first_ref), channel_id=1, source_target_pairs={{0,2},{1,3},{2,4},{3,5},{4,6},{5,7},{6,0},{7,1},{8,10},{9,11},{10,... | collective-permute-start | bytes 98312 | tf_op jit(solution)/shard_map/ppermute | solution.py:647
  9.0 0.6 %shifted_reference.1.refs_2_ = bf16[2,2,128,1920]{3,2,1,0:T(8,128)(2,1)S(1)} custom-call(f32[2,16,128]{2,1,0:T(8,128)S(1)} %get-tuple-element.19.tiles_ref), custom_call_target="tpu_custom_call" | custom-call | flops 805000000 | tf_op jit(solution)/shard_map/shifted_reference/pallas_call | solution.py:240
  9.6 3.3 %collective-permute-done.3.refs_1_.second_ref.refs_2_ = f32[2,2,16,128]{3,2,1,0:T(8,128)S(1)} collective-permute-done((f32[2,2,16,128]{3,2,1,0:T(8,128)S(1)}, f32[2,2,16,128]{3,2,1,0:T(8,128)S(1)}, u32[]{:S(2)}, u32[]{:S(2)}) %collective-permute-start.3) | collective-permute-done | bytes 32800 | tf_op jit(solution)/shard_map/ppermute | solution.py:647
  12.9 1.0 %collective-permute-start.4 = (f32[4,2,16,128]{3,2,1,0:T(8,128)S(1)}, f32[4,2,16,128]{3,2,1,0:T(8,128)S(1)}, u32[]{:S(2)}, u32[]{:S(2)}) collective-permute-start(f32[4,2,16,128]{3,2,1,0:T(8,128)S(1)} %reference_joined.3.refs_4_), channel_id=1, source_target_pairs={{0,4},{1,5},{2,6},{3,7},{4,0},{5,1},{6,2},{7,3},{8,12},{9,13},{10,... | collective-permute-start | bytes 196616 | tf_op jit(solution)/shard_map/ppermute | solution.py:647
  14.0 0.2 shifted_first.1.refs_3_
  14.1 0.0 collective-permute-done.1
  14.2 1.6 %lag_products.1.refs_4_ = f32[8,10,8,128]{3,2,1,0:T(8,128)} custom-call(f32[32,2048]{1,0:T(8,128)S(1)} %bitcast.9, f32[32,2048]{1,0:T(8,128)S(1)} %bitcast.10, bf16[2,2,128,1920]{3,2,1,0:T(8,128)(2,1)S(1)} %shifted_reference.1.refs_2_, bf16[2,2,128,256]{3,2,1,0:T(8,128)(2,1)S(1)} %shifted_first.1.refs_3_, f32[4,2,16,128]{3,2,1,0:T(8,128)S(1)} %reference_joined.3.refs_4_), custom_call_target="tpu_custom_call" | custom-call | flops 2415000064 | tf_op jit(solution)/shard_map/lag_products/pallas_call | solution.py:347
  15.7 5.7 %all-to-all-start = ((f32[8,10,8,128]{3,2,1,0:T(8,128)}), f32[8,10,8,128]{3,2,1,0:T(8,128)S(1)}, u32[]{:S(2)}, u32[]{:S(2)}) async-start(f32[8,10,8,128]{3,2,1,0:T(8,128)} %lag_products.1.refs_4_), calls=%async_computation | async-start | bytes 655360 | tf_op jit(solution)/shard_map/all_to_all | solution.py:654
  21.5 0.0 collective-permute-done.4.refs_3_
  21.5 6.5 %reference_products.1 = (bf16[3,2048,128]{2,1,0:T(8,128)(2,1)S(1)}, f32[8,128]{1,0:T(8,128)S(1)}, f32[128,128]{1,0:T(8,128)S(1)}) custom-call(f32[1,2,16,128]{3,2,1,0:T(8,128)S(1)} %bitcast.13, f32[1,2,16,128]{3,2,1,0:T(8,128)S(1)} %collective-permute-done.2.second_ref.refs_0_.refs_1_, ...), custom_call_target="tpu_custom_call" | custom-call | flops 7129999872 | tf_op jit(solution)/shard_map/reference_products/pallas_call | solution.py:459
  27.9 0.0 copy-start
  28.0 2.2 %gram_inverse.1 = (bf16[3,128,128]{2,1,0:T(8,128)(2,1)S(1)}, bf16[3,128,128]{2,1,0:T(8,128)(2,1)S(1)}) custom-call(f32[8,128]{1,0:T(8,128)S(1)} %get-tuple-element.21.line_ref, f32[128,128]{1,0:T(8,128)S(1)} %get-tuple-element.22.tail_ref), custom_call_target="tpu_custom_call" | custom-call | flops 2300000000 | tf_op jit(solution)/shard_map/gram_inverse/pallas_call | solution.py:532
  30.2 1.0 %all-to-all-done.got_ref = f32[8,10,8,128]{3,2,1,0:T(8,128)S(1)} async-done(((f32[8,10,8,128]{3,2,1,0:T(8,128)}), f32[8,10,8,128]{3,2,1,0:T(8,128)S(1)}, u32[]{:S(2)}, u32[]{:S(2)}) %all-to-all-start) | async-done | bytes 327712 | tf_op jit(solution)/shard_map/all_to_all | solution.py:654
  31.2 0.0 copy-done
  31.2 2.6 %range_doppler.1 = f32[4,4,2,32,256]{4,3,2,1,0:T(8,128)} custom-call(f32[8,10,8,128]{3,2,1,0:T(8,128)S(1)} %all-to-all-done.got_ref, bf16[3,2048,128]{2,1,0:T(8,128)(2,1)S(1)} %get-tuple-element.20.own_ref, bf16[3,128,128]{2,1,0:T(8,128)(2,1)S(1)} %get-tuple-element.23.gram_ref, bf16[3,128,128]{2,1,0:T(8,128)(2,1)S(1)} %get-tuple-element.24.solver_ref, ...), custom_call_target="tpu_custom_call" | custom-call | flops 2875000064 | tf_op jit(solution)/shard_map/range_doppler/pallas_call | solution.py:603
  (2 shorter events, 0.0 us)
Async XLA Ops:
  2.1 3.1 %collective-permute-start = (f32[64,2048]{1,0:T(8,128)S(1)}, f32[64,2048]{1,0:T(8,128)S(1)}, u32[]{:S(2)}, u32[]{:S(2)}) collective-permute-start(f32[64,2048]{1,0:T(8,128)S(1)} %get-tuple-element.16), channel_id=1, source_target_pairs={{0,8},{8,0},{16,24},{24,16},{1,9},{9,1},{17,25},{25,17},{2,10},{10... | collective-permute-start | bytes 1572872 | tf_op jit(solution)/shard_map/ppermute | solution.py:622
  2.6 4.5 %collective-permute-start.2 = (f32[1,2,16,128]{3,2,1,0:T(8,128)S(1)}, f32[1,2,16,128]{3,2,1,0:T(8,128)S(1)}, u32[]{:S(2)}, u32[]{:S(2)}) collective-permute-start(f32[1,2,16,128]{3,2,1,0:T(8,128)S(1)} %bitcast.11), channel_id=1, source_target_pairs={{0,1},{1,0},{2,3},{3,2},{4,5},{5,4},{6,7},{7,6},{8,9},{9,8},{10,11... | collective-permute-start | bytes 49160 | tf_op jit(solution)/shard_map/ppermute | solution.py:622
  5.3 8.9 %collective-permute-start.1 = (f32[1,32,2048]{2,1,0:T(8,128)S(1)}, f32[1,32,2048]{2,1,0:T(8,128)S(1)}, u32[]{:S(2)}, u32[]{:S(2)}) collective-permute-start(f32[1,32,2048]{2,1,0:T(8,128)S(1)} %get-tuple-element.18.refs_0_), channel_id=1, source_target_pairs={{0,16},{8,24},{16,0},{24,8},{1,17},{9,25},{17,1},{25,9},{2,18},{10... | collective-permute-start | bytes 786440 | tf_op jit(solution)/shard_map/ppermute | solution.py:622
  7.2 5.8 %collective-permute-start.3 = (f32[2,2,16,128]{3,2,1,0:T(8,128)S(1)}, f32[2,2,16,128]{3,2,1,0:T(8,128)S(1)}, u32[]{:S(2)}, u32[]{:S(2)}) collective-permute-start(f32[2,2,16,128]{3,2,1,0:T(8,128)S(1)} %reference_joined.2.first_ref), channel_id=1, source_target_pairs={{0,2},{1,3},{2,4},{3,5},{4,6},{5,7},{6,0},{7,1},{8,10},{9,11},{10,... | collective-permute-start | bytes 98312 | tf_op jit(solution)/shard_map/ppermute | solution.py:647
  12.9 8.5 %collective-permute-start.4 = (f32[4,2,16,128]{3,2,1,0:T(8,128)S(1)}, f32[4,2,16,128]{3,2,1,0:T(8,128)S(1)}, u32[]{:S(2)}, u32[]{:S(2)}) collective-permute-start(f32[4,2,16,128]{3,2,1,0:T(8,128)S(1)} %reference_joined.3.refs_4_), channel_id=1, source_target_pairs={{0,4},{1,5},{2,6},{3,7},{4,0},{5,1},{6,2},{7,3},{8,12},{9,13},{10,... | collective-permute-start | bytes 196616 | tf_op jit(solution)/shard_map/ppermute | solution.py:647
  15.7 15.4 %all-to-all-start = ((f32[8,10,8,128]{3,2,1,0:T(8,128)}), f32[8,10,8,128]{3,2,1,0:T(8,128)S(1)}, u32[]{:S(2)}, u32[]{:S(2)}) async-start(f32[8,10,8,128]{3,2,1,0:T(8,128)} %lag_products.1.refs_4_), calls=%async_computation | async-start | bytes 655360 | tf_op jit(solution)/shard_map/all_to_all | solution.py:654
  27.9 3.2 %copy-start = (bf16[2,128,512]{2,1,0:T(8,128)(2,1)S(1)}, bf16[2,128,512]{2,1,0:T(8,128)(2,1)}, u32[]{:S(2)}) copy-start(bf16[2,128,512]{2,1,0:T(8,128)(2,1)} %constant.2.clone.wave_ref) | copy-start | bytes 786436

commit v25 on v23

--- a/solution.py
+++ b/solution.py
@@ -38,6 +38,9 @@
     high = x.astype(jnp.bfloat16)
     rest = x - high.astype(jnp.float32)
     return (high,) + halves(rest)
+
+
+PART_PAIRS = ((2, 0), (1, 1), (0, 2), (1, 0), (0, 1), (0, 0))
 
 
 def dot_parts(a, b, across=False):
@@ -485,6 +488,11 @@
     rows = lax.broadcasted_iota(jnp.int32, (TAPS, TAPS), 0)
     above = cols > rows
 
+    def stack(ref, value):
+        parts = thirds(value)
+        for n, (_, part) in enumerate(PART_PAIRS):
+            ref[n * value.shape[0] : (n + 1) * value.shape[0], :] = parts[part]
+
     def upper(x):
         spread = pltpu.roll(jnp.broadcast_to(x, (TAPS, LANES)), 0, 1, stride=1, stride_axis=0)
         return spread[:, :TAPS]
@@ -498,7 +506,7 @@
     gram_i = up_i - up_i.T - (tails[:TAPS, TAPS:] - tails[TAPS:, :TAPS])
     gram = jnp.concatenate([gram_r, gram_i], 1)
     gram_factor = as_factor(gram)
-    gram_ref[...] = gram_factor
+    stack(gram_ref, gram_factor)
     gram_halves = halves(gram_factor)
     one = (
         lax.broadcasted_iota(jnp.int32, gram.shape, 0) == lax.broadcasted_iota(jnp.int32, gram.shape, 1)
@@ -523,13 +531,13 @@
     inverse = inverse + jnp.dot(
         one - seen, as_factor(inverse), precision=HIGHEST, preferred_element_type=jnp.float32
     )
-    solver_ref[...] = as_factor(inverse)
+    stack(solver_ref, as_factor(inverse))
 
 
 def solver_call(line, tail):
     return pl.pallas_call(
         solver_kernel,
-        out_shape=[jax.ShapeDtypeStruct(tail.shape, jnp.float32)] * 2,
+        out_shape=[jax.ShapeDtypeStruct((len(PART_PAIRS) * tail.shape[0], tail.shape[1]), jnp.bfloat16)] * 2,
         compiler_params=params(),
         cost_estimate=cost(2.0),
         name="gram_inverse",
@@ -563,7 +571,10 @@
     cross = jnp.concatenate(rows, 0)
 
     def exact(x, ref):
-        return jnp.dot(x, ref[...], precision=HIGHEST, preferred_element_type=jnp.float32)
+        parts = thirds(x)
+        return jnp.dot(
+            jnp.concatenate([parts[part] for part, _ in PART_PAIRS], 1), ref[...], preferred_element_type=jnp.float32
+        )
 
     taps = exact(cross, solver_ref)
     taps = taps + exact(cross - exact(taps, gram_ref), solver_ref)

time: 34.1 us -> 33.9 us (level)
  Pallas kernels: 16.2 us -> 15.7 us
  transfers between devices with their start and end apart: 6 -> 6, of which waited for: 2 -> 2; matrix products, arithmetic and copies ran while one was open for 0% -> 0% of each run, Pallas kernels for 34% -> 33%
where the time goes in v25:
time: 33.9 us; the launch traced here: 33.7 us
  Pallas kernels  15.7 us (46%)
  starting transfers between devices  13.6 us (40%)
  waiting for transfers between devices  4.34 us (13%)
    pallas_call x1, Pallas kernels, own_call(): pl.pallas_call(functools.partial(own_kernel, lags_local), in_specs=[pl.Bl...  6.49 us
    all_to_all x1, starting transfers between devices, tiled_device(): got = lax.all_to_all(pieces, 'tm', 0, 0, tiled=True)  5.7 us
    ppermute x3, starting transfers between devices, swap(): return lax.ppermute(x, axis, pairs)  4.97 us
    ppermute x2, waiting for transfers between devices, tiled_device(): lax.ppermute(joined, 'tm', [(i, (i + count) % tm_count) for i in range(tm...  3.3 us
    ppermute x2, starting transfers between devices, tiled_device(): lax.ppermute(joined, 'tm', [(i, (i + count) % tm_count) for i in range(tm...  2.88 us
    pallas_call x1, Pallas kernels, map_call(): pl.pallas_call(functools.partial(map_kernel, groups), in_specs=[pl.BlockS...  2.5 us
    pallas_call x1, Pallas kernels, solver_call(): pl.pallas_call(solver_kernel, out_shape=[jax.ShapeDtypeStruct((len(PART_P...  2.2 us
    pallas_call x1, Pallas kernels, beam_call(): pl.pallas_call(functools.partial(beam_kernel, chan_count, beams_local), i...  2.1 us
  transfers between devices with their start and end apart: 6, of which 2 were waited for; matrix products, arithmetic and copies ran while one was open for 0% of the time, Pallas kernels for 33%

profile of v25, /device:TPU:0, one launch (start us, length us, event | category | flops | bytes accessed | tf_op | source)
XLA Modules:
  0.0 33.7 jit_solution(4019547084367673770)
XLA Ops:
  0.0 2.1 %beams.1 = (f32[64,2048]{1,0:T(8,128)S(1)}, f32[64,2048]{1,0:T(8,128)S(1)}, f32[2,16,128]{2,1,0:T(8,128)S(1)}) custom-call(f32[2,64,64]{2,1,0:T(8,128)} %w_hbm.1, f32[128,2048]{1,0:T(8,128)} %bitcast.14, f32[2,2048]{1,0:T(2,128)} %ref_hbm.1), custom_call_target="tpu_custom_call" | custom-call | flops 2529999872 | tf_op jit(solution)/shard_map/beams/pallas_call | solution.py:157
  2.1 0.5 %collective-permute-start = (f32[64,2048]{1,0:T(8,128)S(1)}, f32[64,2048]{1,0:T(8,128)S(1)}, u32[]{:S(2)}, u32[]{:S(2)}) collective-permute-start(f32[64,2048]{1,0:T(8,128)S(1)} %get-tuple-element.16), channel_id=1, source_target_pairs={{0,8},{8,0},{16,24},{24,16},{1,9},{9,1},{17,25},{25,17},{2,10},{10... | collective-permute-start | bytes 1572872 | tf_op jit(solution)/shard_map/ppermute | solution.py:631
  2.6 2.6 %collective-permute-start.2 = (f32[1,2,16,128]{3,2,1,0:T(8,128)S(1)}, f32[1,2,16,128]{3,2,1,0:T(8,128)S(1)}, u32[]{:S(2)}, u32[]{:S(2)}) collective-permute-start(f32[1,2,16,128]{3,2,1,0:T(8,128)S(1)} %bitcast.11), channel_id=1, source_target_pairs={{0,1},{1,0},{2,3},{3,2},{4,5},{5,4},{6,7},{7,6},{8,9},{9,8},{10,11... | collective-permute-start | bytes 49160 | tf_op jit(solution)/shard_map/ppermute | solution.py:631
  5.2 0.0 collective-permute-done
  5.2 0.1 halves_summed.1
  5.3 1.9 %collective-permute-start.1 = (f32[1,32,2048]{2,1,0:T(8,128)S(1)}, f32[1,32,2048]{2,1,0:T(8,128)S(1)}, u32[]{:S(2)}, u32[]{:S(2)}) collective-permute-start(f32[1,32,2048]{2,1,0:T(8,128)S(1)} %get-tuple-element.18.refs_0_), channel_id=1, source_target_pairs={{0,16},{8,24},{16,0},{24,8},{1,17},{9,25},{17,1},{25,9},{2,18},{10... | collective-permute-start | bytes 786440 | tf_op jit(solution)/shard_map/ppermute | solution.py:631
  7.1 0.0 collective-permute-done.2.second_ref.refs_0_.refs_1_
  7.2 1.9 %collective-permute-start.3 = (f32[2,2,16,128]{3,2,1,0:T(8,128)S(1)}, f32[2,2,16,128]{3,2,1,0:T(8,128)S(1)}, u32[]{:S(2)}, u32[]{:S(2)}) collective-permute-start(f32[2,2,16,128]{3,2,1,0:T(8,128)S(1)} %reference_joined.2.first_ref), channel_id=1, source_target_pairs={{0,2},{1,3},{2,4},{3,5},{4,6},{5,7},{6,0},{7,1},{8,10},{9,11},{10,... | collective-permute-start | bytes 98312 | tf_op jit(solution)/shard_map/ppermute | solution.py:656
  9.0 0.6 %shifted_reference.1.refs_2_ = bf16[2,2,128,1920]{3,2,1,0:T(8,128)(2,1)S(1)} custom-call(f32[2,16,128]{2,1,0:T(8,128)S(1)} %get-tuple-element.19.tiles_ref), custom_call_target="tpu_custom_call" | custom-call | flops 805000000 | tf_op jit(solution)/shard_map/shifted_reference/pallas_call | solution.py:243
  9.6 3.3 %collective-permute-done.3.refs_1_.second_ref.refs_2_ = f32[2,2,16,128]{3,2,1,0:T(8,128)S(1)} collective-permute-done((f32[2,2,16,128]{3,2,1,0:T(8,128)S(1)}, f32[2,2,16,128]{3,2,1,0:T(8,128)S(1)}, u32[]{:S(2)}, u32[]{:S(2)}) %collective-permute-start.3) | collective-permute-done | bytes 32800 | tf_op jit(solution)/shard_map/ppermute | solution.py:656
  12.9 1.0 %collective-permute-start.4 = (f32[4,2,16,128]{3,2,1,0:T(8,128)S(1)}, f32[4,2,16,128]{3,2,1,0:T(8,128)S(1)}, u32[]{:S(2)}, u32[]{:S(2)}) collective-permute-start(f32[4,2,16,128]{3,2,1,0:T(8,128)S(1)} %reference_joined.3.refs_4_), channel_id=1, source_target_pairs={{0,4},{1,5},{2,6},{3,7},{4,0},{5,1},{6,2},{7,3},{8,12},{9,13},{10,... | collective-permute-start | bytes 196616 | tf_op jit(solution)/shard_map/ppermute | solution.py:656
  14.0 0.2 shifted_first.1.refs_3_
  14.1 0.0 collective-permute-done.1
  14.2 1.6 %lag_products.1.refs_4_ = f32[8,10,8,128]{3,2,1,0:T(8,128)} custom-call(f32[32,2048]{1,0:T(8,128)S(1)} %bitcast.9, f32[32,2048]{1,0:T(8,128)S(1)} %bitcast.10, bf16[2,2,128,1920]{3,2,1,0:T(8,128)(2,1)S(1)} %shifted_reference.1.refs_2_, bf16[2,2,128,256]{3,2,1,0:T(8,128)(2,1)S(1)} %shifted_first.1.refs_3_, f32[4,2,16,128]{3,2,1,0:T(8,128)S(1)} %reference_joined.3.refs_4_), custom_call_target="tpu_custom_call" | custom-call | flops 2415000064 | tf_op jit(solution)/shard_map/lag_products/pallas_call | solution.py:350
  15.7 5.7 %all-to-all-start = ((f32[8,10,8,128]{3,2,1,0:T(8,128)}), f32[8,10,8,128]{3,2,1,0:T(8,128)S(1)}, u32[]{:S(2)}, u32[]{:S(2)}) async-start(f32[8,10,8,128]{3,2,1,0:T(8,128)} %lag_products.1.refs_4_), calls=%async_computation | async-start | bytes 655360 | tf_op jit(solution)/shard_map/all_to_all | solution.py:663
  21.5 0.0 collective-permute-done.4.refs_3_
  21.5 6.5 %reference_products.1 = (bf16[3,2048,128]{2,1,0:T(8,128)(2,1)S(1)}, f32[8,128]{1,0:T(8,128)S(1)}, f32[128,128]{1,0:T(8,128)S(1)}) custom-call(f32[1,2,16,128]{3,2,1,0:T(8,128)S(1)} %bitcast.13, f32[1,2,16,128]{3,2,1,0:T(8,128)S(1)} %collective-permute-done.2.second_ref.refs_0_.refs_1_, ...), custom_call_target="tpu_custom_call" | custom-call | flops 7129999872 | tf_op jit(solution)/shard_map/reference_products/pallas_call | solution.py:462
  27.9 0.0 copy-start
  28.0 2.2 %gram_inverse.1 = (bf16[768,128]{1,0:T(8,128)(2,1)S(1)}, bf16[768,128]{1,0:T(8,128)(2,1)S(1)}) custom-call(f32[8,128]{1,0:T(8,128)S(1)} %get-tuple-element.21.line_ref, f32[128,128]{1,0:T(8,128)S(1)} %get-tuple-element.22.tail_ref), custom_call_target="tpu_custom_call" | custom-call | flops 2300000000 | tf_op jit(solution)/shard_map/gram_inverse/pallas_call | solution.py:538
  30.2 1.0 %all-to-all-done.got_ref = f32[8,10,8,128]{3,2,1,0:T(8,128)S(1)} async-done(((f32[8,10,8,128]{3,2,1,0:T(8,128)}), f32[8,10,8,128]{3,2,1,0:T(8,128)S(1)}, u32[]{:S(2)}, u32[]{:S(2)}) %all-to-all-start) | async-done | bytes 327712 | tf_op jit(solution)/shard_map/all_to_all | solution.py:663
  31.2 0.0 copy-done
  31.2 2.5 %range_doppler.1 = f32[4,4,2,32,256]{4,3,2,1,0:T(8,128)} custom-call(f32[8,10,8,128]{3,2,1,0:T(8,128)S(1)} %all-to-all-done.got_ref, bf16[3,2048,128]{2,1,0:T(8,128)(2,1)S(1)} %get-tuple-element.20.own_ref, bf16[768,128]{1,0:T(8,128)(2,1)S(1)} %get-tuple-element.23.gram_ref, bf16[768,128]{1,0:T(8,128)(2,1)S(1)} %get-tuple-element.24.solver_ref, ...), custom_call_target="tpu_custom_call" | custom-call | flops 2875000064 | tf_op jit(solution)/shard_map/range_doppler/pallas_call | solution.py:612
  (2 shorter events, 0.0 us)
Async XLA Ops:
  2.1 3.1 %collective-permute-start = (f32[64,2048]{1,0:T(8,128)S(1)}, f32[64,2048]{1,0:T(8,128)S(1)}, u32[]{:S(2)}, u32[]{:S(2)}) collective-permute-start(f32[64,2048]{1,0:T(8,128)S(1)} %get-tuple-element.16), channel_id=1, source_target_pairs={{0,8},{8,0},{16,24},{24,16},{1,9},{9,1},{17,25},{25,17},{2,10},{10... | collective-permute-start | bytes 1572872 | tf_op jit(solution)/shard_map/ppermute | solution.py:631
  2.6 4.5 %collective-permute-start.2 = (f32[1,2,16,128]{3,2,1,0:T(8,128)S(1)}, f32[1,2,16,128]{3,2,1,0:T(8,128)S(1)}, u32[]{:S(2)}, u32[]{:S(2)}) collective-permute-start(f32[1,2,16,128]{3,2,1,0:T(8,128)S(1)} %bitcast.11), channel_id=1, source_target_pairs={{0,1},{1,0},{2,3},{3,2},{4,5},{5,4},{6,7},{7,6},{8,9},{9,8},{10,11... | collective-permute-start | bytes 49160 | tf_op jit(solution)/shard_map/ppermute | solution.py:631
  5.3 8.9 %collective-permute-start.1 = (f32[1,32,2048]{2,1,0:T(8,128)S(1)}, f32[1,32,2048]{2,1,0:T(8,128)S(1)}, u32[]{:S(2)}, u32[]{:S(2)}) collective-permute-start(f32[1,32,2048]{2,1,0:T(8,128)S(1)} %get-tuple-element.18.refs_0_), channel_id=1, source_target_pairs={{0,16},{8,24},{16,0},{24,8},{1,17},{9,25},{17,1},{25,9},{2,18},{10... | collective-permute-start | bytes 786440 | tf_op jit(solution)/shard_map/ppermute | solution.py:631
  7.2 5.8 %collective-permute-start.3 = (f32[2,2,16,128]{3,2,1,0:T(8,128)S(1)}, f32[2,2,16,128]{3,2,1,0:T(8,128)S(1)}, u32[]{:S(2)}, u32[]{:S(2)}) collective-permute-start(f32[2,2,16,128]{3,2,1,0:T(8,128)S(1)} %reference_joined.2.first_ref), channel_id=1, source_target_pairs={{0,2},{1,3},{2,4},{3,5},{4,6},{5,7},{6,0},{7,1},{8,10},{9,11},{10,... | collective-permute-start | bytes 98312 | tf_op jit(solution)/shard_map/ppermute | solution.py:656
  12.9 8.5 %collective-permute-start.4 = (f32[4,2,16,128]{3,2,1,0:T(8,128)S(1)}, f32[4,2,16,128]{3,2,1,0:T(8,128)S(1)}, u32[]{:S(2)}, u32[]{:S(2)}) collective-permute-start(f32[4,2,16,128]{3,2,1,0:T(8,128)S(1)} %reference_joined.3.refs_4_), channel_id=1, source_target_pairs={{0,4},{1,5},{2,6},{3,7},{4,0},{5,1},{6,2},{7,3},{8,12},{9,13},{10,... | collective-permute-start | bytes 196616 | tf_op jit(solution)/shard_map/ppermute | solution.py:656
  15.7 15.4 %all-to-all-start = ((f32[8,10,8,128]{3,2,1,0:T(8,128)}), f32[8,10,8,128]{3,2,1,0:T(8,128)S(1)}, u32[]{:S(2)}, u32[]{:S(2)}) async-start(f32[8,10,8,128]{3,2,1,0:T(8,128)} %lag_products.1.refs_4_), calls=%async_computation | async-start | bytes 655360 | tf_op jit(solution)/shard_map/all_to_all | solution.py:663
  27.9 3.2 %copy-start = (bf16[2,128,512]{2,1,0:T(8,128)(2,1)S(1)}, bf16[2,128,512]{2,1,0:T(8,128)(2,1)}, u32[]{:S(2)}) copy-start(bf16[2,128,512]{2,1,0:T(8,128)(2,1)} %constant.2.clone.wave_ref) | copy-start | bytes 786436

commit v26 on v25

--- a/solution.py
+++ b/solution.py
@@ -99,7 +99,7 @@
     return outs
 
 
-COPIES = 4
+COPIES = 2
 
 
 def beam_kernel(

time: 33.9 us -> 33.9 us (level)
  transfers between devices with their start and end apart: 6 -> 6, of which waited for: 2 -> 2; matrix products, arithmetic and copies ran while one was open for 0% -> 0% of each run, Pallas kernels for 33% -> 34%
where the time goes in v26:
time: 33.9 us; the launch traced here: 33.7 us
  Pallas kernels  16 us (47%)
  starting transfers between devices  13.6 us (40%)
  waiting for transfers between devices  4.07 us (12%)
    pallas_call x1, Pallas kernels, own_call(): pl.pallas_call(functools.partial(own_kernel, lags_local), in_specs=[pl.Bl...  6.49 us
    all_to_all x1, starting transfers between devices, tiled_device(): got = lax.all_to_all(pieces, 'tm', 0, 0, tiled=True)  5.7 us
    ppermute x3, starting transfers between devices, swap(): return lax.ppermute(x, axis, pairs)  4.98 us
    ppermute x2, waiting for transfers between devices, tiled_device(): lax.ppermute(joined, 'tm', [(i, (i + count) % tm_count) for i in range(tm...  3.31 us
    ppermute x2, starting transfers between devices, tiled_device(): lax.ppermute(joined, 'tm', [(i, (i + count) % tm_count) for i in range(tm...  2.87 us
    pallas_call x1, Pallas kernels, map_call(): pl.pallas_call(functools.partial(map_kernel, groups), in_specs=[pl.BlockS...  2.5 us
    pallas_call x1, Pallas kernels, solver_call(): pl.pallas_call(solver_kernel, out_shape=[jax.ShapeDtypeStruct((len(PART_P...  2.48 us
    pallas_call x1, Pallas kernels, beam_call(): pl.pallas_call(functools.partial(beam_kernel, chan_count, beams_local), i...  2.09 us
  transfers between devices with their start and end apart: 6, of which 2 were waited for; matrix products, arithmetic and copies ran while one was open for 0% of the time, Pallas kernels for 34%

profile of v26, /device:TPU:0, one launch (start us, length us, event | category | flops | bytes accessed | tf_op | source)
XLA Modules:
  0.0 33.7 jit_solution(9633177432723107517)
XLA Ops:
  0.0 2.1 %beams.1 = (f32[64,2048]{1,0:T(8,128)S(1)}, f32[64,2048]{1,0:T(8,128)S(1)}, f32[2,16,128]{2,1,0:T(8,128)S(1)}) custom-call(f32[2,64,64]{2,1,0:T(8,128)} %w_hbm.1, f32[128,2048]{1,0:T(8,128)} %bitcast.14, f32[2,2048]{1,0:T(2,128)} %ref_hbm.1), custom_call_target="tpu_custom_call" | custom-call | flops 2529999872 | tf_op jit(solution)/shard_map/beams/pallas_call | solution.py:157
  2.1 0.5 %collective-permute-start = (f32[64,2048]{1,0:T(8,128)S(1)}, f32[64,2048]{1,0:T(8,128)S(1)}, u32[]{:S(2)}, u32[]{:S(2)}) collective-permute-start(f32[64,2048]{1,0:T(8,128)S(1)} %get-tuple-element.16), channel_id=1, source_target_pairs={{0,8},{8,0},{16,24},{24,16},{1,9},{9,1},{17,25},{25,17},{2,10},{10... | collective-permute-start | bytes 1572872 | tf_op jit(solution)/shard_map/ppermute | solution.py:631
  2.6 2.6 %collective-permute-start.2 = (f32[1,2,16,128]{3,2,1,0:T(8,128)S(1)}, f32[1,2,16,128]{3,2,1,0:T(8,128)S(1)}, u32[]{:S(2)}, u32[]{:S(2)}) collective-permute-start(f32[1,2,16,128]{3,2,1,0:T(8,128)S(1)} %bitcast.11), channel_id=1, source_target_pairs={{0,1},{1,0},{2,3},{3,2},{4,5},{5,4},{6,7},{7,6},{8,9},{9,8},{10,11... | collective-permute-start | bytes 49160 | tf_op jit(solution)/shard_map/ppermute | solution.py:631
  5.2 0.0 collective-permute-done
  5.2 0.1 halves_summed.1
  5.3 1.9 %collective-permute-start.1 = (f32[1,32,2048]{2,1,0:T(8,128)S(1)}, f32[1,32,2048]{2,1,0:T(8,128)S(1)}, u32[]{:S(2)}, u32[]{:S(2)}) collective-permute-start(f32[1,32,2048]{2,1,0:T(8,128)S(1)} %get-tuple-element.18.refs_0_), channel_id=1, source_target_pairs={{0,16},{8,24},{16,0},{24,8},{1,17},{9,25},{17,1},{25,9},{2,18},{10... | collective-permute-start | bytes 786440 | tf_op jit(solution)/shard_map/ppermute | solution.py:631
  7.1 0.0 collective-permute-done.2.second_ref.refs_0_.refs_1_
  7.2 1.9 %collective-permute-start.3 = (f32[2,2,16,128]{3,2,1,0:T(8,128)S(1)}, f32[2,2,16,128]{3,2,1,0:T(8,128)S(1)}, u32[]{:S(2)}, u32[]{:S(2)}) collective-permute-start(f32[2,2,16,128]{3,2,1,0:T(8,128)S(1)} %reference_joined.2.first_ref), channel_id=1, source_target_pairs={{0,2},{1,3},{2,4},{3,5},{4,6},{5,7},{6,0},{7,1},{8,10},{9,11},{10,... | collective-permute-start | bytes 98312 | tf_op jit(solution)/shard_map/ppermute | solution.py:656
  9.0 0.6 %shifted_reference.1.refs_2_ = bf16[2,2,128,1920]{3,2,1,0:T(8,128)(2,1)S(1)} custom-call(f32[2,16,128]{2,1,0:T(8,128)S(1)} %get-tuple-element.19.tiles_ref), custom_call_target="tpu_custom_call" | custom-call | flops 805000000 | tf_op jit(solution)/shard_map/shifted_reference/pallas_call | solution.py:243
  9.6 3.3 %collective-permute-done.3.refs_1_.second_ref.refs_2_ = f32[2,2,16,128]{3,2,1,0:T(8,128)S(1)} collective-permute-done((f32[2,2,16,128]{3,2,1,0:T(8,128)S(1)}, f32[2,2,16,128]{3,2,1,0:T(8,128)S(1)}, u32[]{:S(2)}, u32[]{:S(2)}) %collective-permute-start.3) | collective-permute-done | bytes 32800 | tf_op jit(solution)/shard_map/ppermute | solution.py:656
  12.9 1.0 %collective-permute-start.4 = (f32[4,2,16,128]{3,2,1,0:T(8,128)S(1)}, f32[4,2,16,128]{3,2,1,0:T(8,128)S(1)}, u32[]{:S(2)}, u32[]{:S(2)}) collective-permute-start(f32[4,2,16,128]{3,2,1,0:T(8,128)S(1)} %reference_joined.3.refs_4_), channel_id=1, source_target_pairs={{0,4},{1,5},{2,6},{3,7},{4,0},{5,1},{6,2},{7,3},{8,12},{9,13},{10,... | collective-permute-start | bytes 196616 | tf_op jit(solution)/shard_map/ppermute | solution.py:656
  13.9 0.2 shifted_first.1.refs_3_
  14.1 0.0 collective-permute-done.1
  14.1 1.6 %lag_products.1.refs_4_ = f32[8,10,8,128]{3,2,1,0:T(8,128)} custom-call(f32[32,2048]{1,0:T(8,128)S(1)} %bitcast.9, f32[32,2048]{1,0:T(8,128)S(1)} %bitcast.10, bf16[2,2,128,1920]{3,2,1,0:T(8,128)(2,1)S(1)} %shifted_reference.1.refs_2_, bf16[2,2,128,256]{3,2,1,0:T(8,128)(2,1)S(1)} %shifted_first.1.refs_3_, f32[4,2,16,128]{3,2,1,0:T(8,128)S(1)} %reference_joined.3.refs_4_), custom_call_target="tpu_custom_call" | custom-call | flops 2415000064 | tf_op jit(solution)/shard_map/lag_products/pallas_call | solution.py:350
  15.7 5.7 %all-to-all-start = ((f32[8,10,8,128]{3,2,1,0:T(8,128)}), f32[8,10,8,128]{3,2,1,0:T(8,128)S(1)}, u32[]{:S(2)}, u32[]{:S(2)}) async-start(f32[8,10,8,128]{3,2,1,0:T(8,128)} %lag_products.1.refs_4_), calls=%async_computation | async-start | bytes 655360 | tf_op jit(solution)/shard_map/all_to_all | solution.py:663
  21.4 0.0 collective-permute-done.4.refs_3_
  21.4 6.5 %reference_products.1 = (bf16[3,2048,128]{2,1,0:T(8,128)(2,1)S(1)}, f32[8,128]{1,0:T(8,128)S(1)}, f32[128,128]{1,0:T(8,128)S(1)}) custom-call(f32[1,2,16,128]{3,2,1,0:T(8,128)S(1)} %bitcast.13, f32[1,2,16,128]{3,2,1,0:T(8,128)S(1)} %collective-permute-done.2.second_ref.refs_0_.refs_1_, ...), custom_call_target="tpu_custom_call" | custom-call | flops 7129999872 | tf_op jit(solution)/shard_map/reference_products/pallas_call | solution.py:462
  27.9 0.0 copy-start
  28.0 2.5 %gram_inverse.1 = (bf16[768,128]{1,0:T(8,128)(2,1)S(1)}, bf16[768,128]{1,0:T(8,128)(2,1)S(1)}) custom-call(f32[8,128]{1,0:T(8,128)S(1)} %get-tuple-element.21.line_ref, f32[128,128]{1,0:T(8,128)S(1)} %get-tuple-element.22.tail_ref), custom_call_target="tpu_custom_call" | custom-call | flops 2300000000 | tf_op jit(solution)/shard_map/gram_inverse/pallas_call | solution.py:538
  30.4 0.8 %all-to-all-done.got_ref = f32[8,10,8,128]{3,2,1,0:T(8,128)S(1)} async-done(((f32[8,10,8,128]{3,2,1,0:T(8,128)}), f32[8,10,8,128]{3,2,1,0:T(8,128)S(1)}, u32[]{:S(2)}, u32[]{:S(2)}) %all-to-all-start) | async-done | bytes 327712 | tf_op jit(solution)/shard_map/all_to_all | solution.py:663
  31.2 0.0 copy-done
  31.2 2.5 %range_doppler.1 = f32[4,4,2,32,256]{4,3,2,1,0:T(8,128)} custom-call(f32[8,10,8,128]{3,2,1,0:T(8,128)S(1)} %all-to-all-done.got_ref, bf16[3,2048,128]{2,1,0:T(8,128)(2,1)S(1)} %get-tuple-element.20.own_ref, bf16[768,128]{1,0:T(8,128)(2,1)S(1)} %get-tuple-element.23.gram_ref, bf16[768,128]{1,0:T(8,128)(2,1)S(1)} %get-tuple-element.24.solver_ref, ...), custom_call_target="tpu_custom_call" | custom-call | flops 2875000064 | tf_op jit(solution)/shard_map/range_doppler/pallas_call | solution.py:612
  (2 shorter events, 0.0 us)
Async XLA Ops:
  2.1 3.1 %collective-permute-start = (f32[64,2048]{1,0:T(8,128)S(1)}, f32[64,2048]{1,0:T(8,128)S(1)}, u32[]{:S(2)}, u32[]{:S(2)}) collective-permute-start(f32[64,2048]{1,0:T(8,128)S(1)} %get-tuple-element.16), channel_id=1, source_target_pairs={{0,8},{8,0},{16,24},{24,16},{1,9},{9,1},{17,25},{25,17},{2,10},{10... | collective-permute-start | bytes 1572872 | tf_op jit(solution)/shard_map/ppermute | solution.py:631
  2.6 4.5 %collective-permute-start.2 = (f32[1,2,16,128]{3,2,1,0:T(8,128)S(1)}, f32[1,2,16,128]{3,2,1,0:T(8,128)S(1)}, u32[]{:S(2)}, u32[]{:S(2)}) collective-permute-start(f32[1,2,16,128]{3,2,1,0:T(8,128)S(1)} %bitcast.11), channel_id=1, source_target_pairs={{0,1},{1,0},{2,3},{3,2},{4,5},{5,4},{6,7},{7,6},{8,9},{9,8},{10,11... | collective-permute-start | bytes 49160 | tf_op jit(solution)/shard_map/ppermute | solution.py:631
  5.3 8.9 %collective-permute-start.1 = (f32[1,32,2048]{2,1,0:T(8,128)S(1)}, f32[1,32,2048]{2,1,0:T(8,128)S(1)}, u32[]{:S(2)}, u32[]{:S(2)}) collective-permute-start(f32[1,32,2048]{2,1,0:T(8,128)S(1)} %get-tuple-element.18.refs_0_), channel_id=1, source_target_pairs={{0,16},{8,24},{16,0},{24,8},{1,17},{9,25},{17,1},{25,9},{2,18},{10... | collective-permute-start | bytes 786440 | tf_op jit(solution)/shard_map/ppermute | solution.py:631
  7.2 5.8 %collective-permute-start.3 = (f32[2,2,16,128]{3,2,1,0:T(8,128)S(1)}, f32[2,2,16,128]{3,2,1,0:T(8,128)S(1)}, u32[]{:S(2)}, u32[]{:S(2)}) collective-permute-start(f32[2,2,16,128]{3,2,1,0:T(8,128)S(1)} %reference_joined.2.first_ref), channel_id=1, source_target_pairs={{0,2},{1,3},{2,4},{3,5},{4,6},{5,7},{6,0},{7,1},{8,10},{9,11},{10,... | collective-permute-start | bytes 98312 | tf_op jit(solution)/shard_map/ppermute | solution.py:656
  12.9 8.5 %collective-permute-start.4 = (f32[4,2,16,128]{3,2,1,0:T(8,128)S(1)}, f32[4,2,16,128]{3,2,1,0:T(8,128)S(1)}, u32[]{:S(2)}, u32[]{:S(2)}) collective-permute-start(f32[4,2,16,128]{3,2,1,0:T(8,128)S(1)} %reference_joined.3.refs_4_), channel_id=1, source_target_pairs={{0,4},{1,5},{2,6},{3,7},{4,0},{5,1},{6,2},{7,3},{8,12},{9,13},{10,... | collective-permute-start | bytes 196616 | tf_op jit(solution)/shard_map/ppermute | solution.py:656
  15.7 15.4 %all-to-all-start = ((f32[8,10,8,128]{3,2,1,0:T(8,128)}), f32[8,10,8,128]{3,2,1,0:T(8,128)S(1)}, u32[]{:S(2)}, u32[]{:S(2)}) async-start(f32[8,10,8,128]{3,2,1,0:T(8,128)} %lag_products.1.refs_4_), calls=%async_computation | async-start | bytes 655360 | tf_op jit(solution)/shard_map/all_to_all | solution.py:663
  27.9 3.2 %copy-start = (bf16[2,128,512]{2,1,0:T(8,128)(2,1)S(1)}, bf16[2,128,512]{2,1,0:T(8,128)(2,1)}, u32[]{:S(2)}) copy-start(bf16[2,128,512]{2,1,0:T(8,128)(2,1)} %constant.2.clone.wave_ref) | copy-start | bytes 786436

commit v27 on v26

--- a/solution.py
+++ b/solution.py
@@ -142,7 +142,12 @@
             tiles_ref[c, n : n + 1, :] = ref_ref[c : c + 1, n * LANES : (n + 1) * LANES]
     for copy in s_copies:
         copy.wait()
-    product = dot_parts(weights, thirds(s_ref[...]))
+    high, mid, low = thirds(s_ref[...])
+    twice = jnp.concatenate([jnp.concatenate([part, part], 1) for part in weights], 0)
+    product = jnp.dot(twice, jnp.concatenate([high, mid], 0), preferred_element_type=jnp.float32)
+    least = jnp.dot(weights[0], low, preferred_element_type=jnp.float32)
+    count = least.shape[0]
+    product = product[:count] + (product[count:] + least)
     mid = product.shape[0] // 2
     kept_ref[...] = product[:mid]
     sent_ref[...] = product[mid:]
@@ -579,9 +584,14 @@
     taps = exact(cross, solver_ref)
     taps = taps + exact(cross - exact(taps, gram_ref), solver_ref)
     taps = thirds(taps)
+    count = taps[0].shape[0]
+    twice = [jnp.concatenate([part, part], 1) for part in taps[:2]]
+    twice = jnp.concatenate(twice + [jnp.concatenate([taps[2], jnp.zeros_like(taps[2])], 1)], 0)
     for q in range(0, total, 2 * groups):
         own = slice(q * lags_local, (q + 2 * groups) * lags_local)
-        clutter = dot_parts(taps, [own_ref[part, own, :] for part in range(3)], True)
+        by_part = dot_nt(twice, jnp.concatenate([own_ref[0, own, :], own_ref[1, own, :]], 1))
+        least = by_part[2 * count :] + dot_nt(taps[0], own_ref[2, own, :])
+        clutter = by_part[:count] + (by_part[count : 2 * count] + least)
         for h in range(2):
             lanes = slice(h * LANES, (h + 1) * LANES)
             tiles = [clutter[r : r + SUBLANES, lanes] for r in range(0, groups * SUBLANES, SUBLANES)]

time: 33.9 us -> 33.6 us (level)
  Pallas kernels: 16 us -> 15.4 us
  transfers between devices with their start and end apart: 6 -> 6, of which waited for: 2 -> 2; matrix products, arithmetic and copies ran while one was open for 0% -> 0% of each run, Pallas kernels for 34% -> 33%
where the time goes in v27:
time: 33.6 us; the launch traced here: 33.4 us
  Pallas kernels  15.4 us (46%)
  starting transfers between devices  13.5 us (40%)
  waiting for transfers between devices  4.34 us (13%)
    pallas_call x1, Pallas kernels, own_call(): pl.pallas_call(functools.partial(own_kernel, lags_local), in_specs=[pl.Bl...  6.49 us
    all_to_all x1, starting transfers between devices, tiled_device(): got = lax.all_to_all(pieces, 'tm', 0, 0, tiled=True)  5.7 us
    ppermute x3, starting transfers between devices, swap(): return lax.ppermute(x, axis, pairs)  4.98 us
    ppermute x2, waiting for transfers between devices, tiled_device(): lax.ppermute(joined, 'tm', [(i, (i + count) % tm_count) for i in range(tm...  3.3 us
    ppermute x2, starting transfers between devices, tiled_device(): lax.ppermute(joined, 'tm', [(i, (i + count) % tm_count) for i in range(tm...  2.87 us
    pallas_call x1, Pallas kernels, map_call(): pl.pallas_call(functools.partial(map_kernel, groups), in_specs=[pl.BlockS...  2.42 us
    pallas_call x1, Pallas kernels, solver_call(): pl.pallas_call(solver_kernel, out_shape=[jax.ShapeDtypeStruct((len(PART_P...  2.2 us
    pallas_call x1, Pallas kernels, beam_call(): pl.pallas_call(functools.partial(beam_kernel, chan_count, beams_local), i...  1.85 us
  transfers between devices with their start and end apart: 6, of which 2 were waited for; matrix products, arithmetic and copies ran while one was open for 0% of the time, Pallas kernels for 33%

profile of v27, /device:TPU:0, one launch (start us, length us, event | category | flops | bytes accessed | tf_op | source)
XLA Modules:
  0.0 33.4 jit_solution(5252635389576569819)
XLA Ops:
  0.0 1.9 %beams.1 = (f32[64,2048]{1,0:T(8,128)S(1)}, f32[64,2048]{1,0:T(8,128)S(1)}, f32[2,16,128]{2,1,0:T(8,128)S(1)}) custom-call(f32[2,64,64]{2,1,0:T(8,128)} %w_hbm.1, f32[128,2048]{1,0:T(8,128)} %bitcast.14, f32[2,2048]{1,0:T(2,128)} %ref_hbm.1), custom_call_target="tpu_custom_call" | custom-call | flops 2529999872 | tf_op jit(solution)/shard_map/beams/pallas_call | solution.py:162
  1.9 0.5 %collective-permute-start = (f32[64,2048]{1,0:T(8,128)S(1)}, f32[64,2048]{1,0:T(8,128)S(1)}, u32[]{:S(2)}, u32[]{:S(2)}) collective-permute-start(f32[64,2048]{1,0:T(8,128)S(1)} %get-tuple-element.16), channel_id=1, source_target_pairs={{0,8},{8,0},{16,24},{24,16},{1,9},{9,1},{17,25},{25,17},{2,10},{10... | collective-permute-start | bytes 1572872 | tf_op jit(solution)/shard_map/ppermute | solution.py:641
  2.4 2.6 %collective-permute-start.2 = (f32[1,2,16,128]{3,2,1,0:T(8,128)S(1)}, f32[1,2,16,128]{3,2,1,0:T(8,128)S(1)}, u32[]{:S(2)}, u32[]{:S(2)}) collective-permute-start(f32[1,2,16,128]{3,2,1,0:T(8,128)S(1)} %bitcast.11), channel_id=1, source_target_pairs={{0,1},{1,0},{2,3},{3,2},{4,5},{5,4},{6,7},{7,6},{8,9},{9,8},{10,11... | collective-permute-start | bytes 49160 | tf_op jit(solution)/shard_map/ppermute | solution.py:641
  5.0 0.0 collective-permute-done
  5.0 0.1 halves_summed.1
  5.0 1.9 %collective-permute-start.1 = (f32[1,32,2048]{2,1,0:T(8,128)S(1)}, f32[1,32,2048]{2,1,0:T(8,128)S(1)}, u32[]{:S(2)}, u32[]{:S(2)}) collective-permute-start(f32[1,32,2048]{2,1,0:T(8,128)S(1)} %get-tuple-element.18.refs_0_), channel_id=1, source_target_pairs={{0,16},{8,24},{16,0},{24,8},{1,17},{9,25},{17,1},{25,9},{2,18},{10... | collective-permute-start | bytes 786440 | tf_op jit(solution)/shard_map/ppermute | solution.py:641
  6.9 0.0 collective-permute-done.2.second_ref.refs_0_.refs_1_
  6.9 1.9 %collective-permute-start.3 = (f32[2,2,16,128]{3,2,1,0:T(8,128)S(1)}, f32[2,2,16,128]{3,2,1,0:T(8,128)S(1)}, u32[]{:S(2)}, u32[]{:S(2)}) collective-permute-start(f32[2,2,16,128]{3,2,1,0:T(8,128)S(1)} %reference_joined.2.first_ref), channel_id=1, source_target_pairs={{0,2},{1,3},{2,4},{3,5},{4,6},{5,7},{6,0},{7,1},{8,10},{9,11},{10,... | collective-permute-start | bytes 98312 | tf_op jit(solution)/shard_map/ppermute | solution.py:666
  8.8 0.6 %shifted_reference.1.refs_2_ = bf16[2,2,128,1920]{3,2,1,0:T(8,128)(2,1)S(1)} custom-call(f32[2,16,128]{2,1,0:T(8,128)S(1)} %get-tuple-element.19.tiles_ref), custom_call_target="tpu_custom_call" | custom-call | flops 805000000 | tf_op jit(solution)/shard_map/shifted_reference/pallas_call | solution.py:248
  9.4 3.3 %collective-permute-done.3.refs_1_.second_ref.refs_2_ = f32[2,2,16,128]{3,2,1,0:T(8,128)S(1)} collective-permute-done((f32[2,2,16,128]{3,2,1,0:T(8,128)S(1)}, f32[2,2,16,128]{3,2,1,0:T(8,128)S(1)}, u32[]{:S(2)}, u32[]{:S(2)}) %collective-permute-start.3) | collective-permute-done | bytes 32800 | tf_op jit(solution)/shard_map/ppermute | solution.py:666
  12.7 1.0 %collective-permute-start.4 = (f32[4,2,16,128]{3,2,1,0:T(8,128)S(1)}, f32[4,2,16,128]{3,2,1,0:T(8,128)S(1)}, u32[]{:S(2)}, u32[]{:S(2)}) collective-permute-start(f32[4,2,16,128]{3,2,1,0:T(8,128)S(1)} %reference_joined.3.refs_4_), channel_id=1, source_target_pairs={{0,4},{1,5},{2,6},{3,7},{4,0},{5,1},{6,2},{7,3},{8,12},{9,13},{10,... | collective-permute-start | bytes 196616 | tf_op jit(solution)/shard_map/ppermute | solution.py:666
  13.7 0.2 shifted_first.1.refs_3_
  13.9 0.0 collective-permute-done.1
  13.9 1.6 %lag_products.1.refs_4_ = f32[8,10,8,128]{3,2,1,0:T(8,128)} custom-call(f32[32,2048]{1,0:T(8,128)S(1)} %bitcast.9, f32[32,2048]{1,0:T(8,128)S(1)} %bitcast.10, bf16[2,2,128,1920]{3,2,1,0:T(8,128)(2,1)S(1)} %shifted_reference.1.refs_2_, bf16[2,2,128,256]{3,2,1,0:T(8,128)(2,1)S(1)} %shifted_first.1.refs_3_, f32[4,2,16,128]{3,2,1,0:T(8,128)S(1)} %reference_joined.3.refs_4_), custom_call_target="tpu_custom_call" | custom-call | flops 2415000064 | tf_op jit(solution)/shard_map/lag_products/pallas_call | solution.py:355
  15.5 5.7 %all-to-all-start = ((f32[8,10,8,128]{3,2,1,0:T(8,128)}), f32[8,10,8,128]{3,2,1,0:T(8,128)S(1)}, u32[]{:S(2)}, u32[]{:S(2)}) async-start(f32[8,10,8,128]{3,2,1,0:T(8,128)} %lag_products.1.refs_4_), calls=%async_computation | async-start | bytes 655360 | tf_op jit(solution)/shard_map/all_to_all | solution.py:673
  21.2 0.0 collective-permute-done.4.refs_3_
  21.2 6.5 %reference_products.1 = (bf16[3,2048,128]{2,1,0:T(8,128)(2,1)S(1)}, f32[8,128]{1,0:T(8,128)S(1)}, f32[128,128]{1,0:T(8,128)S(1)}) custom-call(f32[1,2,16,128]{3,2,1,0:T(8,128)S(1)} %bitcast.13, f32[1,2,16,128]{3,2,1,0:T(8,128)S(1)} %collective-permute-done.2.second_ref.refs_0_.refs_1_, ...), custom_call_target="tpu_custom_call" | custom-call | flops 7129999872 | tf_op jit(solution)/shard_map/reference_products/pallas_call | solution.py:467
  27.7 0.0 copy-start
  27.7 2.2 %gram_inverse.1 = (bf16[768,128]{1,0:T(8,128)(2,1)S(1)}, bf16[768,128]{1,0:T(8,128)(2,1)S(1)}) custom-call(f32[8,128]{1,0:T(8,128)S(1)} %get-tuple-element.21.line_ref, f32[128,128]{1,0:T(8,128)S(1)} %get-tuple-element.22.tail_ref), custom_call_target="tpu_custom_call" | custom-call | flops 2300000000 | tf_op jit(solution)/shard_map/gram_inverse/pallas_call | solution.py:543
  29.9 1.0 %all-to-all-done.got_ref = f32[8,10,8,128]{3,2,1,0:T(8,128)S(1)} async-done(((f32[8,10,8,128]{3,2,1,0:T(8,128)}), f32[8,10,8,128]{3,2,1,0:T(8,128)S(1)}, u32[]{:S(2)}, u32[]{:S(2)}) %all-to-all-start) | async-done | bytes 327712 | tf_op jit(solution)/shard_map/all_to_all | solution.py:673
  30.9 0.0 copy-done
  30.9 2.4 %range_doppler.1 = f32[4,4,2,32,256]{4,3,2,1,0:T(8,128)} custom-call(f32[8,10,8,128]{3,2,1,0:T(8,128)S(1)} %all-to-all-done.got_ref, bf16[3,2048,128]{2,1,0:T(8,128)(2,1)S(1)} %get-tuple-element.20.own_ref, bf16[768,128]{1,0:T(8,128)(2,1)S(1)} %get-tuple-element.23.gram_ref, bf16[768,128]{1,0:T(8,128)(2,1)S(1)} %get-tuple-element.24.solver_ref, ...), custom_call_target="tpu_custom_call" | custom-call | flops 2875000064 | tf_op jit(solution)/shard_map/range_doppler/pallas_call | solution.py:622
  (2 shorter events, 0.0 us)
Async XLA Ops:
  1.9 3.1 %collective-permute-start = (f32[64,2048]{1,0:T(8,128)S(1)}, f32[64,2048]{1,0:T(8,128)S(1)}, u32[]{:S(2)}, u32[]{:S(2)}) collective-permute-start(f32[64,2048]{1,0:T(8,128)S(1)} %get-tuple-element.16), channel_id=1, source_target_pairs={{0,8},{8,0},{16,24},{24,16},{1,9},{9,1},{17,25},{25,17},{2,10},{10... | collective-permute-start | bytes 1572872 | tf_op jit(solution)/shard_map/ppermute | solution.py:641
  2.4 4.5 %collective-permute-start.2 = (f32[1,2,16,128]{3,2,1,0:T(8,128)S(1)}, f32[1,2,16,128]{3,2,1,0:T(8,128)S(1)}, u32[]{:S(2)}, u32[]{:S(2)}) collective-permute-start(f32[1,2,16,128]{3,2,1,0:T(8,128)S(1)} %bitcast.11), channel_id=1, source_target_pairs={{0,1},{1,0},{2,3},{3,2},{4,5},{5,4},{6,7},{7,6},{8,9},{9,8},{10,11... | collective-permute-start | bytes 49160 | tf_op jit(solution)/shard_map/ppermute | solution.py:641
  5.0 8.8 %collective-permute-start.1 = (f32[1,32,2048]{2,1,0:T(8,128)S(1)}, f32[1,32,2048]{2,1,0:T(8,128)S(1)}, u32[]{:S(2)}, u32[]{:S(2)}) collective-permute-start(f32[1,32,2048]{2,1,0:T(8,128)S(1)} %get-tuple-element.18.refs_0_), channel_id=1, source_target_pairs={{0,16},{8,24},{16,0},{24,8},{1,17},{9,25},{17,1},{25,9},{2,18},{10... | collective-permute-start | bytes 786440 | tf_op jit(solution)/shard_map/ppermute | solution.py:641
  6.9 5.8 %collective-permute-start.3 = (f32[2,2,16,128]{3,2,1,0:T(8,128)S(1)}, f32[2,2,16,128]{3,2,1,0:T(8,128)S(1)}, u32[]{:S(2)}, u32[]{:S(2)}) collective-permute-start(f32[2,2,16,128]{3,2,1,0:T(8,128)S(1)} %reference_joined.2.first_ref), channel_id=1, source_target_pairs={{0,2},{1,3},{2,4},{3,5},{4,6},{5,7},{6,0},{7,1},{8,10},{9,11},{10,... | collective-permute-start | bytes 98312 | tf_op jit(solution)/shard_map/ppermute | solution.py:666
  12.7 8.5 %collective-permute-start.4 = (f32[4,2,16,128]{3,2,1,0:T(8,128)S(1)}, f32[4,2,16,128]{3,2,1,0:T(8,128)S(1)}, u32[]{:S(2)}, u32[]{:S(2)}) collective-permute-start(f32[4,2,16,128]{3,2,1,0:T(8,128)S(1)} %reference_joined.3.refs_4_), channel_id=1, source_target_pairs={{0,4},{1,5},{2,6},{3,7},{4,0},{5,1},{6,2},{7,3},{8,12},{9,13},{10,... | collective-permute-start | bytes 196616 | tf_op jit(solution)/shard_map/ppermute | solution.py:666
  15.5 15.4 %all-to-all-start = ((f32[8,10,8,128]{3,2,1,0:T(8,128)}), f32[8,10,8,128]{3,2,1,0:T(8,128)S(1)}, u32[]{:S(2)}, u32[]{:S(2)}) async-start(f32[8,10,8,128]{3,2,1,0:T(8,128)} %lag_products.1.refs_4_), calls=%async_computation | async-start | bytes 655360 | tf_op jit(solution)/shard_map/all_to_all | solution.py:673
  27.7 3.2 %copy-start = (bf16[2,128,512]{2,1,0:T(8,128)(2,1)S(1)}, bf16[2,128,512]{2,1,0:T(8,128)(2,1)}, u32[]{:S(2)}) copy-start(bf16[2,128,512]{2,1,0:T(8,128)(2,1)} %constant.2.clone.wave_ref) | copy-start | bytes 786436

commit v28 on v27

--- a/solution.py
+++ b/solution.py
@@ -599,11 +599,12 @@
                 at = q + h * groups + j
                 held_ref[at * SUBLANES : (at + 1) * SUBLANES, :] = got_ref[at // blocks, at % blocks] - tile
     half = SUBLANES // 2
-    wave = (wave_ref[0], wave_ref[1])
     copies = []
     for g in range(half):
         parts = [held_ref[pl.ds(c * half + g, total, stride=SUBLANES), :] for c in range(2)]
-        spectrum = dot_split(halves(jnp.concatenate(parts, 0).T), wave)
+        high, low = halves(jnp.concatenate(parts, 0).T)
+        spectrum = jnp.dot(jnp.concatenate([high, high], 1), wave_ref[...], preferred_element_type=jnp.float32)
+        spectrum = spectrum + jnp.dot(low, wave_ref[: low.shape[1]], preferred_element_type=jnp.float32)
         for i in range(groups):
             for c in range(2):
                 out_ref[i, g, c] = spectrum[i * lags_local : (i + 1) * lags_local, c * DOPPLER : (c + 1) * DOPPLER]
@@ -675,7 +676,7 @@
     gram, solver = solver_call(line, tail)
     wave = doppler_table(samples // BLOCK_LEN, 0.125 / math.sqrt(samples))
     high = wave.astype(jnp.bfloat16)
-    wave = np.stack([high, (wave - high.astype(np.float32)).astype(jnp.bfloat16)])
+    wave = np.concatenate([high, (wave - high.astype(np.float32)).astype(jnp.bfloat16)], 0)
     return map_call(got, own, gram, solver, jnp.asarray(wave), groups, beams_local)
 
 

time: 33.6 us -> 33.6 us (level)
  transfers between devices with their start and end apart: 6 -> 6, of which waited for: 2 -> 2; matrix products, arithmetic and copies ran while one was open for 0% -> 0% of each run, Pallas kernels for 33% -> 34%
where the time goes in v28:
time: 33.6 us; the launch traced here: 33.4 us
  Pallas kernels  15.7 us (47%)
  starting transfers between devices  13.6 us (40%)
  waiting for transfers between devices  4.07 us (12%)
    pallas_call x1, Pallas kernels, own_call(): pl.pallas_call(functools.partial(own_kernel, lags_local), in_specs=[pl.Bl...  6.49 us
    all_to_all x1, starting transfers between devices, tiled_device(): got = lax.all_to_all(pieces, 'tm', 0, 0, tiled=True)  5.7 us
    ppermute x3, starting transfers between devices, swap(): return lax.ppermute(x, axis, pairs)  4.98 us
    ppermute x2, waiting for transfers between devices, tiled_device(): lax.ppermute(joined, 'tm', [(i, (i + count) % tm_count) for i in range(tm...  3.3 us
    ppermute x2, starting transfers between devices, tiled_device(): lax.ppermute(joined, 'tm', [(i, (i + count) % tm_count) for i in range(tm...  2.87 us
    pallas_call x1, Pallas kernels, solver_call(): pl.pallas_call(solver_kernel, out_shape=[jax.ShapeDtypeStruct((len(PART_P...  2.47 us
    pallas_call x1, Pallas kernels, map_call(): pl.pallas_call(functools.partial(map_kernel, groups), in_specs=[pl.BlockS...  2.43 us
    pallas_call x1, Pallas kernels, beam_call(): pl.pallas_call(functools.partial(beam_kernel, chan_count, beams_local), i...  1.85 us
  transfers between devices with their start and end apart: 6, of which 2 were waited for; matrix products, arithmetic and copies ran while one was open for 0% of the time, Pallas kernels for 34%

profile of v28, /device:TPU:0, one launch (start us, length us, event | category | flops | bytes accessed | tf_op | source)
XLA Modules:
  0.0 33.4 jit_solution(15603920488015855033)
XLA Ops:
  0.0 1.9 %beams.1 = (f32[64,2048]{1,0:T(8,128)S(1)}, f32[64,2048]{1,0:T(8,128)S(1)}, f32[2,16,128]{2,1,0:T(8,128)S(1)}) custom-call(f32[2,64,64]{2,1,0:T(8,128)} %w_hbm.1, f32[128,2048]{1,0:T(8,128)} %bitcast.14, f32[2,2048]{1,0:T(2,128)} %ref_hbm.1), custom_call_target="tpu_custom_call" | custom-call | flops 2529999872 | tf_op jit(solution)/shard_map/beams/pallas_call | solution.py:162
  1.9 0.5 %collective-permute-start = (f32[64,2048]{1,0:T(8,128)S(1)}, f32[64,2048]{1,0:T(8,128)S(1)}, u32[]{:S(2)}, u32[]{:S(2)}) collective-permute-start(f32[64,2048]{1,0:T(8,128)S(1)} %get-tuple-element.16), channel_id=1, source_target_pairs={{0,8},{8,0},{16,24},{24,16},{1,9},{9,1},{17,25},{25,17},{2,10},{10... | collective-permute-start | bytes 1572872 | tf_op jit(solution)/shard_map/ppermute | solution.py:642
  2.4 2.6 %collective-permute-start.2 = (f32[1,2,16,128]{3,2,1,0:T(8,128)S(1)}, f32[1,2,16,128]{3,2,1,0:T(8,128)S(1)}, u32[]{:S(2)}, u32[]{:S(2)}) collective-permute-start(f32[1,2,16,128]{3,2,1,0:T(8,128)S(1)} %bitcast.11), channel_id=1, source_target_pairs={{0,1},{1,0},{2,3},{3,2},{4,5},{5,4},{6,7},{7,6},{8,9},{9,8},{10,11... | collective-permute-start | bytes 49160 | tf_op jit(solution)/shard_map/ppermute | solution.py:642
  5.0 0.0 collective-permute-done
  5.0 0.1 halves_summed.1
  5.0 1.9 %collective-permute-start.1 = (f32[1,32,2048]{2,1,0:T(8,128)S(1)}, f32[1,32,2048]{2,1,0:T(8,128)S(1)}, u32[]{:S(2)}, u32[]{:S(2)}) collective-permute-start(f32[1,32,2048]{2,1,0:T(8,128)S(1)} %get-tuple-element.18.refs_0_), channel_id=1, source_target_pairs={{0,16},{8,24},{16,0},{24,8},{1,17},{9,25},{17,1},{25,9},{2,18},{10... | collective-permute-start | bytes 786440 | tf_op jit(solution)/shard_map/ppermute | solution.py:642
  6.9 0.0 collective-permute-done.2.second_ref.refs_0_.refs_1_
  6.9 1.9 %collective-permute-start.3 = (f32[2,2,16,128]{3,2,1,0:T(8,128)S(1)}, f32[2,2,16,128]{3,2,1,0:T(8,128)S(1)}, u32[]{:S(2)}, u32[]{:S(2)}) collective-permute-start(f32[2,2,16,128]{3,2,1,0:T(8,128)S(1)} %reference_joined.2.first_ref), channel_id=1, source_target_pairs={{0,2},{1,3},{2,4},{3,5},{4,6},{5,7},{6,0},{7,1},{8,10},{9,11},{10,... | collective-permute-start | bytes 98312 | tf_op jit(solution)/shard_map/ppermute | solution.py:667
  8.8 0.6 %shifted_reference.1.refs_2_ = bf16[2,2,128,1920]{3,2,1,0:T(8,128)(2,1)S(1)} custom-call(f32[2,16,128]{2,1,0:T(8,128)S(1)} %get-tuple-element.19.tiles_ref), custom_call_target="tpu_custom_call" | custom-call | flops 805000000 | tf_op jit(solution)/shard_map/shifted_reference/pallas_call | solution.py:248
  9.4 3.3 %collective-permute-done.3.refs_1_.second_ref.refs_2_ = f32[2,2,16,128]{3,2,1,0:T(8,128)S(1)} collective-permute-done((f32[2,2,16,128]{3,2,1,0:T(8,128)S(1)}, f32[2,2,16,128]{3,2,1,0:T(8,128)S(1)}, u32[]{:S(2)}, u32[]{:S(2)}) %collective-permute-start.3) | collective-permute-done | bytes 32800 | tf_op jit(solution)/shard_map/ppermute | solution.py:667
  12.7 1.0 %collective-permute-start.4 = (f32[4,2,16,128]{3,2,1,0:T(8,128)S(1)}, f32[4,2,16,128]{3,2,1,0:T(8,128)S(1)}, u32[]{:S(2)}, u32[]{:S(2)}) collective-permute-start(f32[4,2,16,128]{3,2,1,0:T(8,128)S(1)} %reference_joined.3.refs_4_), channel_id=1, source_target_pairs={{0,4},{1,5},{2,6},{3,7},{4,0},{5,1},{6,2},{7,3},{8,12},{9,13},{10,... | collective-permute-start | bytes 196616 | tf_op jit(solution)/shard_map/ppermute | solution.py:667
  13.7 0.2 shifted_first.1.refs_3_
  13.9 0.0 collective-permute-done.1
  13.9 1.6 %lag_products.1.refs_4_ = f32[8,10,8,128]{3,2,1,0:T(8,128)} custom-call(f32[32,2048]{1,0:T(8,128)S(1)} %bitcast.9, f32[32,2048]{1,0:T(8,128)S(1)} %bitcast.10, bf16[2,2,128,1920]{3,2,1,0:T(8,128)(2,1)S(1)} %shifted_reference.1.refs_2_, bf16[2,2,128,256]{3,2,1,0:T(8,128)(2,1)S(1)} %shifted_first.1.refs_3_, f32[4,2,16,128]{3,2,1,0:T(8,128)S(1)} %reference_joined.3.refs_4_), custom_call_target="tpu_custom_call" | custom-call | flops 2415000064 | tf_op jit(solution)/shard_map/lag_products/pallas_call | solution.py:355
  15.5 5.7 %all-to-all-start = ((f32[8,10,8,128]{3,2,1,0:T(8,128)}), f32[8,10,8,128]{3,2,1,0:T(8,128)S(1)}, u32[]{:S(2)}, u32[]{:S(2)}) async-start(f32[8,10,8,128]{3,2,1,0:T(8,128)} %lag_products.1.refs_4_), calls=%async_computation | async-start | bytes 655360 | tf_op jit(solution)/shard_map/all_to_all | solution.py:674
  21.2 0.0 collective-permute-done.4.refs_3_
  21.2 6.5 %reference_products.1 = (bf16[3,2048,128]{2,1,0:T(8,128)(2,1)S(1)}, f32[8,128]{1,0:T(8,128)S(1)}, f32[128,128]{1,0:T(8,128)S(1)}) custom-call(f32[1,2,16,128]{3,2,1,0:T(8,128)S(1)} %bitcast.13, f32[1,2,16,128]{3,2,1,0:T(8,128)S(1)} %collective-permute-done.2.second_ref.refs_0_.refs_1_, ...), custom_call_target="tpu_custom_call" | custom-call | flops 7129999872 | tf_op jit(solution)/shard_map/reference_products/pallas_call | solution.py:467
  27.7 0.0 copy-start
  27.7 2.5 %gram_inverse.1 = (bf16[768,128]{1,0:T(8,128)(2,1)S(1)}, bf16[768,128]{1,0:T(8,128)(2,1)S(1)}) custom-call(f32[8,128]{1,0:T(8,128)S(1)} %get-tuple-element.21.line_ref, f32[128,128]{1,0:T(8,128)S(1)} %get-tuple-element.22.tail_ref), custom_call_target="tpu_custom_call" | custom-call | flops 2300000000 | tf_op jit(solution)/shard_map/gram_inverse/pallas_call | solution.py:543
  30.2 0.8 %all-to-all-done.got_ref = f32[8,10,8,128]{3,2,1,0:T(8,128)S(1)} async-done(((f32[8,10,8,128]{3,2,1,0:T(8,128)}), f32[8,10,8,128]{3,2,1,0:T(8,128)S(1)}, u32[]{:S(2)}, u32[]{:S(2)}) %all-to-all-start) | async-done | bytes 327712 | tf_op jit(solution)/shard_map/all_to_all | solution.py:674
  30.9 0.0 copy-done
  30.9 2.4 %range_doppler.1 = f32[4,4,2,32,256]{4,3,2,1,0:T(8,128)} custom-call(f32[8,10,8,128]{3,2,1,0:T(8,128)S(1)} %all-to-all-done.got_ref, bf16[3,2048,128]{2,1,0:T(8,128)(2,1)S(1)} %get-tuple-element.20.own_ref, bf16[768,128]{1,0:T(8,128)(2,1)S(1)} %get-tuple-element.23.gram_ref, bf16[768,128]{1,0:T(8,128)(2,1)S(1)} %get-tuple-element.24.solver_ref, ...), custom_call_target="tpu_custom_call" | custom-call | flops 2875000064 | tf_op jit(solution)/shard_map/range_doppler/pallas_call | solution.py:623
  (2 shorter events, 0.0 us)
Async XLA Ops:
  1.9 3.1 %collective-permute-start = (f32[64,2048]{1,0:T(8,128)S(1)}, f32[64,2048]{1,0:T(8,128)S(1)}, u32[]{:S(2)}, u32[]{:S(2)}) collective-permute-start(f32[64,2048]{1,0:T(8,128)S(1)} %get-tuple-element.16), channel_id=1, source_target_pairs={{0,8},{8,0},{16,24},{24,16},{1,9},{9,1},{17,25},{25,17},{2,10},{10... | collective-permute-start | bytes 1572872 | tf_op jit(solution)/shard_map/ppermute | solution.py:642
  2.4 4.5 %collective-permute-start.2 = (f32[1,2,16,128]{3,2,1,0:T(8,128)S(1)}, f32[1,2,16,128]{3,2,1,0:T(8,128)S(1)}, u32[]{:S(2)}, u32[]{:S(2)}) collective-permute-start(f32[1,2,16,128]{3,2,1,0:T(8,128)S(1)} %bitcast.11), channel_id=1, source_target_pairs={{0,1},{1,0},{2,3},{3,2},{4,5},{5,4},{6,7},{7,6},{8,9},{9,8},{10,11... | collective-permute-start | bytes 49160 | tf_op jit(solution)/shard_map/ppermute | solution.py:642
  5.0 8.8 %collective-permute-start.1 = (f32[1,32,2048]{2,1,0:T(8,128)S(1)}, f32[1,32,2048]{2,1,0:T(8,128)S(1)}, u32[]{:S(2)}, u32[]{:S(2)}) collective-permute-start(f32[1,32,2048]{2,1,0:T(8,128)S(1)} %get-tuple-element.18.refs_0_), channel_id=1, source_target_pairs={{0,16},{8,24},{16,0},{24,8},{1,17},{9,25},{17,1},{25,9},{2,18},{10... | collective-permute-start | bytes 786440 | tf_op jit(solution)/shard_map/ppermute | solution.py:642
  6.9 5.8 %collective-permute-start.3 = (f32[2,2,16,128]{3,2,1,0:T(8,128)S(1)}, f32[2,2,16,128]{3,2,1,0:T(8,128)S(1)}, u32[]{:S(2)}, u32[]{:S(2)}) collective-permute-start(f32[2,2,16,128]{3,2,1,0:T(8,128)S(1)} %reference_joined.2.first_ref), channel_id=1, source_target_pairs={{0,2},{1,3},{2,4},{3,5},{4,6},{5,7},{6,0},{7,1},{8,10},{9,11},{10,... | collective-permute-start | bytes 98312 | tf_op jit(solution)/shard_map/ppermute | solution.py:667
  12.7 8.5 %collective-permute-start.4 = (f32[4,2,16,128]{3,2,1,0:T(8,128)S(1)}, f32[4,2,16,128]{3,2,1,0:T(8,128)S(1)}, u32[]{:S(2)}, u32[]{:S(2)}) collective-permute-start(f32[4,2,16,128]{3,2,1,0:T(8,128)S(1)} %reference_joined.3.refs_4_), channel_id=1, source_target_pairs={{0,4},{1,5},{2,6},{3,7},{4,0},{5,1},{6,2},{7,3},{8,12},{9,13},{10,... | collective-permute-start | bytes 196616 | tf_op jit(solution)/shard_map/ppermute | solution.py:667
  15.5 15.4 %all-to-all-start = ((f32[8,10,8,128]{3,2,1,0:T(8,128)}), f32[8,10,8,128]{3,2,1,0:T(8,128)S(1)}, u32[]{:S(2)}, u32[]{:S(2)}) async-start(f32[8,10,8,128]{3,2,1,0:T(8,128)} %lag_products.1.refs_4_), calls=%async_computation | async-start | bytes 655360 | tf_op jit(solution)/shard_map/all_to_all | solution.py:674
  27.7 3.2 %copy-start = (bf16[256,512]{1,0:T(8,128)(2,1)S(1)}, bf16[256,512]{1,0:T(8,128)(2,1)}, u32[]{:S(2)}) copy-start(bf16[256,512]{1,0:T(8,128)(2,1)} %constant.2.clone.wave_ref) | copy-start | bytes 786436

commit v29 on v28

--- a/solution.py
+++ b/solution.py
@@ -603,8 +603,9 @@
     for g in range(half):
         parts = [held_ref[pl.ds(c * half + g, total, stride=SUBLANES), :] for c in range(2)]
         high, low = halves(jnp.concatenate(parts, 0).T)
-        spectrum = jnp.dot(jnp.concatenate([high, high], 1), wave_ref[...], preferred_element_type=jnp.float32)
-        spectrum = spectrum + jnp.dot(low, wave_ref[: low.shape[1]], preferred_element_type=jnp.float32)
+        left_rows = [jnp.concatenate([high, high], 1), jnp.concatenate([low, jnp.zeros_like(low)], 1)]
+        by_part = jnp.dot(jnp.concatenate(left_rows, 0), wave_ref[...], preferred_element_type=jnp.float32)
+        spectrum = by_part[:LANES] + by_part[LANES:]
         for i in range(groups):
             for c in range(2):
                 out_ref[i, g, c] = spectrum[i * lags_local : (i + 1) * lags_local, c * DOPPLER : (c + 1) * DOPPLER]

time: 33.6 us -> 33.6 us (level)
  no operation moved by 1% of the time
where the time goes in v29:
time: 33.6 us; the launch traced here: 33.4 us
  Pallas kernels  15.7 us (47%)
  starting transfers between devices  13.5 us (40%)
  waiting for transfers between devices  4.07 us (12%)
    pallas_call x1, Pallas kernels, own_call(): pl.pallas_call(functools.partial(own_kernel, lags_local), in_specs=[pl.Bl...  6.49 us
    all_to_all x1, starting transfers between devices, tiled_device(): got = lax.all_to_all(pieces, 'tm', 0, 0, tiled=True)  5.7 us
    ppermute x3, starting transfers between devices, swap(): return lax.ppermute(x, axis, pairs)  4.98 us
    ppermute x2, waiting for transfers between devices, tiled_device(): lax.ppermute(joined, 'tm', [(i, (i + count) % tm_count) for i in range(tm...  3.3 us
    ppermute x2, starting transfers between devices, tiled_device(): lax.ppermute(joined, 'tm', [(i, (i + count) % tm_count) for i in range(tm...  2.87 us
    pallas_call x1, Pallas kernels, solver_call(): pl.pallas_call(solver_kernel, out_shape=[jax.ShapeDtypeStruct((len(PART_P...  2.47 us
    pallas_call x1, Pallas kernels, map_call(): pl.pallas_call(functools.partial(map_kernel, groups), in_specs=[pl.BlockS...  2.43 us
    pallas_call x1, Pallas kernels, beam_call(): pl.pallas_call(functools.partial(beam_kernel, chan_count, beams_local), i...  1.85 us
  transfers between devices with their start and end apart: 6, of which 2 were waited for; matrix products, arithmetic and copies ran while one was open for 0% of the time, Pallas kernels for 34%

profile of v29, /device:TPU:0, one launch (start us, length us, event | category | flops | bytes accessed | tf_op | source)
XLA Modules:
  0.0 33.4 jit_solution(5144395801309448667)
XLA Ops:
  0.0 1.9 %beams.1 = (f32[64,2048]{1,0:T(8,128)S(1)}, f32[64,2048]{1,0:T(8,128)S(1)}, f32[2,16,128]{2,1,0:T(8,128)S(1)}) custom-call(f32[2,64,64]{2,1,0:T(8,128)} %w_hbm.1, f32[128,2048]{1,0:T(8,128)} %bitcast.14, f32[2,2048]{1,0:T(2,128)} %ref_hbm.1), custom_call_target="tpu_custom_call" | custom-call | flops 2529999872 | tf_op jit(solution)/shard_map/beams/pallas_call | solution.py:162
  1.9 0.5 %collective-permute-start = (f32[64,2048]{1,0:T(8,128)S(1)}, f32[64,2048]{1,0:T(8,128)S(1)}, u32[]{:S(2)}, u32[]{:S(2)}) collective-permute-start(f32[64,2048]{1,0:T(8,128)S(1)} %get-tuple-element.16), channel_id=1, source_target_pairs={{0,8},{8,0},{16,24},{24,16},{1,9},{9,1},{17,25},{25,17},{2,10},{10... | collective-permute-start | bytes 1572872 | tf_op jit(solution)/shard_map/ppermute | solution.py:643
  2.4 2.6 %collective-permute-start.2 = (f32[1,2,16,128]{3,2,1,0:T(8,128)S(1)}, f32[1,2,16,128]{3,2,1,0:T(8,128)S(1)}, u32[]{:S(2)}, u32[]{:S(2)}) collective-permute-start(f32[1,2,16,128]{3,2,1,0:T(8,128)S(1)} %bitcast.11), channel_id=1, source_target_pairs={{0,1},{1,0},{2,3},{3,2},{4,5},{5,4},{6,7},{7,6},{8,9},{9,8},{10,11... | collective-permute-start | bytes 49160 | tf_op jit(solution)/shard_map/ppermute | solution.py:643
  5.0 0.0 collective-permute-done
  5.0 0.1 halves_summed.1
  5.0 1.9 %collective-permute-start.1 = (f32[1,32,2048]{2,1,0:T(8,128)S(1)}, f32[1,32,2048]{2,1,0:T(8,128)S(1)}, u32[]{:S(2)}, u32[]{:S(2)}) collective-permute-start(f32[1,32,2048]{2,1,0:T(8,128)S(1)} %get-tuple-element.18.refs_0_), channel_id=1, source_target_pairs={{0,16},{8,24},{16,0},{24,8},{1,17},{9,25},{17,1},{25,9},{2,18},{10... | collective-permute-start | bytes 786440 | tf_op jit(solution)/shard_map/ppermute | solution.py:643
  6.9 0.0 collective-permute-done.2.second_ref.refs_0_.refs_1_
  6.9 1.9 %collective-permute-start.3 = (f32[2,2,16,128]{3,2,1,0:T(8,128)S(1)}, f32[2,2,16,128]{3,2,1,0:T(8,128)S(1)}, u32[]{:S(2)}, u32[]{:S(2)}) collective-permute-start(f32[2,2,16,128]{3,2,1,0:T(8,128)S(1)} %reference_joined.2.first_ref), channel_id=1, source_target_pairs={{0,2},{1,3},{2,4},{3,5},{4,6},{5,7},{6,0},{7,1},{8,10},{9,11},{10,... | collective-permute-start | bytes 98312 | tf_op jit(solution)/shard_map/ppermute | solution.py:668
  8.8 0.6 %shifted_reference.1.refs_2_ = bf16[2,2,128,1920]{3,2,1,0:T(8,128)(2,1)S(1)} custom-call(f32[2,16,128]{2,1,0:T(8,128)S(1)} %get-tuple-element.19.tiles_ref), custom_call_target="tpu_custom_call" | custom-call | flops 805000000 | tf_op jit(solution)/shard_map/shifted_reference/pallas_call | solution.py:248
  9.4 3.3 %collective-permute-done.3.refs_1_.second_ref.refs_2_ = f32[2,2,16,128]{3,2,1,0:T(8,128)S(1)} collective-permute-done((f32[2,2,16,128]{3,2,1,0:T(8,128)S(1)}, f32[2,2,16,128]{3,2,1,0:T(8,128)S(1)}, u32[]{:S(2)}, u32[]{:S(2)}) %collective-permute-start.3) | collective-permute-done | bytes 32800 | tf_op jit(solution)/shard_map/ppermute | solution.py:668
  12.7 1.0 %collective-permute-start.4 = (f32[4,2,16,128]{3,2,1,0:T(8,128)S(1)}, f32[4,2,16,128]{3,2,1,0:T(8,128)S(1)}, u32[]{:S(2)}, u32[]{:S(2)}) collective-permute-start(f32[4,2,16,128]{3,2,1,0:T(8,128)S(1)} %reference_joined.3.refs_4_), channel_id=1, source_target_pairs={{0,4},{1,5},{2,6},{3,7},{4,0},{5,1},{6,2},{7,3},{8,12},{9,13},{10,... | collective-permute-start | bytes 196616 | tf_op jit(solution)/shard_map/ppermute | solution.py:668
  13.7 0.2 shifted_first.1.refs_3_
  13.9 0.0 collective-permute-done.1
  13.9 1.6 %lag_products.1.refs_4_ = f32[8,10,8,128]{3,2,1,0:T(8,128)} custom-call(f32[32,2048]{1,0:T(8,128)S(1)} %bitcast.9, f32[32,2048]{1,0:T(8,128)S(1)} %bitcast.10, bf16[2,2,128,1920]{3,2,1,0:T(8,128)(2,1)S(1)} %shifted_reference.1.refs_2_, bf16[2,2,128,256]{3,2,1,0:T(8,128)(2,1)S(1)} %shifted_first.1.refs_3_, f32[4,2,16,128]{3,2,1,0:T(8,128)S(1)} %reference_joined.3.refs_4_), custom_call_target="tpu_custom_call" | custom-call | flops 2415000064 | tf_op jit(solution)/shard_map/lag_products/pallas_call | solution.py:355
  15.5 5.7 %all-to-all-start = ((f32[8,10,8,128]{3,2,1,0:T(8,128)}), f32[8,10,8,128]{3,2,1,0:T(8,128)S(1)}, u32[]{:S(2)}, u32[]{:S(2)}) async-start(f32[8,10,8,128]{3,2,1,0:T(8,128)} %lag_products.1.refs_4_), calls=%async_computation | async-start | bytes 655360 | tf_op jit(solution)/shard_map/all_to_all | solution.py:675
  21.2 0.0 collective-permute-done.4.refs_3_
  21.2 6.5 %reference_products.1 = (bf16[3,2048,128]{2,1,0:T(8,128)(2,1)S(1)}, f32[8,128]{1,0:T(8,128)S(1)}, f32[128,128]{1,0:T(8,128)S(1)}) custom-call(f32[1,2,16,128]{3,2,1,0:T(8,128)S(1)} %bitcast.13, f32[1,2,16,128]{3,2,1,0:T(8,128)S(1)} %collective-permute-done.2.second_ref.refs_0_.refs_1_, ...), custom_call_target="tpu_custom_call" | custom-call | flops 7129999872 | tf_op jit(solution)/shard_map/reference_products/pallas_call | solution.py:467
  27.7 0.0 copy-start
  27.7 2.5 %gram_inverse.1 = (bf16[768,128]{1,0:T(8,128)(2,1)S(1)}, bf16[768,128]{1,0:T(8,128)(2,1)S(1)}) custom-call(f32[8,128]{1,0:T(8,128)S(1)} %get-tuple-element.21.line_ref, f32[128,128]{1,0:T(8,128)S(1)} %get-tuple-element.22.tail_ref), custom_call_target="tpu_custom_call" | custom-call | flops 2300000000 | tf_op jit(solution)/shard_map/gram_inverse/pallas_call | solution.py:543
  30.2 0.8 %all-to-all-done.got_ref = f32[8,10,8,128]{3,2,1,0:T(8,128)S(1)} async-done(((f32[8,10,8,128]{3,2,1,0:T(8,128)}), f32[8,10,8,128]{3,2,1,0:T(8,128)S(1)}, u32[]{:S(2)}, u32[]{:S(2)}) %all-to-all-start) | async-done | bytes 327712 | tf_op jit(solution)/shard_map/all_to_all | solution.py:675
  30.9 0.0 copy-done
  30.9 2.4 %range_doppler.1 = f32[4,4,2,32,256]{4,3,2,1,0:T(8,128)} custom-call(f32[8,10,8,128]{3,2,1,0:T(8,128)S(1)} %all-to-all-done.got_ref, bf16[3,2048,128]{2,1,0:T(8,128)(2,1)S(1)} %get-tuple-element.20.own_ref, bf16[768,128]{1,0:T(8,128)(2,1)S(1)} %get-tuple-element.23.gram_ref, bf16[768,128]{1,0:T(8,128)(2,1)S(1)} %get-tuple-element.24.solver_ref, ...), custom_call_target="tpu_custom_call" | custom-call | flops 2875000064 | tf_op jit(solution)/shard_map/range_doppler/pallas_call | solution.py:624
  (2 shorter events, 0.0 us)
Async XLA Ops:
  1.9 3.1 %collective-permute-start = (f32[64,2048]{1,0:T(8,128)S(1)}, f32[64,2048]{1,0:T(8,128)S(1)}, u32[]{:S(2)}, u32[]{:S(2)}) collective-permute-start(f32[64,2048]{1,0:T(8,128)S(1)} %get-tuple-element.16), channel_id=1, source_target_pairs={{0,8},{8,0},{16,24},{24,16},{1,9},{9,1},{17,25},{25,17},{2,10},{10... | collective-permute-start | bytes 1572872 | tf_op jit(solution)/shard_map/ppermute | solution.py:643
  2.4 4.5 %collective-permute-start.2 = (f32[1,2,16,128]{3,2,1,0:T(8,128)S(1)}, f32[1,2,16,128]{3,2,1,0:T(8,128)S(1)}, u32[]{:S(2)}, u32[]{:S(2)}) collective-permute-start(f32[1,2,16,128]{3,2,1,0:T(8,128)S(1)} %bitcast.11), channel_id=1, source_target_pairs={{0,1},{1,0},{2,3},{3,2},{4,5},{5,4},{6,7},{7,6},{8,9},{9,8},{10,11... | collective-permute-start | bytes 49160 | tf_op jit(solution)/shard_map/ppermute | solution.py:643
  5.0 8.8 %collective-permute-start.1 = (f32[1,32,2048]{2,1,0:T(8,128)S(1)}, f32[1,32,2048]{2,1,0:T(8,128)S(1)}, u32[]{:S(2)}, u32[]{:S(2)}) collective-permute-start(f32[1,32,2048]{2,1,0:T(8,128)S(1)} %get-tuple-element.18.refs_0_), channel_id=1, source_target_pairs={{0,16},{8,24},{16,0},{24,8},{1,17},{9,25},{17,1},{25,9},{2,18},{10... | collective-permute-start | bytes 786440 | tf_op jit(solution)/shard_map/ppermute | solution.py:643
  6.9 5.8 %collective-permute-start.3 = (f32[2,2,16,128]{3,2,1,0:T(8,128)S(1)}, f32[2,2,16,128]{3,2,1,0:T(8,128)S(1)}, u32[]{:S(2)}, u32[]{:S(2)}) collective-permute-start(f32[2,2,16,128]{3,2,1,0:T(8,128)S(1)} %reference_joined.2.first_ref), channel_id=1, source_target_pairs={{0,2},{1,3},{2,4},{3,5},{4,6},{5,7},{6,0},{7,1},{8,10},{9,11},{10,... | collective-permute-start | bytes 98312 | tf_op jit(solution)/shard_map/ppermute | solution.py:668
  12.7 8.5 %collective-permute-start.4 = (f32[4,2,16,128]{3,2,1,0:T(8,128)S(1)}, f32[4,2,16,128]{3,2,1,0:T(8,128)S(1)}, u32[]{:S(2)}, u32[]{:S(2)}) collective-permute-start(f32[4,2,16,128]{3,2,1,0:T(8,128)S(1)} %reference_joined.3.refs_4_), channel_id=1, source_target_pairs={{0,4},{1,5},{2,6},{3,7},{4,0},{5,1},{6,2},{7,3},{8,12},{9,13},{10,... | collective-permute-start | bytes 196616 | tf_op jit(solution)/shard_map/ppermute | solution.py:668
  15.5 15.4 %all-to-all-start = ((f32[8,10,8,128]{3,2,1,0:T(8,128)}), f32[8,10,8,128]{3,2,1,0:T(8,128)S(1)}, u32[]{:S(2)}, u32[]{:S(2)}) async-start(f32[8,10,8,128]{3,2,1,0:T(8,128)} %lag_products.1.refs_4_), calls=%async_computation | async-start | bytes 655360 | tf_op jit(solution)/shard_map/all_to_all | solution.py:675
  27.7 3.2 %copy-start = (bf16[256,512]{1,0:T(8,128)(2,1)S(1)}, bf16[256,512]{1,0:T(8,128)(2,1)}, u32[]{:S(2)}) copy-start(bf16[256,512]{1,0:T(8,128)(2,1)} %constant.2.clone.wave_ref) | copy-start | bytes 786436
